TPU v7x, 256 devices: a whole 4x4x8 slice. The times are simulated.
256 devices in a mesh: slow: 8 (over y, core), fast: 32 (over z, x).
Axes of the slice: x: 4, y: 4, z: 8, core: 2. Of those that a mesh axis runs over, the one named last changes fastest.
Arguments:
- observed: float32 [64, 512, 256], P('slow', 'fast'), may hold values from -1 to 3
- start_field: float32 [64, 512, 256], P('slow', 'fast'), may hold values from -6 to 6
- diagonal: float32 [64, 512, 256], P('slow', 'fast'), may hold values from 0.02 to 2
- noise: float32 [2, 64, 512, 256], P(None, 'slow', 'fast'), may hold values from -6 to 6
- sweeps: int32 [3], replicated, may hold values from 2 to 4, as said below
Outputs:
- sampled: float32 [64, 512, 256], P('slow', 'fast')
Inputs may be any that keep to these rules, and one draw needn't show every extreme that they name: `sweeps`: a permutation of 2, 3 and 4.
All inputs are finite; a program needn't handle non-finite values.
Results may differ from a plain program's by a relative error of at most 0.0001.
Values sent between devices are 32-bit elements; how exact they have to be, the bound alone decides.
No kernel may reach another device: no remote copies, remote signals or barrier semaphores. Data moves between devices by JAX's collectives and lax.ppermute only.
A program may use at most 128 MiB of HBM per device.

v0:
```python
import jax
import jax.numpy as jnp
from jax import lax
from jax.sharding import PartitionSpec as P

OMEGA = 0.7


def with_halo(block, sides, width):
    for axis, dim in sides:
        count = lax.axis_size(axis)
        forward = [(i, i + 1) for i in range(count - 1)]
        backward = [(target, source) for source, target in forward]
        low = lax.ppermute(
            lax.slice_in_dim(block, block.shape[dim] - width, None, axis=dim), axis, forward
        )
        high = lax.ppermute(lax.slice_in_dim(block, 0, width, axis=dim), axis, backward)
        block = jnp.concatenate([low, block, high], axis=dim)
    return block


def stencil(padded, field, diag, scale):
    padded = jnp.pad(padded, ((0, 0), (0, 0), (1, 1)))
    beside = padded[2:, 1:-1, 1:-1] + padded[:-2, 1:-1, 1:-1]
    beside = beside + padded[1:-1, 2:, 1:-1] + padded[1:-1, :-2, 1:-1]
    beside = beside + padded[1:-1, 1:-1, 2:] + padded[1:-1, 1:-1, :-2]
    return (diag + 6.0 * scale) * field - scale * beside


def apply_top(field, diag):
    padded = with_halo(field, (("slow", 0), ("fast", 1)), 1)
    return stencil(padded, field, diag, 1.0)


def apply_mid(field, diag):
    padded = with_halo(field, (("slow", 0), ("fast", 1)), 1)
    return stencil(padded, field, diag, 0.25)


def apply_whole(field, diag):
    padded = jnp.pad(field, ((1, 1), (1, 1), (0, 0)))
    return stencil(padded, field, diag, 0.0625)


def smooth(operator, error, rhs, diag, scale, count):

    def turn(index, error):
        return error + OMEGA * (rhs - operator(error, diag)) / (diag + 6.0 * scale)

    return lax.fori_loop(0, count, turn, error)


def restrict(field):
    a, b, c = field.shape
    return field.reshape(a // 2, 2, b // 2, 2, c // 2, 2).mean(axis=(1, 3, 5))


def prolong(field):
    return jnp.repeat(jnp.repeat(jnp.repeat(field, 2, 0), 2, 1), 2, 2)


def face_count(first, second, third):
    return 2.0 * (first * second + first * third + second * third)


def gather_low(field):
    columns = lax.all_gather(field, "fast", axis=1, tiled=True)
    return lax.all_gather(columns, "slow", axis=0, tiled=True)


def body(observed, start_field, diagonal, noise, sweeps):
    diag_mid = restrict(diagonal)
    diag_low = restrict(diag_mid)
    rows_top, cols_top, depth_top = diagonal.shape
    low_first = rows_top * lax.axis_size("slow") // 4
    low_second = cols_top * lax.axis_size("fast") // 4
    low_third = depth_top // 4
    faces = face_count(low_first, low_second, low_third)

    def fine_smooth(error, rhs):
        return smooth(apply_top, error, rhs, diagonal, 1.0, sweeps[0])

    diag_all = gather_low(diag_low)
    denom_all = jnp.sum(diag_all) + 0.0625 * faces
    sampled = start_field
    for step in range(noise.shape[0]):
        rhs = observed - apply_top(sampled, diagonal) + 2.0 * noise[step]
        err_top = fine_smooth(jnp.zeros_like(rhs), rhs)
        vcycle_rhs_mid = restrict(rhs - apply_top(err_top, diagonal))
        err_mid = smooth(
            apply_mid, jnp.zeros_like(vcycle_rhs_mid), vcycle_rhs_mid, diag_mid, 0.25, sweeps[1]
        )
        lower_rhs_low = restrict(vcycle_rhs_mid - apply_mid(err_mid, diag_mid))
        rhs_all = gather_low(lower_rhs_low)
        err_all = smooth(apply_whole, jnp.zeros_like(rhs_all), rhs_all, diag_all, 0.0625, sweeps[2])
        numer = jnp.sum(rhs_all - apply_whole(err_all, diag_all))
        err_all = err_all + numer / denom_all
        rows, cols, depth = lower_rhs_low.shape
        first = lax.axis_index("slow") * rows
        second = lax.axis_index("fast") * cols
        err_low = lax.dynamic_slice(err_all, (first, second, jnp.int32(0)), (rows, cols, depth))
        vcycle_err_mid = smooth(
            apply_mid, err_mid + prolong(err_low), vcycle_rhs_mid, diag_mid, 0.25, sweeps[1]
        )
        sampled = sampled + 0.5 * fine_smooth(err_top + prolong(vcycle_err_mid), rhs)
    return sampled


def solution(mesh):
    placed = (
        P("slow", "fast", None),
        P("slow", "fast", None),
        P("slow", "fast", None),
        P(None, "slow", "fast", None),
        P(),
    )
    return jax.shard_map(
        body, mesh=mesh, in_specs=placed, out_specs=P("slow", "fast", None), check_vma=False
    )
```

profile of v0, /device:TPU:129, one launch (start us, length us, event | category | flops | bytes accessed | tf_op | source)
XLA Modules:
  0.0 735.9 jit_solution(3310710167816632013)
XLA Ops:
  0.7 3.8 collective-permute-start.33
  9.6 3.9 collective-permute-start.34
  16.9 10.6 %reshape.59 = f32[4,2,8,2,128,2]{5,4,3,2,1,0:T(8,128)} reshape(f32[8,16,256]{2,1,0:T(8,128)} %param.27) | data formatting | bytes 262144 | tf_op jit(solution)/shard_map/reshape | solution.py:55
  27.4 4.1 reduce_sum.81
  32.0 42.6 %while.120 = (s32[]{:T(128)}, f32[8,16,256]{2,1,0:T(8,128)S(1)}, s32[]{:T(128)}, f32[8,16,256]{2,1,0:T(8,128)S(1)}, f32[8,16,256]{2,1,0:T(8,128)S(1)}, /*index=5*/s32[]{:T(128)}) while((s32[]{:T(128)}, f32[8,16,256]{2,1,0:T(8,128)S(1)}, s32[]{:T(128)}, f32[8,16,256]{2,1,0:T(8,128)S(1)}, f32[8,16,256]{2,1,0:T(8,128)S(1)}, ...), condition=%wide.region_1.0_spmd, body=%wide.region_0.0_spmd.sunk | while | flops 895810 | bytes 2283141 | solution.py:50
  39.9 7.0 collective-permute-start.2
  48.8 5.8 collective-permute-done.3
  55.6 3.4 collective-permute-start
  65.9 3.4 collective-permute-start.3
  69.3 4.4 collective-permute-done.3
  89.3 4.3 collective-permute-done.39
  94.0 9.8 %reshape.60 = f32[4,2,8,2,128,2]{5,4,3,2,1,0:T(8,128)} reshape(f32[8,16,256]{2,1,0:T(8,128)S(1)} %fusion.123) | data formatting | bytes 262144 | tf_op jit(solution)/shard_map/reshape | solution.py:55
  103.8 4.0 reduce_sum.82
  107.9 56.1 %while.121 = (s32[]{:T(128)}, f32[4,8,128]{2,1,0:T(8,128)S(1)}, s32[]{:T(128)}, f32[4,8,128]{2,1,0:T(8,128)S(1)}, f32[4,8,128]{2,1,0:T(8,128)S(1)}, /*index=5*/s32[]{:T(128)}) while((s32[]{:T(128)}, f32[4,8,128]{2,1,0:T(8,128)S(1)}, s32[]{:T(128)}, f32[4,8,128]{2,1,0:T(8,128)S(1)}, f32[4,8,128]{2,1,0:T(8,128)S(1)}, /*index=5*/s32[]{:T(128)}) %tuple.301), condition=%wide.region_5.6_spmd, body=%wide.region_4.5_spmd.sunk | while | flops 132034 | bytes 367301 | solution.py:50
  121.9 4.3 collective-permute-done.7
  140.4 4.3 collective-permute-done.7
  155.5 3.4 collective-permute-start.7
  158.9 4.3 collective-permute-done.7
  167.1 30.1 %all_gather.18 = f32[2,128,64]{2,0,1:T(2,128)S(1)} all-gather(f32[2,4,64]{2,0,1:T(2,128)S(1)} %copy.57), channel_id=1, replica_groups=mesh['slow'=8,'fast'=32] {'fast'}, dimensions={1}, use_global_device_ids=true | all-gather | bytes 67584 | tf_op jit(solution)/shard_map/all_gather | solution.py:67
  197.3 11.0 %collective-permute-start.40 = (f32[1,8,128]{2,1,0:T(8,128)S(1)}, f32[1,8,128]{2,1,0:T(8,128)S(1)}, u32[]{:S(2)}, u32[]{:S(2)}) collective-permute-start(f32[1,8,128]{2,1,0:T(8,128)S(1)} %get-tuple-element.951), channel_id=1, source_target_pairs={{32,0},{64,32},{96,64},{128,96},{160,128},{192,160},{224,192},{33,... | collective-permute-start | bytes 12296 | tf_op jit(solution)/shard_map/ppermute | solution.py:17
  210.8 4.3 collective-permute-start.42
  217.1 12.5 %all_gather.19 = f32[16,128,64]{1,2,0:T(8,128)S(1)} all-gather(f32[2,128,64]{1,2,0:T(8,128)S(1)} %copy.58), channel_id=1, replica_groups=mesh['slow'=8,'fast'=32] {'slow'}, dimensions={0}, use_global_device_ids=true | all-gather | bytes 589824 | tf_op jit(solution)/shard_map/all_gather | solution.py:68
  233.5 34.7 %all_gather.20 = f32[2,128,64]{2,0,1:T(2,128)S(1)} all-gather(f32[2,4,64]{2,0,1:T(2,128)S(1)} %copy.59), channel_id=1, replica_groups=mesh['slow'=8,'fast'=32] {'fast'}, dimensions={1}, use_global_device_ids=true | all-gather | bytes 67584 | tf_op jit(solution)/shard_map/all_gather | solution.py:67
  268.2 23.1 %all_gather.21 = f32[16,128,64]{1,2,0:T(8,128)S(1)} all-gather(f32[2,128,64]{1,2,0:T(8,128)S(1)} %copy.60), channel_id=1, replica_groups=mesh['slow'=8,'fast'=32] {'slow'}, dimensions={0}, use_global_device_ids=true | all-gather | bytes 589824 | tf_op jit(solution)/shard_map/all_gather | solution.py:68
  292.2 8.6 %while.122 = (s32[]{:T(128)}, f32[16,128,64]{2,1,0:T(8,128)S(1)}, s32[]{:T(128)}, f32[16,128,64]{2,1,0:T(8,128)S(1)}, f32[16,128,64]{2,1,0:T(8,128)S(1)}, /*index=5*/s32[]{:T(128)}, f32[]{:T(128)}) while((s32[]{:T(128)}, f32[16,128,64]{2,1,0:T(8,128)S(1)}, s32[]{:T(128)}, f32[16,128,64]{2,1,0:T(8,128)S(1)}, f32[16,128,64]{2,1,0:T(8,128)S(1)}, ...), condition=%wide.region_9.10_spmd, body=%wide.region_8.9_spmd.sunk | while | flops 1703938 | bytes 10241105 | solution.py:50
  307.3 58.2 %while.123 = (s32[]{:T(128)}, f32[4,8,128]{2,1,0:T(8,128)S(1)}, s32[]{:T(128)}, f32[4,8,128]{2,1,0:T(8,128)S(1)}, f32[4,8,128]{2,1,0:T(8,128)S(1)}, /*index=5*/s32[]{:T(128)}) while((s32[]{:T(128)}, f32[4,8,128]{2,1,0:T(8,128)S(1)}, s32[]{:T(128)}, f32[4,8,128]{2,1,0:T(8,128)S(1)}, f32[4,8,128]{2,1,0:T(8,128)S(1)}, ...), condition=%wide.region_13.14_spmd, body=%wide.region_12.13_spmd.sunk | while | flops 132034 | bytes 367301 | solution.py:50
  315.5 4.3 collective-permute-start.10
  321.7 5.7 collective-permute-done.11
  328.3 3.4 collective-permute-start.8
  341.9 4.3 collective-permute-done.11
  360.4 4.3 collective-permute-done.11
  368.1 38.2 %while.124 = (s32[]{:T(128)}, f32[8,16,256]{2,1,0:T(8,128)S(1)}, s32[]{:T(128)}, f32[8,16,256]{2,1,0:T(8,128)S(1)}, f32[8,16,256]{2,1,0:T(8,128)S(1)}, /*index=5*/s32[]{:T(128)}) while((s32[]{:T(128)}, f32[8,16,256]{2,1,0:T(8,128)S(1)}, s32[]{:T(128)}, f32[8,16,256]{2,1,0:T(8,128)S(1)}, f32[8,16,256]{2,1,0:T(8,128)S(1)}, ...), condition=%wide.region_15.16_spmd, body=%wide.region_14.15_spmd.sunk | while | flops 895810 | bytes 2283141 | solution.py:50
  378.9 3.4 collective-permute-start.15
  382.2 4.4 collective-permute-done.15
  397.7 3.4 collective-permute-start.15
  401.1 4.4 collective-permute-done.15
  408.5 3.6 collective-permute-start.45
  414.9 3.4 collective-permute-start.47
  418.3 4.4 collective-permute-done.47
  423.1 40.5 %while.125 = (s32[]{:T(128)}, f32[8,16,256]{2,1,0:T(8,128)S(1)}, s32[]{:T(128)}, f32[8,16,256]{2,1,0:T(8,128)S(1)}, f32[8,16,256]{2,1,0:T(8,128)S(1)}, /*index=5*/s32[]{:T(128)}) while((s32[]{:T(128)}, f32[8,16,256]{2,1,0:T(8,128)S(1)}, s32[]{:T(128)}, f32[8,16,256]{2,1,0:T(8,128)S(1)}, f32[8,16,256]{2,1,0:T(8,128)S(1)}, ...), condition=%wide.region_17.18_spmd, body=%wide.region_16.17_spmd.sunk | while | flops 895810 | bytes 2283141 | solution.py:50
  423.7 5.4 collective-permute-start.16
  439.5 4.4 collective-permute-done.19
  454.9 3.4 collective-permute-start.19
  458.3 4.4 collective-permute-done.19
  477.1 4.4 collective-permute-done.51
  481.8 9.8 %reshape.68 = f32[4,2,8,2,128,2]{5,4,3,2,1,0:T(8,128)} reshape(f32[8,16,256]{2,1,0:T(8,128)S(1)} %fusion.112) | data formatting | bytes 262144 | tf_op jit(solution)/shard_map/reshape | solution.py:55
  491.6 4.0 reduce_sum.87
  495.6 56.1 %while.126 = (s32[]{:T(128)}, f32[4,8,128]{2,1,0:T(8,128)S(1)}, s32[]{:T(128)}, f32[4,8,128]{2,1,0:T(8,128)S(1)}, f32[4,8,128]{2,1,0:T(8,128)S(1)}, /*index=5*/s32[]{:T(128)}) while((s32[]{:T(128)}, f32[4,8,128]{2,1,0:T(8,128)S(1)}, s32[]{:T(128)}, f32[4,8,128]{2,1,0:T(8,128)S(1)}, f32[4,8,128]{2,1,0:T(8,128)S(1)}, ...), condition=%wide.region_20.21_spmd, body=%wide.region_19.20_spmd.sunk | while | flops 132034 | bytes 367301 | solution.py:50
  509.6 4.3 collective-permute-done.23
  528.1 4.3 collective-permute-done.23
  546.6 4.3 collective-permute-done.23
  570.8 30.1 %all_gather.22 = f32[2,128,64]{2,0,1:T(2,128)S(1)} all-gather(f32[2,4,64]{2,0,1:T(2,128)S(1)} %copy.72), channel_id=1, replica_groups=mesh['slow'=8,'fast'=32] {'fast'}, dimensions={1}, use_global_device_ids=true | all-gather | bytes 67584 | tf_op jit(solution)/shard_map/all_gather | solution.py:67
  601.0 22.5 %all_gather.23 = f32[16,128,64]{1,2,0:T(8,128)S(1)} all-gather(f32[2,128,64]{1,2,0:T(8,128)S(1)} %copy.73), channel_id=1, replica_groups=mesh['slow'=8,'fast'=32] {'slow'}, dimensions={0}, use_global_device_ids=true | all-gather | bytes 589824 | tf_op jit(solution)/shard_map/all_gather | solution.py:68
  624.7 8.6 %while.127 = (s32[]{:T(128)}, f32[16,128,64]{2,1,0:T(8,128)S(1)}, s32[]{:T(128)}, f32[16,128,64]{2,1,0:T(8,128)S(1)}, f32[16,128,64]{2,1,0:T(8,128)S(1)}, /*index=5*/s32[]{:T(128)}, f32[]{:T(128)}) while((s32[]{:T(128)}, f32[16,128,64]{2,1,0:T(8,128)S(1)}, s32[]{:T(128)}, f32[16,128,64]{2,1,0:T(8,128)S(1)}, f32[16,128,64]{2,1,0:T(8,128)S(1)}, ...), condition=%wide.region_23.24_spmd, body=%wide.region_22.23_spmd.sunk | while | flops 1703938 | bytes 10241105 | solution.py:50
  636.9 59.3 %while.128 = (s32[]{:T(128)}, f32[4,8,128]{2,1,0:T(8,128)S(1)}, s32[]{:T(128)}, f32[4,8,128]{2,1,0:T(8,128)S(1)}, f32[4,8,128]{2,1,0:T(8,128)S(1)}, /*index=5*/s32[]{:T(128)}) while((s32[]{:T(128)}, f32[4,8,128]{2,1,0:T(8,128)S(1)}, s32[]{:T(128)}, f32[4,8,128]{2,1,0:T(8,128)S(1)}, f32[4,8,128]{2,1,0:T(8,128)S(1)}, ...), condition=%wide.region_26.27_spmd, body=%wide.region_25.26_spmd.sunk | while | flops 132034 | bytes 367301 | solution.py:50
  637.6 3.5 collective-permute-start.24
  646.1 4.3 collective-permute-start.26
  652.4 5.7 collective-permute-done.27
  659.0 3.4 collective-permute-start.24
  672.6 4.3 collective-permute-done.27
  691.1 4.3 collective-permute-done.27
  697.0 38.2 %while.129 = (s32[]{:T(128)}, f32[8,16,256]{2,1,0:T(8,128)S(1)}, s32[]{:T(128)}, f32[8,16,256]{2,1,0:T(8,128)S(1)}, f32[8,16,256]{2,1,0:T(8,128)S(1)}, /*index=5*/s32[]{:T(128)}) while((s32[]{:T(128)}, f32[8,16,256]{2,1,0:T(8,128)S(1)}, s32[]{:T(128)}, f32[8,16,256]{2,1,0:T(8,128)S(1)}, f32[8,16,256]{2,1,0:T(8,128)S(1)}, ...), condition=%wide.region_28.29_spmd, body=%wide.region_27.28_spmd.sunk | while | flops 895810 | bytes 2283141 | solution.py:50
  711.1 4.4 collective-permute-done.31
  729.9 4.4 collective-permute-done.31
  (491 shorter events, 326.0 us)
Async XLA Ops:
  0.7 5.7 collective-permute-start.33
  4.5 5.1 collective-permute-start.32
  9.6 21.9 %collective-permute-start.34 = (f32[10,1,256]{2,1,0:T(1,128)S(1)}, f32[10,1,256]{2,1,0:T(1,128)S(1)}, u32[]{:S(2)}, u32[]{:S(2)}) collective-permute-start(f32[10,1,256]{2,1,0:T(1,128)S(1)} %get-tuple-element.936), channel_id=1, source_target_pairs={{1,0},{2,1},{3,2},{4,3},{5,4},{6,5},{7,6},{8,7},{9,8},{10,9},{11,1... | collective-permute-start | bytes 30728 | tf_op jit(solution)/shard_map/ppermute | solution.py:17
  13.5 18.0 %collective-permute-start.35 = (f32[10,1,256]{2,1,0:T(1,128)S(1)}, f32[10,1,256]{2,1,0:T(1,128)S(1)}, u32[]{:S(2)}, u32[]{:S(2)}) collective-permute-start(f32[10,1,256]{2,1,0:T(1,128)S(1)} %get-tuple-element.935), channel_id=1, source_target_pairs={{0,1},{1,2},{2,3},{3,4},{4,5},{5,6},{6,7},{7,8},{8,9},{9,10},{10,1... | collective-permute-start | bytes 30728 | tf_op jit(solution)/shard_map/ppermute | solution.py:14
  34.8 5.1 collective-permute-start.1
  39.9 8.9 %collective-permute-start.2 = (f32[10,1,256]{2,1,0:T(1,128)S(1)}, f32[10,1,256]{2,1,0:T(1,128)S(1)}, u32[]{:S(2)}, u32[]{:S(2)}) collective-permute-start(f32[10,1,256]{2,1,0:T(1,128)S(1)} %get-tuple-element.1265), channel_id=1, source_target_pairs={{1,0},{2,1},{3,2},{4,3},{5,4},{6,5},{7,6},{8,7},{9,8},{10,9},{11,1... | collective-permute-start | bytes 30728 | tf_op jit(solution)/shard_map/while/body/ppermute | solution.py:17
  46.9 7.7 %collective-permute-start.3 = (f32[10,1,256]{2,1,0:T(1,128)S(1)}, f32[10,1,256]{2,1,0:T(1,128)S(1)}, u32[]{:S(2)}, u32[]{:S(2)}) collective-permute-start(f32[10,1,256]{2,1,0:T(1,128)S(1)} %get-tuple-element.1266), channel_id=1, source_target_pairs={{0,1},{1,2},{2,3},{3,4},{4,5},{5,6},{6,7},{7,8},{8,9},{9,10},{10,1... | collective-permute-start | bytes 30728 | tf_op jit(solution)/shard_map/while/body/ppermute | solution.py:14
  55.6 5.3 collective-permute-start
  64.0 5.3 collective-permute-start.2
  65.9 7.7 %collective-permute-start.3 = (f32[10,1,256]{2,1,0:T(1,128)S(1)}, f32[10,1,256]{2,1,0:T(1,128)S(1)}, u32[]{:S(2)}, u32[]{:S(2)}) collective-permute-start(f32[10,1,256]{2,1,0:T(1,128)S(1)} %get-tuple-element.1266), channel_id=1, source_target_pairs={{0,1},{1,2},{2,3},{3,4},{4,5},{5,6},{6,7},{7,8},{8,9},{9,10},{10,1... | collective-permute-start | bytes 30728 | tf_op jit(solution)/shard_map/while/body/ppermute | solution.py:14
  74.6 6.2 collective-permute-start.37
  84.0 5.3 collective-permute-start.38
  85.9 7.7 %collective-permute-start.39 = (f32[10,1,256]{2,1,0:T(1,128)S(1)}, f32[10,1,256]{2,1,0:T(1,128)S(1)}, u32[]{:S(2)}, u32[]{:S(2)}) collective-permute-start(f32[10,1,256]{2,1,0:T(1,128)S(1)} %get-tuple-element.933), channel_id=1, source_target_pairs={{0,1},{1,2},{2,3},{3,4},{4,5},{5,6},{6,7},{7,8},{8,9},{9,10},{10,1... | collective-permute-start | bytes 30728 | tf_op jit(solution)/shard_map/ppermute | solution.py:14
  116.6 5.3 collective-permute-start.6
  118.5 7.7 %collective-permute-start.7 = (f32[6,1,128]{2,1,0:T(1,128)S(1)}, f32[6,1,128]{2,1,0:T(1,128)S(1)}, u32[]{:S(2)}, u32[]{:S(2)}) collective-permute-start(f32[6,1,128]{2,1,0:T(1,128)S(1)} %get-tuple-element.1275), channel_id=1, source_target_pairs={{0,1},{1,2},{2,3},{3,4},{4,5},{5,6},{6,7},{7,8},{8,9},{9,10},{10,1... | collective-permute-start | bytes 9224 | tf_op jit(solution)/shard_map/while/body/ppermute | solution.py:14
  135.1 5.3 collective-permute-start.6
  137.0 7.7 %collective-permute-start.7 = (f32[6,1,128]{2,1,0:T(1,128)S(1)}, f32[6,1,128]{2,1,0:T(1,128)S(1)}, u32[]{:S(2)}, u32[]{:S(2)}) collective-permute-start(f32[6,1,128]{2,1,0:T(1,128)S(1)} %get-tuple-element.1275), channel_id=1, source_target_pairs={{0,1},{1,2},{2,3},{3,4},{4,5},{5,6},{6,7},{7,8},{8,9},{9,10},{10,1... | collective-permute-start | bytes 9224 | tf_op jit(solution)/shard_map/while/body/ppermute | solution.py:14
  153.6 5.3 collective-permute-start.6
  155.5 7.7 %collective-permute-start.7 = (f32[6,1,128]{2,1,0:T(1,128)S(1)}, f32[6,1,128]{2,1,0:T(1,128)S(1)}, u32[]{:S(2)}, u32[]{:S(2)}) collective-permute-start(f32[6,1,128]{2,1,0:T(1,128)S(1)} %get-tuple-element.1275), channel_id=1, source_target_pairs={{0,1},{1,2},{2,3},{3,4},{4,5},{5,6},{6,7},{7,8},{8,9},{9,10},{10,1... | collective-permute-start | bytes 9224 | tf_op jit(solution)/shard_map/while/body/ppermute | solution.py:14
  164.0 44.3 %collective-permute-start.41 = (f32[1,8,128]{2,1,0:T(8,128)S(1)}, f32[1,8,128]{2,1,0:T(8,128)S(1)}, u32[]{:S(2)}, u32[]{:S(2)}) collective-permute-start(f32[1,8,128]{2,1,0:T(8,128)S(1)} %get-tuple-element.952), channel_id=1, source_target_pairs={{0,32},{32,64},{64,96},{96,128},{128,160},{160,192},{192,224},{1,3... | collective-permute-start | bytes 12296 | tf_op jit(solution)/shard_map/ppermute | solution.py:14
  197.3 13.5 %collective-permute-start.40 = (f32[1,8,128]{2,1,0:T(8,128)S(1)}, f32[1,8,128]{2,1,0:T(8,128)S(1)}, u32[]{:S(2)}, u32[]{:S(2)}) collective-permute-start(f32[1,8,128]{2,1,0:T(8,128)S(1)} %get-tuple-element.951), channel_id=1, source_target_pairs={{32,0},{64,32},{96,64},{128,96},{160,128},{192,160},{224,192},{33,... | collective-permute-start | bytes 12296 | tf_op jit(solution)/shard_map/ppermute | solution.py:17
  210.8 21.2 %collective-permute-start.42 = (f32[6,1,128]{2,1,0:T(1,128)S(1)}, f32[6,1,128]{2,1,0:T(1,128)S(1)}, u32[]{:S(2)}, u32[]{:S(2)}) collective-permute-start(f32[6,1,128]{2,1,0:T(1,128)S(1)} %get-tuple-element.948), channel_id=1, source_target_pairs={{1,0},{2,1},{3,2},{4,3},{5,4},{6,5},{7,6},{8,7},{9,8},{10,9},{11,1... | collective-permute-start | bytes 9224 | tf_op jit(solution)/shard_map/ppermute | solution.py:17
  215.1 16.9 %collective-permute-start.43 = (f32[6,1,128]{2,1,0:T(1,128)S(1)}, f32[6,1,128]{2,1,0:T(1,128)S(1)}, u32[]{:S(2)}, u32[]{:S(2)}) collective-permute-start(f32[6,1,128]{2,1,0:T(1,128)S(1)} %get-tuple-element.947), channel_id=1, source_target_pairs={{0,1},{1,2},{2,3},{3,4},{4,5},{5,6},{6,7},{7,8},{8,9},{9,10},{10,1... | collective-permute-start | bytes 9224 | tf_op jit(solution)/shard_map/ppermute | solution.py:14
  315.5 6.2 collective-permute-start.10
  319.8 7.7 %collective-permute-start.11 = (f32[6,1,128]{2,1,0:T(1,128)S(1)}, f32[6,1,128]{2,1,0:T(1,128)S(1)}, u32[]{:S(2)}, u32[]{:S(2)}) collective-permute-start(f32[6,1,128]{2,1,0:T(1,128)S(1)} %get-tuple-element.1289), channel_id=1, source_target_pairs={{0,1},{1,2},{2,3},{3,4},{4,5},{5,6},{6,7},{7,8},{8,9},{9,10},{10,1... | collective-permute-start | bytes 9224 | tf_op jit(solution)/shard_map/while/body/ppermute | solution.py:14
  328.3 5.3 collective-permute-start.8
  336.6 5.3 collective-permute-start.10
  338.6 7.7 %collective-permute-start.11 = (f32[6,1,128]{2,1,0:T(1,128)S(1)}, f32[6,1,128]{2,1,0:T(1,128)S(1)}, u32[]{:S(2)}, u32[]{:S(2)}) collective-permute-start(f32[6,1,128]{2,1,0:T(1,128)S(1)} %get-tuple-element.1289), channel_id=1, source_target_pairs={{0,1},{1,2},{2,3},{3,4},{4,5},{5,6},{6,7},{7,8},{8,9},{9,10},{10,1... | collective-permute-start | bytes 9224 | tf_op jit(solution)/shard_map/while/body/ppermute | solution.py:14
  355.1 5.3 collective-permute-start.10
  357.0 7.7 %collective-permute-start.11 = (f32[6,1,128]{2,1,0:T(1,128)S(1)}, f32[6,1,128]{2,1,0:T(1,128)S(1)}, u32[]{:S(2)}, u32[]{:S(2)}) collective-permute-start(f32[6,1,128]{2,1,0:T(1,128)S(1)} %get-tuple-element.1289), channel_id=1, source_target_pairs={{0,1},{1,2},{2,3},{3,4},{4,5},{5,6},{6,7},{7,8},{8,9},{9,10},{10,1... | collective-permute-start | bytes 9224 | tf_op jit(solution)/shard_map/while/body/ppermute | solution.py:14
  376.9 5.3 collective-permute-start.14
  378.9 7.7 %collective-permute-start.15 = (f32[10,1,256]{2,1,0:T(1,128)S(1)}, f32[10,1,256]{2,1,0:T(1,128)S(1)}, u32[]{:S(2)}, u32[]{:S(2)}) collective-permute-start(f32[10,1,256]{2,1,0:T(1,128)S(1)} %get-tuple-element.1298), channel_id=1, source_target_pairs={{0,1},{1,2},{2,3},{3,4},{4,5},{5,6},{6,7},{7,8},{8,9},{9,10},{10,1... | collective-permute-start | bytes 30728 | tf_op jit(solution)/shard_map/while/body/ppermute | solution.py:14
  395.8 5.3 collective-permute-start.14
  397.7 7.7 %collective-permute-start.15 = (f32[10,1,256]{2,1,0:T(1,128)S(1)}, f32[10,1,256]{2,1,0:T(1,128)S(1)}, u32[]{:S(2)}, u32[]{:S(2)}) collective-permute-start(f32[10,1,256]{2,1,0:T(1,128)S(1)} %get-tuple-element.1298), channel_id=1, source_target_pairs={{0,1},{1,2},{2,3},{3,4},{4,5},{5,6},{6,7},{7,8},{8,9},{9,10},{10,1... | collective-permute-start | bytes 30728 | tf_op jit(solution)/shard_map/while/body/ppermute | solution.py:14
  406.4 5.7 collective-permute-start.44
  413.0 5.3 collective-permute-start.46
  414.9 7.7 %collective-permute-start.47 = (f32[10,1,256]{2,1,0:T(1,128)S(1)}, f32[10,1,256]{2,1,0:T(1,128)S(1)}, u32[]{:S(2)}, u32[]{:S(2)}) collective-permute-start(f32[10,1,256]{2,1,0:T(1,128)S(1)} %get-tuple-element.931), channel_id=1, source_target_pairs={{0,1},{1,2},{2,3},{3,4},{4,5},{5,6},{6,7},{7,8},{8,9},{9,10},{10,1... | collective-permute-start | bytes 30728 | tf_op jit(solution)/shard_map/ppermute | solution.py:14
  423.7 7.3 collective-permute-start.16
  434.1 5.3 collective-permute-start.18
  436.1 7.7 %collective-permute-start.19 = (f32[10,1,256]{2,1,0:T(1,128)S(1)}, f32[10,1,256]{2,1,0:T(1,128)S(1)}, u32[]{:S(2)}, u32[]{:S(2)}) collective-permute-start(f32[10,1,256]{2,1,0:T(1,128)S(1)} %get-tuple-element.1307), channel_id=1, source_target_pairs={{0,1},{1,2},{2,3},{3,4},{4,5},{5,6},{6,7},{7,8},{8,9},{9,10},{10,1... | collective-permute-start | bytes 30728 | tf_op jit(solution)/shard_map/while/body/ppermute | solution.py:14
  453.0 5.3 collective-permute-start.18
  454.9 7.7 %collective-permute-start.19 = (f32[10,1,256]{2,1,0:T(1,128)S(1)}, f32[10,1,256]{2,1,0:T(1,128)S(1)}, u32[]{:S(2)}, u32[]{:S(2)}) collective-permute-start(f32[10,1,256]{2,1,0:T(1,128)S(1)} %get-tuple-element.1307), channel_id=1, source_target_pairs={{0,1},{1,2},{2,3},{3,4},{4,5},{5,6},{6,7},{7,8},{8,9},{9,10},{10,1... | collective-permute-start | bytes 30728 | tf_op jit(solution)/shard_map/while/body/ppermute | solution.py:14
  471.7 5.3 collective-permute-start.50
  473.7 7.7 %collective-permute-start.51 = (f32[10,1,256]{2,1,0:T(1,128)S(1)}, f32[10,1,256]{2,1,0:T(1,128)S(1)}, u32[]{:S(2)}, u32[]{:S(2)}) collective-permute-start(f32[10,1,256]{2,1,0:T(1,128)S(1)} %get-tuple-element.929), channel_id=1, source_target_pairs={{0,1},{1,2},{2,3},{3,4},{4,5},{5,6},{6,7},{7,8},{8,9},{9,10},{10,1... | collective-permute-start | bytes 30728 | tf_op jit(solution)/shard_map/ppermute | solution.py:14
  504.3 5.3 collective-permute-start.22
  506.3 7.7 %collective-permute-start.23 = (f32[6,1,128]{2,1,0:T(1,128)S(1)}, f32[6,1,128]{2,1,0:T(1,128)S(1)}, u32[]{:S(2)}, u32[]{:S(2)}) collective-permute-start(f32[6,1,128]{2,1,0:T(1,128)S(1)} %get-tuple-element.1316), channel_id=1, source_target_pairs={{0,1},{1,2},{2,3},{3,4},{4,5},{5,6},{6,7},{7,8},{8,9},{9,10},{10,1... | collective-permute-start | bytes 9224 | tf_op jit(solution)/shard_map/while/body/ppermute | solution.py:14
  522.8 5.3 collective-permute-start.22
  524.7 7.7 %collective-permute-start.23 = (f32[6,1,128]{2,1,0:T(1,128)S(1)}, f32[6,1,128]{2,1,0:T(1,128)S(1)}, u32[]{:S(2)}, u32[]{:S(2)}) collective-permute-start(f32[6,1,128]{2,1,0:T(1,128)S(1)} %get-tuple-element.1316), channel_id=1, source_target_pairs={{0,1},{1,2},{2,3},{3,4},{4,5},{5,6},{6,7},{7,8},{8,9},{9,10},{10,1... | collective-permute-start | bytes 9224 | tf_op jit(solution)/shard_map/while/body/ppermute | solution.py:14
  541.3 5.3 collective-permute-start.22
  543.2 7.7 %collective-permute-start.23 = (f32[6,1,128]{2,1,0:T(1,128)S(1)}, f32[6,1,128]{2,1,0:T(1,128)S(1)}, u32[]{:S(2)}, u32[]{:S(2)}) collective-permute-start(f32[6,1,128]{2,1,0:T(1,128)S(1)} %get-tuple-element.1316), channel_id=1, source_target_pairs={{0,1},{1,2},{2,3},{3,4},{4,5},{5,6},{6,7},{7,8},{8,9},{9,10},{10,1... | collective-permute-start | bytes 9224 | tf_op jit(solution)/shard_map/while/body/ppermute | solution.py:14
  559.8 7.4 %collective-permute-start.54 = (f32[6,1,128]{2,1,0:T(1,128)S(1)}, f32[6,1,128]{2,1,0:T(1,128)S(1)}, u32[]{:S(2)}, u32[]{:S(2)}) collective-permute-start(f32[6,1,128]{2,1,0:T(1,128)S(1)} %get-tuple-element.946), channel_id=1, source_target_pairs={{1,0},{2,1},{3,2},{4,3},{5,4},{6,5},{7,6},{8,7},{9,8},{10,9},{11,1... | collective-permute-start | bytes 9224 | tf_op jit(solution)/shard_map/ppermute | solution.py:17
  561.7 7.7 %collective-permute-start.55 = (f32[6,1,128]{2,1,0:T(1,128)S(1)}, f32[6,1,128]{2,1,0:T(1,128)S(1)}, u32[]{:S(2)}, u32[]{:S(2)}) collective-permute-start(f32[6,1,128]{2,1,0:T(1,128)S(1)} %get-tuple-element.945), channel_id=1, source_target_pairs={{0,1},{1,2},{2,3},{3,4},{4,5},{5,6},{6,7},{7,8},{8,9},{9,10},{10,1... | collective-permute-start | bytes 9224 | tf_op jit(solution)/shard_map/ppermute | solution.py:14
  637.6 5.5 collective-permute-start.24
  646.1 6.3 collective-permute-start.26
  650.5 7.7 %collective-permute-start.27 = (f32[6,1,128]{2,1,0:T(1,128)S(1)}, f32[6,1,128]{2,1,0:T(1,128)S(1)}, u32[]{:S(2)}, u32[]{:S(2)}) collective-permute-start(f32[6,1,128]{2,1,0:T(1,128)S(1)} %get-tuple-element.1330), channel_id=1, source_target_pairs={{0,1},{1,2},{2,3},{3,4},{4,5},{5,6},{6,7},{7,8},{8,9},{9,10},{10,1... | collective-permute-start | bytes 9224 | tf_op jit(solution)/shard_map/while/body/ppermute | solution.py:14
  659.0 5.3 collective-permute-start.24
  667.3 5.3 collective-permute-start.26
  669.2 7.7 %collective-permute-start.27 = (f32[6,1,128]{2,1,0:T(1,128)S(1)}, f32[6,1,128]{2,1,0:T(1,128)S(1)}, u32[]{:S(2)}, u32[]{:S(2)}) collective-permute-start(f32[6,1,128]{2,1,0:T(1,128)S(1)} %get-tuple-element.1330), channel_id=1, source_target_pairs={{0,1},{1,2},{2,3},{3,4},{4,5},{5,6},{6,7},{7,8},{8,9},{9,10},{10,1... | collective-permute-start | bytes 9224 | tf_op jit(solution)/shard_map/while/body/ppermute | solution.py:14
  685.8 5.3 collective-permute-start.26
  687.7 7.7 %collective-permute-start.27 = (f32[6,1,128]{2,1,0:T(1,128)S(1)}, f32[6,1,128]{2,1,0:T(1,128)S(1)}, u32[]{:S(2)}, u32[]{:S(2)}) collective-permute-start(f32[6,1,128]{2,1,0:T(1,128)S(1)} %get-tuple-element.1330), channel_id=1, source_target_pairs={{0,1},{1,2},{2,3},{3,4},{4,5},{5,6},{6,7},{7,8},{8,9},{9,10},{10,1... | collective-permute-start | bytes 9224 | tf_op jit(solution)/shard_map/while/body/ppermute | solution.py:14
  705.8 5.3 collective-permute-start.30
  707.7 7.7 %collective-permute-start.31 = (f32[10,1,256]{2,1,0:T(1,128)S(1)}, f32[10,1,256]{2,1,0:T(1,128)S(1)}, u32[]{:S(2)}, u32[]{:S(2)}) collective-permute-start(f32[10,1,256]{2,1,0:T(1,128)S(1)} %get-tuple-element.1339), channel_id=1, source_target_pairs={{0,1},{1,2},{2,3},{3,4},{4,5},{5,6},{6,7},{7,8},{8,9},{9,10},{10,1... | collective-permute-start | bytes 30728 | tf_op jit(solution)/shard_map/while/body/ppermute | solution.py:14
  724.6 5.3 collective-permute-start.30
  726.5 7.7 %collective-permute-start.31 = (f32[10,1,256]{2,1,0:T(1,128)S(1)}, f32[10,1,256]{2,1,0:T(1,128)S(1)}, u32[]{:S(2)}, u32[]{:S(2)}) collective-permute-start(f32[10,1,256]{2,1,0:T(1,128)S(1)} %get-tuple-element.1339), channel_id=1, source_target_pairs={{0,1},{1,2},{2,3},{3,4},{4,5},{5,6},{6,7},{7,8},{8,9},{9,10},{10,1... | collective-permute-start | bytes 30728 | tf_op jit(solution)/shard_map/while/body/ppermute | solution.py:14
  (62 other events, 657.7 us)
where the time goes:
time: 740 us; the launch traced here: 736 us
  starting transfers between devices  287 us (39%)
  waiting for transfers between devices  181 us (24%)
  blocking collectives  153 us (21%)
  local copies, waits for them, and re-layouts  51.3 us (7%)
  other arithmetic  34.1 us (5%)
  loops' own time  26.5 us (4%)
    ppermute x52, starting transfers between devices, with_halo(): lax.ppermute(lax.slice_in_dim(block, block.shape[dim] - width, None, axis...  164 us
    ppermute x52, starting transfers between devices, with_halo(): lax.ppermute(lax.slice_in_dim(block, 0, width, axis=dim), axis, backward)  124 us
    ppermute x52, waiting for transfers between devices, with_halo(): lax.ppermute(lax.slice_in_dim(block, block.shape[dim] - width, None, axis...  107 us
    all_gather x3, blocking collectives, gather_low(): columns = lax.all_gather(field, 'fast', axis=1, tiled=True)  95 us
    ppermute x52, waiting for transfers between devices, with_halo(): lax.ppermute(lax.slice_in_dim(block, 0, width, axis=dim), axis, backward)  73.9 us
    all_gather x3, blocking collectives, gather_low(): return lax.all_gather(columns, 'slow', axis=0, tiled=True)  58 us
    reshape x5, local copies, waits for them, and re-layouts, restrict(): return field.reshape(a // 2, 2, b // 2, 2, c // 2, 2).mean(axis=(1, 3, 5))  32.2 us
    another operation x10, loops' own time, smooth(): return lax.fori_loop(0, count, turn, error)  26.5 us
  transfers between devices with their start and end apart: 104, of which 50 were waited for; matrix products, arithmetic and copies ran while one was open for 3% of the time, Pallas kernels for 0%

commit v1 on v0

v1 whole, which is shorter than its diff:
```python
import functools

import jax
import jax.numpy as jnp
from jax import lax
from jax.experimental import pallas as pl
from jax.experimental.pallas import tpu as pltpu
from jax.sharding import PartitionSpec as P

OMEGA = 0.7
KEEP = 1.0 - OMEGA
F32 = jnp.float32

YB, ZB, LANES = 8, 8, 128
YW, ZW = 3 * YB, 3 * ZB
ZM = 40
YM = 32
YPOST = 16


def lane_iota(rows):
    return lax.broadcasted_iota(jnp.int32, (rows, LANES), 1)


def row_iota(rows):
    return lax.broadcasted_iota(jnp.int32, (rows, LANES), 0)


def parity_matrix(transposed):
    row = lax.broadcasted_iota(jnp.int32, (2 * LANES, 2 * LANES), 0)
    col = lax.broadcasted_iota(jnp.int32, (2 * LANES, 2 * LANES), 1)
    if transposed:
        row, col = col, row
    return jnp.where(row == 2 * (col & (LANES - 1)) + (col >> 7), 1.0, 0.0).astype(F32)


def exact_dot(a, b):
    return lax.dot(a, b, precision=lax.Precision.HIGHEST, preferred_element_type=F32)


def fine_neighbours(u, lead, y, lanes):
    rows = u.shape[-2]
    here = [[u[(*lead, pz, px, y)] for px in range(2)] for pz in range(2)]
    beside = [[None, None], [None, None]]
    for pz in range(2):
        for px in range(2):
            total = u[(*lead, pz, px, y - 1)] + u[(*lead, pz, px, y + 1)]
            other = here[1 - pz][px]
            total = total + (other + pltpu.roll(other, 1 if pz == 0 else rows - 1, 0))
            other = here[pz][1 - px]
            if px == 0:
                moved = jnp.where(lanes == 0, 0.0, pltpu.roll(other, 1, 1))
            else:
                moved = jnp.where(lanes == LANES - 1, 0.0, pltpu.roll(other, LANES - 1, 1))
            beside[pz][px] = total + (other + moved)
    return here, beside


def flat_neighbours(u, lead, y, lanes, step):
    rows = u.shape[-2]
    here = u[(*lead, y)]
    total = u[(*lead, y - 1)] + u[(*lead, y + 1)]
    total = total + (pltpu.roll(here, 1, 0) + pltpu.roll(here, rows - 1, 0))
    left = jnp.where(lanes < step, 0.0, pltpu.roll(here, step, 1))
    right = jnp.where(lanes >= LANES - step, 0.0, pltpu.roll(here, LANES - step, 1))
    return here, total + (left + right)


def fine_sweeps(u, q, k, count, first, rows, lanes):
    def sweep(turn, at):
        def one(y, carry):
            here, beside = fine_neighbours(u, (at,), y + 1, lanes)
            for pz in range(2):
                for px in range(2):
                    u[1 - at, pz, px, y + 1] = (
                        KEEP * here[pz][px] + q[pz, px, y] + k[pz, px, y] * beside[pz][px]
                    )
            return carry

        lax.fori_loop(0, rows, one, 0, unroll=2)
        return 1 - at

    return lax.fori_loop(0, count, sweep, jnp.int32(first))


def flat_sweeps(u, q, k, count, first, low, rows, lanes, step, unroll, shift=0):
    def sweep(turn, at):
        def one(y, carry):
            here, beside = flat_neighbours(u, (at,), y, lanes, step)
            u[1 - at, y] = KEEP * here + q[y - shift] + k[y - shift] * beside
            return carry

        lax.fori_loop(low, low + rows, one, 0, unroll=unroll)
        return 1 - at

    return lax.fori_loop(0, count, sweep, jnp.int32(first))


def split_kernel(observed, start, diagonal, noise, fields, later, halves):
    matrix = parity_matrix(False)
    jobs = (
        (start[...], fields.at[0]),
        (observed[...] + 2.0 * noise[0], fields.at[1]),
        (diagonal[...], fields.at[2]),
        (observed[...] + 2.0 * noise[1], later),
    )
    for n, (value, out) in enumerate(jobs):
        both = exact_dot(value.reshape(YB * 2 * ZB, 2 * LANES), matrix)
        for px in range(2):
            halves[n, px] = both[:, px * LANES : (px + 1) * LANES]
        for pz in range(2):
            for px in range(2):
                part = halves[n, px, pl.ds(pz, YB * ZB, stride=2), :]
                out[pz, px] = part.reshape(YB, ZB, LANES)


def inside(axis, which):
    at = lax.axis_index(axis) + (which - 1)
    return jnp.where((at >= 0) & (at < lax.axis_size(axis)), 1.0, 0.0).astype(F32)


def wide(ref, zb_field, pz, px, y):
    return jnp.concatenate([ref[zb, zb_field, pz, px, y] for zb in range(3)], axis=0)


def before_kernel(first, sweeps, *refs):
    if first:
        mid, low, high = refs[:3]
        left_out, own_out, right_out, epre, qpost, kpost, k, dn = refs[3:11]
        u, q = refs[11:]
    else:
        mid, low, high, k, dn = refs[:5]
        left_out, own_out, right_out, epre, qpost = refs[5:10]
        u, q = refs[10:]
    lanes = lane_iota(ZW)
    rows = row_iota(ZW)
    mask_z = [inside("fast", b) for b in range(3)]
    mask_y = [inside("slow", b) for b in range(3)]
    row_mask = jnp.where(rows < ZB, mask_z[0], jnp.where(rows < 2 * ZB, 1.0, mask_z[2]))
    zero = jnp.zeros((ZW, LANES), F32)
    for at in range(2):
        for pz in range(2):
            for px in range(2):
                u[at, pz, px, 0] = zero
                u[at, pz, px, YW + 1] = zero
    blocks = (low, mid, high)
    for yb, ref in enumerate(blocks):

        def fill(y, carry):
            for pz in range(2):
                for px in range(2):
                    value = wide(ref, 0, pz, px, y)
                    u[0, pz, px, 1 + yb * YB + y] = jnp.where(row_mask * mask_y[yb] > 0.5, value, 0.0)
            return carry

        lax.fori_loop(0, YB, fill, 0, unroll=2)
    for yb, ref in enumerate(blocks):

        def right_side(y, carry):
            row = yb * YB + y
            here, beside = fine_neighbours(u, (0,), row + 1, lanes)
            for pz in range(2):
                for px in range(2):
                    if first:
                        full = wide(ref, 2, pz, px, y) + 6.0
                        gain = (OMEGA / full) * (row_mask * mask_y[yb])
                        k[pz, px, row] = gain
                        if yb == 1:
                            dn[pz, px, y] = full * (1.0 / OMEGA)
                        rhs = wide(ref, 1, pz, px, y) - full * here[pz][px] + beside[pz][px]
                        start = gain * rhs
                    else:
                        gain = k[pz, px, row]
                        start = gain * (wide(ref, 1, pz, px, y) + beside[pz][px]) - OMEGA * here[pz][px]
                    q[pz, px, row] = start
                    u[1, pz, px, row + 1] = start
            return carry

        lax.fori_loop(0, YB, right_side, 0, unroll=2)
    at = fine_sweeps(u, q, k, sweeps[0] - 1, 1, YW, lanes)

    def restrict(ym, carry):
        total = zero
        diag = zero
        for half in range(2):
            row = YB + 2 * ym + half
            here, beside = fine_neighbours(u, (at,), row + 1, lanes)
            for pz in range(2):
                for px in range(2):
                    scaled = q[pz, px, row] - OMEGA * here[pz][px] + k[pz, px, row] * beside[pz][px]
                    total = total + scaled * dn[pz, px, 2 * ym + half]
                    if first:
                        diag = diag + wide(mid, 2, pz, px, 2 * ym + half)
        for n, value in enumerate((total, diag) if first else (total,)):
            value = value * 0.125
            right_out[n, ym] = value[: 2 * ZB]
            own_out[n, ym] = value[ZB : 2 * ZB]
            left_out[n, ym] = value[ZB:]
        return carry

    lax.fori_loop(0, YB // 2, restrict, 0)

    def keep(y, carry):
        for pz in range(2):
            for px in range(2):
                epre[pz, px, y] = u[at, pz, px, y + 5]
                qpost[pz, px, y] = q[pz, px, y + 4]
                if first:
                    kpost[pz, px, y] = k[pz, px, y + 4]
        return carry

    lax.fori_loop(0, YPOST, keep, 0, unroll=2)


PADM, PADL = 8, 4


def coarse_kernel(first, sweeps, *refs):
    window = refs[0]
    if first:
        part, e1_out, q1_out, e2_out, k1_out, k1, d1, k2, d2, g2sum = refs[1:11]
        v, q1, t, w, q2, x2 = refs[11:]
    else:
        k1, d1, k2, d2, g2sum = refs[1:6]
        part, e1_out, q1_out, e2_out = refs[6:10]
        v, q1, t, w, q2, x2 = refs[10:]
    fast = lax.axis_index("fast")
    slow = lax.axis_index("slow")
    lanes = lane_iota(ZM)
    even = (lanes & 1) == 0
    zrow = row_iota(ZM) + (fast * ZB - 2 * ZB)
    mask = jnp.where((zrow >= 0) & (zrow < lax.axis_size("fast") * ZB), 1.0, 0.0).astype(F32)
    zero = jnp.zeros((ZM, LANES), F32)
    for n in range(PADM):
        for at in range(2):
            v[at, n] = zero
            v[at, PADM + YM + n] = zero
        q1[n] = zero
        q1[PADM + YM + n] = zero
        if first:
            k1[n] = zero
            k1[PADM + YM + n] = zero
    for block in range(8):
        for ym in range(4):
            y = block * 4 + ym
            if first:
                full = window[block, 1, ym] + 1.5
                gain = (OMEGA / full) * mask
                k1[PADM + y] = gain * 0.25
                d1[y] = full * (1.0 / OMEGA)
                start = gain * window[block, 0, ym]
            else:
                start = (4.0 * k1[PADM + y]) * window[block, 0, ym]
            q1[PADM + y] = start
            v[0, PADM + y] = start
    at = flat_sweeps(v, q1, k1, sweeps[1] - 1, 0, PADM, YM, lanes, 1, 4)
    for yc in range(YM // 2):
        t[yc, ZM:] = jnp.zeros((8, LANES), F32)

    def pair_sum(value):
        return value + jnp.where(even, pltpu.roll(value, LANES - 1, 1), pltpu.roll(value, 1, 1))

    def restrict(yc, carry):
        total = zero
        for half in range(2):
            y = PADM + 2 * yc + half
            here, beside = flat_neighbours(v, (at,), y, lanes, 1)
            total = total + (q1[y] - OMEGA * here + k1[y] * beside) * d1[2 * yc + half]
        t[yc, :ZM] = pair_sum(total)
        return carry

    lax.fori_loop(0, YM // 2, restrict, 0, unroll=2)
    lanes2 = lane_iota(24)
    rows2 = row_iota(24)
    zrow2 = rows2 + (fast * 4 - 8)
    mask2 = jnp.where(
        (zrow2 >= 0) & (zrow2 < lax.axis_size("fast") * 4) & (rows2 < 20), 1.0, 0.0
    ).astype(F32)
    zero2 = jnp.zeros((24, LANES), F32)
    for n in range(PADL):
        for b in range(2):
            w[b, n] = zero2
            w[b, PADL + 16 + n] = zero2

    def halve(yc):
        return (t[yc, pl.ds(0, 24, stride=2), :] + t[yc, pl.ds(1, 24, stride=2), :]) * 0.125

    if first:
        own = jnp.where((rows2 >= 8) & (rows2 < 12), 0.5, 0.0).astype(F32)
        for yc in range(16):
            w[1, PADL + yc] = halve(yc)

        def coarse_diag(yc, carry):
            y = 2 * yc
            value = window[y // 4, 1, y % 4] + window[(y + 1) // 4, 1, (y + 1) % 4]
            t[yc, :ZM] = pair_sum(value)
            return carry

        lax.fori_loop(0, 16, coarse_diag, 0, unroll=2)
        total = zero2
        for yc in range(16):
            g2 = halve(yc)
            full = g2 + 0.375
            gain = (OMEGA / full) * mask2
            k2[yc] = gain * 0.0625
            d2[yc] = full * (1.0 / OMEGA)
            total = total + g2 * own
            start = gain * w[1, PADL + yc]
            q2[yc] = start
            w[0, PADL + yc] = start
        g2sum[...] = total
    else:
        own = jnp.where((rows2 >= 8) & (rows2 < 12), 0.5, 0.0).astype(F32)
        for yc in range(16):
            start = (16.0 * k2[yc]) * halve(yc)
            q2[yc] = start
            w[0, PADL + yc] = start
    at2 = flat_sweeps(w, q2, k2, sweeps[2] - 1, 0, PADL, 16, lanes2, 2, 4, PADL)

    def left_over(yc, total):
        here, beside = flat_neighbours(w, (at2,), yc + PADL, lanes2, 2)
        return total + (q2[yc] - OMEGA * here + k2[yc] * beside) * d2[yc]

    total = lax.fori_loop(0, 16, left_over, zero2, unroll=4)
    numer = jnp.sum(total * own)
    denom = jnp.sum(g2sum[...])
    lanes_p = lane_iota(part.shape[0])
    part[...] = jnp.where(lanes_p == 0, numer, jnp.where(lanes_p == 1, denom, 0.0))

    def give(y, carry):
        row = 4 * slow + (PADM - 6) + y
        e1_out[y] = v[at, row, ZB : 4 * ZB]
        q1_out[y] = q1[row, ZB : 4 * ZB]
        if first:
            k1_out[y] = k1[row, ZB : 4 * ZB]
        return carry

    lax.fori_loop(0, YPOST, give, 0)

    def give2(y, carry):
        value = w[at2, 2 * slow + (PADL - 3) + y]
        x2[y, pl.ds(0, 24, stride=2), :] = value
        x2[y, pl.ds(1, 24, stride=2), :] = value
        e2_out[y] = x2[y, ZB : 4 * ZB]
        return carry

    lax.fori_loop(0, YPOST // 2, give2, 0)


def after_kernel(last, faces, sweeps, parts, e1, q1, k1, e2, epre, q, k, field, later, out, v, u, halves):
    lanes = lane_iota(ZW)
    lanes_p = lane_iota(parts.shape[0])
    every = parts[...]
    numer = jnp.sum(jnp.where(lanes_p == 0, every, 0.0))
    denom = jnp.sum(jnp.where(lanes_p == 1, every, 0.0)) + 0.0625 * faces
    shift = jnp.full((ZW, LANES), numer, F32) / jnp.full((ZW, LANES), denom, F32)
    zero = jnp.zeros((ZW, LANES), F32)
    for at in range(2):
        for y in (0, YPOST + 1):
            v[at, y] = zero
            for pz in range(2):
                for px in range(2):
                    u[at, pz, px, y] = zero
    for y in range(YPOST):
        raised = e1[y] + (e2[y // 2] + shift)
        v[0, y + 1] = jnp.where(k1[y] > 0.0, raised, 0.0)
    at = flat_sweeps(v, q1, k1, sweeps[1], 0, 1, YPOST, lanes, 1, 4, 1)

    def raise_fine(ym, carry):
        value = v[at, ym + 5]
        for half in range(2):
            y = 2 * ym + half
            for pz in range(2):
                for px in range(2):
                    u[0, pz, px, y + 1] = jnp.where(
                        k[pz, px, y] > 0.0, epre[pz, px, y] + value, 0.0
                    )
        return carry

    lax.fori_loop(0, YPOST // 2, raise_fine, 0)
    at = fine_sweeps(u, q, k, sweeps[0], 0, YPOST, lanes)
    for pz in range(2):
        for px in range(2):
            value = field[pz, px] + 0.5 * u[at, pz, px, 5:13, ZB : 2 * ZB]
            if last:
                halves[px, pl.ds(pz, YB * ZB, stride=2), :] = value.reshape(YB * ZB, LANES)
            else:
                out[0, pz, px] = value
                out[1, pz, px] = later[pz, px]
    if last:
        both = jnp.concatenate([halves[0], halves[1]], axis=1)
        out[...] = exact_dot(both, parity_matrix(True)).reshape(YB, 2 * ZB, 2 * LANES)


def vmem(count):
    return [pl.BlockSpec(memory_space=pltpu.VMEM)] * count


def call(kernel, outs, scratch, scalars, *arrays):
    specs = [pl.BlockSpec(memory_space=pltpu.SMEM)] * len(scalars)
    return pl.pallas_call(
        kernel,
        out_shape=[jax.ShapeDtypeStruct(s, F32) for s in outs],
        in_specs=specs + vmem(len(arrays)),
        out_specs=vmem(len(outs)),
        scratch_shapes=[pltpu.VMEM(s, F32) for s in scratch],
        compiler_params=pltpu.CompilerParams(vmem_limit_bytes=40 * 1024 * 1024),
    )(*scalars, *arrays)


def both_ways(to_right, to_left, axis):
    count = lax.axis_size(axis)
    up = [(i, (i + 1) % count) for i in range(count)]
    down = [(target, source) for source, target in up]
    return lax.ppermute(to_right, axis, up), lax.ppermute(to_left, axis, down)


def window_of(fields):
    left, right = both_ways(fields, fields, "fast")
    mid = jnp.stack([left, fields, right])
    low, high = both_ways(mid, mid, "slow")
    return mid, low, high


def body(observed, start_field, diagonal, noise, sweeps):
    block = (2, 2, YB, ZB, LANES)
    post = (2, 2, YPOST, ZW, LANES)
    whole = (2, 2, YW, ZW, LANES)
    fast_count, slow_count = lax.axis_size("fast"), lax.axis_size("slow")
    first, second, third = YB * slow_count // 4, 2 * ZB * fast_count // 4, 2 * LANES // 4
    faces = 2.0 * (first * second + first * third + second * third)
    fields, later = call(
        split_kernel, [(3, *block), block], [(4, 2, YB * 2 * ZB, LANES)], (),
        observed, start_field, diagonal, noise,
    )
    field = fields[0]
    kept_fine = kept_low = None
    for step in range(2):
        opening = step == 0
        count = 2 if opening else 1
        mid, low, high = window_of(fields)
        outs = [(count, 4, 16, LANES), (count, 4, 8, LANES), (count, 4, 16, LANES), post, post]
        scratch = [(2, 2, 2, YW + 2, ZW, LANES), whole]
        if opening:
            outs += [post, whole, (2, 2, YB, ZW, LANES)]
            given = (mid, low, high)
        else:
            given = (mid, low, high, kept_fine[1], kept_fine[2])
        got = call(functools.partial(before_kernel, opening), outs, scratch, (sweeps,), *given)
        to_left, own, to_right, epre, q = got[:5]
        if opening:
            kept_fine = got[5:]
        left, right = both_ways(to_right, to_left, "fast")
        strip = jnp.concatenate([left, own, right], axis=2)
        strip = jnp.broadcast_to(strip[None], (slow_count, *strip.shape))
        strip = lax.all_to_all(strip, "slow", 0, 0, tiled=True)
        outs = [(fast_count, LANES), (YPOST, ZW, LANES), (YPOST, ZW, LANES), (YPOST // 2, ZW, LANES)]
        scratch = [
            (2, YM + 2 * PADM, ZM, LANES),
            (YM + 2 * PADM, ZM, LANES),
            (16, ZM + 8, LANES),
            (2, 16 + 2 * PADL, 24, LANES),
            (16, 24, LANES),
            (YPOST // 2, 48, LANES),
        ]
        if opening:
            outs += [
                (YPOST, ZW, LANES),
                (YM + 2 * PADM, ZM, LANES), (YM, ZM, LANES),
                (16, 24, LANES), (16, 24, LANES), (24, LANES),
            ]
            given = (strip,)
        else:
            given = (strip, *kept_low[1:])
        got = call(functools.partial(coarse_kernel, opening), outs, scratch, (sweeps,), *given)
        part, e1, q1, e2 = got[:4]
        if opening:
            kept_low = got[4:]
        parts = lax.all_to_all(part, "fast", 0, 0, tiled=True)
        outs = [(2, *block) if opening else (YB, 2 * ZB, 2 * LANES)]
        scratch = [(2, YPOST + 2, ZW, LANES), (2, 2, 2, YPOST + 2, ZW, LANES), (2, YB * 2 * ZB, LANES)]
        (fields,) = call(
            functools.partial(after_kernel, not opening, faces), outs, scratch, (sweeps,),
            parts, e1, q1, kept_low[0], e2, epre, q, kept_fine[0], field, later,
        )
        field = fields[0]
    return fields


def solution(mesh):
    placed = (
        P("slow", "fast", None),
        P("slow", "fast", None),
        P("slow", "fast", None),
        P(None, "slow", "fast", None),
        P(),
    )
    return jax.shard_map(
        body, mesh=mesh, in_specs=placed, out_specs=P("slow", "fast", None), check_vma=False
    )
```

time: 740 us -> 232 us (0.31)
  the two profiles are of different devices: /device:TPU:129 before, /device:TPU:1 now
where the time goes in v1:
time: 232 us; the launch traced here: 231 us
  waiting for transfers between devices  64.6 us (28%)
  Pallas kernels  58.5 us (25%)
  blocking collectives  41.2 us (18%)
  starting transfers between devices  40.6 us (18%)
  local copies, waits for them, and re-layouts  25.6 us (11%)
    pallas_call x7, Pallas kernels, call(): pl.pallas_call(kernel, out_shape=[jax.ShapeDtypeStruct(s, F32) for s in o...  58.5 us
    ppermute x12, waiting for transfers between devices, both_ways(): return (lax.ppermute(to_right, axis, up), lax.ppermute(to_left, axis, down))  48.1 us
    all_to_all x2, blocking collectives, body(): strip = lax.all_to_all(strip, 'slow', 0, 0, tiled=True)  41.2 us
    ppermute x12, starting transfers between devices, both_ways(): return (lax.ppermute(to_right, axis, up), lax.ppermute(to_left, axis, down))  27 us
    unnamed x86, local copies, waits for them, and re-layouts  24.8 us
    all_to_all x2, waiting for transfers between devices, body(): parts = lax.all_to_all(part, 'fast', 0, 0, tiled=True)  16.5 us
    all_to_all x2, starting transfers between devices, body(): parts = lax.all_to_all(part, 'fast', 0, 0, tiled=True)  13.6 us
  transfers between devices with their start and end apart: 14, of which 10 were waited for; matrix products, arithmetic and copies ran while one was open for 0% of the time, Pallas kernels for 0%

profile of v1, /device:TPU:1, one launch (start us, length us, event | category | flops | bytes accessed | tf_op | source)
XLA Modules:
  0.0 231.0 jit_solution(8087464593488353548)
XLA Ops:
  0.0 0.9 copy-done.16
  1.0 0.9 copy-done.29
  1.9 0.9 copy-done.30
  2.8 0.9 copy-done.31
  3.7 0.7 shard_map.55
  4.4 8.7 %collective-permute-start.1 = (f32[3,2,2,8,8,128]{5,4,3,2,1,0:T(8,128)S(1)}, f32[3,2,2,8,8,128]{5,4,3,2,1,0:T(8,128)S(1)}, u32[]{:S(2)}, u32[]{:S(2)}) collective-permute-start(f32[3,2,2,8,8,128]{5,4,3,2,1,0:T(8,128)S(1)} %get-tuple-element.34), channel_id=1, source_target_pairs={{1,0},{2,1},{3,2},{4,3},{5,4},{6,5},{7,6},{8,7},{9,8},{10,9},{11,1... | collective-permute-start | bytes 1179656 | tf_op jit(solution)/shard_map/ppermute | solution.py:415
  13.0 7.8 %collective-permute-done.1 = f32[3,2,2,8,8,128]{5,4,3,2,1,0:T(8,128)S(1)} collective-permute-done((f32[3,2,2,8,8,128]{5,4,3,2,1,0:T(8,128)S(1)}, f32[3,2,2,8,8,128]{5,4,3,2,1,0:T(8,128)S(1)}, u32[]{:S(2)}, u32[]{:S(2)}) %collective-permute-start.1) | collective-permute-done | bytes 393248 | tf_op jit(solution)/shard_map/ppermute | solution.py:415
  20.8 5.2 %collective-permute-done = f32[3,2,2,8,8,128]{5,4,3,2,1,0:T(8,128)S(1)} collective-permute-done((f32[3,2,2,8,8,128]{5,4,3,2,1,0:T(8,128)S(1)}, f32[3,2,2,8,8,128]{5,4,3,2,1,0:T(8,128)S(1)}, u32[]{:S(2)}, u32[]{:S(2)}) %collective-permute-start) | collective-permute-done | bytes 393248 | tf_op jit(solution)/shard_map/ppermute | solution.py:415
  26.0 0.1 pad_maximum_fusion.refs_0_
  26.1 1.9 collective-permute-start.3
  28.0 1.2 collective-permute-start.2
  29.2 14.2 %collective-permute-done.3.refs_2_ = f32[3,3,2,2,8,8,128]{6,5,4,3,2,1,0:T(8,128)S(1)} collective-permute-done((f32[3,3,2,2,8,8,128]{6,5,4,3,2,1,0:T(8,128)S(1)}, f32[3,3,2,2,8,8,128]{6,5,4,3,2,1,0:T(8,128)S(1)}, u32[]{:S(2)}, u32[]{:S(2)}) %collective-permute-start.3) | collective-permute-done | bytes 1179680 | tf_op jit(solution)/shard_map/ppermute | solution.py:415
  43.4 8.5 %shard_map.56 = (f32[2,4,16,128]{3,2,1,0:T(8,128)S(1)}, f32[2,4,8,128]{3,2,1,0:T(8,128)S(1)}, f32[2,4,16,128]{3,2,1,0:T(8,128)S(1)}, f32[2,2,16,24,128]{4,3,2,1,...) custom-call(s32[3]{0:T(128)S(1)} %copy-done.36, ...), custom_call_target="tpu_custom_call" | custom-call | tf_op jit(solution)/shard_map/pallas_call | solution.py:401
  52.0 0.9 copy-done.6
  52.9 4.8 %collective-permute-start.5 = (f32[2,4,16,128]{3,2,1,0:T(8,128)S(1)}, f32[2,4,16,128]{3,2,1,0:T(8,128)S(1)}, u32[]{:S(2)}, u32[]{:S(2)}) collective-permute-start(f32[2,4,16,128]{3,2,1,0:T(8,128)S(1)} %get-tuple-element.37), channel_id=1, source_target_pairs={{1,0},{2,1},{3,2},{4,3},{5,4},{6,5},{7,6},{8,7},{9,8},{10,9},{11,1... | collective-permute-start | bytes 196616 | tf_op jit(solution)/shard_map/ppermute | solution.py:415
  57.7 1.6 collective-permute-done.4
  59.3 0.1 broadcast_in_dim.6
  59.5 24.2 %all_to_all.32.refs_0_ = f32[8,2,4,40,128]{4,3,2,1,0:T(8,128)S(1)} all-to-all(f32[8,2,4,40,128]{4,3,2,1,0:T(8,128)S(1)} %broadcast_in_dim.6), channel_id=1, replica_groups=mesh['slow'=8,'fast'=32] {'slow'}, dimensions={0} | all-to-all | bytes 2621440 | tf_op jit(solution)/shard_map/all_to_all | solution.py:456
  83.7 10.4 %shard_map.57 = (f32[32,128]{1,0:T(8,128)S(1)}, f32[16,24,128]{2,1,0:T(8,128)S(1)}, f32[16,24,128]{2,1,0:T(8,128)S(1)}, f32[8,24,128]{2,1,0:T(8,128)S(1)}, f32[1...) custom-call(s32[3]{0:T(128)S(1)} %copy-done.36, ...), custom_call_target="tpu_custom_call" | custom-call | tf_op jit(solution)/shard_map/pallas_call | solution.py:401
  94.1 0.8 copy-done.8
  95.0 0.7 copy-done.17
  95.7 0.7 copy-done.19
  96.3 0.7 copy-done.25
  97.0 0.7 copy-done.27
  97.7 0.6 copy-done.34
  98.3 0.6 copy-done.41
  98.9 0.6 copy-done.39
  99.5 6.7 %all-to-all-start.1 = ((f32[32,1,128]{2,1,0:T(1,128)}), f32[32,1,128]{2,1,0:T(1,128)S(1)}, u32[]{:S(2)}, u32[]{:S(2)}) async-start(f32[32,1,128]{2,1,0:T(1,128)} %bitcast.24), calls=%async_computation.1 | async-start | bytes 32768 | tf_op jit(solution)/shard_map/all_to_all | solution.py:479
  106.2 0.7 slice_bitcast_fusion.1.field
  106.9 7.9 %all-to-all-done.1 = f32[32,1,128]{2,1,0:T(1,128)S(1)} async-done(((f32[32,1,128]{2,1,0:T(1,128)}), f32[32,1,128]{2,1,0:T(1,128)S(1)}, u32[]{:S(2)}, u32[]{:S(2)}) %all-to-all-start.1) | async-done | bytes 16416 | tf_op jit(solution)/shard_map/all_to_all | solution.py:479
  114.8 1.1 copy-done.5
  116.0 1.1 copy-done.7
  117.1 0.9 copy-done.11
  118.0 0.9 copy-done.13
  118.9 0.9 copy-done.26
  119.8 0.9 copy-done.28
  120.8 0.9 copy-done.35
  121.7 0.7 copy-done.37
  122.3 10.0 %shard_map.58 = f32[2,2,2,8,8,128]{5,4,3,2,1,0:T(8,128)S(1)} custom-call(s32[3]{0:T(128)S(1)} %copy-done.37, f32[32,128]{1,0:T(8,128)S(1)} %bitcast.23, f32[16,24,128]{2,1,0:T(8,128)S(1)} %copy-done.26, f32[16,24,128]{2,1,0:T(8,128)S(1)} %copy-done.28, f32[16,24,128]{2,1,0:T(8,128)S(1)} %get-tuple-element.41.k1, f32[8,24,128]{2,1,0:T(8,128)S(1)} %copy-done.35, ...), custom_call_target="tpu_custom_call" | custom-call | tf_op jit(solution)/shard_map/pallas_call | solution.py:401
  132.3 1.0 collective-permute-start.7
  133.4 0.5 collective-permute-start.6
  133.9 3.8 %collective-permute-done.7 = f32[2,2,2,8,8,128]{5,4,3,2,1,0:T(8,128)S(1)} collective-permute-done((f32[2,2,2,8,8,128]{5,4,3,2,1,0:T(8,128)S(1)}, f32[2,2,2,8,8,128]{5,4,3,2,1,0:T(8,128)S(1)}, u32[]{:S(2)}, u32[]{:S(2)}) %collective-permute-start.7) | collective-permute-done | bytes 262176 | tf_op jit(solution)/shard_map/ppermute | solution.py:415
  137.6 4.3 %collective-permute-done.6 = f32[2,2,2,8,8,128]{5,4,3,2,1,0:T(8,128)S(1)} collective-permute-done((f32[2,2,2,8,8,128]{5,4,3,2,1,0:T(8,128)S(1)}, f32[2,2,2,8,8,128]{5,4,3,2,1,0:T(8,128)S(1)}, u32[]{:S(2)}, u32[]{:S(2)}) %collective-permute-start.6) | collective-permute-done | bytes 262176 | tf_op jit(solution)/shard_map/ppermute | solution.py:415
  142.0 3.9 %collective-permute-start.9 = (f32[3,2,2,2,8,8,128]{6,5,4,3,2,1,0:T(8,128)S(1)}, f32[3,2,2,2,8,8,128]{6,5,4,3,2,1,0:T(8,128)S(1)}, u32[]{:S(2)}, u32[]{:S(2)}) collective-permute-start(f32[3,2,2,2,8,8,128]{6,5,4,3,2,1,0:T(8,128)S(1)} %pad_maximum_fusion.1.refs_0_), channel_id=1, source_target_pairs={{32,0},{64,32},{96,64},{128,96},{160,128},{192,160},{224,192},{0,2... | collective-permute-start | bytes 2359304 | tf_op jit(solution)/shard_map/ppermute | solution.py:415
  145.8 0.2 collective-permute-start.8
  146.0 9.9 %collective-permute-done.9.refs_2_ = f32[3,2,2,2,8,8,128]{6,5,4,3,2,1,0:T(8,128)S(1)} collective-permute-done((f32[3,2,2,2,8,8,128]{6,5,4,3,2,1,0:T(8,128)S(1)}, f32[3,2,2,2,8,8,128]{6,5,4,3,2,1,0:T(8,128)S(1)}, u32[]{:S(2)}, u32[]{:S(2)}) %collective-permute-start.9) | collective-permute-done | bytes 786464 | tf_op jit(solution)/shard_map/ppermute | solution.py:415
  156.0 8.5 %shard_map.59 = (f32[1,4,16,128]{3,2,1,0:T(8,128)S(1)}, f32[1,4,8,128]{3,2,1,0:T(8,128)S(1)}, f32[1,4,16,128]{3,2,1,0:T(8,128)S(1)}, f32[2,2,16,24,128]{4,3,2,1,0:T(8,128)S(1)}, f32[2,2,16,24,128]{4,3,2,1,0:T(8,128)S(1)}) custom-call(s32[3]{0:T(128)S(1)} %copy-done.37, f32[3,2,2,2,8,8,128]{6,5,4,3,2,1,0:T(8,128)S(1)} %pad_maximum_fusion.1.refs_0_, ...), custom_call_target="tpu_custom_call" | custom-call | tf_op jit(solution)/shard_map/pallas_call | solution.py:401
  164.5 0.9 copy-done
  165.4 0.1 collective-permute-start.10
  165.5 4.8 %collective-permute-start.11 = (f32[1,4,16,128]{3,2,1,0:T(8,128)S(1)}, f32[1,4,16,128]{3,2,1,0:T(8,128)S(1)}, u32[]{:S(2)}, u32[]{:S(2)}) collective-permute-start(f32[1,4,16,128]{3,2,1,0:T(8,128)S(1)} %get-tuple-element.51), channel_id=1, source_target_pairs={{1,0},{2,1},{3,2},{4,3},{5,4},{6,5},{7,6},{8,7},{9,8},{10,9},{11,1... | collective-permute-start | bytes 98312 | tf_op jit(solution)/shard_map/ppermute | solution.py:415
  170.3 1.3 collective-permute-done.10
  171.6 17.0 %all_to_all.33.refs_0_ = f32[8,1,4,40,128]{4,3,2,1,0:T(8,128)S(1)} all-to-all(f32[8,1,4,40,128]{4,3,2,1,0:T(8,128)S(1)} %broadcast_in_dim.16), channel_id=1, replica_groups=mesh['slow'=8,'fast'=32] {'slow'}, dimensions={0} | all-to-all | bytes 1310720 | tf_op jit(solution)/shard_map/all_to_all | solution.py:456
  188.7 9.4 %shard_map.60 = (f32[32,128]{1,0:T(8,128)S(1)}, f32[16,24,128]{2,1,0:T(8,128)S(1)}, f32[16,24,128]{2,1,0:T(8,128)S(1)}, f32[8,24,128]{2,1,0:T(8,128)S(1)}) custom-call(s32[3]{0:T(128)S(1)} %copy-done.38, f32[8,1,4,40,128]{4,3,2,1,0:T(8,128)S(1)} %all_to_all.33.refs_0_, f32[48,40,128]{2,1,0:T(8,128)S(1)} %get-tuple-element.52.refs_1_, ...), custom_call_target="tpu_custom_call" | custom-call | tf_op jit(solution)/shard_map/pallas_call | solution.py:401
  198.1 0.7 copy-done.21
  198.8 0.7 copy-done.23
  199.5 0.6 copy-done.32
  200.1 0.6 copy-done.40
  200.7 6.8 %all-to-all-start.3 = ((f32[32,1,128]{2,1,0:T(1,128)}), f32[32,1,128]{2,1,0:T(1,128)S(1)}, u32[]{:S(2)}, u32[]{:S(2)}) async-start(f32[32,1,128]{2,1,0:T(1,128)} %bitcast.25), calls=%async_computation.3 | async-start | bytes 32768 | tf_op jit(solution)/shard_map/all_to_all | solution.py:479
  207.5 8.6 %all-to-all-done.3 = f32[32,1,128]{2,1,0:T(1,128)S(1)} async-done(((f32[32,1,128]{2,1,0:T(1,128)}), f32[32,1,128]{2,1,0:T(1,128)S(1)}, u32[]{:S(2)}, u32[]{:S(2)}) %all-to-all-start.3) | async-done | bytes 16416 | tf_op jit(solution)/shard_map/all_to_all | solution.py:479
  216.1 1.1 copy-done.3
  217.2 0.9 copy-done.22
  218.2 0.9 copy-done.24
  219.1 0.9 copy-done.33
  220.0 11.0 %shard_map.61 = f32[8,16,256]{2,1,0:T(8,128)} custom-call(s32[3]{0:T(128)S(1)} %copy-done.38, f32[32,128]{1,0:T(8,128)S(1)} %bitcast.22, f32[16,24,128]{2,1,0:T(8,128)S(1)} %copy-done.22, f32[16,24,128]{2,1,0:T(8,128)S(1)} %copy-done.24, f32[16,24,128]{2,1,0:T(8,128)S(1)} %get-tuple-element.41.k1, f32[8,24,128]{2,1,0:T(8,128)S(1)} %copy-done.33, ...), custom_call_target="tpu_custom_call" | custom-call | tf_op jit(solution)/shard_map/pallas_call | solution.py:401
  (67 shorter events, 0.3 us)
Async XLA Ops:
  0.0 0.9 copy-start.16
  1.0 0.9 copy-start.29
  1.9 0.9 copy-start.30
  2.8 0.9 copy-start.31
  4.4 21.8 %copy-start.10 = (f32[2,2,8,8,128]{4,3,2,1,0:T(8,128)}, f32[2,2,8,8,128]{4,3,2,1,0:T(8,128)S(1)}, u32[]{:S(2)}) copy-start(f32[2,2,8,8,128]{4,3,2,1,0:T(8,128)S(1)} %get-tuple-element.46.later) | copy-start | bytes 393220
  4.4 16.5 %collective-permute-start.1 = (f32[3,2,2,8,8,128]{5,4,3,2,1,0:T(8,128)S(1)}, f32[3,2,2,8,8,128]{5,4,3,2,1,0:T(8,128)S(1)}, u32[]{:S(2)}, u32[]{:S(2)}) collective-permute-start(f32[3,2,2,8,8,128]{5,4,3,2,1,0:T(8,128)S(1)} %get-tuple-element.34), channel_id=1, source_target_pairs={{1,0},{2,1},{3,2},{4,3},{5,4},{6,5},{7,6},{8,7},{9,8},{10,9},{11,1... | collective-permute-start | bytes 1179656 | tf_op jit(solution)/shard_map/ppermute | solution.py:415
  13.0 13.0 %collective-permute-start = (f32[3,2,2,8,8,128]{5,4,3,2,1,0:T(8,128)S(1)}, f32[3,2,2,8,8,128]{5,4,3,2,1,0:T(8,128)S(1)}, u32[]{:S(2)}, u32[]{:S(2)}) collective-permute-start(f32[3,2,2,8,8,128]{5,4,3,2,1,0:T(8,128)S(1)} %get-tuple-element.34), channel_id=1, source_target_pairs={{0,1},{1,2},{2,3},{3,4},{4,5},{5,6},{6,7},{7,8},{8,9},{9,10},{10,1... | collective-permute-start | bytes 1179656 | tf_op jit(solution)/shard_map/ppermute | solution.py:415
  26.0 17.4 %copy-start.36 = (s32[3]{0:T(128)S(1)}, s32[3]{0:T(128)}, u32[]{:S(2)}) copy-start(s32[3]{0:T(128)} %sweeps.11) | copy-start | bytes 40
  26.1 17.2 %collective-permute-start.3 = (f32[3,3,2,2,8,8,128]{6,5,4,3,2,1,0:T(8,128)S(1)}, f32[3,3,2,2,8,8,128]{6,5,4,3,2,1,0:T(8,128)S(1)}, u32[]{:S(2)}, u32[]{:S(2)}) collective-permute-start(f32[3,3,2,2,8,8,128]{6,5,4,3,2,1,0:T(8,128)S(1)} %pad_maximum_fusion.refs_0_), channel_id=1, source_target_pairs={{32,0},{64,32},{96,64},{128,96},{160,128},{192,160},{224,192},{0,2... | collective-permute-start | bytes 3538952 | tf_op jit(solution)/shard_map/ppermute | solution.py:415
  28.0 15.4 %collective-permute-start.2 = (f32[3,3,2,2,8,8,128]{6,5,4,3,2,1,0:T(8,128)S(1)}, f32[3,3,2,2,8,8,128]{6,5,4,3,2,1,0:T(8,128)S(1)}, u32[]{:S(2)}, u32[]{:S(2)}) collective-permute-start(f32[3,3,2,2,8,8,128]{6,5,4,3,2,1,0:T(8,128)S(1)} %pad_maximum_fusion.refs_0_), channel_id=1, source_target_pairs={{0,32},{32,64},{64,96},{96,128},{128,160},{160,192},{192,224},{224... | collective-permute-start | bytes 3538952 | tf_op jit(solution)/shard_map/ppermute | solution.py:415
  51.9 0.9 copy-start.6
  52.9 6.6 %copy-start.4 = (f32[2,2,16,24,128]{4,3,2,1,0:T(8,128)}, f32[2,2,16,24,128]{4,3,2,1,0:T(8,128)S(1)}, u32[]{:S(2)}) copy-start(f32[2,2,16,24,128]{4,3,2,1,0:T(8,128)S(1)} %get-tuple-element.43.epre) | copy-start | bytes 2359300
  52.9 30.8 %copy-start.14 = (f32[2,2,8,24,128]{4,3,2,1,0:T(8,128)}, f32[2,2,8,24,128]{4,3,2,1,0:T(8,128)S(1)}, u32[]{:S(2)}) copy-start(f32[2,2,8,24,128]{4,3,2,1,0:T(8,128)S(1)} %get-tuple-element.48.refs_4_) | copy-start | bytes 1179652
  52.9 6.4 %collective-permute-start.4 = (f32[2,4,16,128]{3,2,1,0:T(8,128)S(1)}, f32[2,4,16,128]{3,2,1,0:T(8,128)S(1)}, u32[]{:S(2)}, u32[]{:S(2)}) collective-permute-start(f32[2,4,16,128]{3,2,1,0:T(8,128)S(1)} %get-tuple-element.35), channel_id=1, source_target_pairs={{0,1},{1,2},{2,3},{3,4},{4,5},{5,6},{6,7},{7,8},{8,9},{9,10},{10,1... | collective-permute-start | bytes 196616 | tf_op jit(solution)/shard_map/ppermute | solution.py:415
  52.9 6.4 %collective-permute-start.5 = (f32[2,4,16,128]{3,2,1,0:T(8,128)S(1)}, f32[2,4,16,128]{3,2,1,0:T(8,128)S(1)}, u32[]{:S(2)}, u32[]{:S(2)}) collective-permute-start(f32[2,4,16,128]{3,2,1,0:T(8,128)S(1)} %get-tuple-element.37), channel_id=1, source_target_pairs={{1,0},{2,1},{3,2},{4,3},{5,4},{6,5},{7,6},{8,7},{9,8},{10,9},{11,1... | collective-permute-start | bytes 196616 | tf_op jit(solution)/shard_map/ppermute | solution.py:415
  94.1 0.8 copy-start.8
  95.0 0.7 copy-start.17
  95.7 0.7 copy-start.19
  96.3 0.7 copy-start.25
  97.0 0.7 copy-start.27
  97.7 0.6 copy-start.34
  98.3 0.6 copy-start.41
  98.9 0.6 copy-start.39
  99.5 15.3 %all-to-all-start.1 = ((f32[32,1,128]{2,1,0:T(1,128)}), f32[32,1,128]{2,1,0:T(1,128)S(1)}, u32[]{:S(2)}, u32[]{:S(2)}) async-start(f32[32,1,128]{2,1,0:T(1,128)} %bitcast.24), calls=%async_computation.1 | async-start | bytes 32768 | tf_op jit(solution)/shard_map/all_to_all | solution.py:479
  114.8 1.1 copy-start.5
  116.0 1.1 copy-start.7
  117.1 0.9 copy-start.11
  118.0 0.9 copy-start.13
  118.9 0.9 copy-start.26
  119.8 0.9 copy-start.28
  120.8 0.9 copy-start.35
  121.7 0.7 copy-start.37
  132.3 23.7 %copy-start.15 = (f32[2,2,8,24,128]{4,3,2,1,0:T(8,128)S(1)}, f32[2,2,8,24,128]{4,3,2,1,0:T(8,128)}, u32[]{:S(2)}) copy-start(f32[2,2,8,24,128]{4,3,2,1,0:T(8,128)} %copy-done.14) | copy-start | bytes 1179652
  132.3 5.3 %collective-permute-start.7 = (f32[2,2,2,8,8,128]{5,4,3,2,1,0:T(8,128)S(1)}, f32[2,2,2,8,8,128]{5,4,3,2,1,0:T(8,128)S(1)}, u32[]{:S(2)}, u32[]{:S(2)}) collective-permute-start(f32[2,2,2,8,8,128]{5,4,3,2,1,0:T(8,128)S(1)} %shard_map.58), channel_id=1, source_target_pairs={{1,0},{2,1},{3,2},{4,3},{5,4},{6,5},{7,6},{8,7},{9,8},{10,9},{11,1... | collective-permute-start | bytes 786440 | tf_op jit(solution)/shard_map/ppermute | solution.py:415
  133.4 8.5 %collective-permute-start.6 = (f32[2,2,2,8,8,128]{5,4,3,2,1,0:T(8,128)S(1)}, f32[2,2,2,8,8,128]{5,4,3,2,1,0:T(8,128)S(1)}, u32[]{:S(2)}, u32[]{:S(2)}) collective-permute-start(f32[2,2,2,8,8,128]{5,4,3,2,1,0:T(8,128)S(1)} %shard_map.58), channel_id=1, source_target_pairs={{0,1},{1,2},{2,3},{3,4},{4,5},{5,6},{6,7},{7,8},{8,9},{9,10},{10,1... | collective-permute-start | bytes 786440 | tf_op jit(solution)/shard_map/ppermute | solution.py:415
  142.0 14.0 %collective-permute-start.9 = (f32[3,2,2,2,8,8,128]{6,5,4,3,2,1,0:T(8,128)S(1)}, f32[3,2,2,2,8,8,128]{6,5,4,3,2,1,0:T(8,128)S(1)}, u32[]{:S(2)}, u32[]{:S(2)}) collective-permute-start(f32[3,2,2,2,8,8,128]{6,5,4,3,2,1,0:T(8,128)S(1)} %pad_maximum_fusion.1.refs_0_), channel_id=1, source_target_pairs={{32,0},{64,32},{96,64},{128,96},{160,128},{192,160},{224,192},{0,2... | collective-permute-start | bytes 2359304 | tf_op jit(solution)/shard_map/ppermute | solution.py:415
  145.8 10.1 %collective-permute-start.8 = (f32[3,2,2,2,8,8,128]{6,5,4,3,2,1,0:T(8,128)S(1)}, f32[3,2,2,2,8,8,128]{6,5,4,3,2,1,0:T(8,128)S(1)}, u32[]{:S(2)}, u32[]{:S(2)}) collective-permute-start(f32[3,2,2,2,8,8,128]{6,5,4,3,2,1,0:T(8,128)S(1)} %pad_maximum_fusion.1.refs_0_), channel_id=1, source_target_pairs={{0,32},{32,64},{64,96},{96,128},{128,160},{160,192},{192,224},{224... | collective-permute-start | bytes 2359304 | tf_op jit(solution)/shard_map/ppermute | solution.py:415
  164.5 0.9 copy-start
  165.4 32.7 %copy-start.2 = (f32[2,2,16,24,128]{4,3,2,1,0:T(8,128)}, f32[2,2,16,24,128]{4,3,2,1,0:T(8,128)S(1)}, u32[]{:S(2)}) copy-start(f32[2,2,16,24,128]{4,3,2,1,0:T(8,128)S(1)} %get-tuple-element.62.q) | copy-start | bytes 2359300
  165.4 23.2 %copy-start.9 = (f32[32,40,128]{2,1,0:T(8,128)S(1)}, f32[32,40,128]{2,1,0:T(8,128)}, u32[]{:S(2)}) copy-start(f32[32,40,128]{2,1,0:T(8,128)} %copy-done.8) | copy-start | bytes 1966084
  165.4 23.2 %copy-start.18 = (f32[16,24,128]{2,1,0:T(8,128)S(1)}, f32[16,24,128]{2,1,0:T(8,128)}, u32[]{:S(2)}) copy-start(f32[16,24,128]{2,1,0:T(8,128)} %copy-done.17) | copy-start | bytes 589828
  165.4 23.2 %copy-start.20 = (f32[16,24,128]{2,1,0:T(8,128)S(1)}, f32[16,24,128]{2,1,0:T(8,128)}, u32[]{:S(2)}) copy-start(f32[16,24,128]{2,1,0:T(8,128)} %copy-done.19) | copy-start | bytes 589828
  165.4 23.2 %copy-start.38 = (s32[3]{0:T(128)S(1)}, s32[3]{0:T(128)}, u32[]{:S(2)}) copy-start(s32[3]{0:T(128)} %sweeps.11) | copy-start | bytes 40
  165.4 23.2 %copy-start.42 = (f32[24,128]{1,0:T(8,128)S(1)}, f32[24,128]{1,0:T(8,128)}, u32[]{:S(2)}) copy-start(f32[24,128]{1,0:T(8,128)} %copy-done.41) | copy-start | bytes 36868
  165.4 6.2 %collective-permute-start.10 = (f32[1,4,16,128]{3,2,1,0:T(8,128)S(1)}, f32[1,4,16,128]{3,2,1,0:T(8,128)S(1)}, u32[]{:S(2)}, u32[]{:S(2)}) collective-permute-start(f32[1,4,16,128]{3,2,1,0:T(8,128)S(1)} %get-tuple-element.49), channel_id=1, source_target_pairs={{0,1},{1,2},{2,3},{3,4},{4,5},{5,6},{6,7},{7,8},{8,9},{9,10},{10,1... | collective-permute-start | bytes 98312 | tf_op jit(solution)/shard_map/ppermute | solution.py:415
  165.5 6.1 %collective-permute-start.11 = (f32[1,4,16,128]{3,2,1,0:T(8,128)S(1)}, f32[1,4,16,128]{3,2,1,0:T(8,128)S(1)}, u32[]{:S(2)}, u32[]{:S(2)}) collective-permute-start(f32[1,4,16,128]{3,2,1,0:T(8,128)S(1)} %get-tuple-element.51), channel_id=1, source_target_pairs={{1,0},{2,1},{3,2},{4,3},{5,4},{6,5},{7,6},{8,7},{9,8},{10,9},{11,1... | collective-permute-start | bytes 98312 | tf_op jit(solution)/shard_map/ppermute | solution.py:415
  188.6 27.5 %copy-start.1 = (f32[2,2,16,24,128]{4,3,2,1,0:T(8,128)S(1)}, f32[2,2,16,24,128]{4,3,2,1,0:T(8,128)}, u32[]{:S(2)}) copy-start(f32[2,2,16,24,128]{4,3,2,1,0:T(8,128)} %copy-done) | copy-start | bytes 2359300
  188.6 27.5 %copy-start.12 = (f32[2,2,8,8,128]{4,3,2,1,0:T(8,128)S(1)}, f32[2,2,8,8,128]{4,3,2,1,0:T(8,128)}, u32[]{:S(2)}) copy-start(f32[2,2,8,8,128]{4,3,2,1,0:T(8,128)} %copy-done.10) | copy-start | bytes 393220
  198.1 0.7 copy-start.21
  198.8 0.7 copy-start.23
  199.4 0.6 copy-start.32
  200.1 0.6 copy-start.40
  200.7 15.4 %all-to-all-start.3 = ((f32[32,1,128]{2,1,0:T(1,128)}), f32[32,1,128]{2,1,0:T(1,128)S(1)}, u32[]{:S(2)}, u32[]{:S(2)}) async-start(f32[32,1,128]{2,1,0:T(1,128)} %bitcast.25), calls=%async_computation.3 | async-start | bytes 32768 | tf_op jit(solution)/shard_map/all_to_all | solution.py:479
  216.1 1.1 copy-start.3
  217.2 0.9 copy-start.22
  218.2 0.9 copy-start.24
  219.1 0.9 copy-start.33

commit v2 on v1

v2 whole, which is shorter than its diff:
```python
import functools

import jax
import jax.numpy as jnp
from jax import lax
from jax.experimental import pallas as pl
from jax.experimental.pallas import tpu as pltpu
from jax.sharding import PartitionSpec as P

OMEGA = 0.7
KEEP = 1.0 - OMEGA
F32 = jnp.float32

YB, ZB, LANES = 8, 8, 128
YW, ZW = 3 * YB, 3 * ZB
ZM, YM = 40, 32
YPOST = 16
PADM, PADL = 8, 4
PARITIES = ((0, 0), (0, 1), (1, 0), (1, 1))


def lane_iota(rows):
    return lax.broadcasted_iota(jnp.int32, (rows, LANES), 1)


def row_iota(rows):
    return lax.broadcasted_iota(jnp.int32, (rows, LANES), 0)


def parity_matrix(transposed):
    row = lax.broadcasted_iota(jnp.int32, (2 * LANES, 2 * LANES), 0)
    col = lax.broadcasted_iota(jnp.int32, (2 * LANES, 2 * LANES), 1)
    if transposed:
        row, col = col, row
    return jnp.where(row == 2 * (col & (LANES - 1)) + (col >> 7), 1.0, 0.0).astype(F32)


def exact_dot(a, b):
    return lax.dot(a, b, precision=lax.Precision.HIGHEST, preferred_element_type=F32)


def over(low, high, chunk, one):
    turns, rest = divmod(high - low, chunk)
    assert rest == 0
    if turns == 1:
        for n in range(chunk):
            one(low + n)
        return

    def turn(at, carry):
        for n in range(chunk):
            one(low + at * chunk + n)
        return carry

    lax.fori_loop(0, turns, turn, 0)


def fine_neighbours(u, y, lanes):
    rows = u.shape[-2]
    here = {p: u[(*p, y)] for p in PARITIES}
    beside = {}
    for pz, px in PARITIES:
        total = u[pz, px, y - 1] + u[pz, px, y + 1]
        other = here[1 - pz, px]
        total = total + (other + pltpu.roll(other, 1 if pz == 0 else rows - 1, 0))
        other = here[pz, 1 - px]
        if px == 0:
            moved = jnp.where(lanes == 0, 0.0, pltpu.roll(other, 1, 1))
        else:
            moved = jnp.where(lanes == LANES - 1, 0.0, pltpu.roll(other, LANES - 1, 1))
        beside[pz, px] = total + (other + moved)
    return here, beside


def flat_neighbours(u, y, lanes, step):
    rows = u.shape[-2]
    here = u[y]
    total = u[y - 1] + u[y + 1]
    total = total + (pltpu.roll(here, 1, 0) + pltpu.roll(here, rows - 1, 0))
    left = jnp.where(lanes < step, 0.0, pltpu.roll(here, step, 1))
    right = jnp.where(lanes >= LANES - step, 0.0, pltpu.roll(here, LANES - step, 1))
    return here, total + (left + right)


def fine_sweep(source, target, q, k, low, high, chunk, lanes, shift=0, offset=0):
    def one(y):
        here, beside = fine_neighbours(source, y, lanes)
        for p in PARITIES:
            target[(*p, y - shift)] = (
                KEEP * here[p] + q[(*p, y + offset)] + k[(*p, y + offset)] * beside[p]
            )

    over(low, high, chunk, one)


def flat_sweep(source, target, q, k, low, high, chunk, lanes, step):
    def one(y):
        here, beside = flat_neighbours(source, y, lanes, step)
        target[y] = KEEP * here + q(y) + k(y) * beside

    over(low, high, chunk, one)


def split_kernel(observed, start, diagonal, noise, fields, later, a, b, c, d, halves, sems):
    copies = [
        pltpu.make_async_copy(source, target, sems.at[n])
        for n, (source, target) in enumerate(((start, a), (diagonal, b), (observed, c), (noise, d)))
    ]
    for copy in copies:
        copy.start()
    matrix = parity_matrix(False)

    def split(n, value, out):
        both = exact_dot(value.reshape(YB * 2 * ZB, 2 * LANES), matrix)
        for px in range(2):
            halves[n, px] = both[:, px * LANES : (px + 1) * LANES]
        for pz, px in PARITIES:
            part = halves[n, px, pl.ds(pz, YB * ZB, stride=2), :]
            out[pz, px] = part.reshape(YB, ZB, LANES)

    copies[0].wait()
    split(0, a[...], fields.at[0])
    copies[1].wait()
    split(1, b[...], fields.at[2])
    copies[2].wait()
    copies[3].wait()
    split(2, c[...] + 2.0 * d[0], fields.at[1])
    split(3, c[...] + 2.0 * d[1], later)


def inside(axis, which):
    at = lax.axis_index(axis) + (which - 1)
    return jnp.where((at >= 0) & (at < lax.axis_size(axis)), 1.0, 0.0).astype(F32)


def wide(ref, field, p, y):
    return jnp.concatenate([ref[(zb, field, *p, y)] for zb in range(3)], axis=0)


def before_kernel(first, sweeps, *refs):
    if first:
        mid, low, high = refs[:3]
        left_out, own_out, right_out, epre, q, k, dn = refs[3:10]
        s, a, b = refs[10:]
    else:
        mid, low, high, k, dn = refs[:5]
        left_out, own_out, right_out, epre, q = refs[5:10]
        s, a, b = refs[10:]
    lanes = lane_iota(ZW)
    rows = row_iota(ZW)
    row_mask = jnp.where(
        rows < ZB, inside("fast", 0), jnp.where(rows < 2 * ZB, 1.0, inside("fast", 2))
    )
    blocks = (low, mid, high)
    masks = [row_mask * inside("slow", 0), row_mask, row_mask * inside("slow", 2)]
    for yb, ref in enumerate(blocks):

        def fill(y):
            for p in PARITIES:
                value = wide(ref, 0, p, y)
                s[(*p, yb * YB + y)] = jnp.where(masks[yb] > 0.5, value, 0.0)

        over(0, YB, 8, fill)
    for yb, ref in enumerate(blocks):

        def right_side(y):
            row = yb * YB + y
            here, beside = fine_neighbours(s, row, lanes)
            for p in PARITIES:
                if first:
                    full = wide(ref, 2, p, y) + 6.0
                    gain = (OMEGA / full) * masks[yb]
                    k[(*p, row)] = gain
                    if yb == 1:
                        dn[(*p, y)] = full * (1.0 / OMEGA)
                else:
                    gain = k[(*p, row)]
                start = gain * (wide(ref, 1, p, y) + beside[p]) - OMEGA * here[p]
                q[(*p, row)] = start
                a[(*p, row)] = start
                b[(*p, row)] = start

        if yb == 1:
            over(0, YB, 4, right_side)
        else:
            over(1 - yb // 2, YB - yb // 2, 7, right_side)

    @pl.when(sweeps[0] >= 4)
    def _():
        fine_sweep(a, b, q, k, 2, 22, 10, lanes)

    @pl.when(sweeps[0] >= 3)
    def _():
        fine_sweep(b, a, q, k, 3, 21, 9, lanes)

    fine_sweep(a, epre, q, k, 4, 20, 8, lanes, shift=4)
    zero = jnp.zeros((ZW, LANES), F32)

    def restrict(ym):
        total = zero
        diag = zero
        for half in range(2):
            row = YB + 2 * ym + half
            here, beside = fine_neighbours(epre, row - 4, lanes)
            for p in PARITIES:
                scaled = q[(*p, row)] - OMEGA * here[p] + k[(*p, row)] * beside[p]
                total = total + scaled * dn[(*p, 2 * ym + half)]
                if first:
                    diag = diag + wide(mid, 2, p, 2 * ym + half)
        for n, value in enumerate((total, diag) if first else (total,)):
            value = value * 0.125
            right_out[n, ym] = value[: 2 * ZB]
            own_out[n, ym] = value[ZB : 2 * ZB]
            left_out[n, ym] = value[ZB:]

    over(0, YB // 2, 4, restrict)


def coarse_kernel(first, sweeps, *refs):
    window = refs[0]
    if first:
        part, e1, q1, e2_out, k1, d1, k2, d2, g2sum = refs[1:10]
        va, t, wa, wb, q2, x2 = refs[10:]
    else:
        k1, d1, k2, d2, g2sum = refs[1:6]
        part, e1, q1, e2_out = refs[6:10]
        va, t, wa, wb, q2, x2 = refs[10:]
    fast = lax.axis_index("fast")
    slow = lax.axis_index("slow")
    lanes = lane_iota(ZM)
    even = (lanes & 1) == 0
    zrow = row_iota(ZM) + (fast * ZB - 2 * ZB)
    mask = jnp.where((zrow >= 0) & (zrow < lax.axis_size("fast") * ZB), 1.0, 0.0).astype(F32)
    zero = jnp.zeros((ZM, LANES), F32)
    for n in (*range(PADM), *range(PADM + YM, YM + 2 * PADM)):
        va[n] = zero
        e1[n] = zero
        q1[n] = zero
        if first:
            k1[n] = zero

    def opening(block):
        for ym in range(4):
            y = block * 4 + ym
            if first:
                full = window[block, 1, ym] + 1.5
                gain = (OMEGA / full) * mask
                k1[PADM + y] = gain * 0.25
                d1[y] = full * (1.0 / OMEGA)
                start = gain * window[block, 0, ym]
            else:
                start = (4.0 * k1[PADM + y]) * window[block, 0, ym]
            q1[PADM + y] = start
            va[PADM + y] = start
            e1[PADM + y] = start

    over(0, YM // 4, 2, opening)
    of_q1, of_k1 = (lambda y: q1[y]), (lambda y: k1[y])

    @pl.when(sweeps[1] >= 4)
    def _():
        flat_sweep(va, e1, of_q1, of_k1, PADM, PADM + YM, 8, lanes, 1)

    @pl.when(sweeps[1] >= 3)
    def _():
        flat_sweep(e1, va, of_q1, of_k1, PADM, PADM + YM, 8, lanes, 1)

    flat_sweep(va, e1, of_q1, of_k1, PADM, PADM + YM, 8, lanes, 1)

    def pair_sum(value):
        return value + jnp.where(even, pltpu.roll(value, LANES - 1, 1), pltpu.roll(value, 1, 1))

    def restrict(yc):
        total = zero
        for half in range(2):
            y = PADM + 2 * yc + half
            here, beside = flat_neighbours(e1, y, lanes, 1)
            total = total + (q1[y] - OMEGA * here + k1[y] * beside) * d1[2 * yc + half]
        t[yc, :ZM] = pair_sum(total)
        t[yc, ZM:] = jnp.zeros((8, LANES), F32)

    over(0, YM // 2, 4, restrict)
    lanes2 = lane_iota(24)
    rows2 = row_iota(24)
    zrow2 = rows2 + (fast * 4 - 8)
    mask2 = jnp.where(
        (zrow2 >= 0) & (zrow2 < lax.axis_size("fast") * 4) & (rows2 < 20), 1.0, 0.0
    ).astype(F32)
    own = jnp.where((rows2 >= 8) & (rows2 < 12), 0.5, 0.0).astype(F32)
    zero2 = jnp.zeros((24, LANES), F32)
    for n in (*range(PADL), *range(PADL + 16, 16 + 2 * PADL)):
        wa[n] = zero2
        wb[n] = zero2

    def halve(yc):
        return (t[yc, pl.ds(0, 24, stride=2), :] + t[yc, pl.ds(1, 24, stride=2), :]) * 0.125

    if first:
        for yc in range(16):
            q2[yc] = halve(yc)

        def coarse_diag(yc):
            block, ym = yc // 2, 2 * (yc % 2)
            t[yc, :ZM] = pair_sum(window[block, 1, ym] + window[block, 1, ym + 1])

        over(0, 16, 4, coarse_diag)
        total = zero2
        for yc in range(16):
            g2 = halve(yc)
            full = g2 + 0.375
            gain = (OMEGA / full) * mask2
            k2[yc] = gain * 0.0625
            d2[yc] = full * (1.0 / OMEGA)
            total = total + g2 * own
            start = gain * q2[yc]
            q2[yc] = start
            wa[PADL + yc] = start
            wb[PADL + yc] = start
        g2sum[...] = total
    else:
        for yc in range(16):
            start = (16.0 * k2[yc]) * halve(yc)
            q2[yc] = start
            wa[PADL + yc] = start
            wb[PADL + yc] = start
    of_q2, of_k2 = (lambda y: q2[y - PADL]), (lambda y: k2[y - PADL])

    @pl.when(sweeps[2] >= 4)
    def _():
        flat_sweep(wa, wb, of_q2, of_k2, PADL, PADL + 16, 16, lanes2, 2)

    @pl.when(sweeps[2] >= 3)
    def _():
        flat_sweep(wb, wa, of_q2, of_k2, PADL, PADL + 16, 16, lanes2, 2)

    flat_sweep(wa, wb, of_q2, of_k2, PADL, PADL + 16, 16, lanes2, 2)
    total = zero2
    for yc in range(16):
        here, beside = flat_neighbours(wb, yc + PADL, lanes2, 2)
        total = total + (q2[yc] - OMEGA * here + k2[yc] * beside) * d2[yc]
    numer = jnp.sum(total * own)
    denom = jnp.sum(g2sum[...])
    lanes_p = lane_iota(part.shape[0])
    part[...] = jnp.where(lanes_p == 0, numer, jnp.where(lanes_p == 1, denom, 0.0))
    for y in range(YPOST // 2):
        value = wb[2 * slow + (PADL - 3) + y]
        x2[y, pl.ds(0, 24, stride=2), :] = value
        x2[y, pl.ds(1, 24, stride=2), :] = value
        e2_out[y] = x2[y, ZB : 4 * ZB]


def after_kernel(last, faces, sweeps, parts, e1, q1, k1, e2, epre, q, k, field, later, out, va, vb, a, b, halves):
    lanes = lane_iota(ZW)
    lanes_p = lane_iota(parts.shape[0])
    every = parts[...]
    numer = jnp.sum(jnp.where(lanes_p == 0, every, 0.0))
    denom = jnp.sum(jnp.where(lanes_p == 1, every, 0.0)) + 0.0625 * faces
    shift = jnp.full((ZW, LANES), numer, F32) / jnp.full((ZW, LANES), denom, F32)
    base = 4 * lax.axis_index("slow") + (PADM - 6)

    def of_q1(y):
        return q1[base + y, ZB : 4 * ZB]

    def of_k1(y):
        return k1[base + y, ZB : 4 * ZB]

    for y in range(YPOST):
        raised = e1[base + y, ZB : 4 * ZB] + (e2[y // 2] + shift)
        raised = jnp.where(of_k1(y) > 0.0, raised, 0.0)
        va[y] = raised
        vb[y] = raised

    @pl.when(sweeps[1] >= 4)
    def _():
        flat_sweep(vb, va, of_q1, of_k1, 1, 15, 14, lanes, 1)

    @pl.when(sweeps[1] >= 3)
    def _():
        flat_sweep(va, vb, of_q1, of_k1, 2, 14, 12, lanes, 1)

    flat_sweep(vb, va, of_q1, of_k1, 3, 13, 10, lanes, 1)
    flat_sweep(va, vb, of_q1, of_k1, 4, 12, 8, lanes, 1)

    def raise_fine(ym):
        value = vb[ym + 4]
        for half in range(2):
            y = 2 * ym + half
            for p in PARITIES:
                raised = jnp.where(k[(*p, y + 4)] > 0.0, epre[(*p, y)] + value, 0.0)
                a[(*p, y)] = raised
                b[(*p, y)] = raised

    over(0, YPOST // 2, 4, raise_fine)

    @pl.when(sweeps[0] >= 4)
    def _():
        fine_sweep(b, a, q, k, 1, 15, 7, lanes, offset=4)

    @pl.when(sweeps[0] >= 3)
    def _():
        fine_sweep(a, b, q, k, 2, 14, 6, lanes, offset=4)

    fine_sweep(b, a, q, k, 3, 13, 10, lanes, offset=4)
    fine_sweep(a, b, q, k, 4, 12, 8, lanes, offset=4)
    for pz, px in PARITIES:
        value = field[pz, px] + 0.5 * b[pz, px, 4:12, ZB : 2 * ZB]
        if last:
            halves[px, pl.ds(pz, YB * ZB, stride=2), :] = value.reshape(YB * ZB, LANES)
        else:
            out[0, pz, px] = value
            out[1, pz, px] = later[pz, px]
    if last:
        both = jnp.concatenate([halves[0], halves[1]], axis=1)
        out[...] = exact_dot(both, parity_matrix(True)).reshape(YB, 2 * ZB, 2 * LANES)


def call(kernel, outs, scratch, scalars, *arrays, space=pltpu.VMEM, megabytes=16):
    specs = [pl.BlockSpec(memory_space=pltpu.SMEM)] * len(scalars)
    return pl.pallas_call(
        kernel,
        out_shape=[jax.ShapeDtypeStruct(s, F32) for s in outs],
        in_specs=specs + [pl.BlockSpec(memory_space=space)] * len(arrays),
        out_specs=[pl.BlockSpec(memory_space=pltpu.VMEM)] * len(outs),
        scratch_shapes=[pltpu.VMEM(s, F32) if isinstance(s, tuple) else s for s in scratch],
        compiler_params=pltpu.CompilerParams(vmem_limit_bytes=megabytes * 1024 * 1024),
    )(*scalars, *arrays)


def both_ways(to_right, to_left, axis):
    count = lax.axis_size(axis)
    up = [(i, (i + 1) % count) for i in range(count)]
    down = [(target, source) for source, target in up]
    return lax.ppermute(to_right, axis, up), lax.ppermute(to_left, axis, down)


def window_of(fields):
    left, right = both_ways(fields, fields, "fast")
    mid = jnp.stack([left, fields, right])
    low, high = both_ways(mid, mid, "slow")
    return mid, low, high


def body(observed, start_field, diagonal, noise, sweeps):
    natural = observed.shape
    block = (2, 2, YB, ZB, LANES)
    post = (2, 2, YPOST, ZW, LANES)
    whole = (2, 2, YW, ZW, LANES)
    middle = (YM + 2 * PADM, ZM, LANES)
    low_window = (16, 24, LANES)
    fast_count, slow_count = lax.axis_size("fast"), lax.axis_size("slow")
    first, second, third = YB * slow_count // 4, 2 * ZB * fast_count // 4, 2 * LANES // 4
    faces = 2.0 * (first * second + first * third + second * third)
    fields, later = call(
        split_kernel, [(3, *block), block],
        [natural, natural, natural, (2, *natural), (4, 2, YB * 2 * ZB, LANES), pltpu.SemaphoreType.DMA((4,))],
        (), observed, start_field, diagonal, noise, space=pltpu.HBM,
    )
    field = fields[0]
    kept_fine = kept_low = None
    for step in range(2):
        opening = step == 0
        count = 2 if opening else 1
        mid, low, high = window_of(fields)
        outs = [(count, 4, 16, LANES), (count, 4, 8, LANES), (count, 4, 16, LANES), post, whole]
        if opening:
            outs += [whole, (2, 2, YB, ZW, LANES)]
            given = (mid, low, high)
        else:
            given = (mid, low, high, *kept_fine)
        got = call(functools.partial(before_kernel, opening), outs, [whole] * 3, (sweeps,), *given)
        to_left, own, to_right, epre, q = got[:5]
        if opening:
            kept_fine = got[5:]
        left, right = both_ways(to_right, to_left, "fast")
        strip = jnp.concatenate([left, own, right], axis=2)
        strip = jnp.broadcast_to(strip[None], (slow_count, *strip.shape))
        strip = lax.all_to_all(strip, "slow", 0, 0, tiled=True)
        outs = [(fast_count, LANES), middle, middle, (YPOST // 2, ZW, LANES)]
        scratch = [
            middle, (16, ZM + 8, LANES), (16 + 2 * PADL, 24, LANES), (16 + 2 * PADL, 24, LANES),
            low_window, (YPOST // 2, 48, LANES),
        ]
        if opening:
            outs += [middle, (YM, ZM, LANES), low_window, low_window, (24, LANES)]
            given = (strip,)
        else:
            given = (strip, *kept_low)
        got = call(functools.partial(coarse_kernel, opening), outs, scratch, (sweeps,), *given)
        part, e1, q1, e2 = got[:4]
        if opening:
            kept_low = got[4:]
        parts = lax.all_to_all(part, "fast", 0, 0, tiled=True)
        outs = [(2, *block) if opening else natural]
        scratch = [(YPOST, ZW, LANES)] * 2 + [post] * 2 + [(2, YB * 2 * ZB, LANES)]
        (fields,) = call(
            functools.partial(after_kernel, not opening, faces), outs, scratch, (sweeps,),
            parts, e1, q1, kept_low[0], e2, epre, q, kept_fine[0], field, later,
        )
        field = fields[0]
    return fields


def solution(mesh):
    placed = (
        P("slow", "fast", None),
        P("slow", "fast", None),
        P("slow", "fast", None),
        P(None, "slow", "fast", None),
        P(),
    )
    return jax.shard_map(
        body, mesh=mesh, in_specs=placed, out_specs=P("slow", "fast", None), check_vma=False
    )
```

time: 232 us -> 192 us (0.83)
  Pallas kernels: 58.5 us -> 19 us
    pallas_call x7, Pallas kernels: 58.5 us -> 19 us  [call(): pl.pallas_call(kernel, out_shape=[jax.ShapeDtypeStruct(s, F32) for s in o...]
    unnamed x86 -> x80, local copies, waits for them, and re-layouts: 24.8 us -> 24.3 us
  transfers between devices with their start and end apart: 14 -> 14, of which waited for: 10 -> 10; matrix products, arithmetic and copies ran while one was open for 0% -> 1% of each run, Pallas kernels for 0% -> 0%
where the time goes in v2:
time: 192 us; the launch traced here: 191 us
  waiting for transfers between devices  63.7 us (33%)
  blocking collectives  41.2 us (21%)
  starting transfers between devices  40.6 us (21%)
  local copies, waits for them, and re-layouts  26.1 us (14%)
  Pallas kernels  19 us (10%)
    ppermute x12, waiting for transfers between devices, both_ways(): return (lax.ppermute(to_right, axis, up), lax.ppermute(to_left, axis, down))  48.2 us
    all_to_all x2, blocking collectives, body(): strip = lax.all_to_all(strip, 'slow', 0, 0, tiled=True)  41.2 us
    ppermute x12, starting transfers between devices, both_ways(): return (lax.ppermute(to_right, axis, up), lax.ppermute(to_left, axis, down))  27 us
    unnamed x80, local copies, waits for them, and re-layouts  24.3 us
    pallas_call x7, Pallas kernels, call(): pl.pallas_call(kernel, out_shape=[jax.ShapeDtypeStruct(s, F32) for s in o...  19 us
    all_to_all x2, waiting for transfers between devices, body(): parts = lax.all_to_all(part, 'fast', 0, 0, tiled=True)  15.5 us
    all_to_all x2, starting transfers between devices, body(): parts = lax.all_to_all(part, 'fast', 0, 0, tiled=True)  13.6 us
  transfers between devices with their start and end apart: 14, of which 10 were waited for; matrix products, arithmetic and copies ran while one was open for 1% of the time, Pallas kernels for 0%

profile of v2, /device:TPU:1, one launch (start us, length us, event | category | flops | bytes accessed | tf_op | source)
XLA Modules:
  0.0 191.0 jit_solution(12847080064746540803)
XLA Ops:
  0.0 0.9 copy-done.21
  1.0 0.9 copy-done.26
  1.9 0.9 copy-done.27
  2.8 0.9 copy-done.28
  3.7 1.7 shard_map.55
  5.4 8.7 %collective-permute-start.1 = (f32[3,2,2,8,8,128]{5,4,3,2,1,0:T(8,128)S(1)}, f32[3,2,2,8,8,128]{5,4,3,2,1,0:T(8,128)S(1)}, u32[]{:S(2)}, u32[]{:S(2)}) collective-permute-start(f32[3,2,2,8,8,128]{5,4,3,2,1,0:T(8,128)S(1)} %get-tuple-element.32), channel_id=1, source_target_pairs={{1,0},{2,1},{3,2},{4,3},{5,4},{6,5},{7,6},{8,7},{9,8},{10,9},{11,1... | collective-permute-start | bytes 1179656 | tf_op jit(solution)/shard_map/ppermute | solution.py:433
  14.1 7.8 %collective-permute-done.1 = f32[3,2,2,8,8,128]{5,4,3,2,1,0:T(8,128)S(1)} collective-permute-done((f32[3,2,2,8,8,128]{5,4,3,2,1,0:T(8,128)S(1)}, f32[3,2,2,8,8,128]{5,4,3,2,1,0:T(8,128)S(1)}, u32[]{:S(2)}, u32[]{:S(2)}) %collective-permute-start.1) | collective-permute-done | bytes 393248 | tf_op jit(solution)/shard_map/ppermute | solution.py:433
  21.9 5.2 %collective-permute-done = f32[3,2,2,8,8,128]{5,4,3,2,1,0:T(8,128)S(1)} collective-permute-done((f32[3,2,2,8,8,128]{5,4,3,2,1,0:T(8,128)S(1)}, f32[3,2,2,8,8,128]{5,4,3,2,1,0:T(8,128)S(1)}, u32[]{:S(2)}, u32[]{:S(2)}) %collective-permute-start) | collective-permute-done | bytes 393248 | tf_op jit(solution)/shard_map/ppermute | solution.py:433
  27.1 0.1 pad_maximum_fusion.refs_0_
  27.2 1.9 collective-permute-start.3
  29.1 1.2 collective-permute-start.2
  30.3 14.2 %collective-permute-done.3.refs_2_ = f32[3,3,2,2,8,8,128]{6,5,4,3,2,1,0:T(8,128)S(1)} collective-permute-done((f32[3,3,2,2,8,8,128]{6,5,4,3,2,1,0:T(8,128)S(1)}, f32[3,3,2,2,8,8,128]{6,5,4,3,2,1,0:T(8,128)S(1)}, u32[]{:S(2)}, u32[]{:S(2)}) %collective-permute-start.3) | collective-permute-done | bytes 1179680 | tf_op jit(solution)/shard_map/ppermute | solution.py:433
  44.5 2.0 %shard_map.56 = (f32[2,4,16,128]{3,2,1,0:T(8,128)S(1)}, f32[2,4,8,128]{3,2,1,0:T(8,128)S(1)}, f32[2,4,16,128]{3,2,1,0:T(8,128)S(1)}, f32[2,2,16,24,128]{4,3,2,1,...) custom-call(s32[3]{0:T(128)S(1)} %copy-done.33, ...), custom_call_target="tpu_custom_call" | custom-call | tf_op jit(solution)/shard_map/pallas_call | solution.py:419
  46.5 1.0 copy-done.2
  47.5 4.8 %collective-permute-start.5 = (f32[2,4,16,128]{3,2,1,0:T(8,128)S(1)}, f32[2,4,16,128]{3,2,1,0:T(8,128)S(1)}, u32[]{:S(2)}, u32[]{:S(2)}) collective-permute-start(f32[2,4,16,128]{3,2,1,0:T(8,128)S(1)} %get-tuple-element.35), channel_id=1, source_target_pairs={{1,0},{2,1},{3,2},{4,3},{5,4},{6,5},{7,6},{8,7},{9,8},{10,9},{11,1... | collective-permute-start | bytes 196616 | tf_op jit(solution)/shard_map/ppermute | solution.py:433
  52.3 1.6 collective-permute-done.4
  54.0 0.1 broadcast_in_dim.6
  54.1 24.2 %all_to_all.32.refs_0_ = f32[8,2,4,40,128]{4,3,2,1,0:T(8,128)S(1)} all-to-all(f32[8,2,4,40,128]{4,3,2,1,0:T(8,128)S(1)} %broadcast_in_dim.6), channel_id=1, replica_groups=mesh['slow'=8,'fast'=32] {'slow'}, dimensions={0} | all-to-all | bytes 2621440 | tf_op jit(solution)/shard_map/all_to_all | solution.py:477
  78.3 5.2 %shard_map.57 = (f32[32,128]{1,0:T(8,128)}, f32[48,40,128]{2,1,0:T(8,128)S(1)}, f32[48,40,128]{2,1,0:T(8,128)S(1)}, f32[8,24,128]{2,1,0:T(8,128)S(1)}, f32[48,40...) custom-call(s32[3]{0:T(128)S(1)} %copy-done.33, ...), custom_call_target="tpu_custom_call" | custom-call | tf_op jit(solution)/shard_map/pallas_call | solution.py:419
  83.5 1.0 copy-done.6
  84.5 0.8 copy-done.13
  85.3 0.7 copy-done.22
  86.0 0.7 copy-done.24
  86.6 0.6 copy-done.29
  87.3 0.6 copy-done.38
  87.9 6.7 %all-to-all-start.1 = ((f32[32,1,128]{2,1,0:T(1,128)}), f32[32,1,128]{2,1,0:T(1,128)S(1)}, u32[]{:S(2)}, u32[]{:S(2)}) async-start(f32[32,1,128]{2,1,0:T(1,128)} %bitcast.4), calls=%async_computation.1 | async-start | bytes 32768 | tf_op jit(solution)/shard_map/all_to_all | solution.py:492
  94.6 0.9 slice_bitcast_fusion.1.field
  95.5 7.5 %all-to-all-done.1 = f32[32,1,128]{2,1,0:T(1,128)S(1)} async-done(((f32[32,1,128]{2,1,0:T(1,128)}), f32[32,1,128]{2,1,0:T(1,128)S(1)}, u32[]{:S(2)}, u32[]{:S(2)}) %all-to-all-start.1) | async-done | bytes 16416 | tf_op jit(solution)/shard_map/all_to_all | solution.py:492
  103.1 1.3 copy-done.3
  104.3 1.2 copy-done.7
  105.5 1.1 copy-done.11
  106.7 0.9 copy-done.16
  107.6 0.9 copy-done.30
  108.5 0.7 copy-done.34
  109.1 1.6 shard_map.58
  110.7 1.2 collective-permute-start.7
  111.9 0.4 collective-permute-start.6
  112.3 3.8 %collective-permute-done.7 = f32[2,2,2,8,8,128]{5,4,3,2,1,0:T(8,128)S(1)} collective-permute-done((f32[2,2,2,8,8,128]{5,4,3,2,1,0:T(8,128)S(1)}, f32[2,2,2,8,8,128]{5,4,3,2,1,0:T(8,128)S(1)}, u32[]{:S(2)}, u32[]{:S(2)}) %collective-permute-start.7) | collective-permute-done | bytes 262176 | tf_op jit(solution)/shard_map/ppermute | solution.py:433
  116.0 4.4 %collective-permute-done.6 = f32[2,2,2,8,8,128]{5,4,3,2,1,0:T(8,128)S(1)} collective-permute-done((f32[2,2,2,8,8,128]{5,4,3,2,1,0:T(8,128)S(1)}, f32[2,2,2,8,8,128]{5,4,3,2,1,0:T(8,128)S(1)}, u32[]{:S(2)}, u32[]{:S(2)}) %collective-permute-start.6) | collective-permute-done | bytes 262176 | tf_op jit(solution)/shard_map/ppermute | solution.py:433
  120.5 0.1 pad_maximum_fusion.1.refs_0_
  120.5 3.9 %collective-permute-start.9 = (f32[3,2,2,2,8,8,128]{6,5,4,3,2,1,0:T(8,128)S(1)}, f32[3,2,2,2,8,8,128]{6,5,4,3,2,1,0:T(8,128)S(1)}, u32[]{:S(2)}, u32[]{:S(2)}) collective-permute-start(f32[3,2,2,2,8,8,128]{6,5,4,3,2,1,0:T(8,128)S(1)} %pad_maximum_fusion.1.refs_0_), channel_id=1, source_target_pairs={{32,0},{64,32},{96,64},{128,96},{160,128},{192,160},{224,192},{0,2... | collective-permute-start | bytes 2359304 | tf_op jit(solution)/shard_map/ppermute | solution.py:433
  124.4 0.2 collective-permute-start.8
  124.6 9.9 %collective-permute-done.9.refs_2_ = f32[3,2,2,2,8,8,128]{6,5,4,3,2,1,0:T(8,128)S(1)} collective-permute-done((f32[3,2,2,2,8,8,128]{6,5,4,3,2,1,0:T(8,128)S(1)}, f32[3,2,2,2,8,8,128]{6,5,4,3,2,1,0:T(8,128)S(1)}, u32[]{:S(2)}, u32[]{:S(2)}) %collective-permute-start.9) | collective-permute-done | bytes 786464 | tf_op jit(solution)/shard_map/ppermute | solution.py:433
  134.6 2.1 %shard_map.59 = (f32[1,4,16,128]{3,2,1,0:T(8,128)S(1)}, f32[1,4,8,128]{3,2,1,0:T(8,128)S(1)}, f32[1,4,16,128]{3,2,1,0:T(8,128)S(1)}, f32[2,2,16,24,128]{4,3,2,1,0:T(8,128)S(1)}, f32[2,2,24,24,128]{4,3,2,1,0:T(8,128)S(1)}) custom-call(s32[3]{0:T(128)S(1)} %copy-done.35, f32[3,2,2,2,8,8,128]{6,5,4,3,2,1,0:T(8,128)S(1)} %pad_maximum_fusion.1.refs_0_, ...), custom_call_target="tpu_custom_call" | custom-call | tf_op jit(solution)/shard_map/pallas_call | solution.py:419
  136.7 0.9 copy-done.8
  137.6 0.1 collective-permute-start.10
  137.7 4.8 %collective-permute-start.11 = (f32[1,4,16,128]{3,2,1,0:T(8,128)S(1)}, f32[1,4,16,128]{3,2,1,0:T(8,128)S(1)}, u32[]{:S(2)}, u32[]{:S(2)}) collective-permute-start(f32[1,4,16,128]{3,2,1,0:T(8,128)S(1)} %get-tuple-element.48), channel_id=1, source_target_pairs={{1,0},{2,1},{3,2},{4,3},{5,4},{6,5},{7,6},{8,7},{9,8},{10,9},{11,1... | collective-permute-start | bytes 98312 | tf_op jit(solution)/shard_map/ppermute | solution.py:433
  142.5 1.3 collective-permute-done.10
  143.8 17.0 %all_to_all.33.refs_0_ = f32[8,1,4,40,128]{4,3,2,1,0:T(8,128)S(1)} all-to-all(f32[8,1,4,40,128]{4,3,2,1,0:T(8,128)S(1)} %broadcast_in_dim.16), channel_id=1, replica_groups=mesh['slow'=8,'fast'=32] {'slow'}, dimensions={0} | all-to-all | bytes 1310720 | tf_op jit(solution)/shard_map/all_to_all | solution.py:477
  160.8 0.0 copy-start.17
  160.8 4.0 %shard_map.60 = (f32[32,128]{1,0:T(8,128)S(1)}, f32[48,40,128]{2,1,0:T(8,128)S(1)}, f32[48,40,128]{2,1,0:T(8,128)S(1)}, f32[8,24,128]{2,1,0:T(8,128)S(1)}) custom-call(s32[3]{0:T(128)S(1)} %copy-done.35, f32[8,1,4,40,128]{4,3,2,1,0:T(8,128)S(1)} %all_to_all.33.refs_0_, f32[48,40,128]{2,1,0:T(8,128)S(1)} %get-tuple-element.39.k1.refs_1_, ...), custom_call_target="tpu_custom_call" | custom-call | tf_op jit(solution)/shard_map/pallas_call | solution.py:419
  164.8 1.0 copy-done.4
  165.8 0.6 copy-done.31
  166.5 0.6 copy-done.37
  167.1 6.8 %all-to-all-start.3 = ((f32[32,1,128]{2,1,0:T(1,128)}), f32[32,1,128]{2,1,0:T(1,128)S(1)}, u32[]{:S(2)}, u32[]{:S(2)}) async-start(f32[32,1,128]{2,1,0:T(1,128)} %bitcast.24), calls=%async_computation.3 | async-start | bytes 32768 | tf_op jit(solution)/shard_map/all_to_all | solution.py:492
  173.9 0.7 slice_bitcast_fusion.field
  174.5 7.9 %all-to-all-done.3 = f32[32,1,128]{2,1,0:T(1,128)S(1)} async-done(((f32[32,1,128]{2,1,0:T(1,128)}), f32[32,1,128]{2,1,0:T(1,128)S(1)}, u32[]{:S(2)}, u32[]{:S(2)}) %all-to-all-start.3) | async-done | bytes 16416 | tf_op jit(solution)/shard_map/all_to_all | solution.py:492
  182.5 1.3 copy-done.1
  183.8 1.2 copy-done.5
  185.0 1.1 copy-done.9
  186.1 0.9 copy-done.18
  187.0 0.9 copy-done.32
  187.9 0.7 copy-done.36
  188.6 2.4 %shard_map.61 = f32[8,16,256]{2,1,0:T(8,128)} custom-call(s32[3]{0:T(128)S(1)} %copy-done.36, f32[32,128]{1,0:T(8,128)S(1)} %bitcast.22, f32[48,40,128]{2,1,0:T(8,128)S(1)} %get-tuple-element.54.e1, f32[48,40,128]{2,1,0:T(8,128)S(1)} %copy-done.5, f32[48,40,128]{2,1,0:T(8,128)S(1)} %get-tuple-element.39.k1.refs_1_, f32[8,24,128]{2,1,0:T(8,128)S(1)} %copy-done.32, ...), custom_call_target="tpu_custom_call" | custom-call | tf_op jit(solution)/shard_map/pallas_call | solution.py:419
  (61 shorter events, 0.2 us)
Async XLA Ops:
  0.0 0.9 copy-start.21
  1.0 0.9 copy-start.26
  1.9 0.9 copy-start.27
  2.8 0.9 copy-start.28
  5.4 21.8 %copy-start.12 = (f32[3,2,2,8,8,128]{5,4,3,2,1,0:T(8,128)}, f32[3,2,2,8,8,128]{5,4,3,2,1,0:T(8,128)S(1)}, u32[]{:S(2)}) copy-start(f32[3,2,2,8,8,128]{5,4,3,2,1,0:T(8,128)S(1)} %get-tuple-element.32) | copy-start | bytes 1179652
  5.4 21.8 %copy-start.15 = (f32[2,2,8,8,128]{4,3,2,1,0:T(8,128)}, f32[2,2,8,8,128]{4,3,2,1,0:T(8,128)S(1)}, u32[]{:S(2)}) copy-start(f32[2,2,8,8,128]{4,3,2,1,0:T(8,128)S(1)} %get-tuple-element.44.later) | copy-start | bytes 393220
  5.4 16.5 %collective-permute-start.1 = (f32[3,2,2,8,8,128]{5,4,3,2,1,0:T(8,128)S(1)}, f32[3,2,2,8,8,128]{5,4,3,2,1,0:T(8,128)S(1)}, u32[]{:S(2)}, u32[]{:S(2)}) collective-permute-start(f32[3,2,2,8,8,128]{5,4,3,2,1,0:T(8,128)S(1)} %get-tuple-element.32), channel_id=1, source_target_pairs={{1,0},{2,1},{3,2},{4,3},{5,4},{6,5},{7,6},{8,7},{9,8},{10,9},{11,1... | collective-permute-start | bytes 1179656 | tf_op jit(solution)/shard_map/ppermute | solution.py:433
  14.1 13.0 %collective-permute-start = (f32[3,2,2,8,8,128]{5,4,3,2,1,0:T(8,128)S(1)}, f32[3,2,2,8,8,128]{5,4,3,2,1,0:T(8,128)S(1)}, u32[]{:S(2)}, u32[]{:S(2)}) collective-permute-start(f32[3,2,2,8,8,128]{5,4,3,2,1,0:T(8,128)S(1)} %get-tuple-element.32), channel_id=1, source_target_pairs={{0,1},{1,2},{2,3},{3,4},{4,5},{5,6},{6,7},{7,8},{8,9},{9,10},{10,1... | collective-permute-start | bytes 1179656 | tf_op jit(solution)/shard_map/ppermute | solution.py:433
  27.1 17.4 %copy-start.33 = (s32[3]{0:T(128)S(1)}, s32[3]{0:T(128)}, u32[]{:S(2)}) copy-start(s32[3]{0:T(128)} %sweeps.11) | copy-start | bytes 40
  27.2 17.2 %collective-permute-start.3 = (f32[3,3,2,2,8,8,128]{6,5,4,3,2,1,0:T(8,128)S(1)}, f32[3,3,2,2,8,8,128]{6,5,4,3,2,1,0:T(8,128)S(1)}, u32[]{:S(2)}, u32[]{:S(2)}) collective-permute-start(f32[3,3,2,2,8,8,128]{6,5,4,3,2,1,0:T(8,128)S(1)} %pad_maximum_fusion.refs_0_), channel_id=1, source_target_pairs={{32,0},{64,32},{96,64},{128,96},{160,128},{192,160},{224,192},{0,2... | collective-permute-start | bytes 3538952 | tf_op jit(solution)/shard_map/ppermute | solution.py:433
  29.1 15.4 %collective-permute-start.2 = (f32[3,3,2,2,8,8,128]{6,5,4,3,2,1,0:T(8,128)S(1)}, f32[3,3,2,2,8,8,128]{6,5,4,3,2,1,0:T(8,128)S(1)}, u32[]{:S(2)}, u32[]{:S(2)}) collective-permute-start(f32[3,3,2,2,8,8,128]{6,5,4,3,2,1,0:T(8,128)S(1)} %pad_maximum_fusion.refs_0_), channel_id=1, source_target_pairs={{0,32},{32,64},{64,96},{96,128},{128,160},{160,192},{192,224},{224... | collective-permute-start | bytes 3538952 | tf_op jit(solution)/shard_map/ppermute | solution.py:433
  46.5 1.0 copy-start.2
  47.5 6.6 %copy-start.10 = (f32[2,2,16,24,128]{4,3,2,1,0:T(8,128)}, f32[2,2,16,24,128]{4,3,2,1,0:T(8,128)S(1)}, u32[]{:S(2)}) copy-start(f32[2,2,16,24,128]{4,3,2,1,0:T(8,128)S(1)} %get-tuple-element.41.epre) | copy-start | bytes 2359300
  47.5 30.8 %copy-start.19 = (f32[2,2,8,24,128]{4,3,2,1,0:T(8,128)}, f32[2,2,8,24,128]{4,3,2,1,0:T(8,128)S(1)}, u32[]{:S(2)}) copy-start(f32[2,2,8,24,128]{4,3,2,1,0:T(8,128)S(1)} %get-tuple-element.45.refs_4_) | copy-start | bytes 1179652
  47.5 6.4 %collective-permute-start.4 = (f32[2,4,16,128]{3,2,1,0:T(8,128)S(1)}, f32[2,4,16,128]{3,2,1,0:T(8,128)S(1)}, u32[]{:S(2)}, u32[]{:S(2)}) collective-permute-start(f32[2,4,16,128]{3,2,1,0:T(8,128)S(1)} %get-tuple-element.33), channel_id=1, source_target_pairs={{0,1},{1,2},{2,3},{3,4},{4,5},{5,6},{6,7},{7,8},{8,9},{9,10},{10,1... | collective-permute-start | bytes 196616 | tf_op jit(solution)/shard_map/ppermute | solution.py:433
  47.5 6.4 %collective-permute-start.5 = (f32[2,4,16,128]{3,2,1,0:T(8,128)S(1)}, f32[2,4,16,128]{3,2,1,0:T(8,128)S(1)}, u32[]{:S(2)}, u32[]{:S(2)}) collective-permute-start(f32[2,4,16,128]{3,2,1,0:T(8,128)S(1)} %get-tuple-element.35), channel_id=1, source_target_pairs={{1,0},{2,1},{3,2},{4,3},{5,4},{6,5},{7,6},{8,7},{9,8},{10,9},{11,1... | collective-permute-start | bytes 196616 | tf_op jit(solution)/shard_map/ppermute | solution.py:433
  83.5 1.0 copy-start.6
  84.5 0.8 copy-start.13
  85.3 0.7 copy-start.22
  86.0 0.7 copy-start.24
  86.6 0.7 copy-start.29
  87.3 0.6 copy-start.38
  87.9 15.2 %all-to-all-start.1 = ((f32[32,1,128]{2,1,0:T(1,128)}), f32[32,1,128]{2,1,0:T(1,128)S(1)}, u32[]{:S(2)}, u32[]{:S(2)}) async-start(f32[32,1,128]{2,1,0:T(1,128)} %bitcast.4), calls=%async_computation.1 | async-start | bytes 32768 | tf_op jit(solution)/shard_map/all_to_all | solution.py:492
  103.1 1.3 copy-start.3
  104.3 1.2 copy-start.7
  105.5 1.1 copy-start.11
  106.7 0.9 copy-start.16
  107.6 0.9 copy-start.30
  108.5 0.7 copy-start.34
  110.7 23.9 %copy-start.20 = (f32[2,2,8,24,128]{4,3,2,1,0:T(8,128)S(1)}, f32[2,2,8,24,128]{4,3,2,1,0:T(8,128)}, u32[]{:S(2)}) copy-start(f32[2,2,8,24,128]{4,3,2,1,0:T(8,128)} %copy-done.19) | copy-start | bytes 1179652
  110.7 23.9 %copy-start.35 = (s32[3]{0:T(128)S(1)}, s32[3]{0:T(128)}, u32[]{:S(2)}) copy-start(s32[3]{0:T(128)} %sweeps.11) | copy-start | bytes 40
  110.7 5.3 %collective-permute-start.7 = (f32[2,2,2,8,8,128]{5,4,3,2,1,0:T(8,128)S(1)}, f32[2,2,2,8,8,128]{5,4,3,2,1,0:T(8,128)S(1)}, u32[]{:S(2)}, u32[]{:S(2)}) collective-permute-start(f32[2,2,2,8,8,128]{5,4,3,2,1,0:T(8,128)S(1)} %shard_map.58), channel_id=1, source_target_pairs={{1,0},{2,1},{3,2},{4,3},{5,4},{6,5},{7,6},{8,7},{9,8},{10,9},{11,1... | collective-permute-start | bytes 786440 | tf_op jit(solution)/shard_map/ppermute | solution.py:433
  111.9 8.5 %collective-permute-start.6 = (f32[2,2,2,8,8,128]{5,4,3,2,1,0:T(8,128)S(1)}, f32[2,2,2,8,8,128]{5,4,3,2,1,0:T(8,128)S(1)}, u32[]{:S(2)}, u32[]{:S(2)}) collective-permute-start(f32[2,2,2,8,8,128]{5,4,3,2,1,0:T(8,128)S(1)} %shard_map.58), channel_id=1, source_target_pairs={{0,1},{1,2},{2,3},{3,4},{4,5},{5,6},{6,7},{7,8},{8,9},{9,10},{10,1... | collective-permute-start | bytes 786440 | tf_op jit(solution)/shard_map/ppermute | solution.py:433
  120.5 14.0 %collective-permute-start.9 = (f32[3,2,2,2,8,8,128]{6,5,4,3,2,1,0:T(8,128)S(1)}, f32[3,2,2,2,8,8,128]{6,5,4,3,2,1,0:T(8,128)S(1)}, u32[]{:S(2)}, u32[]{:S(2)}) collective-permute-start(f32[3,2,2,2,8,8,128]{6,5,4,3,2,1,0:T(8,128)S(1)} %pad_maximum_fusion.1.refs_0_), channel_id=1, source_target_pairs={{32,0},{64,32},{96,64},{128,96},{160,128},{192,160},{224,192},{0,2... | collective-permute-start | bytes 2359304 | tf_op jit(solution)/shard_map/ppermute | solution.py:433
  124.4 10.1 %collective-permute-start.8 = (f32[3,2,2,2,8,8,128]{6,5,4,3,2,1,0:T(8,128)S(1)}, f32[3,2,2,2,8,8,128]{6,5,4,3,2,1,0:T(8,128)S(1)}, u32[]{:S(2)}, u32[]{:S(2)}) collective-permute-start(f32[3,2,2,2,8,8,128]{6,5,4,3,2,1,0:T(8,128)S(1)} %pad_maximum_fusion.1.refs_0_), channel_id=1, source_target_pairs={{0,32},{32,64},{64,96},{96,128},{128,160},{160,192},{192,224},{224... | collective-permute-start | bytes 2359304 | tf_op jit(solution)/shard_map/ppermute | solution.py:433
  136.7 0.9 copy-start.8
  137.6 27.2 %copy-start = (f32[2,2,24,24,128]{4,3,2,1,0:T(8,128)}, f32[2,2,24,24,128]{4,3,2,1,0:T(8,128)S(1)}, u32[]{:S(2)}) copy-start(f32[2,2,24,24,128]{4,3,2,1,0:T(8,128)S(1)} %get-tuple-element.58.q) | copy-start | bytes 3538948
  137.6 23.2 %copy-start.14 = (f32[32,40,128]{2,1,0:T(8,128)S(1)}, f32[32,40,128]{2,1,0:T(8,128)}, u32[]{:S(2)}) copy-start(f32[32,40,128]{2,1,0:T(8,128)} %copy-done.13) | copy-start | bytes 1966084
  137.6 23.2 %copy-start.23 = (f32[16,24,128]{2,1,0:T(8,128)S(1)}, f32[16,24,128]{2,1,0:T(8,128)}, u32[]{:S(2)}) copy-start(f32[16,24,128]{2,1,0:T(8,128)} %copy-done.22) | copy-start | bytes 589828
  137.6 23.2 %copy-start.25 = (f32[16,24,128]{2,1,0:T(8,128)S(1)}, f32[16,24,128]{2,1,0:T(8,128)}, u32[]{:S(2)}) copy-start(f32[16,24,128]{2,1,0:T(8,128)} %copy-done.24) | copy-start | bytes 589828
  137.6 23.2 %copy-start.39 = (f32[24,128]{1,0:T(8,128)S(1)}, f32[24,128]{1,0:T(8,128)}, u32[]{:S(2)}) copy-start(f32[24,128]{1,0:T(8,128)} %copy-done.38) | copy-start | bytes 36868
  137.6 6.2 %collective-permute-start.10 = (f32[1,4,16,128]{3,2,1,0:T(8,128)S(1)}, f32[1,4,16,128]{3,2,1,0:T(8,128)S(1)}, u32[]{:S(2)}, u32[]{:S(2)}) collective-permute-start(f32[1,4,16,128]{3,2,1,0:T(8,128)S(1)} %get-tuple-element.46), channel_id=1, source_target_pairs={{0,1},{1,2},{2,3},{3,4},{4,5},{5,6},{6,7},{7,8},{8,9},{9,10},{10,1... | collective-permute-start | bytes 98312 | tf_op jit(solution)/shard_map/ppermute | solution.py:433
  137.7 6.1 %collective-permute-start.11 = (f32[1,4,16,128]{3,2,1,0:T(8,128)S(1)}, f32[1,4,16,128]{3,2,1,0:T(8,128)S(1)}, u32[]{:S(2)}, u32[]{:S(2)}) collective-permute-start(f32[1,4,16,128]{3,2,1,0:T(8,128)S(1)} %get-tuple-element.48), channel_id=1, source_target_pairs={{1,0},{2,1},{3,2},{4,3},{5,4},{6,5},{7,6},{8,7},{9,8},{10,9},{11,1... | collective-permute-start | bytes 98312 | tf_op jit(solution)/shard_map/ppermute | solution.py:433
  160.8 21.7 %copy-start.17 = (f32[2,2,8,8,128]{4,3,2,1,0:T(8,128)S(1)}, f32[2,2,8,8,128]{4,3,2,1,0:T(8,128)}, u32[]{:S(2)}) copy-start(f32[2,2,8,8,128]{4,3,2,1,0:T(8,128)} %copy-done.15) | copy-start | bytes 393220
  164.8 1.0 copy-start.4
  165.8 0.7 copy-start.31
  166.5 0.6 copy-start.37
  167.1 15.4 %all-to-all-start.3 = ((f32[32,1,128]{2,1,0:T(1,128)}), f32[32,1,128]{2,1,0:T(1,128)S(1)}, u32[]{:S(2)}, u32[]{:S(2)}) async-start(f32[32,1,128]{2,1,0:T(1,128)} %bitcast.24), calls=%async_computation.3 | async-start | bytes 32768 | tf_op jit(solution)/shard_map/all_to_all | solution.py:492
  182.5 1.3 copy-start.1
  183.8 1.2 copy-start.5
  185.0 1.1 copy-start.9
  186.1 0.9 copy-start.18
  187.0 0.9 copy-start.32
  187.9 0.7 copy-start.36

commit v3 on v2

--- a/solution.py
+++ b/solution.py
@@ -414,11 +414,13 @@
         out[...] = exact_dot(both, parity_matrix(True)).reshape(YB, 2 * ZB, 2 * LANES)
 
 
-def call(kernel, outs, scratch, scalars, *arrays, space=pltpu.VMEM, megabytes=16):
+def call(kernel, outs, scratch, scalars, *arrays, space=pltpu.VMEM, megabytes=16, kept=True):
     specs = [pl.BlockSpec(memory_space=pltpu.SMEM)] * len(scalars)
+    if space == pltpu.HBM:
+        arrays = [pltpu.with_memory_space_constraint(x, pltpu.HBM) for x in arrays]
     return pl.pallas_call(
         kernel,
-        out_shape=[jax.ShapeDtypeStruct(s, F32) for s in outs],
+        out_shape=[pltpu.VMEM(s, F32) if kept else jax.ShapeDtypeStruct(s, F32) for s in outs],
         in_specs=specs + [pl.BlockSpec(memory_space=space)] * len(arrays),
         out_specs=[pl.BlockSpec(memory_space=pltpu.VMEM)] * len(outs),
         scratch_shapes=[pltpu.VMEM(s, F32) if isinstance(s, tuple) else s for s in scratch],
@@ -494,7 +496,7 @@
         scratch = [(YPOST, ZW, LANES)] * 2 + [post] * 2 + [(2, YB * 2 * ZB, LANES)]
         (fields,) = call(
             functools.partial(after_kernel, not opening, faces), outs, scratch, (sweeps,),
-            parts, e1, q1, kept_low[0], e2, epre, q, kept_fine[0], field, later,
+            parts, e1, q1, kept_low[0], e2, epre, q, kept_fine[0], field, later, kept=opening,
         )
         field = fields[0]
     return fields

time: 192 us -> 190 us (0.990)
  local copies, waits for them, and re-layouts: 26.1 us -> 22.5 us
    unnamed x80 -> x72, local copies, waits for them, and re-layouts: 24.3 us -> 20.7 us
where the time goes in v3:
time: 190 us; the launch traced here: 189 us
  waiting for transfers between devices  63.7 us (34%)
  blocking collectives  41.2 us (22%)
  starting transfers between devices  40.6 us (21%)
  local copies, waits for them, and re-layouts  22.5 us (12%)
  Pallas kernels  20.6 us (11%)
    ppermute x12, waiting for transfers between devices, both_ways(): return (lax.ppermute(to_right, axis, up), lax.ppermute(to_left, axis, down))  48.2 us
    all_to_all x2, blocking collectives, body(): strip = lax.all_to_all(strip, 'slow', 0, 0, tiled=True)  41.2 us
    ppermute x12, starting transfers between devices, both_ways(): return (lax.ppermute(to_right, axis, up), lax.ppermute(to_left, axis, down))  27 us
    unnamed x72, local copies, waits for them, and re-layouts  20.7 us
    pallas_call x7, Pallas kernels, call(): pl.pallas_call(kernel, out_shape=[pltpu.VMEM(s, F32) if kept else jax.Sha...  20.6 us
    all_to_all x2, waiting for transfers between devices, body(): parts = lax.all_to_all(part, 'fast', 0, 0, tiled=True)  15.5 us
    all_to_all x2, starting transfers between devices, body(): parts = lax.all_to_all(part, 'fast', 0, 0, tiled=True)  13.6 us
  transfers between devices with their start and end apart: 14, of which 10 were waited for; matrix products, arithmetic and copies ran while one was open for 1% of the time, Pallas kernels for 0%

profile of v3, /device:TPU:1, one launch (start us, length us, event | category | flops | bytes accessed | tf_op | source)
XLA Modules:
  0.0 189.0 jit_solution(8878981476627360483)
XLA Ops:
  0.0 2.1 %shard_map.55 = (f32[3,2,2,8,8,128]{5,4,3,2,1,0:T(8,128)S(1)}, f32[2,2,8,8,128]{4,3,2,1,0:T(8,128)S(1)}) custom-call(f32[8,16,256]{2,1,0:T(8,128)} %observed.1, f32[8,16,256]{2,1,0:T(8,128)} %start.1, f32[8,16,256]{2,1,0:T(8,128)} %diagonal.1, f32[2,8,16,256]{3,2,1,0:T(8,128)} %noise.1), custom_call_target="tpu_custom_call" | custom-call | tf_op jit(solution)/shard_map/pallas_call | solution.py:421
  2.1 0.0 copy-start.15
  2.1 8.7 %collective-permute-start.1 = (f32[3,2,2,8,8,128]{5,4,3,2,1,0:T(8,128)S(1)}, f32[3,2,2,8,8,128]{5,4,3,2,1,0:T(8,128)S(1)}, u32[]{:S(2)}, u32[]{:S(2)}) collective-permute-start(f32[3,2,2,8,8,128]{5,4,3,2,1,0:T(8,128)S(1)} %get-tuple-element.32), channel_id=1, source_target_pairs={{1,0},{2,1},{3,2},{4,3},{5,4},{6,5},{7,6},{8,7},{9,8},{10,9},{11,1... | collective-permute-start | bytes 1179656 | tf_op jit(solution)/shard_map/ppermute | solution.py:435
  10.8 0.0 collective-permute-start
  10.8 7.8 %collective-permute-done.1 = f32[3,2,2,8,8,128]{5,4,3,2,1,0:T(8,128)S(1)} collective-permute-done((f32[3,2,2,8,8,128]{5,4,3,2,1,0:T(8,128)S(1)}, f32[3,2,2,8,8,128]{5,4,3,2,1,0:T(8,128)S(1)}, u32[]{:S(2)}, u32[]{:S(2)}) %collective-permute-start.1) | collective-permute-done | bytes 393248 | tf_op jit(solution)/shard_map/ppermute | solution.py:435
  18.6 5.2 %collective-permute-done = f32[3,2,2,8,8,128]{5,4,3,2,1,0:T(8,128)S(1)} collective-permute-done((f32[3,2,2,8,8,128]{5,4,3,2,1,0:T(8,128)S(1)}, f32[3,2,2,8,8,128]{5,4,3,2,1,0:T(8,128)S(1)}, u32[]{:S(2)}, u32[]{:S(2)}) %collective-permute-start) | collective-permute-done | bytes 393248 | tf_op jit(solution)/shard_map/ppermute | solution.py:435
  23.8 0.1 pad_maximum_fusion.refs_0_
  23.9 1.9 collective-permute-start.3
  25.8 1.2 collective-permute-start.2
  27.0 14.2 %collective-permute-done.3.refs_2_ = f32[3,3,2,2,8,8,128]{6,5,4,3,2,1,0:T(8,128)S(1)} collective-permute-done((f32[3,3,2,2,8,8,128]{6,5,4,3,2,1,0:T(8,128)S(1)}, f32[3,3,2,2,8,8,128]{6,5,4,3,2,1,0:T(8,128)S(1)}, u32[]{:S(2)}, u32[]{:S(2)}) %collective-permute-start.3) | collective-permute-done | bytes 1179680 | tf_op jit(solution)/shard_map/ppermute | solution.py:435
  41.1 0.0 collective-permute-done.2.refs_1_
  41.2 2.9 %shard_map.56 = (f32[2,4,16,128]{3,2,1,0:T(8,128)S(1)}, f32[2,4,8,128]{3,2,1,0:T(8,128)S(1)}, f32[2,4,16,128]{3,2,1,0:T(8,128)S(1)}, f32[2,2,16,24,128]{4,3,2,1,...) custom-call(s32[3]{0:T(128)S(1)} %copy-done.29, ...), custom_call_target="tpu_custom_call" | custom-call | tf_op jit(solution)/shard_map/pallas_call | solution.py:421
  44.1 1.1 copy-done.2
  45.2 4.8 %collective-permute-start.5 = (f32[2,4,16,128]{3,2,1,0:T(8,128)S(1)}, f32[2,4,16,128]{3,2,1,0:T(8,128)S(1)}, u32[]{:S(2)}, u32[]{:S(2)}) collective-permute-start(f32[2,4,16,128]{3,2,1,0:T(8,128)S(1)} %get-tuple-element.35), channel_id=1, source_target_pairs={{1,0},{2,1},{3,2},{4,3},{5,4},{6,5},{7,6},{8,7},{9,8},{10,9},{11,1... | collective-permute-start | bytes 196616 | tf_op jit(solution)/shard_map/ppermute | solution.py:435
  49.9 1.6 collective-permute-done.4
  51.6 0.1 broadcast_in_dim.6
  51.8 24.2 %all_to_all.32.refs_0_ = f32[8,2,4,40,128]{4,3,2,1,0:T(8,128)S(1)} all-to-all(f32[8,2,4,40,128]{4,3,2,1,0:T(8,128)S(1)} %broadcast_in_dim.6), channel_id=1, replica_groups=mesh['slow'=8,'fast'=32] {'slow'}, dimensions={0} | all-to-all | bytes 2621440 | tf_op jit(solution)/shard_map/all_to_all | solution.py:479
  76.0 4.4 %shard_map.57 = (f32[32,128]{1,0:T(8,128)}, f32[48,40,128]{2,1,0:T(8,128)S(1)}, f32[48,40,128]{2,1,0:T(8,128)S(1)}, f32[8,24,128]{2,1,0:T(8,128)S(1)}, f32[48,40...) custom-call(s32[3]{0:T(128)S(1)} %copy-done.29, ...), custom_call_target="tpu_custom_call" | custom-call | tf_op jit(solution)/shard_map/pallas_call | solution.py:421
  80.3 1.0 copy-done.6
  81.3 0.8 copy-done.13
  82.1 0.7 copy-done.21
  82.8 0.7 copy-done.23
  83.5 0.6 copy-done.25
  84.1 0.6 copy-done.34
  84.7 6.7 %all-to-all-start.1 = ((f32[32,1,128]{2,1,0:T(1,128)}), f32[32,1,128]{2,1,0:T(1,128)S(1)}, u32[]{:S(2)}, u32[]{:S(2)}) async-start(f32[32,1,128]{2,1,0:T(1,128)} %bitcast.4), calls=%async_computation.1 | async-start | bytes 32768 | tf_op jit(solution)/shard_map/all_to_all | solution.py:494
  91.5 0.9 slice_bitcast_fusion.1.field
  92.4 7.5 %all-to-all-done.1 = f32[32,1,128]{2,1,0:T(1,128)S(1)} async-done(((f32[32,1,128]{2,1,0:T(1,128)}), f32[32,1,128]{2,1,0:T(1,128)S(1)}, u32[]{:S(2)}, u32[]{:S(2)}) %all-to-all-start.1) | async-done | bytes 16416 | tf_op jit(solution)/shard_map/all_to_all | solution.py:494
  99.9 1.3 copy-done.3
  101.2 1.2 copy-done.7
  102.4 1.1 copy-done.11
  103.5 0.9 copy-done.16
  104.4 0.9 copy-done.26
  105.3 0.7 copy-done.30
  106.0 2.1 %shard_map.58 = f32[2,2,2,8,8,128]{5,4,3,2,1,0:T(8,128)S(1)} custom-call(s32[3]{0:T(128)S(1)} %copy-done.30, f32[32,128]{1,0:T(8,128)S(1)} %bitcast.23, f32[48,40,128]{2,1,0:T(8,128)S(1)} %get-tuple-element.37.e1, f32[48,40,128]{2,1,0:T(8,128)S(1)} %copy-done.7, f32[48,40,128]{2,1,0:T(8,128)S(1)} %get-tuple-element.39.k1.refs_1_, ...), custom_call_target="tpu_custom_call" | custom-call | tf_op jit(solution)/shard_map/pallas_call | solution.py:421
  108.1 0.0 copy-start.31
  108.1 1.2 collective-permute-start.7
  109.3 0.4 collective-permute-start.6
  109.6 3.8 %collective-permute-done.7 = f32[2,2,2,8,8,128]{5,4,3,2,1,0:T(8,128)S(1)} collective-permute-done((f32[2,2,2,8,8,128]{5,4,3,2,1,0:T(8,128)S(1)}, f32[2,2,2,8,8,128]{5,4,3,2,1,0:T(8,128)S(1)}, u32[]{:S(2)}, u32[]{:S(2)}) %collective-permute-start.7) | collective-permute-done | bytes 262176 | tf_op jit(solution)/shard_map/ppermute | solution.py:435
  113.4 4.4 %collective-permute-done.6 = f32[2,2,2,8,8,128]{5,4,3,2,1,0:T(8,128)S(1)} collective-permute-done((f32[2,2,2,8,8,128]{5,4,3,2,1,0:T(8,128)S(1)}, f32[2,2,2,8,8,128]{5,4,3,2,1,0:T(8,128)S(1)}, u32[]{:S(2)}, u32[]{:S(2)}) %collective-permute-start.6) | collective-permute-done | bytes 262176 | tf_op jit(solution)/shard_map/ppermute | solution.py:435
  117.8 0.1 pad_maximum_fusion.1.refs_0_
  117.9 3.9 %collective-permute-start.9 = (f32[3,2,2,2,8,8,128]{6,5,4,3,2,1,0:T(8,128)S(1)}, f32[3,2,2,2,8,8,128]{6,5,4,3,2,1,0:T(8,128)S(1)}, u32[]{:S(2)}, u32[]{:S(2)}) collective-permute-start(f32[3,2,2,2,8,8,128]{6,5,4,3,2,1,0:T(8,128)S(1)} %pad_maximum_fusion.1.refs_0_), channel_id=1, source_target_pairs={{32,0},{64,32},{96,64},{128,96},{160,128},{192,160},{224,192},{0,2... | collective-permute-start | bytes 2359304 | tf_op jit(solution)/shard_map/ppermute | solution.py:435
  121.8 0.2 collective-permute-start.8
  122.0 9.9 %collective-permute-done.9.refs_2_ = f32[3,2,2,2,8,8,128]{6,5,4,3,2,1,0:T(8,128)S(1)} collective-permute-done((f32[3,2,2,2,8,8,128]{6,5,4,3,2,1,0:T(8,128)S(1)}, f32[3,2,2,2,8,8,128]{6,5,4,3,2,1,0:T(8,128)S(1)}, u32[]{:S(2)}, u32[]{:S(2)}) %collective-permute-start.9) | collective-permute-done | bytes 786464 | tf_op jit(solution)/shard_map/ppermute | solution.py:435
  131.9 3.0 %shard_map.59 = (f32[1,4,16,128]{3,2,1,0:T(8,128)S(1)}, f32[1,4,8,128]{3,2,1,0:T(8,128)S(1)}, f32[1,4,16,128]{3,2,1,0:T(8,128)S(1)}, f32[2,2,16,24,128]{4,3,2,1,0:T(8,128)S(1)}, f32[2,2,24,24,128]{4,3,2,1,0:T(8,128)S(1)}) custom-call(s32[3]{0:T(128)S(1)} %copy-done.31, f32[3,2,2,2,8,8,128]{6,5,4,3,2,1,0:T(8,128)S(1)} %pad_maximum_fusion.1.refs_0_, ...), custom_call_target="tpu_custom_call" | custom-call | tf_op jit(solution)/shard_map/pallas_call | solution.py:421
  135.0 0.9 copy-done.8
  135.9 0.1 collective-permute-start.10
  136.0 4.8 %collective-permute-start.11 = (f32[1,4,16,128]{3,2,1,0:T(8,128)S(1)}, f32[1,4,16,128]{3,2,1,0:T(8,128)S(1)}, u32[]{:S(2)}, u32[]{:S(2)}) collective-permute-start(f32[1,4,16,128]{3,2,1,0:T(8,128)S(1)} %get-tuple-element.48), channel_id=1, source_target_pairs={{1,0},{2,1},{3,2},{4,3},{5,4},{6,5},{7,6},{8,7},{9,8},{10,9},{11,1... | collective-permute-start | bytes 98312 | tf_op jit(solution)/shard_map/ppermute | solution.py:435
  140.7 1.3 collective-permute-done.10
  142.1 17.0 %all_to_all.33.refs_0_ = f32[8,1,4,40,128]{4,3,2,1,0:T(8,128)S(1)} all-to-all(f32[8,1,4,40,128]{4,3,2,1,0:T(8,128)S(1)} %broadcast_in_dim.16), channel_id=1, replica_groups=mesh['slow'=8,'fast'=32] {'slow'}, dimensions={0} | all-to-all | bytes 1310720 | tf_op jit(solution)/shard_map/all_to_all | solution.py:479
  159.1 0.0 copy-start.17
  159.1 3.2 %shard_map.60 = (f32[32,128]{1,0:T(8,128)S(1)}, f32[48,40,128]{2,1,0:T(8,128)S(1)}, f32[48,40,128]{2,1,0:T(8,128)S(1)}, f32[8,24,128]{2,1,0:T(8,128)S(1)}) custom-call(s32[3]{0:T(128)S(1)} %copy-done.31, f32[8,1,4,40,128]{4,3,2,1,0:T(8,128)S(1)} %all_to_all.33.refs_0_, f32[48,40,128]{2,1,0:T(8,128)S(1)} %get-tuple-element.39.k1.refs_1_, ...), custom_call_target="tpu_custom_call" | custom-call | tf_op jit(solution)/shard_map/pallas_call | solution.py:421
  162.3 1.0 copy-done.4
  163.3 0.7 copy-done.27
  163.9 0.6 copy-done.33
  164.5 6.8 %all-to-all-start.3 = ((f32[32,1,128]{2,1,0:T(1,128)}), f32[32,1,128]{2,1,0:T(1,128)S(1)}, u32[]{:S(2)}, u32[]{:S(2)}) async-start(f32[32,1,128]{2,1,0:T(1,128)} %bitcast.24), calls=%async_computation.3 | async-start | bytes 32768 | tf_op jit(solution)/shard_map/all_to_all | solution.py:494
  171.3 0.7 slice_bitcast_fusion.field
  172.0 7.9 %all-to-all-done.3 = f32[32,1,128]{2,1,0:T(1,128)S(1)} async-done(((f32[32,1,128]{2,1,0:T(1,128)}), f32[32,1,128]{2,1,0:T(1,128)S(1)}, u32[]{:S(2)}, u32[]{:S(2)}) %all-to-all-start.3) | async-done | bytes 16416 | tf_op jit(solution)/shard_map/all_to_all | solution.py:494
  179.9 1.3 copy-done.1
  181.2 1.2 copy-done.5
  182.4 1.1 copy-done.9
  183.6 0.9 copy-done.18
  184.5 0.9 copy-done.28
  185.3 0.7 copy-done.32
  186.0 3.0 %shard_map.61 = f32[8,16,256]{2,1,0:T(8,128)} custom-call(s32[3]{0:T(128)S(1)} %copy-done.32, f32[32,128]{1,0:T(8,128)S(1)} %bitcast.22, f32[48,40,128]{2,1,0:T(8,128)S(1)} %get-tuple-element.54.e1, f32[48,40,128]{2,1,0:T(8,128)S(1)} %copy-done.5, f32[48,40,128]{2,1,0:T(8,128)S(1)} %get-tuple-element.39.k1.refs_1_, f32[8,24,128]{2,1,0:T(8,128)S(1)} %copy-done.28, ...), custom_call_target="tpu_custom_call" | custom-call | tf_op jit(solution)/shard_map/pallas_call | solution.py:421
  (53 shorter events, 0.2 us)
Async XLA Ops:
  2.1 21.8 %copy-start.12 = (f32[3,2,2,8,8,128]{5,4,3,2,1,0:T(8,128)}, f32[3,2,2,8,8,128]{5,4,3,2,1,0:T(8,128)S(1)}, u32[]{:S(2)}) copy-start(f32[3,2,2,8,8,128]{5,4,3,2,1,0:T(8,128)S(1)} %get-tuple-element.32) | copy-start | bytes 1179652
  2.1 21.8 %copy-start.15 = (f32[2,2,8,8,128]{4,3,2,1,0:T(8,128)}, f32[2,2,8,8,128]{4,3,2,1,0:T(8,128)S(1)}, u32[]{:S(2)}) copy-start(f32[2,2,8,8,128]{4,3,2,1,0:T(8,128)S(1)} %get-tuple-element.44.later) | copy-start | bytes 393220
  2.1 16.5 %collective-permute-start.1 = (f32[3,2,2,8,8,128]{5,4,3,2,1,0:T(8,128)S(1)}, f32[3,2,2,8,8,128]{5,4,3,2,1,0:T(8,128)S(1)}, u32[]{:S(2)}, u32[]{:S(2)}) collective-permute-start(f32[3,2,2,8,8,128]{5,4,3,2,1,0:T(8,128)S(1)} %get-tuple-element.32), channel_id=1, source_target_pairs={{1,0},{2,1},{3,2},{4,3},{5,4},{6,5},{7,6},{8,7},{9,8},{10,9},{11,1... | collective-permute-start | bytes 1179656 | tf_op jit(solution)/shard_map/ppermute | solution.py:435
  10.8 13.0 %collective-permute-start = (f32[3,2,2,8,8,128]{5,4,3,2,1,0:T(8,128)S(1)}, f32[3,2,2,8,8,128]{5,4,3,2,1,0:T(8,128)S(1)}, u32[]{:S(2)}, u32[]{:S(2)}) collective-permute-start(f32[3,2,2,8,8,128]{5,4,3,2,1,0:T(8,128)S(1)} %get-tuple-element.32), channel_id=1, source_target_pairs={{0,1},{1,2},{2,3},{3,4},{4,5},{5,6},{6,7},{7,8},{8,9},{9,10},{10,1... | collective-permute-start | bytes 1179656 | tf_op jit(solution)/shard_map/ppermute | solution.py:435
  23.8 17.4 %copy-start.29 = (s32[3]{0:T(128)S(1)}, s32[3]{0:T(128)}, u32[]{:S(2)}) copy-start(s32[3]{0:T(128)} %sweeps.11) | copy-start | bytes 40
  23.9 17.2 %collective-permute-start.3 = (f32[3,3,2,2,8,8,128]{6,5,4,3,2,1,0:T(8,128)S(1)}, f32[3,3,2,2,8,8,128]{6,5,4,3,2,1,0:T(8,128)S(1)}, u32[]{:S(2)}, u32[]{:S(2)}) collective-permute-start(f32[3,3,2,2,8,8,128]{6,5,4,3,2,1,0:T(8,128)S(1)} %pad_maximum_fusion.refs_0_), channel_id=1, source_target_pairs={{32,0},{64,32},{96,64},{128,96},{160,128},{192,160},{224,192},{0,2... | collective-permute-start | bytes 3538952 | tf_op jit(solution)/shard_map/ppermute | solution.py:435
  25.8 15.4 %collective-permute-start.2 = (f32[3,3,2,2,8,8,128]{6,5,4,3,2,1,0:T(8,128)S(1)}, f32[3,3,2,2,8,8,128]{6,5,4,3,2,1,0:T(8,128)S(1)}, u32[]{:S(2)}, u32[]{:S(2)}) collective-permute-start(f32[3,3,2,2,8,8,128]{6,5,4,3,2,1,0:T(8,128)S(1)} %pad_maximum_fusion.refs_0_), channel_id=1, source_target_pairs={{0,32},{32,64},{64,96},{96,128},{128,160},{160,192},{192,224},{224... | collective-permute-start | bytes 3538952 | tf_op jit(solution)/shard_map/ppermute | solution.py:435
  44.1 1.1 copy-start.2
  45.2 6.6 %copy-start.10 = (f32[2,2,16,24,128]{4,3,2,1,0:T(8,128)}, f32[2,2,16,24,128]{4,3,2,1,0:T(8,128)S(1)}, u32[]{:S(2)}) copy-start(f32[2,2,16,24,128]{4,3,2,1,0:T(8,128)S(1)} %get-tuple-element.41.epre) | copy-start | bytes 2359300
  45.2 30.8 %copy-start.19 = (f32[2,2,8,24,128]{4,3,2,1,0:T(8,128)}, f32[2,2,8,24,128]{4,3,2,1,0:T(8,128)S(1)}, u32[]{:S(2)}) copy-start(f32[2,2,8,24,128]{4,3,2,1,0:T(8,128)S(1)} %get-tuple-element.45.refs_4_) | copy-start | bytes 1179652
  45.2 6.4 %collective-permute-start.4 = (f32[2,4,16,128]{3,2,1,0:T(8,128)S(1)}, f32[2,4,16,128]{3,2,1,0:T(8,128)S(1)}, u32[]{:S(2)}, u32[]{:S(2)}) collective-permute-start(f32[2,4,16,128]{3,2,1,0:T(8,128)S(1)} %get-tuple-element.33), channel_id=1, source_target_pairs={{0,1},{1,2},{2,3},{3,4},{4,5},{5,6},{6,7},{7,8},{8,9},{9,10},{10,1... | collective-permute-start | bytes 196616 | tf_op jit(solution)/shard_map/ppermute | solution.py:435
  45.2 6.4 %collective-permute-start.5 = (f32[2,4,16,128]{3,2,1,0:T(8,128)S(1)}, f32[2,4,16,128]{3,2,1,0:T(8,128)S(1)}, u32[]{:S(2)}, u32[]{:S(2)}) collective-permute-start(f32[2,4,16,128]{3,2,1,0:T(8,128)S(1)} %get-tuple-element.35), channel_id=1, source_target_pairs={{1,0},{2,1},{3,2},{4,3},{5,4},{6,5},{7,6},{8,7},{9,8},{10,9},{11,1... | collective-permute-start | bytes 196616 | tf_op jit(solution)/shard_map/ppermute | solution.py:435
  80.3 1.0 copy-start.6
  81.3 0.8 copy-start.13
  82.1 0.7 copy-start.21
  82.8 0.7 copy-start.23
  83.5 0.6 copy-start.25
  84.1 0.6 copy-start.34
  84.7 15.2 %all-to-all-start.1 = ((f32[32,1,128]{2,1,0:T(1,128)}), f32[32,1,128]{2,1,0:T(1,128)S(1)}, u32[]{:S(2)}, u32[]{:S(2)}) async-start(f32[32,1,128]{2,1,0:T(1,128)} %bitcast.4), calls=%async_computation.1 | async-start | bytes 32768 | tf_op jit(solution)/shard_map/all_to_all | solution.py:494
  99.9 1.3 copy-start.3
  101.2 1.2 copy-start.7
  102.4 1.1 copy-start.11
  103.5 0.9 copy-start.16
  104.4 0.9 copy-start.26
  105.3 0.7 copy-start.30
  108.1 23.8 %copy-start.20 = (f32[2,2,8,24,128]{4,3,2,1,0:T(8,128)S(1)}, f32[2,2,8,24,128]{4,3,2,1,0:T(8,128)}, u32[]{:S(2)}) copy-start(f32[2,2,8,24,128]{4,3,2,1,0:T(8,128)} %copy-done.19) | copy-start | bytes 1179652
  108.1 23.8 %copy-start.31 = (s32[3]{0:T(128)S(1)}, s32[3]{0:T(128)}, u32[]{:S(2)}) copy-start(s32[3]{0:T(128)} %sweeps.11) | copy-start | bytes 40
  108.1 5.3 %collective-permute-start.7 = (f32[2,2,2,8,8,128]{5,4,3,2,1,0:T(8,128)S(1)}, f32[2,2,2,8,8,128]{5,4,3,2,1,0:T(8,128)S(1)}, u32[]{:S(2)}, u32[]{:S(2)}) collective-permute-start(f32[2,2,2,8,8,128]{5,4,3,2,1,0:T(8,128)S(1)} %shard_map.58), channel_id=1, source_target_pairs={{1,0},{2,1},{3,2},{4,3},{5,4},{6,5},{7,6},{8,7},{9,8},{10,9},{11,1... | collective-permute-start | bytes 786440 | tf_op jit(solution)/shard_map/ppermute | solution.py:435
  109.3 8.5 %collective-permute-start.6 = (f32[2,2,2,8,8,128]{5,4,3,2,1,0:T(8,128)S(1)}, f32[2,2,2,8,8,128]{5,4,3,2,1,0:T(8,128)S(1)}, u32[]{:S(2)}, u32[]{:S(2)}) collective-permute-start(f32[2,2,2,8,8,128]{5,4,3,2,1,0:T(8,128)S(1)} %shard_map.58), channel_id=1, source_target_pairs={{0,1},{1,2},{2,3},{3,4},{4,5},{5,6},{6,7},{7,8},{8,9},{9,10},{10,1... | collective-permute-start | bytes 786440 | tf_op jit(solution)/shard_map/ppermute | solution.py:435
  117.9 14.0 %collective-permute-start.9 = (f32[3,2,2,2,8,8,128]{6,5,4,3,2,1,0:T(8,128)S(1)}, f32[3,2,2,2,8,8,128]{6,5,4,3,2,1,0:T(8,128)S(1)}, u32[]{:S(2)}, u32[]{:S(2)}) collective-permute-start(f32[3,2,2,2,8,8,128]{6,5,4,3,2,1,0:T(8,128)S(1)} %pad_maximum_fusion.1.refs_0_), channel_id=1, source_target_pairs={{32,0},{64,32},{96,64},{128,96},{160,128},{192,160},{224,192},{0,2... | collective-permute-start | bytes 2359304 | tf_op jit(solution)/shard_map/ppermute | solution.py:435
  121.8 10.1 %collective-permute-start.8 = (f32[3,2,2,2,8,8,128]{6,5,4,3,2,1,0:T(8,128)S(1)}, f32[3,2,2,2,8,8,128]{6,5,4,3,2,1,0:T(8,128)S(1)}, u32[]{:S(2)}, u32[]{:S(2)}) collective-permute-start(f32[3,2,2,2,8,8,128]{6,5,4,3,2,1,0:T(8,128)S(1)} %pad_maximum_fusion.1.refs_0_), channel_id=1, source_target_pairs={{0,32},{32,64},{64,96},{96,128},{128,160},{160,192},{192,224},{224... | collective-permute-start | bytes 2359304 | tf_op jit(solution)/shard_map/ppermute | solution.py:435
  134.9 0.9 copy-start.8
  135.8 26.4 %copy-start = (f32[2,2,24,24,128]{4,3,2,1,0:T(8,128)}, f32[2,2,24,24,128]{4,3,2,1,0:T(8,128)S(1)}, u32[]{:S(2)}) copy-start(f32[2,2,24,24,128]{4,3,2,1,0:T(8,128)S(1)} %get-tuple-element.58.q) | copy-start | bytes 3538948
  135.8 23.2 %copy-start.14 = (f32[32,40,128]{2,1,0:T(8,128)S(1)}, f32[32,40,128]{2,1,0:T(8,128)}, u32[]{:S(2)}) copy-start(f32[32,40,128]{2,1,0:T(8,128)} %copy-done.13) | copy-start | bytes 1966084
  135.8 23.2 %copy-start.22 = (f32[16,24,128]{2,1,0:T(8,128)S(1)}, f32[16,24,128]{2,1,0:T(8,128)}, u32[]{:S(2)}) copy-start(f32[16,24,128]{2,1,0:T(8,128)} %copy-done.21) | copy-start | bytes 589828
  135.9 23.2 %copy-start.24 = (f32[16,24,128]{2,1,0:T(8,128)S(1)}, f32[16,24,128]{2,1,0:T(8,128)}, u32[]{:S(2)}) copy-start(f32[16,24,128]{2,1,0:T(8,128)} %copy-done.23) | copy-start | bytes 589828
  135.9 23.2 %copy-start.35 = (f32[24,128]{1,0:T(8,128)S(1)}, f32[24,128]{1,0:T(8,128)}, u32[]{:S(2)}) copy-start(f32[24,128]{1,0:T(8,128)} %copy-done.34) | copy-start | bytes 36868
  135.9 6.2 %collective-permute-start.10 = (f32[1,4,16,128]{3,2,1,0:T(8,128)S(1)}, f32[1,4,16,128]{3,2,1,0:T(8,128)S(1)}, u32[]{:S(2)}, u32[]{:S(2)}) collective-permute-start(f32[1,4,16,128]{3,2,1,0:T(8,128)S(1)} %get-tuple-element.46), channel_id=1, source_target_pairs={{0,1},{1,2},{2,3},{3,4},{4,5},{5,6},{6,7},{7,8},{8,9},{9,10},{10,1... | collective-permute-start | bytes 98312 | tf_op jit(solution)/shard_map/ppermute | solution.py:435
  136.0 6.1 %collective-permute-start.11 = (f32[1,4,16,128]{3,2,1,0:T(8,128)S(1)}, f32[1,4,16,128]{3,2,1,0:T(8,128)S(1)}, u32[]{:S(2)}, u32[]{:S(2)}) collective-permute-start(f32[1,4,16,128]{3,2,1,0:T(8,128)S(1)} %get-tuple-element.48), channel_id=1, source_target_pairs={{1,0},{2,1},{3,2},{4,3},{5,4},{6,5},{7,6},{8,7},{9,8},{10,9},{11,1... | collective-permute-start | bytes 98312 | tf_op jit(solution)/shard_map/ppermute | solution.py:435
  159.1 20.8 %copy-start.17 = (f32[2,2,8,8,128]{4,3,2,1,0:T(8,128)S(1)}, f32[2,2,8,8,128]{4,3,2,1,0:T(8,128)}, u32[]{:S(2)}) copy-start(f32[2,2,8,8,128]{4,3,2,1,0:T(8,128)} %copy-done.15) | copy-start | bytes 393220
  162.3 1.0 copy-start.4
  163.3 0.7 copy-start.27
  163.9 0.6 copy-start.33
  164.5 15.4 %all-to-all-start.3 = ((f32[32,1,128]{2,1,0:T(1,128)}), f32[32,1,128]{2,1,0:T(1,128)S(1)}, u32[]{:S(2)}, u32[]{:S(2)}) async-start(f32[32,1,128]{2,1,0:T(1,128)} %bitcast.24), calls=%async_computation.3 | async-start | bytes 32768 | tf_op jit(solution)/shard_map/all_to_all | solution.py:494
  179.9 1.3 copy-start.1
  181.2 1.2 copy-start.5
  182.4 1.1 copy-start.9
  183.5 0.9 copy-start.18
  184.5 0.9 copy-start.28
  185.3 0.7 copy-start.32

commit v4 on v3

--- a/solution.py
+++ b/solution.py
@@ -349,7 +349,7 @@
         e2_out[y] = x2[y, ZB : 4 * ZB]
 
 
-def after_kernel(last, faces, sweeps, parts, e1, q1, k1, e2, epre, q, k, field, later, out, va, vb, a, b, halves):
+def after_kernel(last, faces, sweeps, parts, e1, q1, k1, e2, epre, q, k, fields, later, out, va, vb, a, b, halves):
     lanes = lane_iota(ZW)
     lanes_p = lane_iota(parts.shape[0])
     every = parts[...]
@@ -403,7 +403,7 @@
     fine_sweep(b, a, q, k, 3, 13, 10, lanes, offset=4)
     fine_sweep(a, b, q, k, 4, 12, 8, lanes, offset=4)
     for pz, px in PARITIES:
-        value = field[pz, px] + 0.5 * b[pz, px, 4:12, ZB : 2 * ZB]
+        value = fields[0, pz, px] + 0.5 * b[pz, px, 4:12, ZB : 2 * ZB]
         if last:
             halves[px, pl.ds(pz, YB * ZB, stride=2), :] = value.reshape(YB * ZB, LANES)
         else:
@@ -457,7 +457,6 @@
         [natural, natural, natural, (2, *natural), (4, 2, YB * 2 * ZB, LANES), pltpu.SemaphoreType.DMA((4,))],
         (), observed, start_field, diagonal, noise, space=pltpu.HBM,
     )
-    field = fields[0]
     kept_fine = kept_low = None
     for step in range(2):
         opening = step == 0
@@ -496,9 +495,8 @@
         scratch = [(YPOST, ZW, LANES)] * 2 + [post] * 2 + [(2, YB * 2 * ZB, LANES)]
         (fields,) = call(
             functools.partial(after_kernel, not opening, faces), outs, scratch, (sweeps,),
-            parts, e1, q1, kept_low[0], e2, epre, q, kept_fine[0], field, later, kept=opening,
+            parts, e1, q1, kept_low[0], e2, epre, q, kept_fine[0], fields, later, kept=opening,
         )
-        field = fields[0]
     return fields
 
 

time: 190 us -> 168 us (0.88)
  blocking collectives: 41.2 us -> 71.5 us
  local copies, waits for them, and re-layouts: 22.5 us -> 0.17 us
  waiting for transfers between devices: 63.7 us -> 48.1 us
  starting transfers between devices: 40.6 us -> 27.3 us
    all_to_all x0 -> x2, blocking collectives: none -> 30.3 us  [body(): parts = lax.all_to_all(part, 'fast', 0, 0, tiled=True)]
    unnamed x72 -> x2, local copies, waits for them, and re-layouts: 20.7 us -> 0.01 us
    all_to_all x2 -> x0, waiting for transfers between devices: 15.5 us -> none  [body(): parts = lax.all_to_all(part, 'fast', 0, 0, tiled=True)]
    all_to_all x2 -> x0, starting transfers between devices: 13.6 us -> none  [body(): parts = lax.all_to_all(part, 'fast', 0, 0, tiled=True)]
  transfers between devices with their start and end apart: 14 -> 12, of which waited for: 10 -> 8; matrix products, arithmetic and copies ran while one was open for 1% -> 0% of each run, Pallas kernels for 0% -> 0%
where the time goes in v4:
time: 168 us; the launch traced here: 167 us
  blocking collectives  71.5 us (43%)
  waiting for transfers between devices  48.1 us (29%)
  starting transfers between devices  27.3 us (16%)
  Pallas kernels  20 us (12%)
    ppermute x12, waiting for transfers between devices, both_ways(): return (lax.ppermute(to_right, axis, up), lax.ppermute(to_left, axis, down))  48.1 us
    all_to_all x2, blocking collectives, body(): strip = lax.all_to_all(strip, 'slow', 0, 0, tiled=True)  41.2 us
    all_to_all x2, blocking collectives, body(): parts = lax.all_to_all(part, 'fast', 0, 0, tiled=True)  30.3 us
    ppermute x12, starting transfers between devices, both_ways(): return (lax.ppermute(to_right, axis, up), lax.ppermute(to_left, axis, down))  27.3 us
    pallas_call x7, Pallas kernels, call(): pl.pallas_call(kernel, out_shape=[pltpu.VMEM(s, F32) if kept else jax.Sha...  20 us
  transfers between devices with their start and end apart: 12, of which 8 were waited for; matrix products, arithmetic and copies ran while one was open for 0% of the time, Pallas kernels for 0%

profile of v4, /device:TPU:1, one launch (start us, length us, event | category | flops | bytes accessed | tf_op | source)
XLA Modules:
  0.0 167.3 jit_solution(6100476307386601950)
XLA Ops:
  0.0 2.1 %shard_map.55 = (f32[3,2,2,8,8,128]{5,4,3,2,1,0:T(8,128)S(1)}, f32[2,2,8,8,128]{4,3,2,1,0:T(8,128)S(1)}) custom-call(f32[8,16,256]{2,1,0:T(8,128)} %observed.1, f32[8,16,256]{2,1,0:T(8,128)} %start.1, f32[8,16,256]{2,1,0:T(8,128)} %diagonal.1, f32[2,8,16,256]{3,2,1,0:T(8,128)} %noise.1), custom_call_target="tpu_custom_call" | custom-call | tf_op jit(solution)/shard_map/pallas_call | solution.py:421
  2.1 8.7 %collective-permute-start.1 = (f32[3,2,2,8,8,128]{5,4,3,2,1,0:T(8,128)S(1)}, f32[3,2,2,8,8,128]{5,4,3,2,1,0:T(8,128)S(1)}, u32[]{:S(2)}, u32[]{:S(2)}) collective-permute-start(f32[3,2,2,8,8,128]{5,4,3,2,1,0:T(8,128)S(1)} %get-tuple-element.32.fields), channel_id=1, source_target_pairs={{1,0},{2,1},{3,2},{4,3},{5,4},{6,5},{7,6},{8,7},{9,8},{10,9},{11,1... | collective-permute-start | bytes 1179656 | tf_op jit(solution)/shard_map/ppermute | solution.py:435
  10.8 0.0 collective-permute-start
  10.8 7.8 %collective-permute-done.1 = f32[3,2,2,8,8,128]{5,4,3,2,1,0:T(8,128)S(1)} collective-permute-done((f32[3,2,2,8,8,128]{5,4,3,2,1,0:T(8,128)S(1)}, f32[3,2,2,8,8,128]{5,4,3,2,1,0:T(8,128)S(1)}, u32[]{:S(2)}, u32[]{:S(2)}) %collective-permute-start.1) | collective-permute-done | bytes 393248 | tf_op jit(solution)/shard_map/ppermute | solution.py:435
  18.5 5.2 %collective-permute-done = f32[3,2,2,8,8,128]{5,4,3,2,1,0:T(8,128)S(1)} collective-permute-done((f32[3,2,2,8,8,128]{5,4,3,2,1,0:T(8,128)S(1)}, f32[3,2,2,8,8,128]{5,4,3,2,1,0:T(8,128)S(1)}, u32[]{:S(2)}, u32[]{:S(2)}) %collective-permute-start) | collective-permute-done | bytes 393248 | tf_op jit(solution)/shard_map/ppermute | solution.py:435
  23.7 0.0 copy-start
  23.7 0.1 pad_maximum_fusion.refs_0_
  23.9 1.9 %collective-permute-start.3 = (f32[3,3,2,2,8,8,128]{6,5,4,3,2,1,0:T(8,128)S(1)}, f32[3,3,2,2,8,8,128]{6,5,4,3,2,1,0:T(8,128)S(1)}, u32[]{:S(2)}, u32[]{:S(2)}) collective-permute-start(f32[3,3,2,2,8,8,128]{6,5,4,3,2,1,0:T(8,128)S(1)} %pad_maximum_fusion.refs_0_), channel_id=1, source_target_pairs={{32,0},{64,32},{96,64},{128,96},{160,128},{192,160},{224,192},{0,2... | collective-permute-start | bytes 3538952 | tf_op jit(solution)/shard_map/ppermute | solution.py:435
  25.7 1.2 collective-permute-start.2
  27.0 14.2 %collective-permute-done.3.refs_2_ = f32[3,3,2,2,8,8,128]{6,5,4,3,2,1,0:T(8,128)S(1)} collective-permute-done((f32[3,3,2,2,8,8,128]{6,5,4,3,2,1,0:T(8,128)S(1)}, f32[3,3,2,2,8,8,128]{6,5,4,3,2,1,0:T(8,128)S(1)}, u32[]{:S(2)}, u32[]{:S(2)}) %collective-permute-start.3) | collective-permute-done | bytes 1179680 | tf_op jit(solution)/shard_map/ppermute | solution.py:435
  41.1 0.0 collective-permute-done.2.refs_1_
  41.1 0.0 copy-done
  41.1 2.0 %shard_map.56 = (f32[2,4,16,128]{3,2,1,0:T(8,128)S(1)}, f32[2,4,8,128]{3,2,1,0:T(8,128)S(1)}, f32[2,4,16,128]{3,2,1,0:T(8,128)S(1)}, f32[2,2,16,24,128]{4,3,2,1,...) custom-call(s32[3]{0:T(128)S(1)} %copy-done, ...), custom_call_target="tpu_custom_call" | custom-call | tf_op jit(solution)/shard_map/pallas_call | solution.py:421
  43.2 0.1 collective-permute-start.4
  43.2 4.8 %collective-permute-start.5 = (f32[2,4,16,128]{3,2,1,0:T(8,128)S(1)}, f32[2,4,16,128]{3,2,1,0:T(8,128)S(1)}, u32[]{:S(2)}, u32[]{:S(2)}) collective-permute-start(f32[2,4,16,128]{3,2,1,0:T(8,128)S(1)} %get-tuple-element.35), channel_id=1, source_target_pairs={{1,0},{2,1},{3,2},{4,3},{5,4},{6,5},{7,6},{8,7},{9,8},{10,9},{11,1... | collective-permute-start | bytes 196616 | tf_op jit(solution)/shard_map/ppermute | solution.py:435
  48.0 1.6 collective-permute-done.4
  49.7 0.0 collective-permute-done.5
  49.7 0.1 broadcast_in_dim.6
  49.8 24.2 %all_to_all.32.refs_0_ = f32[8,2,4,40,128]{4,3,2,1,0:T(8,128)S(1)} all-to-all(f32[8,2,4,40,128]{4,3,2,1,0:T(8,128)S(1)} %broadcast_in_dim.6), channel_id=1, replica_groups=mesh['slow'=8,'fast'=32] {'slow'}, dimensions={0} | all-to-all | bytes 2621440 | tf_op jit(solution)/shard_map/all_to_all | solution.py:478
  74.1 5.0 %shard_map.57 = (f32[32,128]{1,0:T(8,128)S(1)}, f32[48,40,128]{2,1,0:T(8,128)S(1)}, f32[48,40,128]{2,1,0:T(8,128)S(1)}, f32[8,24,128]{2,1,0:T(8,128)S(1)}, f32[4...) custom-call(s32[3]{0:T(128)S(1)} %copy-done, ...), custom_call_target="tpu_custom_call" | custom-call | tf_op jit(solution)/shard_map/pallas_call | solution.py:421
  79.1 15.1 %all_to_all.33 = f32[32,1,128]{2,1,0:T(1,128)S(1)} all-to-all(f32[32,1,128]{2,1,0:T(1,128)S(1)} %bitcast.20), channel_id=1, replica_groups=mesh['slow'=8,'fast'=32] {'fast'}, dimensions={0} | all-to-all | bytes 32768 | tf_op jit(solution)/shard_map/all_to_all | solution.py:493
  94.2 1.8 %shard_map.58.fields = f32[2,2,2,8,8,128]{5,4,3,2,1,0:T(8,128)S(1)} custom-call(s32[3]{0:T(128)S(1)} %copy-done, f32[32,128]{1,0:T(8,128)S(1)} %bitcast.19, f32[48,40,128]{2,1,0:T(8,128)S(1)} %get-tuple-element.37.e1, f32[48,40,128]{2,1,0:T(8,128)S(1)} %get-tuple-element.38.q1, f32[48,40,128]{2,1,0:T(8,128)S(1)} %get-tuple-element.39.k1.refs_1_, ...), custom_call_target="tpu_custom_call" | custom-call | tf_op jit(solution)/shard_map/pallas_call | solution.py:421
  96.0 1.0 collective-permute-start.7
  97.0 0.5 collective-permute-start.6
  97.5 3.8 %collective-permute-done.7 = f32[2,2,2,8,8,128]{5,4,3,2,1,0:T(8,128)S(1)} collective-permute-done((f32[2,2,2,8,8,128]{5,4,3,2,1,0:T(8,128)S(1)}, f32[2,2,2,8,8,128]{5,4,3,2,1,0:T(8,128)S(1)}, u32[]{:S(2)}, u32[]{:S(2)}) %collective-permute-start.7) | collective-permute-done | bytes 262176 | tf_op jit(solution)/shard_map/ppermute | solution.py:435
  101.3 4.3 %collective-permute-done.6 = f32[2,2,2,8,8,128]{5,4,3,2,1,0:T(8,128)S(1)} collective-permute-done((f32[2,2,2,8,8,128]{5,4,3,2,1,0:T(8,128)S(1)}, f32[2,2,2,8,8,128]{5,4,3,2,1,0:T(8,128)S(1)}, u32[]{:S(2)}, u32[]{:S(2)}) %collective-permute-start.6) | collective-permute-done | bytes 262176 | tf_op jit(solution)/shard_map/ppermute | solution.py:435
  105.6 0.1 pad_maximum_fusion.1.refs_0_
  105.6 3.9 %collective-permute-start.9 = (f32[3,2,2,2,8,8,128]{6,5,4,3,2,1,0:T(8,128)S(1)}, f32[3,2,2,2,8,8,128]{6,5,4,3,2,1,0:T(8,128)S(1)}, u32[]{:S(2)}, u32[]{:S(2)}) collective-permute-start(f32[3,2,2,2,8,8,128]{6,5,4,3,2,1,0:T(8,128)S(1)} %pad_maximum_fusion.1.refs_0_), channel_id=1, source_target_pairs={{32,0},{64,32},{96,64},{128,96},{160,128},{192,160},{224,192},{0,2... | collective-permute-start | bytes 2359304 | tf_op jit(solution)/shard_map/ppermute | solution.py:435
  109.5 0.2 collective-permute-start.8
  109.7 9.9 %collective-permute-done.9.refs_2_ = f32[3,2,2,2,8,8,128]{6,5,4,3,2,1,0:T(8,128)S(1)} collective-permute-done((f32[3,2,2,2,8,8,128]{6,5,4,3,2,1,0:T(8,128)S(1)}, f32[3,2,2,2,8,8,128]{6,5,4,3,2,1,0:T(8,128)S(1)}, u32[]{:S(2)}, u32[]{:S(2)}) %collective-permute-start.9) | collective-permute-done | bytes 786464 | tf_op jit(solution)/shard_map/ppermute | solution.py:435
  119.7 0.0 collective-permute-done.8.refs_1_
  119.7 2.0 %shard_map.59 = (f32[1,4,16,128]{3,2,1,0:T(8,128)S(1)}, f32[1,4,8,128]{3,2,1,0:T(8,128)S(1)}, f32[1,4,16,128]{3,2,1,0:T(8,128)S(1)}, f32[2,2,16,24,128]{4,3,2,1,0:T(8,128)S(1)}, f32[2,2,24,24,128]{4,3,2,1,0:T(8,128)S(1)}) custom-call(s32[3]{0:T(128)S(1)} %copy-done, f32[3,2,2,2,8,8,128]{6,5,4,3,2,1,0:T(8,128)S(1)} %pad_maximum_fusion.1.refs_0_, ...), custom_call_target="tpu_custom_call" | custom-call | tf_op jit(solution)/shard_map/pallas_call | solution.py:421
  121.7 0.3 collective-permute-start.10
  122.0 4.8 %collective-permute-start.11 = (f32[1,4,16,128]{3,2,1,0:T(8,128)S(1)}, f32[1,4,16,128]{3,2,1,0:T(8,128)S(1)}, u32[]{:S(2)}, u32[]{:S(2)}) collective-permute-start(f32[1,4,16,128]{3,2,1,0:T(8,128)S(1)} %get-tuple-element.48), channel_id=1, source_target_pairs={{1,0},{2,1},{3,2},{4,3},{5,4},{6,5},{7,6},{8,7},{9,8},{10,9},{11,1... | collective-permute-start | bytes 98312 | tf_op jit(solution)/shard_map/ppermute | solution.py:435
  126.7 1.3 collective-permute-done.10
  128.0 0.0 collective-permute-done.11
  128.1 17.0 %all_to_all.34.refs_0_ = f32[8,1,4,40,128]{4,3,2,1,0:T(8,128)S(1)} all-to-all(f32[8,1,4,40,128]{4,3,2,1,0:T(8,128)S(1)} %broadcast_in_dim.16), channel_id=1, replica_groups=mesh['slow'=8,'fast'=32] {'slow'}, dimensions={0} | all-to-all | bytes 1310720 | tf_op jit(solution)/shard_map/all_to_all | solution.py:478
  145.1 4.4 %shard_map.60 = (f32[32,128]{1,0:T(8,128)S(1)}, f32[48,40,128]{2,1,0:T(8,128)S(1)}, f32[48,40,128]{2,1,0:T(8,128)S(1)}, f32[8,24,128]{2,1,0:T(8,128)S(1)}) custom-call(s32[3]{0:T(128)S(1)} %copy-done, f32[8,1,4,40,128]{4,3,2,1,0:T(8,128)S(1)} %all_to_all.34.refs_0_, f32[48,40,128]{2,1,0:T(8,128)S(1)} %get-tuple-element.39.k1.refs_1_, ...), custom_call_target="tpu_custom_call" | custom-call | tf_op jit(solution)/shard_map/pallas_call | solution.py:421
  149.4 15.2 %all_to_all.35 = f32[32,1,128]{2,1,0:T(1,128)S(1)} all-to-all(f32[32,1,128]{2,1,0:T(1,128)S(1)} %bitcast.21), channel_id=1, replica_groups=mesh['slow'=8,'fast'=32] {'fast'}, dimensions={0} | all-to-all | bytes 32768 | tf_op jit(solution)/shard_map/all_to_all | solution.py:493
  164.7 2.7 %shard_map.61 = f32[8,16,256]{2,1,0:T(8,128)} custom-call(s32[3]{0:T(128)S(1)} %copy-done, f32[32,128]{1,0:T(8,128)S(1)} %bitcast.18, f32[48,40,128]{2,1,0:T(8,128)S(1)} %get-tuple-element.54.e1, f32[48,40,128]{2,1,0:T(8,128)S(1)} %get-tuple-element.55.q1, f32[48,40,128]{2,1,0:T(8,128)S(1)} %get-tuple-element.39.k1.refs_1_, ...), custom_call_target="tpu_custom_call" | custom-call | tf_op jit(solution)/shard_map/pallas_call | solution.py:421
  (3 shorter events, 0.1 us)
Async XLA Ops:
  2.1 16.5 %collective-permute-start.1 = (f32[3,2,2,8,8,128]{5,4,3,2,1,0:T(8,128)S(1)}, f32[3,2,2,8,8,128]{5,4,3,2,1,0:T(8,128)S(1)}, u32[]{:S(2)}, u32[]{:S(2)}) collective-permute-start(f32[3,2,2,8,8,128]{5,4,3,2,1,0:T(8,128)S(1)} %get-tuple-element.32.fields), channel_id=1, source_target_pairs={{1,0},{2,1},{3,2},{4,3},{5,4},{6,5},{7,6},{8,7},{9,8},{10,9},{11,1... | collective-permute-start | bytes 1179656 | tf_op jit(solution)/shard_map/ppermute | solution.py:435
  10.8 13.0 %collective-permute-start = (f32[3,2,2,8,8,128]{5,4,3,2,1,0:T(8,128)S(1)}, f32[3,2,2,8,8,128]{5,4,3,2,1,0:T(8,128)S(1)}, u32[]{:S(2)}, u32[]{:S(2)}) collective-permute-start(f32[3,2,2,8,8,128]{5,4,3,2,1,0:T(8,128)S(1)} %get-tuple-element.32.fields), channel_id=1, source_target_pairs={{0,1},{1,2},{2,3},{3,4},{4,5},{5,6},{6,7},{7,8},{8,9},{9,10},{10,1... | collective-permute-start | bytes 1179656 | tf_op jit(solution)/shard_map/ppermute | solution.py:435
  23.7 17.4 %copy-start = (s32[3]{0:T(128)S(1)}, s32[3]{0:T(128)}, u32[]{:S(2)}) copy-start(s32[3]{0:T(128)} %sweeps.11) | copy-start | bytes 40
  23.9 17.2 %collective-permute-start.3 = (f32[3,3,2,2,8,8,128]{6,5,4,3,2,1,0:T(8,128)S(1)}, f32[3,3,2,2,8,8,128]{6,5,4,3,2,1,0:T(8,128)S(1)}, u32[]{:S(2)}, u32[]{:S(2)}) collective-permute-start(f32[3,3,2,2,8,8,128]{6,5,4,3,2,1,0:T(8,128)S(1)} %pad_maximum_fusion.refs_0_), channel_id=1, source_target_pairs={{32,0},{64,32},{96,64},{128,96},{160,128},{192,160},{224,192},{0,2... | collective-permute-start | bytes 3538952 | tf_op jit(solution)/shard_map/ppermute | solution.py:435
  25.7 15.4 %collective-permute-start.2 = (f32[3,3,2,2,8,8,128]{6,5,4,3,2,1,0:T(8,128)S(1)}, f32[3,3,2,2,8,8,128]{6,5,4,3,2,1,0:T(8,128)S(1)}, u32[]{:S(2)}, u32[]{:S(2)}) collective-permute-start(f32[3,3,2,2,8,8,128]{6,5,4,3,2,1,0:T(8,128)S(1)} %pad_maximum_fusion.refs_0_), channel_id=1, source_target_pairs={{0,32},{32,64},{64,96},{96,128},{128,160},{160,192},{192,224},{224... | collective-permute-start | bytes 3538952 | tf_op jit(solution)/shard_map/ppermute | solution.py:435
  43.2 6.5 %collective-permute-start.4 = (f32[2,4,16,128]{3,2,1,0:T(8,128)S(1)}, f32[2,4,16,128]{3,2,1,0:T(8,128)S(1)}, u32[]{:S(2)}, u32[]{:S(2)}) collective-permute-start(f32[2,4,16,128]{3,2,1,0:T(8,128)S(1)} %get-tuple-element.33), channel_id=1, source_target_pairs={{0,1},{1,2},{2,3},{3,4},{4,5},{5,6},{6,7},{7,8},{8,9},{9,10},{10,1... | collective-permute-start | bytes 196616 | tf_op jit(solution)/shard_map/ppermute | solution.py:435
  43.2 6.4 %collective-permute-start.5 = (f32[2,4,16,128]{3,2,1,0:T(8,128)S(1)}, f32[2,4,16,128]{3,2,1,0:T(8,128)S(1)}, u32[]{:S(2)}, u32[]{:S(2)}) collective-permute-start(f32[2,4,16,128]{3,2,1,0:T(8,128)S(1)} %get-tuple-element.35), channel_id=1, source_target_pairs={{1,0},{2,1},{3,2},{4,3},{5,4},{6,5},{7,6},{8,7},{9,8},{10,9},{11,1... | collective-permute-start | bytes 196616 | tf_op jit(solution)/shard_map/ppermute | solution.py:435
  96.0 5.3 %collective-permute-start.7 = (f32[2,2,2,8,8,128]{5,4,3,2,1,0:T(8,128)S(1)}, f32[2,2,2,8,8,128]{5,4,3,2,1,0:T(8,128)S(1)}, u32[]{:S(2)}, u32[]{:S(2)}) collective-permute-start(f32[2,2,2,8,8,128]{5,4,3,2,1,0:T(8,128)S(1)} %shard_map.58.fields), channel_id=1, source_target_pairs={{1,0},{2,1},{3,2},{4,3},{5,4},{6,5},{7,6},{8,7},{9,8},{10,9},{11,1... | collective-permute-start | bytes 786440 | tf_op jit(solution)/shard_map/ppermute | solution.py:435
  97.0 8.5 %collective-permute-start.6 = (f32[2,2,2,8,8,128]{5,4,3,2,1,0:T(8,128)S(1)}, f32[2,2,2,8,8,128]{5,4,3,2,1,0:T(8,128)S(1)}, u32[]{:S(2)}, u32[]{:S(2)}) collective-permute-start(f32[2,2,2,8,8,128]{5,4,3,2,1,0:T(8,128)S(1)} %shard_map.58.fields), channel_id=1, source_target_pairs={{0,1},{1,2},{2,3},{3,4},{4,5},{5,6},{6,7},{7,8},{8,9},{9,10},{10,1... | collective-permute-start | bytes 786440 | tf_op jit(solution)/shard_map/ppermute | solution.py:435
  105.6 14.0 %collective-permute-start.9 = (f32[3,2,2,2,8,8,128]{6,5,4,3,2,1,0:T(8,128)S(1)}, f32[3,2,2,2,8,8,128]{6,5,4,3,2,1,0:T(8,128)S(1)}, u32[]{:S(2)}, u32[]{:S(2)}) collective-permute-start(f32[3,2,2,2,8,8,128]{6,5,4,3,2,1,0:T(8,128)S(1)} %pad_maximum_fusion.1.refs_0_), channel_id=1, source_target_pairs={{32,0},{64,32},{96,64},{128,96},{160,128},{192,160},{224,192},{0,2... | collective-permute-start | bytes 2359304 | tf_op jit(solution)/shard_map/ppermute | solution.py:435
  109.5 10.1 %collective-permute-start.8 = (f32[3,2,2,2,8,8,128]{6,5,4,3,2,1,0:T(8,128)S(1)}, f32[3,2,2,2,8,8,128]{6,5,4,3,2,1,0:T(8,128)S(1)}, u32[]{:S(2)}, u32[]{:S(2)}) collective-permute-start(f32[3,2,2,2,8,8,128]{6,5,4,3,2,1,0:T(8,128)S(1)} %pad_maximum_fusion.1.refs_0_), channel_id=1, source_target_pairs={{0,32},{32,64},{64,96},{96,128},{128,160},{160,192},{192,224},{224... | collective-permute-start | bytes 2359304 | tf_op jit(solution)/shard_map/ppermute | solution.py:435
  121.7 6.3 %collective-permute-start.10 = (f32[1,4,16,128]{3,2,1,0:T(8,128)S(1)}, f32[1,4,16,128]{3,2,1,0:T(8,128)S(1)}, u32[]{:S(2)}, u32[]{:S(2)}) collective-permute-start(f32[1,4,16,128]{3,2,1,0:T(8,128)S(1)} %get-tuple-element.46), channel_id=1, source_target_pairs={{0,1},{1,2},{2,3},{3,4},{4,5},{5,6},{6,7},{7,8},{8,9},{9,10},{10,1... | collective-permute-start | bytes 98312 | tf_op jit(solution)/shard_map/ppermute | solution.py:435
  122.0 6.1 %collective-permute-start.11 = (f32[1,4,16,128]{3,2,1,0:T(8,128)S(1)}, f32[1,4,16,128]{3,2,1,0:T(8,128)S(1)}, u32[]{:S(2)}, u32[]{:S(2)}) collective-permute-start(f32[1,4,16,128]{3,2,1,0:T(8,128)S(1)} %get-tuple-element.48), channel_id=1, source_target_pairs={{1,0},{2,1},{3,2},{4,3},{5,4},{6,5},{7,6},{8,7},{9,8},{10,9},{11,1... | collective-permute-start | bytes 98312 | tf_op jit(solution)/shard_map/ppermute | solution.py:435

commit v5 on v4

--- a/solution.py
+++ b/solution.py
@@ -101,7 +101,63 @@
     over(low, high, chunk, one)
 
 
-def split_kernel(observed, start, diagonal, noise, fields, later, a, b, c, d, halves, sems):
+def closed_neighbours(u, y, lanes):
+    rows = row_iota(ZB)
+    here = {p: u[(*p, y)] for p in PARITIES}
+    beside = {}
+    for pz, px in PARITIES:
+        total = u[pz, px, y - 1] + u[pz, px, y + 1]
+        other = here[1 - pz, px]
+        if pz == 0:
+            moved = jnp.where(rows == 0, 0.0, pltpu.roll(other, 1, 0))
+        else:
+            moved = jnp.where(rows == ZB - 1, 0.0, pltpu.roll(other, ZB - 1, 0))
+        total = total + (other + moved)
+        other = here[pz, 1 - px]
+        if px == 0:
+            moved = jnp.where(lanes == 0, 0.0, pltpu.roll(other, 1, 1))
+        else:
+            moved = jnp.where(lanes == LANES - 1, 0.0, pltpu.roll(other, LANES - 1, 1))
+        beside[pz, px] = total + (other + moved)
+    return here, beside
+
+
+def tile_of(p):
+    return 2 * p[0] + p[1]
+
+
+def pack_tiles(each):
+    return 12 + 8 * each
+
+
+def write_pack(s, linear, diag, out, each, lanes):
+    for p in PARITIES:
+        n = tile_of(p)
+        out[n] = s[(*p, 1)]
+        out[4 + 8 * each + n] = s[(*p, 8)]
+
+    def one(y):
+        here, beside = closed_neighbours(s, y + 1, lanes)
+        for p in PARITIES:
+            g = diag(p, y)
+            out[4 + each * y + tile_of(p)] = linear(p, y) - (g + 6.0) * here[p] + beside[p]
+            if each == 8:
+                out[8 + each * y + tile_of(p)] = g
+
+    for y in range(YB):
+        one(y)
+        for px in range(2):
+            out[8 + 8 * each + px, y : y + 1] = s[0, px, y + 1, 0:1]
+            out[10 + 8 * each + px, y : y + 1] = s[1, px, y + 1, ZB - 1 : ZB]
+
+
+def zero_edges(s):
+    for p in PARITIES:
+        s[(*p, 0)] = jnp.zeros((ZB, LANES), F32)
+        s[(*p, YB + 1)] = jnp.zeros((ZB, LANES), F32)
+
+
+def split_kernel(observed, start, diagonal, noise, pack, field, later, a, b, c, d, halves, s, g, linear, sems):
     copies = [
         pltpu.make_async_copy(source, target, sems.at[n])
         for n, (source, target) in enumerate(((start, a), (diagonal, b), (observed, c), (noise, d)))
@@ -109,22 +165,25 @@
     for copy in copies:
         copy.start()
     matrix = parity_matrix(False)
-
-    def split(n, value, out):
+    zero_edges(s)
+
+    def split(n, value, *outs):
         both = exact_dot(value.reshape(YB * 2 * ZB, 2 * LANES), matrix)
         for px in range(2):
             halves[n, px] = both[:, px * LANES : (px + 1) * LANES]
         for pz, px in PARITIES:
-            part = halves[n, px, pl.ds(pz, YB * ZB, stride=2), :]
-            out[pz, px] = part.reshape(YB, ZB, LANES)
+            part = halves[n, px, pl.ds(pz, YB * ZB, stride=2), :].reshape(YB, ZB, LANES)
+            for out in outs:
+                out[pz, px] = part
 
     copies[0].wait()
-    split(0, a[...], fields.at[0])
+    split(0, a[...], field, s.at[:, :, 1 : YB + 1])
     copies[1].wait()
-    split(1, b[...], fields.at[2])
+    split(1, b[...], g)
     copies[2].wait()
     copies[3].wait()
-    split(2, c[...] + 2.0 * d[0], fields.at[1])
+    split(2, c[...] + 2.0 * d[0], linear)
+    write_pack(s, lambda p, y: linear[(*p, y)], lambda p, y: g[(*p, y)], pack, 8, lane_iota(ZB))
     split(3, c[...] + 2.0 * d[1], later)
 
 
@@ -133,57 +192,77 @@
     return jnp.where((at >= 0) & (at < lax.axis_size(axis)), 1.0, 0.0).astype(F32)
 
 
-def wide(ref, field, p, y):
-    return jnp.concatenate([ref[(zb, field, *p, y)] for zb in range(3)], axis=0)
-
-
 def before_kernel(first, sweeps, *refs):
+    across, low, high = refs[:3], refs[3], refs[4]
     if first:
-        mid, low, high = refs[:3]
-        left_out, own_out, right_out, epre, q, k, dn = refs[3:10]
-        s, a, b = refs[10:]
+        left_out, own_out, right_out, epre, q, k, dn = refs[5:12]
+        a, b = refs[12:]
     else:
-        mid, low, high, k, dn = refs[:5]
-        left_out, own_out, right_out, epre, q = refs[5:10]
-        s, a, b = refs[10:]
+        k, dn = refs[5:7]
+        left_out, own_out, right_out, epre, q = refs[7:12]
+        a, b = refs[12:]
+    each = 8 if first else 4
     lanes = lane_iota(ZW)
     rows = row_iota(ZW)
-    row_mask = jnp.where(
-        rows < ZB, inside("fast", 0), jnp.where(rows < 2 * ZB, 1.0, inside("fast", 2))
-    )
-    blocks = (low, mid, high)
-    masks = [row_mask * inside("slow", 0), row_mask, row_mask * inside("slow", 2)]
-    for yb, ref in enumerate(blocks):
-
-        def fill(y):
-            for p in PARITIES:
-                value = wide(ref, 0, p, y)
-                s[(*p, yb * YB + y)] = jnp.where(masks[yb] > 0.5, value, 0.0)
-
-        over(0, YB, 8, fill)
-    for yb, ref in enumerate(blocks):
-
-        def right_side(y):
-            row = yb * YB + y
-            here, beside = fine_neighbours(s, row, lanes)
-            for p in PARITIES:
-                if first:
-                    full = wide(ref, 2, p, y) + 6.0
-                    gain = (OMEGA / full) * masks[yb]
-                    k[(*p, row)] = gain
-                    if yb == 1:
-                        dn[(*p, y)] = full * (1.0 / OMEGA)
-                else:
-                    gain = k[(*p, row)]
-                start = gain * (wide(ref, 1, p, y) + beside[p]) - OMEGA * here[p]
-                q[(*p, row)] = start
-                a[(*p, row)] = start
-                b[(*p, row)] = start
-
+    tile_rows = row_iota(ZB)
+    in_z = [inside("fast", n) for n in range(3)]
+    in_y = [inside("slow", n) for n in range(3)]
+    row_mask = jnp.where(rows < ZB, in_z[0], jnp.where(rows < 2 * ZB, 1.0, in_z[2]))
+    masks = [row_mask * in_y[0], row_mask, row_mask * in_y[2]]
+
+    def tile(yb, zb, n):
         if yb == 1:
-            over(0, YB, 4, right_side)
-        else:
-            over(1 - yb // 2, YB - yb // 2, 7, right_side)
+            return across[zb].at[n]
+        if yb == 0:
+            return low.at[zb, n - (4 + each)]
+        return high.at[zb, n]
+
+    def z_face(yb, zb, which, px, y):
+        n = 8 + 8 * each + 2 * which + px
+        if yb == 2:
+            n = 4 + 7 * each + 2 * which + px
+        return tile(yb, zb, n)[pl.ds(y, 1), :]
+
+    def wide(yb, n):
+        return jnp.concatenate([tile(yb, zb, n)[...] for zb in range(3)], axis=0)
+
+    def right_side(yb, y):
+        row = yb * YB + y
+        for p in PARITIES:
+            pz, px = p
+            tiles = [tile(yb, zb, 4 + each * y + tile_of(p))[...] for zb in range(3)]
+            if pz == 1:
+                edge = tile_rows == ZB - 1
+                tiles[0] = tiles[0] + jnp.where(edge, z_face(yb, 1, 0, px, y), 0.0)
+                tiles[1] = tiles[1] + jnp.where(edge, z_face(yb, 2, 0, px, y) * in_z[2], 0.0)
+            else:
+                edge = tile_rows == 0
+                tiles[1] = tiles[1] + jnp.where(edge, z_face(yb, 0, 1, px, y) * in_z[0], 0.0)
+                tiles[2] = tiles[2] + jnp.where(edge, z_face(yb, 1, 1, px, y), 0.0)
+            rhs = jnp.concatenate(tiles, axis=0)
+            if isinstance(y, int) and y == 0 and yb > 0:
+                rhs = rhs + wide(yb - 1, 4 + 8 * each + tile_of(p)) * in_y[yb - 1]
+            if isinstance(y, int) and y == YB - 1 and yb < 2:
+                rhs = rhs + wide(yb + 1, tile_of(p)) * in_y[yb + 1]
+            if first:
+                full = wide(yb, 8 + each * y + tile_of(p)) + 6.0
+                gain = (OMEGA / full) * masks[yb]
+                k[(*p, row)] = gain
+                if yb == 1:
+                    dn[(*p, y)] = full * (1.0 / OMEGA)
+            else:
+                gain = k[(*p, row)]
+            start = gain * rhs
+            q[(*p, row)] = start
+            a[(*p, row)] = start
+            b[(*p, row)] = start
+
+    for yb in range(3):
+        over(1, YB - 1, 6, functools.partial(right_side, yb))
+    right_side(0, YB - 1)
+    right_side(1, 0)
+    right_side(1, YB - 1)
+    right_side(2, 0)
 
     @pl.when(sweeps[0] >= 4)
     def _():
@@ -206,7 +285,7 @@
                 scaled = q[(*p, row)] - OMEGA * here[p] + k[(*p, row)] * beside[p]
                 total = total + scaled * dn[(*p, 2 * ym + half)]
                 if first:
-                    diag = diag + wide(mid, 2, p, 2 * ym + half)
+                    diag = diag + wide(1, 8 + each * (2 * ym + half) + tile_of(p))
         for n, value in enumerate((total, diag) if first else (total,)):
             value = value * 0.125
             right_out[n, ym] = value[: 2 * ZB]
@@ -349,7 +428,11 @@
         e2_out[y] = x2[y, ZB : 4 * ZB]
 
 
-def after_kernel(last, faces, sweeps, parts, e1, q1, k1, e2, epre, q, k, fields, later, out, va, vb, a, b, halves):
+def after_kernel(last, faces, sweeps, *refs):
+    if last:
+        parts, e1, q1, k1, e2, epre, q, k, field, out, va, vb, a, b, halves = refs
+    else:
+        parts, e1, q1, k1, e2, epre, q, k, field, later, pack, out, field_out, va, vb, a, b, s = refs
     lanes = lane_iota(ZW)
     lanes_p = lane_iota(parts.shape[0])
     every = parts[...]
@@ -402,16 +485,22 @@
 
     fine_sweep(b, a, q, k, 3, 13, 10, lanes, offset=4)
     fine_sweep(a, b, q, k, 4, 12, 8, lanes, offset=4)
+    if not last:
+        zero_edges(s)
     for pz, px in PARITIES:
-        value = fields[0, pz, px] + 0.5 * b[pz, px, 4:12, ZB : 2 * ZB]
+        value = field[pz, px] + 0.5 * b[pz, px, 4:12, ZB : 2 * ZB]
         if last:
             halves[px, pl.ds(pz, YB * ZB, stride=2), :] = value.reshape(YB * ZB, LANES)
         else:
-            out[0, pz, px] = value
-            out[1, pz, px] = later[pz, px]
+            field_out[pz, px] = value
+            s[pz, px, 1 : YB + 1] = value
     if last:
         both = jnp.concatenate([halves[0], halves[1]], axis=1)
         out[...] = exact_dot(both, parity_matrix(True)).reshape(YB, 2 * ZB, 2 * LANES)
+    else:
+        write_pack(
+            s, lambda p, y: later[(*p, y)], lambda p, y: pack[8 + 8 * y + tile_of(p)], out, 4, lane_iota(ZB)
+        )
 
 
 def call(kernel, outs, scratch, scalars, *arrays, space=pltpu.VMEM, megabytes=16, kept=True):
@@ -435,16 +524,19 @@
     return lax.ppermute(to_right, axis, up), lax.ppermute(to_left, axis, down)
 
 
-def window_of(fields):
-    left, right = both_ways(fields, fields, "fast")
-    mid = jnp.stack([left, fields, right])
-    low, high = both_ways(mid, mid, "slow")
-    return mid, low, high
+def window_of(pack, each):
+    left, right = both_ways(pack, pack, "fast")
+    strip = jnp.stack([left, pack, right])
+    upward = strip[:, 4 + each :]
+    downward = jnp.concatenate([strip[:, : 4 + 7 * each], strip[:, 8 + 8 * each :]], axis=1)
+    low, high = both_ways(upward, downward, "slow")
+    return left, pack, right, low, high
 
 
 def body(observed, start_field, diagonal, noise, sweeps):
     natural = observed.shape
     block = (2, 2, YB, ZB, LANES)
+    edged = (2, 2, YB + 2, ZB, LANES)
     post = (2, 2, YPOST, ZW, LANES)
     whole = (2, 2, YW, ZW, LANES)
     middle = (YM + 2 * PADM, ZM, LANES)
@@ -452,23 +544,26 @@
     fast_count, slow_count = lax.axis_size("fast"), lax.axis_size("slow")
     first, second, third = YB * slow_count // 4, 2 * ZB * fast_count // 4, 2 * LANES // 4
     faces = 2.0 * (first * second + first * third + second * third)
-    fields, later = call(
-        split_kernel, [(3, *block), block],
-        [natural, natural, natural, (2, *natural), (4, 2, YB * 2 * ZB, LANES), pltpu.SemaphoreType.DMA((4,))],
+    pack, field, later = call(
+        split_kernel, [(pack_tiles(8), ZB, LANES), block, block],
+        [
+            natural, natural, natural, (2, *natural), (4, 2, YB * 2 * ZB, LANES),
+            edged, block, block, pltpu.SemaphoreType.DMA((4,)),
+        ],
         (), observed, start_field, diagonal, noise, space=pltpu.HBM,
     )
+    own_pack = pack
     kept_fine = kept_low = None
     for step in range(2):
         opening = step == 0
         count = 2 if opening else 1
-        mid, low, high = window_of(fields)
+        given = window_of(pack, 8 if opening else 4)
         outs = [(count, 4, 16, LANES), (count, 4, 8, LANES), (count, 4, 16, LANES), post, whole]
         if opening:
             outs += [whole, (2, 2, YB, ZW, LANES)]
-            given = (mid, low, high)
         else:
-            given = (mid, low, high, *kept_fine)
-        got = call(functools.partial(before_kernel, opening), outs, [whole] * 3, (sweeps,), *given)
+            given = (*given, *kept_fine)
+        got = call(functools.partial(before_kernel, opening), outs, [whole] * 2, (sweeps,), *given)
         to_left, own, to_right, epre, q = got[:5]
         if opening:
             kept_fine = got[5:]
@@ -491,13 +586,17 @@
         if opening:
             kept_low = got[4:]
         parts = lax.all_to_all(part, "fast", 0, 0, tiled=True)
-        outs = [(2, *block) if opening else natural]
-        scratch = [(YPOST, ZW, LANES)] * 2 + [post] * 2 + [(2, YB * 2 * ZB, LANES)]
-        (fields,) = call(
-            functools.partial(after_kernel, not opening, faces), outs, scratch, (sweeps,),
-            parts, e1, q1, kept_low[0], e2, epre, q, kept_fine[0], fields, later, kept=opening,
-        )
-    return fields
+        given = (parts, e1, q1, kept_low[0], e2, epre, q, kept_fine[0], field)
+        scratch = [(YPOST, ZW, LANES)] * 2 + [post] * 2
+        kernel = functools.partial(after_kernel, not opening, faces)
+        if opening:
+            outs = [(pack_tiles(4), ZB, LANES), block]
+            given = (*given, later, own_pack)
+            pack, field = call(kernel, outs, scratch + [edged], (sweeps,), *given)
+        else:
+            halves = [(2, YB * 2 * ZB, LANES)]
+            (out,) = call(kernel, [natural], scratch + halves, (sweeps,), *given, kept=False)
+    return out
 
 
 def solution(mesh):

time: 168 us -> 157 us (0.935)
  waiting for transfers between devices: 48.1 us -> 37.5 us
    ppermute x12, waiting for transfers between devices: 48.1 us -> 37.5 us  [both_ways(): return (lax.ppermute(to_right, axis, up), lax.ppermute(to_left, axis, down))]
where the time goes in v5:
time: 157 us; the launch traced here: 156 us
  blocking collectives  71.5 us (46%)
  waiting for transfers between devices  37.5 us (24%)
  starting transfers between devices  27.3 us (17%)
  Pallas kernels  19.1 us (12%)
    all_to_all x2, blocking collectives, body(): strip = lax.all_to_all(strip, 'slow', 0, 0, tiled=True)  41.2 us
    ppermute x12, waiting for transfers between devices, both_ways(): return (lax.ppermute(to_right, axis, up), lax.ppermute(to_left, axis, down))  37.5 us
    all_to_all x2, blocking collectives, body(): parts = lax.all_to_all(part, 'fast', 0, 0, tiled=True)  30.3 us
    ppermute x12, starting transfers between devices, both_ways(): return (lax.ppermute(to_right, axis, up), lax.ppermute(to_left, axis, down))  27.3 us
    pallas_call x7, Pallas kernels, call(): pl.pallas_call(kernel, out_shape=[pltpu.VMEM(s, F32) if kept else jax.Sha...  19.1 us
  transfers between devices with their start and end apart: 12, of which 8 were waited for; matrix products, arithmetic and copies ran while one was open for 0% of the time, Pallas kernels for 0%

profile of v5, /device:TPU:1, one launch (start us, length us, event | category | flops | bytes accessed | tf_op | source)
XLA Modules:
  0.0 156.1 jit_solution(2920683747747118283)
XLA Ops:
  0.0 2.1 %shard_map.55 = (f32[76,8,128]{2,1,0:T(8,128)S(1)}, f32[2,2,8,8,128]{4,3,2,1,0:T(8,128)S(1)}, f32[2,2,8,8,128]{4,3,2,1,0:T(8,128)S(1)}) custom-call(f32[8,16,256]{2,1,0:T(8,128)} %observed.1, f32[8,16,256]{2,1,0:T(8,128)} %start.1, f32[8,16,256]{2,1,0:T(8,128)} %diagonal.1, f32[2,8,16,256]{3,2,1,0:T(8,128)} %noise.1), custom_call_target="tpu_custom_call" | custom-call | tf_op jit(solution)/shard_map/pallas_call | solution.py:510
  2.1 8.7 %collective-permute-start.1 = (f32[76,8,128]{2,1,0:T(8,128)S(1)}, f32[76,8,128]{2,1,0:T(8,128)S(1)}, u32[]{:S(2)}, u32[]{:S(2)}) collective-permute-start(f32[76,8,128]{2,1,0:T(8,128)S(1)} %get-tuple-element.35.refs_1_.refs_10_), channel_id=1, source_target_pairs={{1,0},{2,1},{3,2},{4,3},{5,4},{6,5},{7,6},{8,7},{9,8},{10,9},{11,1... | collective-permute-start | bytes 933896 | tf_op jit(solution)/shard_map/ppermute | solution.py:524
  10.8 0.0 collective-permute-start
  10.8 6.0 %collective-permute-done.1.refs_2_ = f32[76,8,128]{2,1,0:T(8,128)S(1)} collective-permute-done((f32[76,8,128]{2,1,0:T(8,128)S(1)}, f32[76,8,128]{2,1,0:T(8,128)S(1)}, u32[]{:S(2)}, u32[]{:S(2)}) %collective-permute-start.1) | collective-permute-done | bytes 311328 | tf_op jit(solution)/shard_map/ppermute | solution.py:524
  16.8 5.2 %collective-permute-done.refs_0_ = f32[76,8,128]{2,1,0:T(8,128)S(1)} collective-permute-done((f32[76,8,128]{2,1,0:T(8,128)S(1)}, f32[76,8,128]{2,1,0:T(8,128)S(1)}, u32[]{:S(2)}, u32[]{:S(2)}) %collective-permute-start) | collective-permute-done | bytes 311328 | tf_op jit(solution)/shard_map/ppermute | solution.py:524
  22.0 0.1 pad_maximum_fusion
  22.1 0.1 slice.24
  22.2 0.0 copy-start
  22.2 0.1 fusion
  22.3 1.9 %collective-permute-start.3 = (f32[3,64,8,128]{3,2,1,0:T(8,128)S(1)}, f32[3,64,8,128]{3,2,1,0:T(8,128)S(1)}, u32[]{:S(2)}, u32[]{:S(2)}) collective-permute-start(f32[3,64,8,128]{3,2,1,0:T(8,128)S(1)} %fusion), channel_id=1, source_target_pairs={{32,0},{64,32},{96,64},{128,96},{160,128},{192,160},{224,192},{0,2... | collective-permute-start | bytes 2359304 | tf_op jit(solution)/shard_map/ppermute | solution.py:524
  24.1 1.2 collective-permute-start.2
  25.3 9.9 %collective-permute-done.3.refs_4_ = f32[3,64,8,128]{3,2,1,0:T(8,128)S(1)} collective-permute-done((f32[3,64,8,128]{3,2,1,0:T(8,128)S(1)}, f32[3,64,8,128]{3,2,1,0:T(8,128)S(1)}, u32[]{:S(2)}, u32[]{:S(2)}) %collective-permute-start.3) | collective-permute-done | bytes 786464 | tf_op jit(solution)/shard_map/ppermute | solution.py:524
  35.3 0.0 collective-permute-done.2.refs_3_
  35.3 0.0 copy-done
  35.3 1.6 %shard_map.56 = (f32[2,4,16,128]{3,2,1,0:T(8,128)S(1)}, f32[2,4,8,128]{3,2,1,0:T(8,128)S(1)}, f32[2,4,16,128]{3,2,1,0:T(8,128)S(1)}, f32[2,2,16,24,128]{4,3,2,1,...) custom-call(s32[3]{0:T(128)S(1)} %copy-done, ...), custom_call_target="tpu_custom_call" | custom-call | tf_op jit(solution)/shard_map/pallas_call | solution.py:510
  36.9 0.1 collective-permute-start.4
  37.0 4.8 %collective-permute-start.5 = (f32[2,4,16,128]{3,2,1,0:T(8,128)S(1)}, f32[2,4,16,128]{3,2,1,0:T(8,128)S(1)}, u32[]{:S(2)}, u32[]{:S(2)}) collective-permute-start(f32[2,4,16,128]{3,2,1,0:T(8,128)S(1)} %get-tuple-element.38), channel_id=1, source_target_pairs={{1,0},{2,1},{3,2},{4,3},{5,4},{6,5},{7,6},{8,7},{9,8},{10,9},{11,1... | collective-permute-start | bytes 196616 | tf_op jit(solution)/shard_map/ppermute | solution.py:524
  41.7 1.6 %collective-permute-done.4 = f32[2,4,16,128]{3,2,1,0:T(8,128)S(1)} collective-permute-done((f32[2,4,16,128]{3,2,1,0:T(8,128)S(1)}, f32[2,4,16,128]{3,2,1,0:T(8,128)S(1)}, u32[]{:S(2)}, u32[]{:S(2)}) %collective-permute-start.4) | collective-permute-done | bytes 65568 | tf_op jit(solution)/shard_map/ppermute | solution.py:524
  43.4 0.0 collective-permute-done.5
  43.4 0.1 broadcast_in_dim.6
  43.5 24.2 %all_to_all.32.refs_0_ = f32[8,2,4,40,128]{4,3,2,1,0:T(8,128)S(1)} all-to-all(f32[8,2,4,40,128]{4,3,2,1,0:T(8,128)S(1)} %broadcast_in_dim.6), channel_id=1, replica_groups=mesh['slow'=8,'fast'=32] {'slow'}, dimensions={0} | all-to-all | bytes 2621440 | tf_op jit(solution)/shard_map/all_to_all | solution.py:573
  67.8 5.0 %shard_map.57 = (f32[32,128]{1,0:T(8,128)S(1)}, f32[48,40,128]{2,1,0:T(8,128)S(1)}, f32[48,40,128]{2,1,0:T(8,128)S(1)}, f32[8,24,128]{2,1,0:T(8,128)S(1)}, f32[4...) custom-call(s32[3]{0:T(128)S(1)} %copy-done, ...), custom_call_target="tpu_custom_call" | custom-call | tf_op jit(solution)/shard_map/pallas_call | solution.py:510
  72.8 15.1 %all_to_all.33 = f32[32,1,128]{2,1,0:T(1,128)S(1)} all-to-all(f32[32,1,128]{2,1,0:T(1,128)S(1)} %bitcast.30), channel_id=1, replica_groups=mesh['slow'=8,'fast'=32] {'fast'}, dimensions={0} | all-to-all | bytes 32768 | tf_op jit(solution)/shard_map/all_to_all | solution.py:588
  87.9 1.9 %shard_map.58 = (f32[44,8,128]{2,1,0:T(8,128)S(1)}, f32[2,2,8,8,128]{4,3,2,1,0:T(8,128)S(1)}) custom-call(s32[3]{0:T(128)S(1)} %copy-done, f32[32,128]{1,0:T(8,128)S(1)} %bitcast.28, f32[48,40,128]{2,1,0:T(8,128)S(1)} %get-tuple-element.40.refs_1_, f32[48,40,128]{2,1,0:T(8,128)S(1)} %get-tuple-element.41.refs_2_, ...), custom_call_target="tpu_custom_call" | custom-call | tf_op jit(solution)/shard_map/pallas_call | solution.py:510
  89.8 1.0 collective-permute-start.7
  90.8 0.5 collective-permute-start.6
  91.3 2.9 %collective-permute-done.7.refs_2_ = f32[44,8,128]{2,1,0:T(8,128)S(1)} collective-permute-done((f32[44,8,128]{2,1,0:T(8,128)S(1)}, f32[44,8,128]{2,1,0:T(8,128)S(1)}, u32[]{:S(2)}, u32[]{:S(2)}) %collective-permute-start.7) | collective-permute-done | bytes 180256 | tf_op jit(solution)/shard_map/ppermute | solution.py:524
  94.2 4.3 %collective-permute-done.6.refs_0_ = f32[44,8,128]{2,1,0:T(8,128)S(1)} collective-permute-done((f32[44,8,128]{2,1,0:T(8,128)S(1)}, f32[44,8,128]{2,1,0:T(8,128)S(1)}, u32[]{:S(2)}, u32[]{:S(2)}) %collective-permute-start.6) | collective-permute-done | bytes 180256 | tf_op jit(solution)/shard_map/ppermute | solution.py:524
  98.6 3.9 %collective-permute-start.9 = (f32[3,36,8,128]{3,2,1,0:T(8,128)S(1)}, f32[3,36,8,128]{3,2,1,0:T(8,128)S(1)}, u32[]{:S(2)}, u32[]{:S(2)}) collective-permute-start(f32[3,36,8,128]{3,2,1,0:T(8,128)S(1)} %fusion.1), channel_id=1, source_target_pairs={{32,0},{64,32},{96,64},{128,96},{160,128},{192,160},{224,192},{0,2... | collective-permute-start | bytes 1327112 | tf_op jit(solution)/shard_map/ppermute | solution.py:524
  102.5 0.2 collective-permute-start.8
  102.7 6.3 %collective-permute-done.9.refs_4_ = f32[3,36,8,128]{3,2,1,0:T(8,128)S(1)} collective-permute-done((f32[3,36,8,128]{3,2,1,0:T(8,128)S(1)}, f32[3,36,8,128]{3,2,1,0:T(8,128)S(1)}, u32[]{:S(2)}, u32[]{:S(2)}) %collective-permute-start.9) | collective-permute-done | bytes 442400 | tf_op jit(solution)/shard_map/ppermute | solution.py:524
  109.0 0.0 collective-permute-done.8.refs_3_
  109.0 1.5 shard_map.59
  110.4 0.3 collective-permute-start.10
  110.7 4.8 %collective-permute-start.11 = (f32[1,4,16,128]{3,2,1,0:T(8,128)S(1)}, f32[1,4,16,128]{3,2,1,0:T(8,128)S(1)}, u32[]{:S(2)}, u32[]{:S(2)}) collective-permute-start(f32[1,4,16,128]{3,2,1,0:T(8,128)S(1)} %get-tuple-element.53), channel_id=1, source_target_pairs={{1,0},{2,1},{3,2},{4,3},{5,4},{6,5},{7,6},{8,7},{9,8},{10,9},{11,1... | collective-permute-start | bytes 98312 | tf_op jit(solution)/shard_map/ppermute | solution.py:524
  115.5 1.3 collective-permute-done.10
  116.8 0.0 collective-permute-done.11
  116.8 17.0 %all_to_all.34.refs_0_ = f32[8,1,4,40,128]{4,3,2,1,0:T(8,128)S(1)} all-to-all(f32[8,1,4,40,128]{4,3,2,1,0:T(8,128)S(1)} %broadcast_in_dim.16), channel_id=1, replica_groups=mesh['slow'=8,'fast'=32] {'slow'}, dimensions={0} | all-to-all | bytes 1310720 | tf_op jit(solution)/shard_map/all_to_all | solution.py:573
  133.8 4.4 %shard_map.60 = (f32[32,128]{1,0:T(8,128)S(1)}, f32[48,40,128]{2,1,0:T(8,128)S(1)}, f32[48,40,128]{2,1,0:T(8,128)S(1)}, f32[8,24,128]{2,1,0:T(8,128)S(1)}) custom-call(s32[3]{0:T(128)S(1)} %copy-done, f32[8,1,4,40,128]{4,3,2,1,0:T(8,128)S(1)} %all_to_all.34.refs_0_, f32[48,40,128]{2,1,0:T(8,128)S(1)} %get-tuple-element.42.refs_3_.refs_1_, ...), custom_call_target="tpu_custom_call" | custom-call | tf_op jit(solution)/shard_map/pallas_call | solution.py:510
  138.2 15.2 %all_to_all.35 = f32[32,1,128]{2,1,0:T(1,128)S(1)} all-to-all(f32[32,1,128]{2,1,0:T(1,128)S(1)} %bitcast.31), channel_id=1, replica_groups=mesh['slow'=8,'fast'=32] {'fast'}, dimensions={0} | all-to-all | bytes 32768 | tf_op jit(solution)/shard_map/all_to_all | solution.py:588
  153.4 2.7 %shard_map.61 = f32[8,16,256]{2,1,0:T(8,128)} custom-call(s32[3]{0:T(128)S(1)} %copy-done, f32[32,128]{1,0:T(8,128)S(1)} %bitcast.29, f32[48,40,128]{2,1,0:T(8,128)S(1)} %get-tuple-element.59.refs_1_, f32[48,40,128]{2,1,0:T(8,128)S(1)} %get-tuple-element.60.refs_2_, f32[48,40,128]{2,1,0:T(8,128)S(1)} %get-tuple-element.42.refs_3_.refs_1_, ...), custom_call_target="tpu_custom_call" | custom-call | tf_op jit(solution)/shard_map/pallas_call | solution.py:510
  (8 shorter events, 0.2 us)
Async XLA Ops:
  2.1 14.7 %collective-permute-start.1 = (f32[76,8,128]{2,1,0:T(8,128)S(1)}, f32[76,8,128]{2,1,0:T(8,128)S(1)}, u32[]{:S(2)}, u32[]{:S(2)}) collective-permute-start(f32[76,8,128]{2,1,0:T(8,128)S(1)} %get-tuple-element.35.refs_1_.refs_10_), channel_id=1, source_target_pairs={{1,0},{2,1},{3,2},{4,3},{5,4},{6,5},{7,6},{8,7},{9,8},{10,9},{11,1... | collective-permute-start | bytes 933896 | tf_op jit(solution)/shard_map/ppermute | solution.py:524
  10.8 11.2 %collective-permute-start = (f32[76,8,128]{2,1,0:T(8,128)S(1)}, f32[76,8,128]{2,1,0:T(8,128)S(1)}, u32[]{:S(2)}, u32[]{:S(2)}) collective-permute-start(f32[76,8,128]{2,1,0:T(8,128)S(1)} %get-tuple-element.35.refs_1_.refs_10_), channel_id=1, source_target_pairs={{0,1},{1,2},{2,3},{3,4},{4,5},{5,6},{6,7},{7,8},{8,9},{9,10},{10,1... | collective-permute-start | bytes 933896 | tf_op jit(solution)/shard_map/ppermute | solution.py:524
  22.2 13.1 %copy-start = (s32[3]{0:T(128)S(1)}, s32[3]{0:T(128)}, u32[]{:S(2)}) copy-start(s32[3]{0:T(128)} %sweeps.11) | copy-start | bytes 40
  22.3 13.0 %collective-permute-start.3 = (f32[3,64,8,128]{3,2,1,0:T(8,128)S(1)}, f32[3,64,8,128]{3,2,1,0:T(8,128)S(1)}, u32[]{:S(2)}, u32[]{:S(2)}) collective-permute-start(f32[3,64,8,128]{3,2,1,0:T(8,128)S(1)} %fusion), channel_id=1, source_target_pairs={{32,0},{64,32},{96,64},{128,96},{160,128},{192,160},{224,192},{0,2... | collective-permute-start | bytes 2359304 | tf_op jit(solution)/shard_map/ppermute | solution.py:524
  24.1 11.2 %collective-permute-start.2 = (f32[3,64,8,128]{3,2,1,0:T(8,128)S(1)}, f32[3,64,8,128]{3,2,1,0:T(8,128)S(1)}, u32[]{:S(2)}, u32[]{:S(2)}) collective-permute-start(f32[3,64,8,128]{3,2,1,0:T(8,128)S(1)} %slice.24), channel_id=1, source_target_pairs={{0,32},{32,64},{64,96},{96,128},{128,160},{160,192},{192,224},{224... | collective-permute-start | bytes 2359304 | tf_op jit(solution)/shard_map/ppermute | solution.py:524
  36.9 6.5 %collective-permute-start.4 = (f32[2,4,16,128]{3,2,1,0:T(8,128)S(1)}, f32[2,4,16,128]{3,2,1,0:T(8,128)S(1)}, u32[]{:S(2)}, u32[]{:S(2)}) collective-permute-start(f32[2,4,16,128]{3,2,1,0:T(8,128)S(1)} %get-tuple-element.36), channel_id=1, source_target_pairs={{0,1},{1,2},{2,3},{3,4},{4,5},{5,6},{6,7},{7,8},{8,9},{9,10},{10,1... | collective-permute-start | bytes 196616 | tf_op jit(solution)/shard_map/ppermute | solution.py:524
  37.0 6.4 %collective-permute-start.5 = (f32[2,4,16,128]{3,2,1,0:T(8,128)S(1)}, f32[2,4,16,128]{3,2,1,0:T(8,128)S(1)}, u32[]{:S(2)}, u32[]{:S(2)}) collective-permute-start(f32[2,4,16,128]{3,2,1,0:T(8,128)S(1)} %get-tuple-element.38), channel_id=1, source_target_pairs={{1,0},{2,1},{3,2},{4,3},{5,4},{6,5},{7,6},{8,7},{9,8},{10,9},{11,1... | collective-permute-start | bytes 196616 | tf_op jit(solution)/shard_map/ppermute | solution.py:524
  89.8 4.4 %collective-permute-start.7 = (f32[44,8,128]{2,1,0:T(8,128)S(1)}, f32[44,8,128]{2,1,0:T(8,128)S(1)}, u32[]{:S(2)}, u32[]{:S(2)}) collective-permute-start(f32[44,8,128]{2,1,0:T(8,128)S(1)} %get-tuple-element.49.refs_1_), channel_id=1, source_target_pairs={{1,0},{2,1},{3,2},{4,3},{5,4},{6,5},{7,6},{8,7},{9,8},{10,9},{11,1... | collective-permute-start | bytes 540680 | tf_op jit(solution)/shard_map/ppermute | solution.py:524
  90.8 7.7 %collective-permute-start.6 = (f32[44,8,128]{2,1,0:T(8,128)S(1)}, f32[44,8,128]{2,1,0:T(8,128)S(1)}, u32[]{:S(2)}, u32[]{:S(2)}) collective-permute-start(f32[44,8,128]{2,1,0:T(8,128)S(1)} %get-tuple-element.49.refs_1_), channel_id=1, source_target_pairs={{0,1},{1,2},{2,3},{3,4},{4,5},{5,6},{6,7},{7,8},{8,9},{9,10},{10,1... | collective-permute-start | bytes 540680 | tf_op jit(solution)/shard_map/ppermute | solution.py:524
  98.6 10.3 %collective-permute-start.9 = (f32[3,36,8,128]{3,2,1,0:T(8,128)S(1)}, f32[3,36,8,128]{3,2,1,0:T(8,128)S(1)}, u32[]{:S(2)}, u32[]{:S(2)}) collective-permute-start(f32[3,36,8,128]{3,2,1,0:T(8,128)S(1)} %fusion.1), channel_id=1, source_target_pairs={{32,0},{64,32},{96,64},{128,96},{160,128},{192,160},{224,192},{0,2... | collective-permute-start | bytes 1327112 | tf_op jit(solution)/shard_map/ppermute | solution.py:524
  102.5 6.5 %collective-permute-start.8 = (f32[3,36,8,128]{3,2,1,0:T(8,128)S(1)}, f32[3,36,8,128]{3,2,1,0:T(8,128)S(1)}, u32[]{:S(2)}, u32[]{:S(2)}) collective-permute-start(f32[3,36,8,128]{3,2,1,0:T(8,128)S(1)} %slice.26), channel_id=1, source_target_pairs={{0,32},{32,64},{64,96},{96,128},{128,160},{160,192},{192,224},{224... | collective-permute-start | bytes 1327112 | tf_op jit(solution)/shard_map/ppermute | solution.py:524
  110.4 6.3 %collective-permute-start.10 = (f32[1,4,16,128]{3,2,1,0:T(8,128)S(1)}, f32[1,4,16,128]{3,2,1,0:T(8,128)S(1)}, u32[]{:S(2)}, u32[]{:S(2)}) collective-permute-start(f32[1,4,16,128]{3,2,1,0:T(8,128)S(1)} %get-tuple-element.51), channel_id=1, source_target_pairs={{0,1},{1,2},{2,3},{3,4},{4,5},{5,6},{6,7},{7,8},{8,9},{9,10},{10,1... | collective-permute-start | bytes 98312 | tf_op jit(solution)/shard_map/ppermute | solution.py:524
  110.7 6.1 %collective-permute-start.11 = (f32[1,4,16,128]{3,2,1,0:T(8,128)S(1)}, f32[1,4,16,128]{3,2,1,0:T(8,128)S(1)}, u32[]{:S(2)}, u32[]{:S(2)}) collective-permute-start(f32[1,4,16,128]{3,2,1,0:T(8,128)S(1)} %get-tuple-element.53), channel_id=1, source_target_pairs={{1,0},{2,1},{3,2},{4,3},{5,4},{6,5},{7,6},{8,7},{9,8},{10,9},{11,1... | collective-permute-start | bytes 98312 | tf_op jit(solution)/shard_map/ppermute | solution.py:524

commit v6 on v5

--- a/solution.py
+++ b/solution.py
@@ -296,16 +296,20 @@
 
 
 def coarse_kernel(first, sweeps, *refs):
-    window = refs[0]
+    mine, other = refs[:2]
     if first:
-        part, e1, q1, e2_out, k1, d1, k2, d2, g2sum = refs[1:10]
-        va, t, wa, wb, q2, x2 = refs[10:]
+        part, e1, q1, e2_out, k1, d1, k2, d2, g2sum = refs[2:11]
+        va, t, wa, wb, q2, x2 = refs[11:]
     else:
-        k1, d1, k2, d2, g2sum = refs[1:6]
-        part, e1, q1, e2_out = refs[6:10]
-        va, t, wa, wb, q2, x2 = refs[10:]
+        k1, d1, k2, d2, g2sum = refs[2:7]
+        part, e1, q1, e2_out = refs[7:11]
+        va, t, wa, wb, q2, x2 = refs[11:]
     fast = lax.axis_index("fast")
     slow = lax.axis_index("slow")
+
+    def window(chip, core, n, ym):
+        return jnp.where((slow & 1) == core, mine[chip, n, ym], other[chip, n, ym])
+
     lanes = lane_iota(ZM)
     even = (lanes & 1) == 0
     zrow = row_iota(ZM) + (fast * ZB - 2 * ZB)
@@ -318,22 +322,25 @@
         if first:
             k1[n] = zero
 
-    def opening(block):
-        for ym in range(4):
-            y = block * 4 + ym
-            if first:
-                full = window[block, 1, ym] + 1.5
-                gain = (OMEGA / full) * mask
-                k1[PADM + y] = gain * 0.25
-                d1[y] = full * (1.0 / OMEGA)
-                start = gain * window[block, 0, ym]
-            else:
-                start = (4.0 * k1[PADM + y]) * window[block, 0, ym]
-            q1[PADM + y] = start
-            va[PADM + y] = start
-            e1[PADM + y] = start
-
-    over(0, YM // 4, 2, opening)
+    def opening(chip):
+        for core in range(2):
+            for ym in range(4):
+                y = chip * 8 + core * 4 + ym
+                rhs = window(chip, core, 0, ym)
+                if first:
+                    diag = window(chip, core, 1, ym)
+                    d1[y] = diag
+                    full = diag + 1.5
+                    gain = (OMEGA / full) * mask
+                    k1[PADM + y] = gain * 0.25
+                    start = gain * rhs
+                else:
+                    start = (4.0 * k1[PADM + y]) * rhs
+                q1[PADM + y] = start
+                va[PADM + y] = start
+                e1[PADM + y] = start
+
+    over(0, YM // 8, 1, opening)
     of_q1, of_k1 = (lambda y: q1[y]), (lambda y: k1[y])
 
     @pl.when(sweeps[1] >= 4)
@@ -354,8 +361,8 @@
         for half in range(2):
             y = PADM + 2 * yc + half
             here, beside = flat_neighbours(e1, y, lanes, 1)
-            total = total + (q1[y] - OMEGA * here + k1[y] * beside) * d1[2 * yc + half]
-        t[yc, :ZM] = pair_sum(total)
+            total = total + (q1[y] - OMEGA * here + k1[y] * beside) * (d1[2 * yc + half] + 1.5)
+        t[yc, :ZM] = pair_sum(total * (1.0 / OMEGA))
         t[yc, ZM:] = jnp.zeros((8, LANES), F32)
 
     over(0, YM // 2, 4, restrict)
@@ -379,8 +386,7 @@
             q2[yc] = halve(yc)
 
         def coarse_diag(yc):
-            block, ym = yc // 2, 2 * (yc % 2)
-            t[yc, :ZM] = pair_sum(window[block, 1, ym] + window[block, 1, ym + 1])
+            t[yc, :ZM] = pair_sum(d1[2 * yc] + d1[2 * yc + 1])
 
         over(0, 16, 4, coarse_diag)
         total = zero2
@@ -569,8 +575,10 @@
             kept_fine = got[5:]
         left, right = both_ways(to_right, to_left, "fast")
         strip = jnp.concatenate([left, own, right], axis=2)
-        strip = jnp.broadcast_to(strip[None], (slow_count, *strip.shape))
-        strip = lax.all_to_all(strip, "slow", 0, 0, tiled=True)
+        strip = jnp.broadcast_to(strip[None], (slow_count // 2, *strip.shape))
+        chips = [[2 * n + core for n in range(slow_count // 2)] for core in range(2)]
+        mine = lax.all_to_all(strip, "slow", 0, 0, axis_index_groups=chips, tiled=True)
+        other = lax.ppermute(mine, "slow", [(n, n ^ 1) for n in range(slow_count)])
         outs = [(fast_count, LANES), middle, middle, (YPOST // 2, ZW, LANES)]
         scratch = [
             middle, (16, ZM + 8, LANES), (16 + 2 * PADL, 24, LANES), (16 + 2 * PADL, 24, LANES),
@@ -578,9 +586,9 @@
         ]
         if opening:
             outs += [middle, (YM, ZM, LANES), low_window, low_window, (24, LANES)]
-            given = (strip,)
+            given = (mine, other)
         else:
-            given = (strip, *kept_low)
+            given = (mine, other, *kept_low)
         got = call(functools.partial(coarse_kernel, opening), outs, scratch, (sweeps,), *given)
         part, e1, q1, e2 = got[:4]
         if opening:

time: 157 us -> 146 us (0.930)
  blocking collectives: 71.5 us -> 51.1 us
  starting transfers between devices: 27.3 us -> 34 us
  waiting for transfers between devices: 37.5 us -> 40.5 us
    all_to_all x2, blocking collectives: 41.2 us -> 21.1 us  [body(): lax.all_to_all(strip, 'slow', 0, 0, axis_index_groups=chips, tiled=True)]
    ppermute x0 -> x2, starting transfers between devices: none -> 7.51 us  [body(): other = lax.ppermute(mine, 'slow', [(n, n ^ 1) for n in range(slow_count)])]
    ppermute x0 -> x2, waiting for transfers between devices: none -> 2.98 us  [body(): other = lax.ppermute(mine, 'slow', [(n, n ^ 1) for n in range(slow_count)])]
  transfers between devices with their start and end apart: 12 -> 14, of which waited for: 8 -> 10; matrix products, arithmetic and copies ran while one was open for 0% -> 0% of each run, Pallas kernels for 0% -> 0%
where the time goes in v6:
time: 146 us
  blocking collectives  51.1 us (35%)
  waiting for transfers between devices  40.5 us (28%)
  starting transfers between devices  34 us (23%)
  Pallas kernels  19.8 us (14%)
    ppermute x12, waiting for transfers between devices, both_ways(): return (lax.ppermute(to_right, axis, up), lax.ppermute(to_left, axis, down))  37.5 us
    all_to_all x2, blocking collectives, body(): parts = lax.all_to_all(part, 'fast', 0, 0, tiled=True)  30 us
    ppermute x12, starting transfers between devices, both_ways(): return (lax.ppermute(to_right, axis, up), lax.ppermute(to_left, axis, down))  26.5 us
    all_to_all x2, blocking collectives, body(): lax.all_to_all(strip, 'slow', 0, 0, axis_index_groups=chips, tiled=True)  21.1 us
    pallas_call x7, Pallas kernels, call(): pl.pallas_call(kernel, out_shape=[pltpu.VMEM(s, F32) if kept else jax.Sha...  19.8 us
    ppermute x2, starting transfers between devices, body(): other = lax.ppermute(mine, 'slow', [(n, n ^ 1) for n in range(slow_count)])  7.51 us
    ppermute x2, waiting for transfers between devices, body(): other = lax.ppermute(mine, 'slow', [(n, n ^ 1) for n in range(slow_count)])  2.98 us
  transfers between devices with their start and end apart: 14, of which 10 were waited for; matrix products, arithmetic and copies ran while one was open for 0% of the time, Pallas kernels for 0%

profile of v6, /device:TPU:1, one launch (start us, length us, event | category | flops | bytes accessed | tf_op | source)
XLA Modules:
  0.0 146.0 jit_solution(906350761728450609)
XLA Ops:
  0.0 2.1 %shard_map.55 = (f32[76,8,128]{2,1,0:T(8,128)S(1)}, f32[2,2,8,8,128]{4,3,2,1,0:T(8,128)S(1)}, f32[2,2,8,8,128]{4,3,2,1,0:T(8,128)S(1)}) custom-call(f32[8,16,256]{2,1,0:T(8,128)} %observed.1, f32[8,16,256]{2,1,0:T(8,128)} %start.1, f32[8,16,256]{2,1,0:T(8,128)} %diagonal.1, f32[2,8,16,256]{3,2,1,0:T(8,128)} %noise.1), custom_call_target="tpu_custom_call" | custom-call | tf_op jit(solution)/shard_map/pallas_call | solution.py:516
  2.1 8.7 %collective-permute-start.1 = (f32[76,8,128]{2,1,0:T(8,128)S(1)}, f32[76,8,128]{2,1,0:T(8,128)S(1)}, u32[]{:S(2)}, u32[]{:S(2)}) collective-permute-start(f32[76,8,128]{2,1,0:T(8,128)S(1)} %get-tuple-element.35.refs_1_.refs_10_), channel_id=1, source_target_pairs={{1,0},{2,1},{3,2},{4,3},{5,4},{6,5},{7,6},{8,7},{9,8},{10,9},{11,1... | collective-permute-start | bytes 933896 | tf_op jit(solution)/shard_map/ppermute | solution.py:530
  10.8 0.0 collective-permute-start
  10.8 6.0 %collective-permute-done.1.refs_2_ = f32[76,8,128]{2,1,0:T(8,128)S(1)} collective-permute-done((f32[76,8,128]{2,1,0:T(8,128)S(1)}, f32[76,8,128]{2,1,0:T(8,128)S(1)}, u32[]{:S(2)}, u32[]{:S(2)}) %collective-permute-start.1) | collective-permute-done | bytes 311328 | tf_op jit(solution)/shard_map/ppermute | solution.py:530
  16.8 5.2 %collective-permute-done.refs_0_ = f32[76,8,128]{2,1,0:T(8,128)S(1)} collective-permute-done((f32[76,8,128]{2,1,0:T(8,128)S(1)}, f32[76,8,128]{2,1,0:T(8,128)S(1)}, u32[]{:S(2)}, u32[]{:S(2)}) %collective-permute-start) | collective-permute-done | bytes 311328 | tf_op jit(solution)/shard_map/ppermute | solution.py:530
  22.0 0.1 pad_maximum_fusion
  22.1 0.1 slice.24
  22.2 0.0 copy-start
  22.2 0.1 fusion
  22.3 1.9 %collective-permute-start.3 = (f32[3,64,8,128]{3,2,1,0:T(8,128)S(1)}, f32[3,64,8,128]{3,2,1,0:T(8,128)S(1)}, u32[]{:S(2)}, u32[]{:S(2)}) collective-permute-start(f32[3,64,8,128]{3,2,1,0:T(8,128)S(1)} %fusion), channel_id=1, source_target_pairs={{32,0},{64,32},{96,64},{128,96},{160,128},{192,160},{224,192},{0,2... | collective-permute-start | bytes 2359304 | tf_op jit(solution)/shard_map/ppermute | solution.py:530
  24.1 1.2 collective-permute-start.2
  25.3 9.9 %collective-permute-done.3.refs_4_ = f32[3,64,8,128]{3,2,1,0:T(8,128)S(1)} collective-permute-done((f32[3,64,8,128]{3,2,1,0:T(8,128)S(1)}, f32[3,64,8,128]{3,2,1,0:T(8,128)S(1)}, u32[]{:S(2)}, u32[]{:S(2)}) %collective-permute-start.3) | collective-permute-done | bytes 786464 | tf_op jit(solution)/shard_map/ppermute | solution.py:530
  35.3 0.0 collective-permute-done.2.refs_3_
  35.3 0.0 copy-done
  35.3 2.7 %shard_map.56 = (f32[2,4,16,128]{3,2,1,0:T(8,128)S(1)}, f32[2,4,8,128]{3,2,1,0:T(8,128)S(1)}, f32[2,4,16,128]{3,2,1,0:T(8,128)S(1)}, f32[2,2,16,24,128]{4,3,2,1,...) custom-call(s32[3]{0:T(128)S(1)} %copy-done, ...), custom_call_target="tpu_custom_call" | custom-call | tf_op jit(solution)/shard_map/pallas_call | solution.py:516
  38.0 0.1 collective-permute-start.4
  38.1 4.8 %collective-permute-start.5 = (f32[2,4,16,128]{3,2,1,0:T(8,128)S(1)}, f32[2,4,16,128]{3,2,1,0:T(8,128)S(1)}, u32[]{:S(2)}, u32[]{:S(2)}) collective-permute-start(f32[2,4,16,128]{3,2,1,0:T(8,128)S(1)} %get-tuple-element.38), channel_id=1, source_target_pairs={{1,0},{2,1},{3,2},{4,3},{5,4},{6,5},{7,6},{8,7},{9,8},{10,9},{11,1... | collective-permute-start | bytes 196616 | tf_op jit(solution)/shard_map/ppermute | solution.py:530
  42.8 1.6 %collective-permute-done.4 = f32[2,4,16,128]{3,2,1,0:T(8,128)S(1)} collective-permute-done((f32[2,4,16,128]{3,2,1,0:T(8,128)S(1)}, f32[2,4,16,128]{3,2,1,0:T(8,128)S(1)}, u32[]{:S(2)}, u32[]{:S(2)}) %collective-permute-start.4) | collective-permute-done | bytes 65568 | tf_op jit(solution)/shard_map/ppermute | solution.py:530
  44.5 0.0 collective-permute-done.5
  44.6 12.0 %all_to_all.32.refs_0_ = f32[4,2,4,40,128]{4,3,2,1,0:T(8,128)S(1)} all-to-all(f32[4,2,4,40,128]{4,3,2,1,0:T(8,128)S(1)} %broadcast_in_dim.6), channel_id=1, replica_groups={{0,64,128,192},{32,96,160,224},{1,65,129,193},{33,97,161,225},{2,66,130..., dimensions={0} | all-to-all | bytes 1310720 | tf_op jit(solution)/shard_map/all_to_all | solution.py:580
  56.6 3.5 %collective-permute-start.6 = (f32[4,2,4,40,128]{4,3,2,1,0:T(8,128)S(1)}, f32[4,2,4,40,128]{4,3,2,1,0:T(8,128)S(1)}, u32[]{:S(2)}, u32[]{:S(2)}) collective-permute-start(f32[4,2,4,40,128]{4,3,2,1,0:T(8,128)S(1)} %all_to_all.32.refs_0_), channel_id=1, source_target_pairs={{0,32},{32,0},{64,96},{96,64},{128,160},{160,128},{192,224},{224,1... | collective-permute-start | bytes 1966088 | tf_op jit(solution)/shard_map/ppermute | solution.py:581
  60.1 1.7 %collective-permute-done.6.refs_1_ = f32[4,2,4,40,128]{4,3,2,1,0:T(8,128)S(1)} collective-permute-done((f32[4,2,4,40,128]{4,3,2,1,0:T(8,128)S(1)}, f32[4,2,4,40,128]{4,3,2,1,0:T(8,128)S(1)}, u32[]{:S(2)}, u32[]{:S(2)}) %collective-permute-start.6) | collective-permute-done | bytes 655392 | tf_op jit(solution)/shard_map/ppermute | solution.py:581
  61.8 3.8 %shard_map.57 = (f32[32,128]{1,0:T(8,128)S(1)}, f32[48,40,128]{2,1,0:T(8,128)S(1)}, f32[48,40,128]{2,1,0:T(8,128)S(1)}, f32[8,24,128]{2,1,0:T(8,128)S(1)}, f32[4...) custom-call(s32[3]{0:T(128)S(1)} %copy-done, ...), custom_call_target="tpu_custom_call" | custom-call | tf_op jit(solution)/shard_map/pallas_call | solution.py:516
  65.6 14.8 %all_to_all.33 = f32[32,1,128]{2,1,0:T(1,128)S(1)} all-to-all(f32[32,1,128]{2,1,0:T(1,128)S(1)} %bitcast.30), channel_id=1, replica_groups=mesh['slow'=8,'fast'=32] {'fast'}, dimensions={0} | all-to-all | bytes 32768 | tf_op jit(solution)/shard_map/all_to_all | solution.py:596
  80.4 2.3 %shard_map.58 = (f32[44,8,128]{2,1,0:T(8,128)S(1)}, f32[2,2,8,8,128]{4,3,2,1,0:T(8,128)S(1)}) custom-call(s32[3]{0:T(128)S(1)} %copy-done, f32[32,128]{1,0:T(8,128)S(1)} %bitcast.28, f32[48,40,128]{2,1,0:T(8,128)S(1)} %get-tuple-element.40.refs_1_, f32[48,40,128]{2,1,0:T(8,128)S(1)} %get-tuple-element.41.refs_2_, ...), custom_call_target="tpu_custom_call" | custom-call | tf_op jit(solution)/shard_map/pallas_call | solution.py:516
  82.8 1.0 collective-permute-start.8
  83.8 0.5 collective-permute-start.7
  84.3 2.9 %collective-permute-done.8.refs_2_ = f32[44,8,128]{2,1,0:T(8,128)S(1)} collective-permute-done((f32[44,8,128]{2,1,0:T(8,128)S(1)}, f32[44,8,128]{2,1,0:T(8,128)S(1)}, u32[]{:S(2)}, u32[]{:S(2)}) %collective-permute-start.8) | collective-permute-done | bytes 180256 | tf_op jit(solution)/shard_map/ppermute | solution.py:530
  87.2 4.3 %collective-permute-done.7.refs_0_ = f32[44,8,128]{2,1,0:T(8,128)S(1)} collective-permute-done((f32[44,8,128]{2,1,0:T(8,128)S(1)}, f32[44,8,128]{2,1,0:T(8,128)S(1)}, u32[]{:S(2)}, u32[]{:S(2)}) %collective-permute-start.7) | collective-permute-done | bytes 180256 | tf_op jit(solution)/shard_map/ppermute | solution.py:530
  91.6 3.2 %collective-permute-start.10 = (f32[3,36,8,128]{3,2,1,0:T(8,128)S(1)}, f32[3,36,8,128]{3,2,1,0:T(8,128)S(1)}, u32[]{:S(2)}, u32[]{:S(2)}) collective-permute-start(f32[3,36,8,128]{3,2,1,0:T(8,128)S(1)} %fusion.1), channel_id=1, source_target_pairs={{32,0},{64,32},{96,64},{128,96},{160,128},{192,160},{224,192},{0,2... | collective-permute-start | bytes 1327112 | tf_op jit(solution)/shard_map/ppermute | solution.py:530
  94.8 0.2 collective-permute-start.9
  95.0 6.3 %collective-permute-done.10.refs_4_ = f32[3,36,8,128]{3,2,1,0:T(8,128)S(1)} collective-permute-done((f32[3,36,8,128]{3,2,1,0:T(8,128)S(1)}, f32[3,36,8,128]{3,2,1,0:T(8,128)S(1)}, u32[]{:S(2)}, u32[]{:S(2)}) %collective-permute-start.10) | collective-permute-done | bytes 442400 | tf_op jit(solution)/shard_map/ppermute | solution.py:530
  101.3 0.0 collective-permute-done.9.refs_3_
  101.3 2.7 %shard_map.59 = (f32[1,4,16,128]{3,2,1,0:T(8,128)S(1)}, f32[1,4,8,128]{3,2,1,0:T(8,128)S(1)}, f32[1,4,16,128]{3,2,1,0:T(8,128)S(1)}, f32[2,2,16,24,128]{4,3,2,1,0:T(8,128)S(1)}, f32[2,2,24,24,128]{4,3,2,1,0:T(8,128)S(1)}) custom-call(s32[3]{0:T(128)S(1)} %copy-done, f32[44,8,128]{2,1,0:T(8,128)S(1)} %collective-permute-done.7.refs_0_, ...), custom_call_target="tpu_custom_call" | custom-call | tf_op jit(solution)/shard_map/pallas_call | solution.py:516
  104.0 0.1 collective-permute-start.11
  104.1 4.8 %collective-permute-start.12 = (f32[1,4,16,128]{3,2,1,0:T(8,128)S(1)}, f32[1,4,16,128]{3,2,1,0:T(8,128)S(1)}, u32[]{:S(2)}, u32[]{:S(2)}) collective-permute-start(f32[1,4,16,128]{3,2,1,0:T(8,128)S(1)} %get-tuple-element.53), channel_id=1, source_target_pairs={{1,0},{2,1},{3,2},{4,3},{5,4},{6,5},{7,6},{8,7},{9,8},{10,9},{11,1... | collective-permute-start | bytes 98312 | tf_op jit(solution)/shard_map/ppermute | solution.py:530
  108.9 1.3 collective-permute-done.11
  110.2 0.0 collective-permute-done.12
  110.2 9.1 %all_to_all.34.refs_0_ = f32[4,1,4,40,128]{4,3,2,1,0:T(8,128)S(1)} all-to-all(f32[4,1,4,40,128]{4,3,2,1,0:T(8,128)S(1)} %broadcast_in_dim.16), channel_id=1, replica_groups={{0,64,128,192},{32,96,160,224},{1,65,129,193},{33,97,161,225},{2,66,130..., dimensions={0} | all-to-all | bytes 655360 | tf_op jit(solution)/shard_map/all_to_all | solution.py:580
  119.3 4.0 %collective-permute-start.13 = (f32[4,1,4,40,128]{4,3,2,1,0:T(8,128)S(1)}, f32[4,1,4,40,128]{4,3,2,1,0:T(8,128)S(1)}, u32[]{:S(2)}, u32[]{:S(2)}) collective-permute-start(f32[4,1,4,40,128]{4,3,2,1,0:T(8,128)S(1)} %all_to_all.34.refs_0_), channel_id=1, source_target_pairs={{0,32},{32,0},{64,96},{96,64},{128,160},{160,128},{192,224},{224,1... | collective-permute-start | bytes 983048 | tf_op jit(solution)/shard_map/ppermute | solution.py:581
  123.3 1.3 collective-permute-done.13.refs_1_
  124.5 3.1 %shard_map.60 = (f32[32,128]{1,0:T(8,128)S(1)}, f32[48,40,128]{2,1,0:T(8,128)S(1)}, f32[48,40,128]{2,1,0:T(8,128)S(1)}, f32[8,24,128]{2,1,0:T(8,128)S(1)}) custom-call(s32[3]{0:T(128)S(1)} %copy-done, f32[4,1,4,40,128]{4,3,2,1,0:T(8,128)S(1)} %all_to_all.34.refs_0_, f32[4,1,4,40,128]{4,3,2,1,0:T(8,128)S(1)} %collective-permute-done.13.refs_1_, ...), custom_call_target="tpu_custom_call" | custom-call | tf_op jit(solution)/shard_map/pallas_call | solution.py:516
  127.7 15.2 %all_to_all.35 = f32[32,1,128]{2,1,0:T(1,128)S(1)} all-to-all(f32[32,1,128]{2,1,0:T(1,128)S(1)} %bitcast.31), channel_id=1, replica_groups=mesh['slow'=8,'fast'=32] {'fast'}, dimensions={0} | all-to-all | bytes 32768 | tf_op jit(solution)/shard_map/all_to_all | solution.py:596
  142.9 3.1 %shard_map.61 = f32[8,16,256]{2,1,0:T(8,128)} custom-call(s32[3]{0:T(128)S(1)} %copy-done, f32[32,128]{1,0:T(8,128)S(1)} %bitcast.29, f32[48,40,128]{2,1,0:T(8,128)S(1)} %get-tuple-element.59.refs_1_, f32[48,40,128]{2,1,0:T(8,128)S(1)} %get-tuple-element.60.refs_2_, f32[48,40,128]{2,1,0:T(8,128)S(1)} %get-tuple-element.42.refs_3_.refs_2_, ...), custom_call_target="tpu_custom_call" | custom-call | tf_op jit(solution)/shard_map/pallas_call | solution.py:516
  (9 shorter events, 0.3 us)
Async XLA Ops:
  2.1 14.7 %collective-permute-start.1 = (f32[76,8,128]{2,1,0:T(8,128)S(1)}, f32[76,8,128]{2,1,0:T(8,128)S(1)}, u32[]{:S(2)}, u32[]{:S(2)}) collective-permute-start(f32[76,8,128]{2,1,0:T(8,128)S(1)} %get-tuple-element.35.refs_1_.refs_10_), channel_id=1, source_target_pairs={{1,0},{2,1},{3,2},{4,3},{5,4},{6,5},{7,6},{8,7},{9,8},{10,9},{11,1... | collective-permute-start | bytes 933896 | tf_op jit(solution)/shard_map/ppermute | solution.py:530
  10.8 11.2 %collective-permute-start = (f32[76,8,128]{2,1,0:T(8,128)S(1)}, f32[76,8,128]{2,1,0:T(8,128)S(1)}, u32[]{:S(2)}, u32[]{:S(2)}) collective-permute-start(f32[76,8,128]{2,1,0:T(8,128)S(1)} %get-tuple-element.35.refs_1_.refs_10_), channel_id=1, source_target_pairs={{0,1},{1,2},{2,3},{3,4},{4,5},{5,6},{6,7},{7,8},{8,9},{9,10},{10,1... | collective-permute-start | bytes 933896 | tf_op jit(solution)/shard_map/ppermute | solution.py:530
  22.2 13.1 %copy-start = (s32[3]{0:T(128)S(1)}, s32[3]{0:T(128)}, u32[]{:S(2)}) copy-start(s32[3]{0:T(128)} %sweeps.11) | copy-start | bytes 40
  22.3 13.0 %collective-permute-start.3 = (f32[3,64,8,128]{3,2,1,0:T(8,128)S(1)}, f32[3,64,8,128]{3,2,1,0:T(8,128)S(1)}, u32[]{:S(2)}, u32[]{:S(2)}) collective-permute-start(f32[3,64,8,128]{3,2,1,0:T(8,128)S(1)} %fusion), channel_id=1, source_target_pairs={{32,0},{64,32},{96,64},{128,96},{160,128},{192,160},{224,192},{0,2... | collective-permute-start | bytes 2359304 | tf_op jit(solution)/shard_map/ppermute | solution.py:530
  24.1 11.2 %collective-permute-start.2 = (f32[3,64,8,128]{3,2,1,0:T(8,128)S(1)}, f32[3,64,8,128]{3,2,1,0:T(8,128)S(1)}, u32[]{:S(2)}, u32[]{:S(2)}) collective-permute-start(f32[3,64,8,128]{3,2,1,0:T(8,128)S(1)} %slice.24), channel_id=1, source_target_pairs={{0,32},{32,64},{64,96},{96,128},{128,160},{160,192},{192,224},{224... | collective-permute-start | bytes 2359304 | tf_op jit(solution)/shard_map/ppermute | solution.py:530
  38.0 6.5 %collective-permute-start.4 = (f32[2,4,16,128]{3,2,1,0:T(8,128)S(1)}, f32[2,4,16,128]{3,2,1,0:T(8,128)S(1)}, u32[]{:S(2)}, u32[]{:S(2)}) collective-permute-start(f32[2,4,16,128]{3,2,1,0:T(8,128)S(1)} %get-tuple-element.36), channel_id=1, source_target_pairs={{0,1},{1,2},{2,3},{3,4},{4,5},{5,6},{6,7},{7,8},{8,9},{9,10},{10,1... | collective-permute-start | bytes 196616 | tf_op jit(solution)/shard_map/ppermute | solution.py:530
  38.1 6.4 %collective-permute-start.5 = (f32[2,4,16,128]{3,2,1,0:T(8,128)S(1)}, f32[2,4,16,128]{3,2,1,0:T(8,128)S(1)}, u32[]{:S(2)}, u32[]{:S(2)}) collective-permute-start(f32[2,4,16,128]{3,2,1,0:T(8,128)S(1)} %get-tuple-element.38), channel_id=1, source_target_pairs={{1,0},{2,1},{3,2},{4,3},{5,4},{6,5},{7,6},{8,7},{9,8},{10,9},{11,1... | collective-permute-start | bytes 196616 | tf_op jit(solution)/shard_map/ppermute | solution.py:530
  56.6 5.2 %collective-permute-start.6 = (f32[4,2,4,40,128]{4,3,2,1,0:T(8,128)S(1)}, f32[4,2,4,40,128]{4,3,2,1,0:T(8,128)S(1)}, u32[]{:S(2)}, u32[]{:S(2)}) collective-permute-start(f32[4,2,4,40,128]{4,3,2,1,0:T(8,128)S(1)} %all_to_all.32.refs_0_), channel_id=1, source_target_pairs={{0,32},{32,0},{64,96},{96,64},{128,160},{160,128},{192,224},{224,1... | collective-permute-start | bytes 1966088 | tf_op jit(solution)/shard_map/ppermute | solution.py:581
  82.8 4.4 %collective-permute-start.8 = (f32[44,8,128]{2,1,0:T(8,128)S(1)}, f32[44,8,128]{2,1,0:T(8,128)S(1)}, u32[]{:S(2)}, u32[]{:S(2)}) collective-permute-start(f32[44,8,128]{2,1,0:T(8,128)S(1)} %get-tuple-element.49.refs_1_), channel_id=1, source_target_pairs={{1,0},{2,1},{3,2},{4,3},{5,4},{6,5},{7,6},{8,7},{9,8},{10,9},{11,1... | collective-permute-start | bytes 540680 | tf_op jit(solution)/shard_map/ppermute | solution.py:530
  83.8 7.7 %collective-permute-start.7 = (f32[44,8,128]{2,1,0:T(8,128)S(1)}, f32[44,8,128]{2,1,0:T(8,128)S(1)}, u32[]{:S(2)}, u32[]{:S(2)}) collective-permute-start(f32[44,8,128]{2,1,0:T(8,128)S(1)} %get-tuple-element.49.refs_1_), channel_id=1, source_target_pairs={{0,1},{1,2},{2,3},{3,4},{4,5},{5,6},{6,7},{7,8},{8,9},{9,10},{10,1... | collective-permute-start | bytes 540680 | tf_op jit(solution)/shard_map/ppermute | solution.py:530
  91.6 9.7 %collective-permute-start.10 = (f32[3,36,8,128]{3,2,1,0:T(8,128)S(1)}, f32[3,36,8,128]{3,2,1,0:T(8,128)S(1)}, u32[]{:S(2)}, u32[]{:S(2)}) collective-permute-start(f32[3,36,8,128]{3,2,1,0:T(8,128)S(1)} %fusion.1), channel_id=1, source_target_pairs={{32,0},{64,32},{96,64},{128,96},{160,128},{192,160},{224,192},{0,2... | collective-permute-start | bytes 1327112 | tf_op jit(solution)/shard_map/ppermute | solution.py:530
  94.8 6.5 %collective-permute-start.9 = (f32[3,36,8,128]{3,2,1,0:T(8,128)S(1)}, f32[3,36,8,128]{3,2,1,0:T(8,128)S(1)}, u32[]{:S(2)}, u32[]{:S(2)}) collective-permute-start(f32[3,36,8,128]{3,2,1,0:T(8,128)S(1)} %slice.26), channel_id=1, source_target_pairs={{0,32},{32,64},{64,96},{96,128},{128,160},{160,192},{192,224},{224... | collective-permute-start | bytes 1327112 | tf_op jit(solution)/shard_map/ppermute | solution.py:530
  104.0 6.2 %collective-permute-start.11 = (f32[1,4,16,128]{3,2,1,0:T(8,128)S(1)}, f32[1,4,16,128]{3,2,1,0:T(8,128)S(1)}, u32[]{:S(2)}, u32[]{:S(2)}) collective-permute-start(f32[1,4,16,128]{3,2,1,0:T(8,128)S(1)} %get-tuple-element.51), channel_id=1, source_target_pairs={{0,1},{1,2},{2,3},{3,4},{4,5},{5,6},{6,7},{7,8},{8,9},{9,10},{10,1... | collective-permute-start | bytes 98312 | tf_op jit(solution)/shard_map/ppermute | solution.py:530
  104.1 6.1 %collective-permute-start.12 = (f32[1,4,16,128]{3,2,1,0:T(8,128)S(1)}, f32[1,4,16,128]{3,2,1,0:T(8,128)S(1)}, u32[]{:S(2)}, u32[]{:S(2)}) collective-permute-start(f32[1,4,16,128]{3,2,1,0:T(8,128)S(1)} %get-tuple-element.53), channel_id=1, source_target_pairs={{1,0},{2,1},{3,2},{4,3},{5,4},{6,5},{7,6},{8,7},{9,8},{10,9},{11,1... | collective-permute-start | bytes 98312 | tf_op jit(solution)/shard_map/ppermute | solution.py:530
  119.3 5.3 %collective-permute-start.13 = (f32[4,1,4,40,128]{4,3,2,1,0:T(8,128)S(1)}, f32[4,1,4,40,128]{4,3,2,1,0:T(8,128)S(1)}, u32[]{:S(2)}, u32[]{:S(2)}) collective-permute-start(f32[4,1,4,40,128]{4,3,2,1,0:T(8,128)S(1)} %all_to_all.34.refs_0_), channel_id=1, source_target_pairs={{0,32},{32,0},{64,96},{96,64},{128,160},{160,128},{192,224},{224,1... | collective-permute-start | bytes 983048 | tf_op jit(solution)/shard_map/ppermute | solution.py:581

commit v7 on v6

--- a/solution.py
+++ b/solution.py
@@ -16,6 +16,7 @@
 ZM, YM = 40, 32
 YPOST = 16
 PADM, PADL = 8, 4
+FINE, FLAT = 24, 32
 PARITIES = ((0, 0), (0, 1), (1, 0), (1, 1))
 
 
@@ -40,8 +41,10 @@
 
 
 def over(low, high, chunk, one):
+    chunk = min(chunk, high - low)
     turns, rest = divmod(high - low, chunk)
-    assert rest == 0
+    for n in range(rest):
+        one(high - rest + n)
     if turns == 1:
         for n in range(chunk):
             one(low + n)
@@ -157,34 +160,41 @@
         s[(*p, YB + 1)] = jnp.zeros((ZB, LANES), F32)
 
 
-def split_kernel(observed, start, diagonal, noise, pack, field, later, a, b, c, d, halves, s, g, linear, sems):
-    copies = [
-        pltpu.make_async_copy(source, target, sems.at[n])
-        for n, (source, target) in enumerate(((start, a), (diagonal, b), (observed, c), (noise, d)))
-    ]
+def split_by_parity(value, matrix, halves, *outs):
+    both = exact_dot(value.reshape(YB * 2 * ZB, 2 * LANES), matrix)
+    for px in range(2):
+        halves[px] = both[:, px * LANES : (px + 1) * LANES]
+    for pz, px in PARITIES:
+        part = halves[px, pl.ds(pz, YB * ZB, stride=2), :].reshape(YB, ZB, LANES)
+        for out in outs:
+            out[pz, px] = part
+
+
+def copies_of(pairs, sems):
+    copies = [pltpu.make_async_copy(*pair, sems.at[n]) for n, pair in enumerate(pairs)]
     for copy in copies:
         copy.start()
+    return copies
+
+
+def pack_kernel(observed, start, diagonal, noise, pack, field, a, b, c, d, halves, s, g, linear, sems):
+    copies = copies_of(((start, a), (diagonal, b), (observed, c), (noise.at[0], d)), sems)
     matrix = parity_matrix(False)
     zero_edges(s)
-
-    def split(n, value, *outs):
-        both = exact_dot(value.reshape(YB * 2 * ZB, 2 * LANES), matrix)
-        for px in range(2):
-            halves[n, px] = both[:, px * LANES : (px + 1) * LANES]
-        for pz, px in PARITIES:
-            part = halves[n, px, pl.ds(pz, YB * ZB, stride=2), :].reshape(YB, ZB, LANES)
-            for out in outs:
-                out[pz, px] = part
-
     copies[0].wait()
-    split(0, a[...], field, s.at[:, :, 1 : YB + 1])
+    split_by_parity(a[...], matrix, halves.at[0], field, s.at[:, :, 1 : YB + 1])
     copies[1].wait()
-    split(1, b[...], g)
+    split_by_parity(b[...], matrix, halves.at[1], g)
     copies[2].wait()
     copies[3].wait()
-    split(2, c[...] + 2.0 * d[0], linear)
+    split_by_parity(c[...] + 2.0 * d[...], matrix, halves.at[2], linear)
     write_pack(s, lambda p, y: linear[(*p, y)], lambda p, y: g[(*p, y)], pack, 8, lane_iota(ZB))
-    split(3, c[...] + 2.0 * d[1], later)
+
+
+def later_kernel(observed, noise, later, c, d, halves, sems):
+    for copy in copies_of(((observed, c), (noise.at[1], d)), sems):
+        copy.wait()
+    split_by_parity(c[...] + 2.0 * d[...], parity_matrix(False), halves, later)
 
 
 def inside(axis, which):
@@ -213,24 +223,40 @@
     def tile(yb, zb, n):
         if yb == 1:
             return across[zb].at[n]
-        if yb == 0:
-            return low.at[zb, n - (4 + each)]
-        return high.at[zb, n]
+        rows, y = (7, (n - 4) // each) if zb == 1 else (6, (n - 4) // each)
+        base = (0, 6 * each + 6, 13 * each + 14)[zb]
+        if n < 4:
+            at = n
+        elif y < YB:
+            left_out_rows = YB - rows if yb == 0 else 0
+            if y < left_out_rows or y >= left_out_rows + rows:
+                return None
+            at = n - (4 + left_out_rows * each) + (0 if yb == 0 else 4)
+        else:
+            at = n - (4 + 8 * each) + rows * each
+        return (low if yb == 0 else high).at[base + at]
 
     def z_face(yb, zb, which, px, y):
-        n = 8 + 8 * each + 2 * which + px
-        if yb == 2:
-            n = 4 + 7 * each + 2 * which + px
-        return tile(yb, zb, n)[pl.ds(y, 1), :]
+        n = 2 * which + px
+        if yb == 1:
+            face = across[zb].at[8 + 8 * each + n]
+        else:
+            base = (6 * each + 4 - 2, 13 * each + 10, 19 * each + 18)[zb]
+            face = (low if yb == 0 else high).at[base + n]
+        return face[pl.ds(y, 1), :]
 
     def wide(yb, n):
-        return jnp.concatenate([tile(yb, zb, n)[...] for zb in range(3)], axis=0)
+        return jnp.concatenate([load(yb, zb, n) for zb in range(3)], axis=0)
+
+    def load(yb, zb, n):
+        at = tile(yb, zb, n)
+        return jnp.zeros((ZB, LANES), F32) if at is None else at[...]
 
     def right_side(yb, y):
         row = yb * YB + y
         for p in PARITIES:
             pz, px = p
-            tiles = [tile(yb, zb, 4 + each * y + tile_of(p))[...] for zb in range(3)]
+            tiles = [load(yb, zb, 4 + each * y + tile_of(p)) for zb in range(3)]
             if pz == 1:
                 edge = tile_rows == ZB - 1
                 tiles[0] = tiles[0] + jnp.where(edge, z_face(yb, 1, 0, px, y), 0.0)
@@ -258,7 +284,7 @@
             b[(*p, row)] = start
 
     for yb in range(3):
-        over(1, YB - 1, 6, functools.partial(right_side, yb))
+        over(1, YB - 1, YB, functools.partial(right_side, yb))
     right_side(0, YB - 1)
     right_side(1, 0)
     right_side(1, YB - 1)
@@ -266,13 +292,13 @@
 
     @pl.when(sweeps[0] >= 4)
     def _():
-        fine_sweep(a, b, q, k, 2, 22, 10, lanes)
+        fine_sweep(a, b, q, k, 2, 22, FINE, lanes)
 
     @pl.when(sweeps[0] >= 3)
     def _():
-        fine_sweep(b, a, q, k, 3, 21, 9, lanes)
-
-    fine_sweep(a, epre, q, k, 4, 20, 8, lanes, shift=4)
+        fine_sweep(b, a, q, k, 3, 21, FINE, lanes)
+
+    fine_sweep(a, epre, q, k, 4, 20, FINE, lanes, shift=4)
     zero = jnp.zeros((ZW, LANES), F32)
 
     def restrict(ym):
@@ -307,9 +333,6 @@
     fast = lax.axis_index("fast")
     slow = lax.axis_index("slow")
 
-    def window(chip, core, n, ym):
-        return jnp.where((slow & 1) == core, mine[chip, n, ym], other[chip, n, ym])
-
     lanes = lane_iota(ZM)
     even = (lanes & 1) == 0
     zrow = row_iota(ZM) + (fast * ZB - 2 * ZB)
@@ -322,13 +345,15 @@
         if first:
             k1[n] = zero
 
+    here_first = slow & 1
+
     def opening(chip):
-        for core in range(2):
+        for gathered, core in ((mine, here_first), (other, 1 - here_first)):
             for ym in range(4):
                 y = chip * 8 + core * 4 + ym
-                rhs = window(chip, core, 0, ym)
+                rhs = gathered[chip, 0, ym]
                 if first:
-                    diag = window(chip, core, 1, ym)
+                    diag = gathered[chip, 1, ym]
                     d1[y] = diag
                     full = diag + 1.5
                     gain = (OMEGA / full) * mask
@@ -340,18 +365,18 @@
                 va[PADM + y] = start
                 e1[PADM + y] = start
 
-    over(0, YM // 8, 1, opening)
+    over(0, YM // 8, 4, opening)
     of_q1, of_k1 = (lambda y: q1[y]), (lambda y: k1[y])
 
     @pl.when(sweeps[1] >= 4)
     def _():
-        flat_sweep(va, e1, of_q1, of_k1, PADM, PADM + YM, 8, lanes, 1)
+        flat_sweep(va, e1, of_q1, of_k1, PADM, PADM + YM, FLAT, lanes, 1)
 
     @pl.when(sweeps[1] >= 3)
     def _():
-        flat_sweep(e1, va, of_q1, of_k1, PADM, PADM + YM, 8, lanes, 1)
-
-    flat_sweep(va, e1, of_q1, of_k1, PADM, PADM + YM, 8, lanes, 1)
+        flat_sweep(e1, va, of_q1, of_k1, PADM, PADM + YM, FLAT, lanes, 1)
+
+    flat_sweep(va, e1, of_q1, of_k1, PADM, PADM + YM, FLAT, lanes, 1)
 
     def pair_sum(value):
         return value + jnp.where(even, pltpu.roll(value, LANES - 1, 1), pltpu.roll(value, 1, 1))
@@ -365,7 +390,7 @@
         t[yc, :ZM] = pair_sum(total * (1.0 / OMEGA))
         t[yc, ZM:] = jnp.zeros((8, LANES), F32)
 
-    over(0, YM // 2, 4, restrict)
+    over(0, YM // 2, 16, restrict)
     lanes2 = lane_iota(24)
     rows2 = row_iota(24)
     zrow2 = rows2 + (fast * 4 - 8)
@@ -412,13 +437,13 @@
 
     @pl.when(sweeps[2] >= 4)
     def _():
-        flat_sweep(wa, wb, of_q2, of_k2, PADL, PADL + 16, 16, lanes2, 2)
+        flat_sweep(wa, wb, of_q2, of_k2, PADL, PADL + 16, FLAT, lanes2, 2)
 
     @pl.when(sweeps[2] >= 3)
     def _():
-        flat_sweep(wb, wa, of_q2, of_k2, PADL, PADL + 16, 16, lanes2, 2)
-
-    flat_sweep(wa, wb, of_q2, of_k2, PADL, PADL + 16, 16, lanes2, 2)
+        flat_sweep(wb, wa, of_q2, of_k2, PADL, PADL + 16, FLAT, lanes2, 2)
+
+    flat_sweep(wa, wb, of_q2, of_k2, PADL, PADL + 16, FLAT, lanes2, 2)
     total = zero2
     for yc in range(16):
         here, beside = flat_neighbours(wb, yc + PADL, lanes2, 2)
@@ -461,14 +486,14 @@
 
     @pl.when(sweeps[1] >= 4)
     def _():
-        flat_sweep(vb, va, of_q1, of_k1, 1, 15, 14, lanes, 1)
+        flat_sweep(vb, va, of_q1, of_k1, 1, 15, FLAT, lanes, 1)
 
     @pl.when(sweeps[1] >= 3)
     def _():
-        flat_sweep(va, vb, of_q1, of_k1, 2, 14, 12, lanes, 1)
-
-    flat_sweep(vb, va, of_q1, of_k1, 3, 13, 10, lanes, 1)
-    flat_sweep(va, vb, of_q1, of_k1, 4, 12, 8, lanes, 1)
+        flat_sweep(va, vb, of_q1, of_k1, 2, 14, FLAT, lanes, 1)
+
+    flat_sweep(vb, va, of_q1, of_k1, 3, 13, FLAT, lanes, 1)
+    flat_sweep(va, vb, of_q1, of_k1, 4, 12, FLAT, lanes, 1)
 
     def raise_fine(ym):
         value = vb[ym + 4]
@@ -479,18 +504,18 @@
                 a[(*p, y)] = raised
                 b[(*p, y)] = raised
 
-    over(0, YPOST // 2, 4, raise_fine)
+    over(0, YPOST // 2, 8, raise_fine)
 
     @pl.when(sweeps[0] >= 4)
     def _():
-        fine_sweep(b, a, q, k, 1, 15, 7, lanes, offset=4)
+        fine_sweep(b, a, q, k, 1, 15, FINE, lanes, offset=4)
 
     @pl.when(sweeps[0] >= 3)
     def _():
-        fine_sweep(a, b, q, k, 2, 14, 6, lanes, offset=4)
-
-    fine_sweep(b, a, q, k, 3, 13, 10, lanes, offset=4)
-    fine_sweep(a, b, q, k, 4, 12, 8, lanes, offset=4)
+        fine_sweep(a, b, q, k, 2, 14, FINE, lanes, offset=4)
+
+    fine_sweep(b, a, q, k, 3, 13, FINE, lanes, offset=4)
+    fine_sweep(a, b, q, k, 4, 12, FINE, lanes, offset=4)
     if not last:
         zero_edges(s)
     for pz, px in PARITIES:
@@ -532,10 +557,16 @@
 
 def window_of(pack, each):
     left, right = both_ways(pack, pack, "fast")
-    strip = jnp.stack([left, pack, right])
-    upward = strip[:, 4 + each :]
-    downward = jnp.concatenate([strip[:, : 4 + 7 * each], strip[:, 8 + 8 * each :]], axis=1)
-    low, high = both_ways(upward, downward, "slow")
+    faces = 8 + 8 * each
+    upward = [
+        left[4 + 2 * each : faces], left[faces + 2 :], pack[4 + each :],
+        right[4 + 2 * each : faces], right[faces : faces + 2],
+    ]
+    downward = [
+        left[: 4 + 6 * each], left[faces + 2 :], pack[: 4 + 7 * each], pack[faces:],
+        right[: 4 + 6 * each], right[faces : faces + 2],
+    ]
+    low, high = both_ways(jnp.concatenate(upward), jnp.concatenate(downward), "slow")
     return left, pack, right, low, high
 
 
@@ -550,13 +581,15 @@
     fast_count, slow_count = lax.axis_size("fast"), lax.axis_size("slow")
     first, second, third = YB * slow_count // 4, 2 * ZB * fast_count // 4, 2 * LANES // 4
     faces = 2.0 * (first * second + first * third + second * third)
-    pack, field, later = call(
-        split_kernel, [(pack_tiles(8), ZB, LANES), block, block],
-        [
-            natural, natural, natural, (2, *natural), (4, 2, YB * 2 * ZB, LANES),
-            edged, block, block, pltpu.SemaphoreType.DMA((4,)),
-        ],
+    lines = (2, YB * 2 * ZB, LANES)
+    pack, field = call(
+        pack_kernel, [(pack_tiles(8), ZB, LANES), block],
+        [*[natural] * 4, (3, *lines), edged, block, block, pltpu.SemaphoreType.DMA((4,))],
         (), observed, start_field, diagonal, noise, space=pltpu.HBM,
+    )
+    (later,) = call(
+        later_kernel, [block], [natural, natural, lines, pltpu.SemaphoreType.DMA((2,))],
+        (), observed, noise, space=pltpu.HBM,
     )
     own_pack = pack
     kept_fine = kept_low = None
@@ -566,6 +599,7 @@
         given = window_of(pack, 8 if opening else 4)
         outs = [(count, 4, 16, LANES), (count, 4, 8, LANES), (count, 4, 16, LANES), post, whole]
         if opening:
+            *given, later = lax.optimization_barrier((*given, later))
             outs += [whole, (2, 2, YB, ZW, LANES)]
         else:
             given = (*given, *kept_fine)

time: 146 us -> 143 us (0.979)
  waiting for transfers between devices: 40.5 us -> 32.9 us
  blocking collectives: 51.1 us -> 57.6 us
  starting transfers between devices: 34 us -> 31.3 us
    ppermute x12, waiting for transfers between devices: 37.5 us -> 29.9 us  [both_ways(): return (lax.ppermute(to_right, axis, up), lax.ppermute(to_left, axis, down))]
    ppermute x2, starting transfers between devices: 7.51 us -> 1.88 us  [body(): other = lax.ppermute(mine, 'slow', [(n, n ^ 1) for n in range(slow_count)])]
    all_to_all x2, blocking collectives: 21.1 us -> 26 us  [body(): lax.all_to_all(strip, 'slow', 0, 0, axis_index_groups=chips, tiled=True)]
    ppermute x12, starting transfers between devices: 26.5 us -> 29.5 us  [both_ways(): return (lax.ppermute(to_right, axis, up), lax.ppermute(to_left, axis, down))]
    all_to_all x2, blocking collectives: 30 us -> 31.7 us  [body(): parts = lax.all_to_all(part, 'fast', 0, 0, tiled=True)]
    pallas_call x7 -> x8, Pallas kernels: 19.8 us -> 19.8 us  [call(): pl.pallas_call(kernel, out_shape=[pltpu.VMEM(s, F32) if kept else jax.Sha...]
  transfers between devices with their start and end apart: 14 -> 14, of which waited for: 10 -> 10; matrix products, arithmetic and copies ran while one was open for 0% -> 0% of each run, Pallas kernels for 0% -> 1%
where the time goes in v7:
time: 143 us; the launch traced here: 142 us
  blocking collectives  57.6 us (40%)
  waiting for transfers between devices  32.9 us (23%)
  starting transfers between devices  31.3 us (22%)
  Pallas kernels  19.8 us (14%)
    all_to_all x2, blocking collectives, body(): parts = lax.all_to_all(part, 'fast', 0, 0, tiled=True)  31.7 us
    ppermute x12, waiting for transfers between devices, both_ways(): return (lax.ppermute(to_right, axis, up), lax.ppermute(to_left, axis, down))  29.9 us
    ppermute x12, starting transfers between devices, both_ways(): return (lax.ppermute(to_right, axis, up), lax.ppermute(to_left, axis, down))  29.5 us
    all_to_all x2, blocking collectives, body(): lax.all_to_all(strip, 'slow', 0, 0, axis_index_groups=chips, tiled=True)  26 us
    pallas_call x8, Pallas kernels, call(): pl.pallas_call(kernel, out_shape=[pltpu.VMEM(s, F32) if kept else jax.Sha...  19.8 us
    ppermute x2, waiting for transfers between devices, body(): other = lax.ppermute(mine, 'slow', [(n, n ^ 1) for n in range(slow_count)])  2.98 us
  transfers between devices with their start and end apart: 14, of which 10 were waited for; matrix products, arithmetic and copies ran while one was open for 0% of the time, Pallas kernels for 1%

profile of v7, /device:TPU:1, one launch (start us, length us, event | category | flops | bytes accessed | tf_op | source)
XLA Modules:
  0.0 142.2 jit_solution(748480713725533918)
XLA Ops:
  0.0 2.0 %shard_map.55 = (f32[76,8,128]{2,1,0:T(8,128)S(1)}, f32[2,2,8,8,128]{4,3,2,1,0:T(8,128)S(1)}) custom-call(f32[8,16,256]{2,1,0:T(8,128)} %observed.3, f32[8,16,256]{2,1,0:T(8,128)} %start.1, f32[8,16,256]{2,1,0:T(8,128)} %diagonal.1, f32[2,8,16,256]{3,2,1,0:T(8,128)} %noise.3), custom_call_target="tpu_custom_call" | custom-call | tf_op jit(solution)/shard_map/pallas_call | solution.py:541
  2.0 2.1 %collective-permute-start = (f32[76,8,128]{2,1,0:T(8,128)S(1)}, f32[76,8,128]{2,1,0:T(8,128)S(1)}, u32[]{:S(2)}, u32[]{:S(2)}) collective-permute-start(f32[76,8,128]{2,1,0:T(8,128)S(1)} %get-tuple-element.42.refs_1_.refs_10_), channel_id=1, source_target_pairs={{0,1},{1,2},{2,3},{3,4},{4,5},{5,6},{6,7},{7,8},{8,9},{9,10},{10,1... | collective-permute-start | bytes 933896 | tf_op jit(solution)/shard_map/ppermute | solution.py:555
  4.1 6.6 %collective-permute-start.1 = (f32[76,8,128]{2,1,0:T(8,128)S(1)}, f32[76,8,128]{2,1,0:T(8,128)S(1)}, u32[]{:S(2)}, u32[]{:S(2)}) collective-permute-start(f32[76,8,128]{2,1,0:T(8,128)S(1)} %get-tuple-element.42.refs_1_.refs_10_), channel_id=1, source_target_pairs={{1,0},{2,1},{3,2},{4,3},{5,4},{6,5},{7,6},{8,7},{9,8},{10,9},{11,1... | collective-permute-start | bytes 933896 | tf_op jit(solution)/shard_map/ppermute | solution.py:555
  10.8 7.0 %collective-permute-done.refs_0_ = f32[76,8,128]{2,1,0:T(8,128)S(1)} collective-permute-done((f32[76,8,128]{2,1,0:T(8,128)S(1)}, f32[76,8,128]{2,1,0:T(8,128)S(1)}, u32[]{:S(2)}, u32[]{:S(2)}) %collective-permute-start) | collective-permute-done | bytes 311328 | tf_op jit(solution)/shard_map/ppermute | solution.py:555
  17.8 0.0 collective-permute-done.1.refs_2_
  17.8 0.0 copy-start
  17.9 2.4 %collective-permute-start.2 = (f32[172,8,128]{2,1,0:T(8,128)S(1)}, f32[172,8,128]{2,1,0:T(8,128)S(1)}, u32[]{:S(2)}, u32[]{:S(2)}) collective-permute-start(f32[172,8,128]{2,1,0:T(8,128)S(1)} %pad_maximum_fusion), channel_id=1, source_target_pairs={{0,32},{32,64},{64,96},{96,128},{128,160},{160,192},{192,224},{224... | collective-permute-start | bytes 2113544 | tf_op jit(solution)/shard_map/ppermute | solution.py:555
  20.4 0.0 collective-permute-start.3
  20.4 1.3 shard_map.56.refs_9_
  21.7 6.7 %collective-permute-done.2.refs_3_ = f32[172,8,128]{2,1,0:T(8,128)S(1)} collective-permute-done((f32[172,8,128]{2,1,0:T(8,128)S(1)}, f32[172,8,128]{2,1,0:T(8,128)S(1)}, u32[]{:S(2)}, u32[]{:S(2)}) %collective-permute-start.2) | collective-permute-done | bytes 704544 | tf_op jit(solution)/shard_map/ppermute | solution.py:555
  28.4 2.5 %collective-permute-done.3.refs_4_ = f32[172,8,128]{2,1,0:T(8,128)S(1)} collective-permute-done((f32[172,8,128]{2,1,0:T(8,128)S(1)}, f32[172,8,128]{2,1,0:T(8,128)S(1)}, u32[]{:S(2)}, u32[]{:S(2)}) %collective-permute-start.3) | collective-permute-done | bytes 704544 | tf_op jit(solution)/shard_map/ppermute | solution.py:555
  30.9 0.0 copy-done
  30.9 1.5 %shard_map.57 = (f32[2,4,16,128]{3,2,1,0:T(8,128)S(1)}, f32[2,4,8,128]{3,2,1,0:T(8,128)S(1)}, f32[2,4,16,128]{3,2,1,0:T(8,128)S(1)}, f32[2,2,16,24,128]{4,3,2,1,...) custom-call(s32[3]{0:T(128)S(1)} %copy-done, ...), custom_call_target="tpu_custom_call" | custom-call | tf_op jit(solution)/shard_map/pallas_call | solution.py:541
  32.5 0.1 collective-permute-start.4
  32.6 4.8 %collective-permute-start.5 = (f32[2,4,16,128]{3,2,1,0:T(8,128)S(1)}, f32[2,4,16,128]{3,2,1,0:T(8,128)S(1)}, u32[]{:S(2)}, u32[]{:S(2)}) collective-permute-start(f32[2,4,16,128]{3,2,1,0:T(8,128)S(1)} %get-tuple-element.48), channel_id=1, source_target_pairs={{1,0},{2,1},{3,2},{4,3},{5,4},{6,5},{7,6},{8,7},{9,8},{10,9},{11,1... | collective-permute-start | bytes 196616 | tf_op jit(solution)/shard_map/ppermute | solution.py:555
  37.4 2.2 %collective-permute-done.4 = f32[2,4,16,128]{3,2,1,0:T(8,128)S(1)} collective-permute-done((f32[2,4,16,128]{3,2,1,0:T(8,128)S(1)}, f32[2,4,16,128]{3,2,1,0:T(8,128)S(1)}, u32[]{:S(2)}, u32[]{:S(2)}) %collective-permute-start.4) | collective-permute-done | bytes 65568 | tf_op jit(solution)/shard_map/ppermute | solution.py:555
  39.6 0.0 collective-permute-done.5
  39.7 13.7 %all_to_all.32.refs_0_ = f32[4,2,4,40,128]{4,3,2,1,0:T(8,128)S(1)} all-to-all(f32[4,2,4,40,128]{4,3,2,1,0:T(8,128)S(1)} %broadcast_in_dim.6), channel_id=1, replica_groups={{0,64,128,192},{32,96,160,224},{1,65,129,193},{33,97,161,225},{2,66,130..., dimensions={0} | all-to-all | bytes 1310720 | tf_op jit(solution)/shard_map/all_to_all | solution.py:614
  53.4 1.4 %collective-permute-start.6 = (f32[4,2,4,40,128]{4,3,2,1,0:T(8,128)S(1)}, f32[4,2,4,40,128]{4,3,2,1,0:T(8,128)S(1)}, u32[]{:S(2)}, u32[]{:S(2)}) collective-permute-start(f32[4,2,4,40,128]{4,3,2,1,0:T(8,128)S(1)} %all_to_all.32.refs_0_), channel_id=1, source_target_pairs={{0,32},{32,0},{64,96},{96,64},{128,160},{160,128},{192,224},{224,1... | collective-permute-start | bytes 1966088 | tf_op jit(solution)/shard_map/ppermute | solution.py:615
  54.8 1.7 %collective-permute-done.6.refs_1_ = f32[4,2,4,40,128]{4,3,2,1,0:T(8,128)S(1)} collective-permute-done((f32[4,2,4,40,128]{4,3,2,1,0:T(8,128)S(1)}, f32[4,2,4,40,128]{4,3,2,1,0:T(8,128)S(1)}, u32[]{:S(2)}, u32[]{:S(2)}) %collective-permute-start.6) | collective-permute-done | bytes 655392 | tf_op jit(solution)/shard_map/ppermute | solution.py:615
  56.6 4.7 %shard_map.58 = (f32[32,128]{1,0:T(8,128)S(1)}, f32[48,40,128]{2,1,0:T(8,128)S(1)}, f32[48,40,128]{2,1,0:T(8,128)S(1)}, f32[8,24,128]{2,1,0:T(8,128)S(1)}, f32[4...) custom-call(s32[3]{0:T(128)S(1)} %copy-done, ...), custom_call_target="tpu_custom_call" | custom-call | tf_op jit(solution)/shard_map/pallas_call | solution.py:541
  61.3 16.7 %all_to_all.33 = f32[32,1,128]{2,1,0:T(1,128)S(1)} all-to-all(f32[32,1,128]{2,1,0:T(1,128)S(1)} %bitcast.12), channel_id=1, replica_groups=mesh['slow'=8,'fast'=32] {'fast'}, dimensions={0} | all-to-all | bytes 32768 | tf_op jit(solution)/shard_map/all_to_all | solution.py:630
  78.0 2.1 %shard_map.59 = (f32[44,8,128]{2,1,0:T(8,128)S(1)}, f32[2,2,8,8,128]{4,3,2,1,0:T(8,128)S(1)}) custom-call(s32[3]{0:T(128)S(1)} %copy-done, f32[32,128]{1,0:T(8,128)S(1)} %bitcast.10, f32[48,40,128]{2,1,0:T(8,128)S(1)} %get-tuple-element.50.refs_1_, f32[48,40,128]{2,1,0:T(8,128)S(1)} %get-tuple-element.51.refs_2_, ...), custom_call_target="tpu_custom_call" | custom-call | tf_op jit(solution)/shard_map/pallas_call | solution.py:541
  80.1 0.4 collective-permute-start.7
  80.5 4.6 %collective-permute-start.8 = (f32[44,8,128]{2,1,0:T(8,128)S(1)}, f32[44,8,128]{2,1,0:T(8,128)S(1)}, u32[]{:S(2)}, u32[]{:S(2)}) collective-permute-start(f32[44,8,128]{2,1,0:T(8,128)S(1)} %get-tuple-element.59.refs_1_), channel_id=1, source_target_pairs={{1,0},{2,1},{3,2},{4,3},{5,4},{6,5},{7,6},{8,7},{9,8},{10,9},{11,1... | collective-permute-start | bytes 540680 | tf_op jit(solution)/shard_map/ppermute | solution.py:555
  85.1 2.8 %collective-permute-done.7.refs_0_ = f32[44,8,128]{2,1,0:T(8,128)S(1)} collective-permute-done((f32[44,8,128]{2,1,0:T(8,128)S(1)}, f32[44,8,128]{2,1,0:T(8,128)S(1)}, u32[]{:S(2)}, u32[]{:S(2)}) %collective-permute-start.7) | collective-permute-done | bytes 180256 | tf_op jit(solution)/shard_map/ppermute | solution.py:555
  87.9 0.0 collective-permute-done.8.refs_2_
  88.0 3.1 %collective-permute-start.9 = (f32[96,8,128]{2,1,0:T(8,128)S(1)}, f32[96,8,128]{2,1,0:T(8,128)S(1)}, u32[]{:S(2)}, u32[]{:S(2)}) collective-permute-start(f32[96,8,128]{2,1,0:T(8,128)S(1)} %pad_maximum_fusion.1), channel_id=1, source_target_pairs={{0,32},{32,64},{64,96},{96,128},{128,160},{160,192},{192,224},{224... | collective-permute-start | bytes 1179656 | tf_op jit(solution)/shard_map/ppermute | solution.py:555
  91.1 0.0 collective-permute-start.10
  91.2 4.7 %collective-permute-done.9.refs_3_ = f32[96,8,128]{2,1,0:T(8,128)S(1)} collective-permute-done((f32[96,8,128]{2,1,0:T(8,128)S(1)}, f32[96,8,128]{2,1,0:T(8,128)S(1)}, u32[]{:S(2)}, u32[]{:S(2)}) %collective-permute-start.9) | collective-permute-done | bytes 393248 | tf_op jit(solution)/shard_map/ppermute | solution.py:555
  95.8 2.8 %collective-permute-done.10.refs_4_ = f32[96,8,128]{2,1,0:T(8,128)S(1)} collective-permute-done((f32[96,8,128]{2,1,0:T(8,128)S(1)}, f32[96,8,128]{2,1,0:T(8,128)S(1)}, u32[]{:S(2)}, u32[]{:S(2)}) %collective-permute-start.10) | collective-permute-done | bytes 393248 | tf_op jit(solution)/shard_map/ppermute | solution.py:555
  98.6 1.4 %shard_map.60 = (f32[1,4,16,128]{3,2,1,0:T(8,128)S(1)}, f32[1,4,8,128]{3,2,1,0:T(8,128)S(1)}, f32[1,4,16,128]{3,2,1,0:T(8,128)S(1)}, f32[2,2,16,24,128]{4,3,2,1,0:T(8,128)S(1)}, f32[2,2,24,24,128]{4,3,2,1,0:T(8,128)S(1)}) custom-call(s32[3]{0:T(128)S(1)} %copy-done, f32[44,8,128]{2,1,0:T(8,128)S(1)} %collective-permute-done.7.refs_0_, ...), custom_call_target="tpu_custom_call" | custom-call | tf_op jit(solution)/shard_map/pallas_call | solution.py:541
  100.1 0.1 collective-permute-start.11
  100.2 5.2 %collective-permute-start.12 = (f32[1,4,16,128]{3,2,1,0:T(8,128)S(1)}, f32[1,4,16,128]{3,2,1,0:T(8,128)S(1)}, u32[]{:S(2)}, u32[]{:S(2)}) collective-permute-start(f32[1,4,16,128]{3,2,1,0:T(8,128)S(1)} %get-tuple-element.63), channel_id=1, source_target_pairs={{1,0},{2,1},{3,2},{4,3},{5,4},{6,5},{7,6},{8,7},{9,8},{10,9},{11,1... | collective-permute-start | bytes 98312 | tf_op jit(solution)/shard_map/ppermute | solution.py:555
  105.3 1.2 collective-permute-done.11
  106.5 0.0 collective-permute-done.12
  106.6 12.3 %all_to_all.34.refs_0_ = f32[4,1,4,40,128]{4,3,2,1,0:T(8,128)S(1)} all-to-all(f32[4,1,4,40,128]{4,3,2,1,0:T(8,128)S(1)} %broadcast_in_dim.16), channel_id=1, replica_groups={{0,64,128,192},{32,96,160,224},{1,65,129,193},{33,97,161,225},{2,66,130..., dimensions={0} | all-to-all | bytes 655360 | tf_op jit(solution)/shard_map/all_to_all | solution.py:614
  118.9 0.4 collective-permute-start.13
  119.3 1.3 collective-permute-done.13.refs_1_
  120.6 4.1 %shard_map.61 = (f32[32,128]{1,0:T(8,128)S(1)}, f32[48,40,128]{2,1,0:T(8,128)S(1)}, f32[48,40,128]{2,1,0:T(8,128)S(1)}, f32[8,24,128]{2,1,0:T(8,128)S(1)}) custom-call(s32[3]{0:T(128)S(1)} %copy-done, f32[4,1,4,40,128]{4,3,2,1,0:T(8,128)S(1)} %all_to_all.34.refs_0_, f32[4,1,4,40,128]{4,3,2,1,0:T(8,128)S(1)} %collective-permute-done.13.refs_1_, ...), custom_call_target="tpu_custom_call" | custom-call | tf_op jit(solution)/shard_map/pallas_call | solution.py:541
  124.6 14.9 %all_to_all.35 = f32[32,1,128]{2,1,0:T(1,128)S(1)} all-to-all(f32[32,1,128]{2,1,0:T(1,128)S(1)} %bitcast.13), channel_id=1, replica_groups=mesh['slow'=8,'fast'=32] {'fast'}, dimensions={0} | all-to-all | bytes 32768 | tf_op jit(solution)/shard_map/all_to_all | solution.py:630
  139.6 2.7 %shard_map.62 = f32[8,16,256]{2,1,0:T(8,128)} custom-call(s32[3]{0:T(128)S(1)} %copy-done, f32[32,128]{1,0:T(8,128)S(1)} %bitcast.11, f32[48,40,128]{2,1,0:T(8,128)S(1)} %get-tuple-element.69.refs_1_, f32[48,40,128]{2,1,0:T(8,128)S(1)} %get-tuple-element.70.refs_2_, f32[48,40,128]{2,1,0:T(8,128)S(1)} %get-tuple-element.52.refs_3_.refs_2_, ...), custom_call_target="tpu_custom_call" | custom-call | tf_op jit(solution)/shard_map/pallas_call | solution.py:541
  (22 shorter events, 0.3 us)
Async XLA Ops:
  2.0 15.8 %collective-permute-start = (f32[76,8,128]{2,1,0:T(8,128)S(1)}, f32[76,8,128]{2,1,0:T(8,128)S(1)}, u32[]{:S(2)}, u32[]{:S(2)}) collective-permute-start(f32[76,8,128]{2,1,0:T(8,128)S(1)} %get-tuple-element.42.refs_1_.refs_10_), channel_id=1, source_target_pairs={{0,1},{1,2},{2,3},{3,4},{4,5},{5,6},{6,7},{7,8},{8,9},{9,10},{10,1... | collective-permute-start | bytes 933896 | tf_op jit(solution)/shard_map/ppermute | solution.py:555
  4.1 13.7 %collective-permute-start.1 = (f32[76,8,128]{2,1,0:T(8,128)S(1)}, f32[76,8,128]{2,1,0:T(8,128)S(1)}, u32[]{:S(2)}, u32[]{:S(2)}) collective-permute-start(f32[76,8,128]{2,1,0:T(8,128)S(1)} %get-tuple-element.42.refs_1_.refs_10_), channel_id=1, source_target_pairs={{1,0},{2,1},{3,2},{4,3},{5,4},{6,5},{7,6},{8,7},{9,8},{10,9},{11,1... | collective-permute-start | bytes 933896 | tf_op jit(solution)/shard_map/ppermute | solution.py:555
  17.8 13.1 %copy-start = (s32[3]{0:T(128)S(1)}, s32[3]{0:T(128)}, u32[]{:S(2)}) copy-start(s32[3]{0:T(128)} %sweeps.11) | copy-start | bytes 40
  17.9 10.5 %collective-permute-start.2 = (f32[172,8,128]{2,1,0:T(8,128)S(1)}, f32[172,8,128]{2,1,0:T(8,128)S(1)}, u32[]{:S(2)}, u32[]{:S(2)}) collective-permute-start(f32[172,8,128]{2,1,0:T(8,128)S(1)} %pad_maximum_fusion), channel_id=1, source_target_pairs={{0,32},{32,64},{64,96},{96,128},{128,160},{160,192},{192,224},{224... | collective-permute-start | bytes 2113544 | tf_op jit(solution)/shard_map/ppermute | solution.py:555
  20.4 10.5 %collective-permute-start.3 = (f32[172,8,128]{2,1,0:T(8,128)S(1)}, f32[172,8,128]{2,1,0:T(8,128)S(1)}, u32[]{:S(2)}, u32[]{:S(2)}) collective-permute-start(f32[172,8,128]{2,1,0:T(8,128)S(1)} %constant_dynamic-update-slice_fusion), channel_id=1, source_target_pairs={{32,0},{64,32},{96,64},{128,96},{160,128},{192,160},{224,192},{0,2... | collective-permute-start | bytes 2113544 | tf_op jit(solution)/shard_map/ppermute | solution.py:555
  32.5 7.1 %collective-permute-start.4 = (f32[2,4,16,128]{3,2,1,0:T(8,128)S(1)}, f32[2,4,16,128]{3,2,1,0:T(8,128)S(1)}, u32[]{:S(2)}, u32[]{:S(2)}) collective-permute-start(f32[2,4,16,128]{3,2,1,0:T(8,128)S(1)} %get-tuple-element.46), channel_id=1, source_target_pairs={{0,1},{1,2},{2,3},{3,4},{4,5},{5,6},{6,7},{7,8},{8,9},{9,10},{10,1... | collective-permute-start | bytes 196616 | tf_op jit(solution)/shard_map/ppermute | solution.py:555
  32.6 7.0 %collective-permute-start.5 = (f32[2,4,16,128]{3,2,1,0:T(8,128)S(1)}, f32[2,4,16,128]{3,2,1,0:T(8,128)S(1)}, u32[]{:S(2)}, u32[]{:S(2)}) collective-permute-start(f32[2,4,16,128]{3,2,1,0:T(8,128)S(1)} %get-tuple-element.48), channel_id=1, source_target_pairs={{1,0},{2,1},{3,2},{4,3},{5,4},{6,5},{7,6},{8,7},{9,8},{10,9},{11,1... | collective-permute-start | bytes 196616 | tf_op jit(solution)/shard_map/ppermute | solution.py:555
  53.4 3.2 %collective-permute-start.6 = (f32[4,2,4,40,128]{4,3,2,1,0:T(8,128)S(1)}, f32[4,2,4,40,128]{4,3,2,1,0:T(8,128)S(1)}, u32[]{:S(2)}, u32[]{:S(2)}) collective-permute-start(f32[4,2,4,40,128]{4,3,2,1,0:T(8,128)S(1)} %all_to_all.32.refs_0_), channel_id=1, source_target_pairs={{0,32},{32,0},{64,96},{96,64},{128,160},{160,128},{192,224},{224,1... | collective-permute-start | bytes 1966088 | tf_op jit(solution)/shard_map/ppermute | solution.py:615
  80.1 7.7 %collective-permute-start.7 = (f32[44,8,128]{2,1,0:T(8,128)S(1)}, f32[44,8,128]{2,1,0:T(8,128)S(1)}, u32[]{:S(2)}, u32[]{:S(2)}) collective-permute-start(f32[44,8,128]{2,1,0:T(8,128)S(1)} %get-tuple-element.59.refs_1_), channel_id=1, source_target_pairs={{0,1},{1,2},{2,3},{3,4},{4,5},{5,6},{6,7},{7,8},{8,9},{9,10},{10,1... | collective-permute-start | bytes 540680 | tf_op jit(solution)/shard_map/ppermute | solution.py:555
  80.5 7.4 %collective-permute-start.8 = (f32[44,8,128]{2,1,0:T(8,128)S(1)}, f32[44,8,128]{2,1,0:T(8,128)S(1)}, u32[]{:S(2)}, u32[]{:S(2)}) collective-permute-start(f32[44,8,128]{2,1,0:T(8,128)S(1)} %get-tuple-element.59.refs_1_), channel_id=1, source_target_pairs={{1,0},{2,1},{3,2},{4,3},{5,4},{6,5},{7,6},{8,7},{9,8},{10,9},{11,1... | collective-permute-start | bytes 540680 | tf_op jit(solution)/shard_map/ppermute | solution.py:555
  88.0 7.9 %collective-permute-start.9 = (f32[96,8,128]{2,1,0:T(8,128)S(1)}, f32[96,8,128]{2,1,0:T(8,128)S(1)}, u32[]{:S(2)}, u32[]{:S(2)}) collective-permute-start(f32[96,8,128]{2,1,0:T(8,128)S(1)} %pad_maximum_fusion.1), channel_id=1, source_target_pairs={{0,32},{32,64},{64,96},{96,128},{128,160},{160,192},{192,224},{224... | collective-permute-start | bytes 1179656 | tf_op jit(solution)/shard_map/ppermute | solution.py:555
  91.1 7.5 %collective-permute-start.10 = (f32[96,8,128]{2,1,0:T(8,128)S(1)}, f32[96,8,128]{2,1,0:T(8,128)S(1)}, u32[]{:S(2)}, u32[]{:S(2)}) collective-permute-start(f32[96,8,128]{2,1,0:T(8,128)S(1)} %constant_dynamic-update-slice_fusion.3), channel_id=1, source_target_pairs={{32,0},{64,32},{96,64},{128,96},{160,128},{192,160},{224,192},{0,2... | collective-permute-start | bytes 1179656 | tf_op jit(solution)/shard_map/ppermute | solution.py:555
  100.1 6.5 %collective-permute-start.11 = (f32[1,4,16,128]{3,2,1,0:T(8,128)S(1)}, f32[1,4,16,128]{3,2,1,0:T(8,128)S(1)}, u32[]{:S(2)}, u32[]{:S(2)}) collective-permute-start(f32[1,4,16,128]{3,2,1,0:T(8,128)S(1)} %get-tuple-element.61), channel_id=1, source_target_pairs={{0,1},{1,2},{2,3},{3,4},{4,5},{5,6},{6,7},{7,8},{8,9},{9,10},{10,1... | collective-permute-start | bytes 98312 | tf_op jit(solution)/shard_map/ppermute | solution.py:555
  100.2 6.4 %collective-permute-start.12 = (f32[1,4,16,128]{3,2,1,0:T(8,128)S(1)}, f32[1,4,16,128]{3,2,1,0:T(8,128)S(1)}, u32[]{:S(2)}, u32[]{:S(2)}) collective-permute-start(f32[1,4,16,128]{3,2,1,0:T(8,128)S(1)} %get-tuple-element.63), channel_id=1, source_target_pairs={{1,0},{2,1},{3,2},{4,3},{5,4},{6,5},{7,6},{8,7},{9,8},{10,9},{11,1... | collective-permute-start | bytes 98312 | tf_op jit(solution)/shard_map/ppermute | solution.py:555
  118.9 1.7 %collective-permute-start.13 = (f32[4,1,4,40,128]{4,3,2,1,0:T(8,128)S(1)}, f32[4,1,4,40,128]{4,3,2,1,0:T(8,128)S(1)}, u32[]{:S(2)}, u32[]{:S(2)}) collective-permute-start(f32[4,1,4,40,128]{4,3,2,1,0:T(8,128)S(1)} %all_to_all.34.refs_0_), channel_id=1, source_target_pairs={{0,32},{32,0},{64,96},{96,64},{128,160},{160,128},{192,224},{224,1... | collective-permute-start | bytes 983048 | tf_op jit(solution)/shard_map/ppermute | solution.py:615

commit v8 on v7

--- a/solution.py
+++ b/solution.py
@@ -220,37 +220,36 @@
     row_mask = jnp.where(rows < ZB, in_z[0], jnp.where(rows < 2 * ZB, 1.0, in_z[2]))
     masks = [row_mask * in_y[0], row_mask, row_mask * in_y[2]]
 
-    def tile(yb, zb, n):
+    corner = 4 * each + 6 + each // 4
+    bases = (0, corner, corner + 7 * each + 8)
+
+    def load(yb, zb, n):
         if yb == 1:
-            return across[zb].at[n]
-        rows, y = (7, (n - 4) // each) if zb == 1 else (6, (n - 4) // each)
-        base = (0, 6 * each + 6, 13 * each + 14)[zb]
-        if n < 4:
-            at = n
-        elif y < YB:
-            left_out_rows = YB - rows if yb == 0 else 0
-            if y < left_out_rows or y >= left_out_rows + rows:
-                return None
-            at = n - (4 + left_out_rows * each) + (0 if yb == 0 else 4)
-        else:
-            at = n - (4 + 8 * each) + rows * each
-        return (low if yb == 0 else high).at[base + at]
+            return across[zb][n]
+        ref, base, y = low if yb == 0 else high, bases[zb], (n - 4) // each
+        if zb == 1:
+            return ref[base + n - (4 + each if yb == 0 else 0)]
+        if yb == 0 and y >= 4:
+            return ref[base + n - (4 + 4 * each)]
+        if yb == 2 and y < 4:
+            return ref[base + n]
+        at = n - 4 - (2 if yb == 0 else 4) * each
+        if not 0 <= at < 2 * each:
+            return jnp.zeros((ZB, LANES), F32)
+        row = ref[base + 4 * each + 4 + at // 8, at % 8 : at % 8 + 1]
+        return jnp.where(tile_rows == (ZB - 1 if zb == 0 else 0), row, 0.0)
 
     def z_face(yb, zb, which, px, y):
-        n = 2 * which + px
         if yb == 1:
-            face = across[zb].at[8 + 8 * each + n]
-        else:
-            base = (6 * each + 4 - 2, 13 * each + 10, 19 * each + 18)[zb]
-            face = (low if yb == 0 else high).at[base + n]
+            face = across[zb].at[8 + 8 * each + 2 * which + px]
+        elif zb == 1:
+            face = (low if yb == 0 else high).at[bases[1] + 7 * each + 4 + 2 * which + px]
+        else:
+            face = (low if yb == 0 else high).at[bases[zb] + corner - 2 + px]
         return face[pl.ds(y, 1), :]
 
     def wide(yb, n):
         return jnp.concatenate([load(yb, zb, n) for zb in range(3)], axis=0)
-
-    def load(yb, zb, n):
-        at = tile(yb, zb, n)
-        return jnp.zeros((ZB, LANES), F32) if at is None else at[...]
 
     def right_side(yb, y):
         row = yb * YB + y
@@ -397,7 +396,7 @@
     mask2 = jnp.where(
         (zrow2 >= 0) & (zrow2 < lax.axis_size("fast") * 4) & (rows2 < 20), 1.0, 0.0
     ).astype(F32)
-    own = jnp.where((rows2 >= 8) & (rows2 < 12), 0.5, 0.0).astype(F32)
+    own = jnp.where((rows2 >= 8) & (rows2 < 12), 1.0, 0.0).astype(F32)
     zero2 = jnp.zeros((24, LANES), F32)
     for n in (*range(PADL), *range(PADL + 16, 16 + 2 * PADL)):
         wa[n] = zero2
@@ -448,10 +447,9 @@
     for yc in range(16):
         here, beside = flat_neighbours(wb, yc + PADL, lanes2, 2)
         total = total + (q2[yc] - OMEGA * here + k2[yc] * beside) * d2[yc]
-    numer = jnp.sum(total * own)
-    denom = jnp.sum(g2sum[...])
-    lanes_p = lane_iota(part.shape[0])
-    part[...] = jnp.where(lanes_p == 0, numer, jnp.where(lanes_p == 1, denom, 0.0))
+    numer = jnp.sum(total * own, axis=0, keepdims=True)
+    denom = jnp.sum(g2sum[...], axis=0, keepdims=True)
+    part[...] = jnp.where((lane_iota(part.shape[0]) & 1) == 0, numer, denom)
     for y in range(YPOST // 2):
         value = wb[2 * slow + (PADL - 3) + y]
         x2[y, pl.ds(0, 24, stride=2), :] = value
@@ -467,8 +465,8 @@
     lanes = lane_iota(ZW)
     lanes_p = lane_iota(parts.shape[0])
     every = parts[...]
-    numer = jnp.sum(jnp.where(lanes_p == 0, every, 0.0))
-    denom = jnp.sum(jnp.where(lanes_p == 1, every, 0.0)) + 0.0625 * faces
+    numer = jnp.sum(jnp.where((lanes_p & 1) == 0, every, 0.0))
+    denom = jnp.sum(jnp.where((lanes_p & 1) == 1, every, 0.0)) + 0.0625 * faces
     shift = jnp.full((ZW, LANES), numer, F32) / jnp.full((ZW, LANES), denom, F32)
     base = 4 * lax.axis_index("slow") + (PADM - 6)
 
@@ -558,13 +556,19 @@
 def window_of(pack, each):
     left, right = both_ways(pack, pack, "fast")
     faces = 8 + 8 * each
+
+    def packed(block, first, half_row):
+        return block[first : first + 2 * each, half_row : half_row + 1].reshape(each // 4, ZB, LANES)
+
     upward = [
-        left[4 + 2 * each : faces], left[faces + 2 :], pack[4 + each :],
-        right[4 + 2 * each : faces], right[faces : faces + 2],
+        left[4 + 4 * each : faces], packed(left, 4 + 2 * each, ZB - 1), left[faces + 2 :],
+        pack[4 + each :],
+        right[4 + 4 * each : faces], packed(right, 4 + 2 * each, 0), right[faces : faces + 2],
     ]
     downward = [
-        left[: 4 + 6 * each], left[faces + 2 :], pack[: 4 + 7 * each], pack[faces:],
-        right[: 4 + 6 * each], right[faces : faces + 2],
+        left[: 4 + 4 * each], packed(left, 4 + 4 * each, ZB - 1), left[faces + 2 :],
+        pack[: 4 + 7 * each], pack[faces:],
+        right[: 4 + 4 * each], packed(right, 4 + 4 * each, 0), right[faces : faces + 2],
     ]
     low, high = both_ways(jnp.concatenate(upward), jnp.concatenate(downward), "slow")
     return left, pack, right, low, high

time: 143 us -> 137 us (0.958)
  waiting for transfers between devices: 32.9 us -> 27.4 us
  starting transfers between devices: 31.3 us -> 36.3 us
  blocking collectives: 57.6 us -> 52.9 us
    ppermute x12, waiting for transfers between devices: 29.9 us -> 24.4 us  [both_ways(): return (lax.ppermute(to_right, axis, up), lax.ppermute(to_left, axis, down))]
    ppermute x2, starting transfers between devices: 1.88 us -> 7.11 us  [body(): other = lax.ppermute(mine, 'slow', [(n, n ^ 1) for n in range(slow_count)])]
    all_to_all x2, blocking collectives: 26 us -> 22.3 us  [body(): lax.all_to_all(strip, 'slow', 0, 0, axis_index_groups=chips, tiled=True)]
  transfers between devices with their start and end apart: 14 -> 14, of which waited for: 10 -> 8; matrix products, arithmetic and copies ran while one was open for 0% -> 0% of each run, Pallas kernels for 1% -> 1%
where the time goes in v8:
time: 137 us; the launch traced here: 136 us
  blocking collectives  52.9 us (39%)
  starting transfers between devices  36.3 us (26%)
  waiting for transfers between devices  27.4 us (20%)
  Pallas kernels  18.8 us (14%)
    all_to_all x2, blocking collectives, body(): parts = lax.all_to_all(part, 'fast', 0, 0, tiled=True)  30.7 us
    ppermute x12, starting transfers between devices, both_ways(): return (lax.ppermute(to_right, axis, up), lax.ppermute(to_left, axis, down))  29.2 us
    ppermute x12, waiting for transfers between devices, both_ways(): return (lax.ppermute(to_right, axis, up), lax.ppermute(to_left, axis, down))  24.4 us
    all_to_all x2, blocking collectives, body(): lax.all_to_all(strip, 'slow', 0, 0, axis_index_groups=chips, tiled=True)  22.3 us
    pallas_call x8, Pallas kernels, call(): pl.pallas_call(kernel, out_shape=[pltpu.VMEM(s, F32) if kept else jax.Sha...  18.8 us
    ppermute x2, starting transfers between devices, body(): other = lax.ppermute(mine, 'slow', [(n, n ^ 1) for n in range(slow_count)])  7.11 us
    ppermute x2, waiting for transfers between devices, body(): other = lax.ppermute(mine, 'slow', [(n, n ^ 1) for n in range(slow_count)])  2.98 us
  transfers between devices with their start and end apart: 14, of which 8 were waited for; matrix products, arithmetic and copies ran while one was open for 0% of the time, Pallas kernels for 1%

profile of v8, /device:TPU:1, one launch (start us, length us, event | category | flops | bytes accessed | tf_op | source)
XLA Modules:
  0.0 136.0 jit_solution(7242274145378446443)
XLA Ops:
  0.0 2.0 %shard_map.55 = (f32[76,8,128]{2,1,0:T(8,128)S(1)}, f32[2,2,8,8,128]{4,3,2,1,0:T(8,128)S(1)}) custom-call(f32[8,16,256]{2,1,0:T(8,128)} %observed.3, f32[8,16,256]{2,1,0:T(8,128)} %start.1, f32[8,16,256]{2,1,0:T(8,128)} %diagonal.1, f32[2,8,16,256]{3,2,1,0:T(8,128)} %noise.3), custom_call_target="tpu_custom_call" | custom-call | tf_op jit(solution)/shard_map/pallas_call | solution.py:539
  2.0 2.1 %collective-permute-start = (f32[76,8,128]{2,1,0:T(8,128)S(1)}, f32[76,8,128]{2,1,0:T(8,128)S(1)}, u32[]{:S(2)}, u32[]{:S(2)}) collective-permute-start(f32[76,8,128]{2,1,0:T(8,128)S(1)} %get-tuple-element.42.refs_1_.refs_10_), channel_id=1, source_target_pairs={{0,1},{1,2},{2,3},{3,4},{4,5},{5,6},{6,7},{7,8},{8,9},{9,10},{10,1... | collective-permute-start | bytes 933896 | tf_op jit(solution)/shard_map/ppermute | solution.py:553
  4.1 6.6 %collective-permute-start.1 = (f32[76,8,128]{2,1,0:T(8,128)S(1)}, f32[76,8,128]{2,1,0:T(8,128)S(1)}, u32[]{:S(2)}, u32[]{:S(2)}) collective-permute-start(f32[76,8,128]{2,1,0:T(8,128)S(1)} %get-tuple-element.42.refs_1_.refs_10_), channel_id=1, source_target_pairs={{1,0},{2,1},{3,2},{4,3},{5,4},{6,5},{7,6},{8,7},{9,8},{10,9},{11,1... | collective-permute-start | bytes 933896 | tf_op jit(solution)/shard_map/ppermute | solution.py:553
  10.7 7.0 %collective-permute-done.refs_0_ = f32[76,8,128]{2,1,0:T(8,128)S(1)} collective-permute-done((f32[76,8,128]{2,1,0:T(8,128)S(1)}, f32[76,8,128]{2,1,0:T(8,128)S(1)}, u32[]{:S(2)}, u32[]{:S(2)}) %collective-permute-start) | collective-permute-done | bytes 311328 | tf_op jit(solution)/shard_map/ppermute | solution.py:553
  17.8 0.0 copy-start
  17.9 0.0 collective-permute-done.1.refs_2_
  18.0 1.2 collective-permute-start.3
  19.2 1.2 collective-permute-start.2
  20.4 1.3 shard_map.56.refs_9_
  21.7 6.5 %collective-permute-done.3.refs_4_ = f32[144,8,128]{2,1,0:T(8,128)S(1)} collective-permute-done((f32[144,8,128]{2,1,0:T(8,128)S(1)}, f32[144,8,128]{2,1,0:T(8,128)S(1)}, u32[]{:S(2)}, u32[]{:S(2)}) %collective-permute-start.3) | collective-permute-done | bytes 589856 | tf_op jit(solution)/shard_map/ppermute | solution.py:553
  28.3 0.0 collective-permute-done.2.refs_3_
  28.3 0.0 copy-done
  28.3 1.5 %shard_map.57 = (f32[2,4,16,128]{3,2,1,0:T(8,128)S(1)}, f32[2,4,8,128]{3,2,1,0:T(8,128)S(1)}, f32[2,4,16,128]{3,2,1,0:T(8,128)S(1)}, f32[2,2,16,24,128]{4,3,2,1,...) custom-call(s32[3]{0:T(128)S(1)} %copy-done, ...), custom_call_target="tpu_custom_call" | custom-call | tf_op jit(solution)/shard_map/pallas_call | solution.py:539
  29.8 0.1 collective-permute-start.4
  29.9 4.8 %collective-permute-start.5 = (f32[2,4,16,128]{3,2,1,0:T(8,128)S(1)}, f32[2,4,16,128]{3,2,1,0:T(8,128)S(1)}, u32[]{:S(2)}, u32[]{:S(2)}) collective-permute-start(f32[2,4,16,128]{3,2,1,0:T(8,128)S(1)} %get-tuple-element.48), channel_id=1, source_target_pairs={{1,0},{2,1},{3,2},{4,3},{5,4},{6,5},{7,6},{8,7},{9,8},{10,9},{11,1... | collective-permute-start | bytes 196616 | tf_op jit(solution)/shard_map/ppermute | solution.py:553
  34.7 1.6 %collective-permute-done.4 = f32[2,4,16,128]{3,2,1,0:T(8,128)S(1)} collective-permute-done((f32[2,4,16,128]{3,2,1,0:T(8,128)S(1)}, f32[2,4,16,128]{3,2,1,0:T(8,128)S(1)}, u32[]{:S(2)}, u32[]{:S(2)}) %collective-permute-start.4) | collective-permute-done | bytes 65568 | tf_op jit(solution)/shard_map/ppermute | solution.py:553
  36.3 0.0 collective-permute-done.5
  36.4 13.2 %all_to_all.32.refs_0_ = f32[4,2,4,40,128]{4,3,2,1,0:T(8,128)S(1)} all-to-all(f32[4,2,4,40,128]{4,3,2,1,0:T(8,128)S(1)} %broadcast_in_dim.6), channel_id=1, replica_groups={{0,64,128,192},{32,96,160,224},{1,65,129,193},{33,97,161,225},{2,66,130..., dimensions={0} | all-to-all | bytes 1310720 | tf_op jit(solution)/shard_map/all_to_all | solution.py:618
  49.6 3.2 %collective-permute-start.6 = (f32[4,2,4,40,128]{4,3,2,1,0:T(8,128)S(1)}, f32[4,2,4,40,128]{4,3,2,1,0:T(8,128)S(1)}, u32[]{:S(2)}, u32[]{:S(2)}) collective-permute-start(f32[4,2,4,40,128]{4,3,2,1,0:T(8,128)S(1)} %all_to_all.32.refs_0_), channel_id=1, source_target_pairs={{0,32},{32,0},{64,96},{96,64},{128,160},{160,128},{192,224},{224,1... | collective-permute-start | bytes 1966088 | tf_op jit(solution)/shard_map/ppermute | solution.py:619
  52.9 1.7 %collective-permute-done.6.refs_1_ = f32[4,2,4,40,128]{4,3,2,1,0:T(8,128)S(1)} collective-permute-done((f32[4,2,4,40,128]{4,3,2,1,0:T(8,128)S(1)}, f32[4,2,4,40,128]{4,3,2,1,0:T(8,128)S(1)}, u32[]{:S(2)}, u32[]{:S(2)}) %collective-permute-start.6) | collective-permute-done | bytes 655392 | tf_op jit(solution)/shard_map/ppermute | solution.py:619
  54.6 4.4 %shard_map.58 = (f32[32,128]{1,0:T(8,128)S(1)}, f32[48,40,128]{2,1,0:T(8,128)S(1)}, f32[48,40,128]{2,1,0:T(8,128)S(1)}, f32[8,24,128]{2,1,0:T(8,128)S(1)}, f32[4...) custom-call(s32[3]{0:T(128)S(1)} %copy-done, ...), custom_call_target="tpu_custom_call" | custom-call | tf_op jit(solution)/shard_map/pallas_call | solution.py:539
  59.0 15.6 %all_to_all.33 = f32[32,1,128]{2,1,0:T(1,128)S(1)} all-to-all(f32[32,1,128]{2,1,0:T(1,128)S(1)} %bitcast.35), channel_id=1, replica_groups=mesh['slow'=8,'fast'=32] {'fast'}, dimensions={0} | all-to-all | bytes 32768 | tf_op jit(solution)/shard_map/all_to_all | solution.py:634
  74.5 1.9 %shard_map.59 = (f32[44,8,128]{2,1,0:T(8,128)S(1)}, f32[2,2,8,8,128]{4,3,2,1,0:T(8,128)S(1)}) custom-call(s32[3]{0:T(128)S(1)} %copy-done, f32[32,128]{1,0:T(8,128)S(1)} %bitcast.33, f32[48,40,128]{2,1,0:T(8,128)S(1)} %get-tuple-element.50.refs_1_, f32[48,40,128]{2,1,0:T(8,128)S(1)} %get-tuple-element.51.refs_2_, ...), custom_call_target="tpu_custom_call" | custom-call | tf_op jit(solution)/shard_map/pallas_call | solution.py:539
  76.4 0.4 collective-permute-start.7
  76.8 4.5 %collective-permute-start.8 = (f32[44,8,128]{2,1,0:T(8,128)S(1)}, f32[44,8,128]{2,1,0:T(8,128)S(1)}, u32[]{:S(2)}, u32[]{:S(2)}) collective-permute-start(f32[44,8,128]{2,1,0:T(8,128)S(1)} %get-tuple-element.59.refs_1_), channel_id=1, source_target_pairs={{1,0},{2,1},{3,2},{4,3},{5,4},{6,5},{7,6},{8,7},{9,8},{10,9},{11,1... | collective-permute-start | bytes 540680 | tf_op jit(solution)/shard_map/ppermute | solution.py:553
  81.3 2.9 %collective-permute-done.7.refs_0_ = f32[44,8,128]{2,1,0:T(8,128)S(1)} collective-permute-done((f32[44,8,128]{2,1,0:T(8,128)S(1)}, f32[44,8,128]{2,1,0:T(8,128)S(1)}, u32[]{:S(2)}, u32[]{:S(2)}) %collective-permute-start.7) | collective-permute-done | bytes 180256 | tf_op jit(solution)/shard_map/ppermute | solution.py:553
  84.3 0.0 collective-permute-done.8.refs_2_
  84.4 3.0 %collective-permute-start.10 = (f32[82,8,128]{2,1,0:T(8,128)S(1)}, f32[82,8,128]{2,1,0:T(8,128)S(1)}, u32[]{:S(2)}, u32[]{:S(2)}) collective-permute-start(f32[82,8,128]{2,1,0:T(8,128)S(1)} %get-tuple-element.87), channel_id=1, source_target_pairs={{32,0},{64,32},{96,64},{128,96},{160,128},{192,160},{224,192},{0,2... | collective-permute-start | bytes 1007624 | tf_op jit(solution)/shard_map/ppermute | solution.py:553
  87.4 0.2 collective-permute-start.9
  87.6 5.1 %collective-permute-done.10.refs_4_ = f32[82,8,128]{2,1,0:T(8,128)S(1)} collective-permute-done((f32[82,8,128]{2,1,0:T(8,128)S(1)}, f32[82,8,128]{2,1,0:T(8,128)S(1)}, u32[]{:S(2)}, u32[]{:S(2)}) %collective-permute-start.10) | collective-permute-done | bytes 335904 | tf_op jit(solution)/shard_map/ppermute | solution.py:553
  92.7 0.0 collective-permute-done.9.refs_3_
  92.7 1.5 %shard_map.60 = (f32[1,4,16,128]{3,2,1,0:T(8,128)S(1)}, f32[1,4,8,128]{3,2,1,0:T(8,128)S(1)}, f32[1,4,16,128]{3,2,1,0:T(8,128)S(1)}, f32[2,2,16,24,128]{4,3,2,1,0:T(8,128)S(1)}, f32[2,2,24,24,128]{4,3,2,1,0:T(8,128)S(1)}) custom-call(s32[3]{0:T(128)S(1)} %copy-done, f32[44,8,128]{2,1,0:T(8,128)S(1)} %collective-permute-done.7.refs_0_, ...), custom_call_target="tpu_custom_call" | custom-call | tf_op jit(solution)/shard_map/pallas_call | solution.py:539
  94.1 0.1 collective-permute-start.11
  94.2 5.0 %collective-permute-start.12 = (f32[1,4,16,128]{3,2,1,0:T(8,128)S(1)}, f32[1,4,16,128]{3,2,1,0:T(8,128)S(1)}, u32[]{:S(2)}, u32[]{:S(2)}) collective-permute-start(f32[1,4,16,128]{3,2,1,0:T(8,128)S(1)} %get-tuple-element.63), channel_id=1, source_target_pairs={{1,0},{2,1},{3,2},{4,3},{5,4},{6,5},{7,6},{8,7},{9,8},{10,9},{11,1... | collective-permute-start | bytes 98312 | tf_op jit(solution)/shard_map/ppermute | solution.py:553
  99.2 1.2 collective-permute-done.11
  100.4 0.0 collective-permute-done.12
  100.5 9.0 %all_to_all.34.refs_0_ = f32[4,1,4,40,128]{4,3,2,1,0:T(8,128)S(1)} all-to-all(f32[4,1,4,40,128]{4,3,2,1,0:T(8,128)S(1)} %broadcast_in_dim.16), channel_id=1, replica_groups={{0,64,128,192},{32,96,160,224},{1,65,129,193},{33,97,161,225},{2,66,130..., dimensions={0} | all-to-all | bytes 655360 | tf_op jit(solution)/shard_map/all_to_all | solution.py:618
  109.5 3.9 %collective-permute-start.13 = (f32[4,1,4,40,128]{4,3,2,1,0:T(8,128)S(1)}, f32[4,1,4,40,128]{4,3,2,1,0:T(8,128)S(1)}, u32[]{:S(2)}, u32[]{:S(2)}) collective-permute-start(f32[4,1,4,40,128]{4,3,2,1,0:T(8,128)S(1)} %all_to_all.34.refs_0_), channel_id=1, source_target_pairs={{0,32},{32,0},{64,96},{96,64},{128,160},{160,128},{192,224},{224,1... | collective-permute-start | bytes 983048 | tf_op jit(solution)/shard_map/ppermute | solution.py:619
  113.4 1.3 collective-permute-done.13.refs_1_
  114.7 3.7 %shard_map.61 = (f32[32,128]{1,0:T(8,128)S(1)}, f32[48,40,128]{2,1,0:T(8,128)S(1)}, f32[48,40,128]{2,1,0:T(8,128)S(1)}, f32[8,24,128]{2,1,0:T(8,128)S(1)}) custom-call(s32[3]{0:T(128)S(1)} %copy-done, f32[4,1,4,40,128]{4,3,2,1,0:T(8,128)S(1)} %all_to_all.34.refs_0_, f32[4,1,4,40,128]{4,3,2,1,0:T(8,128)S(1)} %collective-permute-done.13.refs_1_, ...), custom_call_target="tpu_custom_call" | custom-call | tf_op jit(solution)/shard_map/pallas_call | solution.py:539
  118.4 15.1 %all_to_all.35 = f32[32,1,128]{2,1,0:T(1,128)S(1)} all-to-all(f32[32,1,128]{2,1,0:T(1,128)S(1)} %bitcast.36), channel_id=1, replica_groups=mesh['slow'=8,'fast'=32] {'fast'}, dimensions={0} | all-to-all | bytes 32768 | tf_op jit(solution)/shard_map/all_to_all | solution.py:634
  133.5 2.5 %shard_map.62 = f32[8,16,256]{2,1,0:T(8,128)} custom-call(s32[3]{0:T(128)S(1)} %copy-done, f32[32,128]{1,0:T(8,128)S(1)} %bitcast.34, f32[48,40,128]{2,1,0:T(8,128)S(1)} %get-tuple-element.69.refs_1_, f32[48,40,128]{2,1,0:T(8,128)S(1)} %get-tuple-element.70.refs_2_, f32[48,40,128]{2,1,0:T(8,128)S(1)} %get-tuple-element.52.refs_3_.refs_2_, ...), custom_call_target="tpu_custom_call" | custom-call | tf_op jit(solution)/shard_map/pallas_call | solution.py:539
  (29 shorter events, 0.3 us)
Async XLA Ops:
  2.0 15.8 %collective-permute-start = (f32[76,8,128]{2,1,0:T(8,128)S(1)}, f32[76,8,128]{2,1,0:T(8,128)S(1)}, u32[]{:S(2)}, u32[]{:S(2)}) collective-permute-start(f32[76,8,128]{2,1,0:T(8,128)S(1)} %get-tuple-element.42.refs_1_.refs_10_), channel_id=1, source_target_pairs={{0,1},{1,2},{2,3},{3,4},{4,5},{5,6},{6,7},{7,8},{8,9},{9,10},{10,1... | collective-permute-start | bytes 933896 | tf_op jit(solution)/shard_map/ppermute | solution.py:553
  4.1 13.8 %collective-permute-start.1 = (f32[76,8,128]{2,1,0:T(8,128)S(1)}, f32[76,8,128]{2,1,0:T(8,128)S(1)}, u32[]{:S(2)}, u32[]{:S(2)}) collective-permute-start(f32[76,8,128]{2,1,0:T(8,128)S(1)} %get-tuple-element.42.refs_1_.refs_10_), channel_id=1, source_target_pairs={{1,0},{2,1},{3,2},{4,3},{5,4},{6,5},{7,6},{8,7},{9,8},{10,9},{11,1... | collective-permute-start | bytes 933896 | tf_op jit(solution)/shard_map/ppermute | solution.py:553
  17.8 10.5 %copy-start = (s32[3]{0:T(128)S(1)}, s32[3]{0:T(128)}, u32[]{:S(2)}) copy-start(s32[3]{0:T(128)} %sweeps.11) | copy-start | bytes 40
  18.0 10.3 %collective-permute-start.3 = (f32[144,8,128]{2,1,0:T(8,128)S(1)}, f32[144,8,128]{2,1,0:T(8,128)S(1)}, u32[]{:S(2)}, u32[]{:S(2)}) collective-permute-start(f32[144,8,128]{2,1,0:T(8,128)S(1)} %get-tuple-element.75), channel_id=1, source_target_pairs={{32,0},{64,32},{96,64},{128,96},{160,128},{192,160},{224,192},{0,2... | collective-permute-start | bytes 1769480 | tf_op jit(solution)/shard_map/ppermute | solution.py:553
  19.2 9.0 %collective-permute-start.2 = (f32[144,8,128]{2,1,0:T(8,128)S(1)}, f32[144,8,128]{2,1,0:T(8,128)S(1)}, u32[]{:S(2)}, u32[]{:S(2)}) collective-permute-start(f32[144,8,128]{2,1,0:T(8,128)S(1)} %get-tuple-element.76), channel_id=1, source_target_pairs={{0,32},{32,64},{64,96},{96,128},{128,160},{160,192},{192,224},{224... | collective-permute-start | bytes 1769480 | tf_op jit(solution)/shard_map/ppermute | solution.py:553
  29.8 6.5 %collective-permute-start.4 = (f32[2,4,16,128]{3,2,1,0:T(8,128)S(1)}, f32[2,4,16,128]{3,2,1,0:T(8,128)S(1)}, u32[]{:S(2)}, u32[]{:S(2)}) collective-permute-start(f32[2,4,16,128]{3,2,1,0:T(8,128)S(1)} %get-tuple-element.46), channel_id=1, source_target_pairs={{0,1},{1,2},{2,3},{3,4},{4,5},{5,6},{6,7},{7,8},{8,9},{9,10},{10,1... | collective-permute-start | bytes 196616 | tf_op jit(solution)/shard_map/ppermute | solution.py:553
  29.9 6.4 %collective-permute-start.5 = (f32[2,4,16,128]{3,2,1,0:T(8,128)S(1)}, f32[2,4,16,128]{3,2,1,0:T(8,128)S(1)}, u32[]{:S(2)}, u32[]{:S(2)}) collective-permute-start(f32[2,4,16,128]{3,2,1,0:T(8,128)S(1)} %get-tuple-element.48), channel_id=1, source_target_pairs={{1,0},{2,1},{3,2},{4,3},{5,4},{6,5},{7,6},{8,7},{9,8},{10,9},{11,1... | collective-permute-start | bytes 196616 | tf_op jit(solution)/shard_map/ppermute | solution.py:553
  49.6 5.0 %collective-permute-start.6 = (f32[4,2,4,40,128]{4,3,2,1,0:T(8,128)S(1)}, f32[4,2,4,40,128]{4,3,2,1,0:T(8,128)S(1)}, u32[]{:S(2)}, u32[]{:S(2)}) collective-permute-start(f32[4,2,4,40,128]{4,3,2,1,0:T(8,128)S(1)} %all_to_all.32.refs_0_), channel_id=1, source_target_pairs={{0,32},{32,0},{64,96},{96,64},{128,160},{160,128},{192,224},{224,1... | collective-permute-start | bytes 1966088 | tf_op jit(solution)/shard_map/ppermute | solution.py:619
  76.4 7.7 %collective-permute-start.7 = (f32[44,8,128]{2,1,0:T(8,128)S(1)}, f32[44,8,128]{2,1,0:T(8,128)S(1)}, u32[]{:S(2)}, u32[]{:S(2)}) collective-permute-start(f32[44,8,128]{2,1,0:T(8,128)S(1)} %get-tuple-element.59.refs_1_), channel_id=1, source_target_pairs={{0,1},{1,2},{2,3},{3,4},{4,5},{5,6},{6,7},{7,8},{8,9},{9,10},{10,1... | collective-permute-start | bytes 540680 | tf_op jit(solution)/shard_map/ppermute | solution.py:553
  76.8 7.5 %collective-permute-start.8 = (f32[44,8,128]{2,1,0:T(8,128)S(1)}, f32[44,8,128]{2,1,0:T(8,128)S(1)}, u32[]{:S(2)}, u32[]{:S(2)}) collective-permute-start(f32[44,8,128]{2,1,0:T(8,128)S(1)} %get-tuple-element.59.refs_1_), channel_id=1, source_target_pairs={{1,0},{2,1},{3,2},{4,3},{5,4},{6,5},{7,6},{8,7},{9,8},{10,9},{11,1... | collective-permute-start | bytes 540680 | tf_op jit(solution)/shard_map/ppermute | solution.py:553
  84.4 8.3 %collective-permute-start.10 = (f32[82,8,128]{2,1,0:T(8,128)S(1)}, f32[82,8,128]{2,1,0:T(8,128)S(1)}, u32[]{:S(2)}, u32[]{:S(2)}) collective-permute-start(f32[82,8,128]{2,1,0:T(8,128)S(1)} %get-tuple-element.87), channel_id=1, source_target_pairs={{32,0},{64,32},{96,64},{128,96},{160,128},{192,160},{224,192},{0,2... | collective-permute-start | bytes 1007624 | tf_op jit(solution)/shard_map/ppermute | solution.py:553
  87.4 5.3 %collective-permute-start.9 = (f32[82,8,128]{2,1,0:T(8,128)S(1)}, f32[82,8,128]{2,1,0:T(8,128)S(1)}, u32[]{:S(2)}, u32[]{:S(2)}) collective-permute-start(f32[82,8,128]{2,1,0:T(8,128)S(1)} %get-tuple-element.88), channel_id=1, source_target_pairs={{0,32},{32,64},{64,96},{96,128},{128,160},{160,192},{192,224},{224... | collective-permute-start | bytes 1007624 | tf_op jit(solution)/shard_map/ppermute | solution.py:553
  94.1 6.3 %collective-permute-start.11 = (f32[1,4,16,128]{3,2,1,0:T(8,128)S(1)}, f32[1,4,16,128]{3,2,1,0:T(8,128)S(1)}, u32[]{:S(2)}, u32[]{:S(2)}) collective-permute-start(f32[1,4,16,128]{3,2,1,0:T(8,128)S(1)} %get-tuple-element.61), channel_id=1, source_target_pairs={{0,1},{1,2},{2,3},{3,4},{4,5},{5,6},{6,7},{7,8},{8,9},{9,10},{10,1... | collective-permute-start | bytes 98312 | tf_op jit(solution)/shard_map/ppermute | solution.py:553
  94.2 6.2 %collective-permute-start.12 = (f32[1,4,16,128]{3,2,1,0:T(8,128)S(1)}, f32[1,4,16,128]{3,2,1,0:T(8,128)S(1)}, u32[]{:S(2)}, u32[]{:S(2)}) collective-permute-start(f32[1,4,16,128]{3,2,1,0:T(8,128)S(1)} %get-tuple-element.63), channel_id=1, source_target_pairs={{1,0},{2,1},{3,2},{4,3},{5,4},{6,5},{7,6},{8,7},{9,8},{10,9},{11,1... | collective-permute-start | bytes 98312 | tf_op jit(solution)/shard_map/ppermute | solution.py:553
  109.5 5.1 %collective-permute-start.13 = (f32[4,1,4,40,128]{4,3,2,1,0:T(8,128)S(1)}, f32[4,1,4,40,128]{4,3,2,1,0:T(8,128)S(1)}, u32[]{:S(2)}, u32[]{:S(2)}) collective-permute-start(f32[4,1,4,40,128]{4,3,2,1,0:T(8,128)S(1)} %all_to_all.34.refs_0_), channel_id=1, source_target_pairs={{0,32},{32,0},{64,96},{96,64},{128,160},{160,128},{192,224},{224,1... | collective-permute-start | bytes 983048 | tf_op jit(solution)/shard_map/ppermute | solution.py:619

commit v9 on v8

--- a/solution.py
+++ b/solution.py
@@ -205,11 +205,11 @@
 def before_kernel(first, sweeps, *refs):
     across, low, high = refs[:3], refs[3], refs[4]
     if first:
-        left_out, own_out, right_out, epre, q, k, dn = refs[5:12]
+        outer_out, own_out, inner_out, epre, q, k, dn = refs[5:12]
         a, b = refs[12:]
     else:
         k, dn = refs[5:7]
-        left_out, own_out, right_out, epre, q = refs[7:12]
+        outer_out, own_out, inner_out, epre, q = refs[7:12]
         a, b = refs[12:]
     each = 8 if first else 4
     lanes = lane_iota(ZW)
@@ -299,6 +299,7 @@
 
     fine_sweep(a, epre, q, k, 4, 20, FINE, lanes, shift=4)
     zero = jnp.zeros((ZW, LANES), F32)
+    odd = (lax.axis_index("fast") & 1) == 1
 
     def restrict(ym):
         total = zero
@@ -313,9 +314,9 @@
                     diag = diag + wide(1, 8 + each * (2 * ym + half) + tile_of(p))
         for n, value in enumerate((total, diag) if first else (total,)):
             value = value * 0.125
-            right_out[n, ym] = value[: 2 * ZB]
             own_out[n, ym] = value[ZB : 2 * ZB]
-            left_out[n, ym] = value[ZB:]
+            inner_out[n, ym] = jnp.where(odd, value[ZB:], value[: 2 * ZB])
+            outer_out[n, ym] = jnp.where(odd, value[: 2 * ZB], value[ZB:])
 
     over(0, YB // 2, 4, restrict)
 
@@ -553,8 +554,17 @@
     return lax.ppermute(to_right, axis, up), lax.ppermute(to_left, axis, down)
 
 
+def swap_fast(first, second):
+    count = lax.axis_size("fast")
+    inner = [(i, i ^ 1) for i in range(count)]
+    outer = [(i, (i + (1 if i & 1 else -1)) % count) for i in range(count)]
+    a, b = lax.ppermute(first, "fast", inner), lax.ppermute(second, "fast", outer)
+    odd = (lax.axis_index("fast") & 1) == 1
+    return jnp.where(odd, a, b), jnp.where(odd, b, a)
+
+
 def window_of(pack, each):
-    left, right = both_ways(pack, pack, "fast")
+    left, right = swap_fast(pack, pack)
     faces = 8 + 8 * each
 
     def packed(block, first, half_row):
@@ -608,10 +618,10 @@
         else:
             given = (*given, *kept_fine)
         got = call(functools.partial(before_kernel, opening), outs, [whole] * 2, (sweeps,), *given)
-        to_left, own, to_right, epre, q = got[:5]
+        outer, own, inner, epre, q = got[:5]
         if opening:
             kept_fine = got[5:]
-        left, right = both_ways(to_right, to_left, "fast")
+        left, right = swap_fast(inner, outer)
         strip = jnp.concatenate([left, own, right], axis=2)
         strip = jnp.broadcast_to(strip[None], (slow_count // 2, *strip.shape))
         chips = [[2 * n + core for n in range(slow_count // 2)] for core in range(2)]

time: 137 us -> 134 us (0.978)
  waiting for transfers between devices: 27.4 us -> 36.7 us
  blocking collectives: 52.9 us -> 45.6 us
  starting transfers between devices: 36.3 us -> 29.6 us
  Pallas kernels: 18.8 us -> 20.8 us
    ppermute x12 -> x4, starting transfers between devices: 29.2 us -> 6.24 us  [both_ways(): return (lax.ppermute(to_right, axis, up), lax.ppermute(to_left, axis, down))]
    ppermute x0 -> x8, waiting for transfers between devices: none -> 22.1 us  [the longest x4 20.3 us: swap_fast(): lax.ppermute(second, 'fast', outer)]
    ppermute x0 -> x8, starting transfers between devices: none -> 15.1 us  [the longest x4 14.9 us: swap_fast(): lax.ppermute(second, 'fast', outer)]
    ppermute x12 -> x4, waiting for transfers between devices: 24.4 us -> 11.7 us  [both_ways(): return (lax.ppermute(to_right, axis, up), lax.ppermute(to_left, axis, down))]
    all_to_all x2, blocking collectives: 30.7 us -> 25.2 us  [body(): parts = lax.all_to_all(part, 'fast', 0, 0, tiled=True)]
    pallas_call x8, Pallas kernels: 18.8 us -> 20.8 us  [call(): pl.pallas_call(kernel, out_shape=[pltpu.VMEM(s, F32) if kept else jax.Sha...]
    all_to_all x2, blocking collectives: 22.3 us -> 20.4 us  [body(): lax.all_to_all(strip, 'slow', 0, 0, axis_index_groups=chips, tiled=True)]
  transfers between devices with their start and end apart: 14 -> 14, of which waited for: 8 -> 10; matrix products, arithmetic and copies ran while one was open for 0% -> 0% of each run, Pallas kernels for 1% -> 1%
where the time goes in v9:
time: 134 us; the launch traced here: 133 us
  blocking collectives  45.6 us (34%)
  waiting for transfers between devices  36.7 us (27%)
  starting transfers between devices  29.6 us (22%)
  Pallas kernels  20.8 us (16%)
    all_to_all x2, blocking collectives, body(): parts = lax.all_to_all(part, 'fast', 0, 0, tiled=True)  25.2 us
    pallas_call x8, Pallas kernels, call(): pl.pallas_call(kernel, out_shape=[pltpu.VMEM(s, F32) if kept else jax.Sha...  20.8 us
    all_to_all x2, blocking collectives, body(): lax.all_to_all(strip, 'slow', 0, 0, axis_index_groups=chips, tiled=True)  20.4 us
    ppermute x4, waiting for transfers between devices, swap_fast(): lax.ppermute(second, 'fast', outer)  20.3 us
    ppermute x4, starting transfers between devices, swap_fast(): lax.ppermute(second, 'fast', outer)  14.9 us
    ppermute x4, waiting for transfers between devices, both_ways(): return (lax.ppermute(to_right, axis, up), lax.ppermute(to_left, axis, down))  11.7 us
    ppermute x2, starting transfers between devices, body(): other = lax.ppermute(mine, 'slow', [(n, n ^ 1) for n in range(slow_count)])  8.22 us
    ppermute x4, starting transfers between devices, both_ways(): return (lax.ppermute(to_right, axis, up), lax.ppermute(to_left, axis, down))  6.24 us
  transfers between devices with their start and end apart: 14, of which 10 were waited for; matrix products, arithmetic and copies ran while one was open for 0% of the time, Pallas kernels for 1%

profile of v9, /device:TPU:1, one launch (start us, length us, event | category | flops | bytes accessed | tf_op | source)
XLA Modules:
  0.0 133.4 jit_solution(3074114422440272875)
XLA Ops:
  0.0 2.0 %shard_map.55 = (f32[76,8,128]{2,1,0:T(8,128)S(1)}, f32[2,2,8,8,128]{4,3,2,1,0:T(8,128)S(1)}) custom-call(f32[8,16,256]{2,1,0:T(8,128)} %observed.3, f32[8,16,256]{2,1,0:T(8,128)} %start.1, f32[8,16,256]{2,1,0:T(8,128)} %diagonal.1, f32[2,8,16,256]{3,2,1,0:T(8,128)} %noise.3), custom_call_target="tpu_custom_call" | custom-call | tf_op jit(solution)/shard_map/pallas_call | solution.py:540
  2.0 8.7 %collective-permute-start.1 = (f32[76,8,128]{2,1,0:T(8,128)S(1)}, f32[76,8,128]{2,1,0:T(8,128)S(1)}, u32[]{:S(2)}, u32[]{:S(2)}) collective-permute-start(f32[76,8,128]{2,1,0:T(8,128)S(1)} %get-tuple-element.42.refs_1_.refs_10_), channel_id=1, source_target_pairs={{0,31},{1,2},{2,1},{3,4},{4,3},{5,6},{6,5},{7,8},{8,7},{9,10},{10,... | collective-permute-start | bytes 933896 | tf_op jit(solution)/shard_map/ppermute | solution.py:561
  10.7 0.0 collective-permute-start
  10.7 7.1 %collective-permute-done.1 = f32[76,8,128]{2,1,0:T(8,128)S(1)} collective-permute-done((f32[76,8,128]{2,1,0:T(8,128)S(1)}, f32[76,8,128]{2,1,0:T(8,128)S(1)}, u32[]{:S(2)}, u32[]{:S(2)}) %collective-permute-start.1) | collective-permute-done | bytes 311328 | tf_op jit(solution)/shard_map/ppermute | solution.py:561
  17.7 0.8 collective-permute-done
  18.6 0.0 copy-start
  18.9 1.9 %collective-permute-start.3 = (f32[144,8,128]{2,1,0:T(8,128)S(1)}, f32[144,8,128]{2,1,0:T(8,128)S(1)}, u32[]{:S(2)}, u32[]{:S(2)}) collective-permute-start(f32[144,8,128]{2,1,0:T(8,128)S(1)} %get-tuple-element.79), channel_id=1, source_target_pairs={{32,0},{64,32},{96,64},{128,96},{160,128},{192,160},{224,192},{0,2... | collective-permute-start | bytes 1769480 | tf_op jit(solution)/shard_map/ppermute | solution.py:554
  20.7 1.2 collective-permute-start.2
  21.9 1.3 shard_map.56.refs_9_
  23.2 6.5 %collective-permute-done.3.refs_4_ = f32[144,8,128]{2,1,0:T(8,128)S(1)} collective-permute-done((f32[144,8,128]{2,1,0:T(8,128)S(1)}, f32[144,8,128]{2,1,0:T(8,128)S(1)}, u32[]{:S(2)}, u32[]{:S(2)}) %collective-permute-start.3) | collective-permute-done | bytes 589856 | tf_op jit(solution)/shard_map/ppermute | solution.py:554
  29.8 0.0 collective-permute-done.2.refs_3_
  29.8 0.0 copy-done
  29.8 2.1 %shard_map.57 = (f32[2,4,16,128]{3,2,1,0:T(8,128)S(1)}, f32[2,4,8,128]{3,2,1,0:T(8,128)S(1)}, f32[2,4,16,128]{3,2,1,0:T(8,128)S(1)}, f32[2,2,16,24,128]{4,3,2,1,...) custom-call(s32[3]{0:T(128)S(1)} %copy-done, ...), custom_call_target="tpu_custom_call" | custom-call | tf_op jit(solution)/shard_map/pallas_call | solution.py:540
  31.9 0.1 collective-permute-start.4
  32.0 3.4 %collective-permute-start.5 = (f32[2,4,16,128]{3,2,1,0:T(8,128)S(1)}, f32[2,4,16,128]{3,2,1,0:T(8,128)S(1)}, u32[]{:S(2)}, u32[]{:S(2)}) collective-permute-start(f32[2,4,16,128]{3,2,1,0:T(8,128)S(1)} %get-tuple-element.47), channel_id=1, source_target_pairs={{0,31},{1,2},{2,1},{3,4},{4,3},{5,6},{6,5},{7,8},{8,7},{9,10},{10,... | collective-permute-start | bytes 196616 | tf_op jit(solution)/shard_map/ppermute | solution.py:561
  35.4 0.0 collective-permute-done.4
  35.4 3.1 %collective-permute-done.5 = f32[2,4,16,128]{3,2,1,0:T(8,128)S(1)} collective-permute-done((f32[2,4,16,128]{3,2,1,0:T(8,128)S(1)}, f32[2,4,16,128]{3,2,1,0:T(8,128)S(1)}, u32[]{:S(2)}, u32[]{:S(2)}) %collective-permute-start.5) | collective-permute-done | bytes 65568 | tf_op jit(solution)/shard_map/ppermute | solution.py:561
  38.6 11.3 %all_to_all.32.refs_0_ = f32[4,2,4,40,128]{4,3,2,1,0:T(8,128)S(1)} all-to-all(f32[4,2,4,40,128]{4,3,2,1,0:T(8,128)S(1)} %broadcast_in_dim.6), channel_id=1, replica_groups={{0,64,128,192},{32,96,160,224},{1,65,129,193},{33,97,161,225},{2,66,130..., dimensions={0} | all-to-all | bytes 1310720 | tf_op jit(solution)/shard_map/all_to_all | solution.py:628
  49.9 4.2 %collective-permute-start.6 = (f32[4,2,4,40,128]{4,3,2,1,0:T(8,128)S(1)}, f32[4,2,4,40,128]{4,3,2,1,0:T(8,128)S(1)}, u32[]{:S(2)}, u32[]{:S(2)}) collective-permute-start(f32[4,2,4,40,128]{4,3,2,1,0:T(8,128)S(1)} %all_to_all.32.refs_0_), channel_id=1, source_target_pairs={{0,32},{32,0},{64,96},{96,64},{128,160},{160,128},{192,224},{224,1... | collective-permute-start | bytes 1966088 | tf_op jit(solution)/shard_map/ppermute | solution.py:629
  54.2 1.7 %collective-permute-done.6.refs_1_ = f32[4,2,4,40,128]{4,3,2,1,0:T(8,128)S(1)} collective-permute-done((f32[4,2,4,40,128]{4,3,2,1,0:T(8,128)S(1)}, f32[4,2,4,40,128]{4,3,2,1,0:T(8,128)S(1)}, u32[]{:S(2)}, u32[]{:S(2)}) %collective-permute-start.6) | collective-permute-done | bytes 655392 | tf_op jit(solution)/shard_map/ppermute | solution.py:629
  55.9 4.5 %shard_map.58 = (f32[32,128]{1,0:T(8,128)S(1)}, f32[48,40,128]{2,1,0:T(8,128)S(1)}, f32[48,40,128]{2,1,0:T(8,128)S(1)}, f32[8,24,128]{2,1,0:T(8,128)S(1)}, f32[4...) custom-call(s32[3]{0:T(128)S(1)} %copy-done, ...), custom_call_target="tpu_custom_call" | custom-call | tf_op jit(solution)/shard_map/pallas_call | solution.py:540
  60.3 13.4 %all_to_all.33 = f32[32,1,128]{2,1,0:T(1,128)S(1)} all-to-all(f32[32,1,128]{2,1,0:T(1,128)S(1)} %bitcast.36), channel_id=1, replica_groups=mesh['slow'=8,'fast'=32] {'fast'}, dimensions={0} | all-to-all | bytes 32768 | tf_op jit(solution)/shard_map/all_to_all | solution.py:644
  73.7 2.2 %shard_map.59 = (f32[44,8,128]{2,1,0:T(8,128)S(1)}, f32[2,2,8,8,128]{4,3,2,1,0:T(8,128)S(1)}) custom-call(s32[3]{0:T(128)S(1)} %copy-done, f32[32,128]{1,0:T(8,128)S(1)} %bitcast.34, f32[48,40,128]{2,1,0:T(8,128)S(1)} %get-tuple-element.50.refs_1_, f32[48,40,128]{2,1,0:T(8,128)S(1)} %get-tuple-element.51.refs_2_, ...), custom_call_target="tpu_custom_call" | custom-call | tf_op jit(solution)/shard_map/pallas_call | solution.py:540
  75.9 1.0 collective-permute-start.8
  77.0 0.0 collective-permute-start.7
  77.0 6.7 %collective-permute-done.8 = f32[44,8,128]{2,1,0:T(8,128)S(1)} collective-permute-done((f32[44,8,128]{2,1,0:T(8,128)S(1)}, f32[44,8,128]{2,1,0:T(8,128)S(1)}, u32[]{:S(2)}, u32[]{:S(2)}) %collective-permute-start.8) | collective-permute-done | bytes 180256 | tf_op jit(solution)/shard_map/ppermute | solution.py:561
  83.7 0.0 collective-permute-done.7
  83.9 3.0 %collective-permute-start.10 = (f32[82,8,128]{2,1,0:T(8,128)S(1)}, f32[82,8,128]{2,1,0:T(8,128)S(1)}, u32[]{:S(2)}, u32[]{:S(2)}) collective-permute-start(f32[82,8,128]{2,1,0:T(8,128)S(1)} %get-tuple-element.91), channel_id=1, source_target_pairs={{32,0},{64,32},{96,64},{128,96},{160,128},{192,160},{224,192},{0,2... | collective-permute-start | bytes 1007624 | tf_op jit(solution)/shard_map/ppermute | solution.py:554
  86.9 0.2 collective-permute-start.9
  87.1 5.1 %collective-permute-done.10.refs_4_ = f32[82,8,128]{2,1,0:T(8,128)S(1)} collective-permute-done((f32[82,8,128]{2,1,0:T(8,128)S(1)}, f32[82,8,128]{2,1,0:T(8,128)S(1)}, u32[]{:S(2)}, u32[]{:S(2)}) %collective-permute-start.10) | collective-permute-done | bytes 335904 | tf_op jit(solution)/shard_map/ppermute | solution.py:554
  92.2 0.0 collective-permute-done.9.refs_3_
  92.2 2.0 %shard_map.60 = (f32[1,4,16,128]{3,2,1,0:T(8,128)S(1)}, f32[1,4,8,128]{3,2,1,0:T(8,128)S(1)}, f32[1,4,16,128]{3,2,1,0:T(8,128)S(1)}, f32[2,2,16,24,128]{4,3,2,1,0:T(8,128)S(1)}, f32[2,2,24,24,128]{4,3,2,1,0:T(8,128)S(1)}) custom-call(s32[3]{0:T(128)S(1)} %copy-done, f32[44,8,128]{2,1,0:T(8,128)S(1)} %get-tuple-element.78.refs_0_, ...), custom_call_target="tpu_custom_call" | custom-call | tf_op jit(solution)/shard_map/pallas_call | solution.py:540
  94.2 0.1 collective-permute-start.11
  94.3 1.8 %collective-permute-start.12 = (f32[1,4,16,128]{3,2,1,0:T(8,128)S(1)}, f32[1,4,16,128]{3,2,1,0:T(8,128)S(1)}, u32[]{:S(2)}, u32[]{:S(2)}) collective-permute-start(f32[1,4,16,128]{3,2,1,0:T(8,128)S(1)} %get-tuple-element.62), channel_id=1, source_target_pairs={{0,31},{1,2},{2,1},{3,4},{4,3},{5,6},{6,5},{7,8},{8,7},{9,10},{10,... | collective-permute-start | bytes 98312 | tf_op jit(solution)/shard_map/ppermute | solution.py:561
  96.1 0.9 collective-permute-done.11
  97.0 3.4 %collective-permute-done.12 = f32[1,4,16,128]{3,2,1,0:T(8,128)S(1)} collective-permute-done((f32[1,4,16,128]{3,2,1,0:T(8,128)S(1)}, f32[1,4,16,128]{3,2,1,0:T(8,128)S(1)}, u32[]{:S(2)}, u32[]{:S(2)}) %collective-permute-start.12) | collective-permute-done | bytes 32800 | tf_op jit(solution)/shard_map/ppermute | solution.py:561
  100.5 9.1 %all_to_all.34.refs_0_ = f32[4,1,4,40,128]{4,3,2,1,0:T(8,128)S(1)} all-to-all(f32[4,1,4,40,128]{4,3,2,1,0:T(8,128)S(1)} %broadcast_in_dim.16), channel_id=1, replica_groups={{0,64,128,192},{32,96,160,224},{1,65,129,193},{33,97,161,225},{2,66,130..., dimensions={0} | all-to-all | bytes 655360 | tf_op jit(solution)/shard_map/all_to_all | solution.py:628
  109.6 4.0 %collective-permute-start.13 = (f32[4,1,4,40,128]{4,3,2,1,0:T(8,128)S(1)}, f32[4,1,4,40,128]{4,3,2,1,0:T(8,128)S(1)}, u32[]{:S(2)}, u32[]{:S(2)}) collective-permute-start(f32[4,1,4,40,128]{4,3,2,1,0:T(8,128)S(1)} %all_to_all.34.refs_0_), channel_id=1, source_target_pairs={{0,32},{32,0},{64,96},{96,64},{128,160},{160,128},{192,224},{224,1... | collective-permute-start | bytes 983048 | tf_op jit(solution)/shard_map/ppermute | solution.py:629
  113.6 1.3 collective-permute-done.13.refs_1_
  114.8 3.8 %shard_map.61 = (f32[32,128]{1,0:T(8,128)S(1)}, f32[48,40,128]{2,1,0:T(8,128)S(1)}, f32[48,40,128]{2,1,0:T(8,128)S(1)}, f32[8,24,128]{2,1,0:T(8,128)S(1)}) custom-call(s32[3]{0:T(128)S(1)} %copy-done, f32[4,1,4,40,128]{4,3,2,1,0:T(8,128)S(1)} %all_to_all.34.refs_0_, f32[4,1,4,40,128]{4,3,2,1,0:T(8,128)S(1)} %collective-permute-done.13.refs_1_, ...), custom_call_target="tpu_custom_call" | custom-call | tf_op jit(solution)/shard_map/pallas_call | solution.py:540
  118.6 11.8 %all_to_all.35 = f32[32,1,128]{2,1,0:T(1,128)S(1)} all-to-all(f32[32,1,128]{2,1,0:T(1,128)S(1)} %bitcast.37), channel_id=1, replica_groups=mesh['slow'=8,'fast'=32] {'fast'}, dimensions={0} | all-to-all | bytes 32768 | tf_op jit(solution)/shard_map/all_to_all | solution.py:644
  130.4 3.0 %shard_map.62 = f32[8,16,256]{2,1,0:T(8,128)} custom-call(s32[3]{0:T(128)S(1)} %copy-done, f32[32,128]{1,0:T(8,128)S(1)} %bitcast.35, f32[48,40,128]{2,1,0:T(8,128)S(1)} %get-tuple-element.69.refs_1_, f32[48,40,128]{2,1,0:T(8,128)S(1)} %get-tuple-element.70.refs_2_, f32[48,40,128]{2,1,0:T(8,128)S(1)} %get-tuple-element.52.refs_3_.refs_2_, ...), custom_call_target="tpu_custom_call" | custom-call | tf_op jit(solution)/shard_map/pallas_call | solution.py:540
  (33 shorter events, 0.4 us)
Async XLA Ops:
  2.0 15.8 %collective-permute-start.1 = (f32[76,8,128]{2,1,0:T(8,128)S(1)}, f32[76,8,128]{2,1,0:T(8,128)S(1)}, u32[]{:S(2)}, u32[]{:S(2)}) collective-permute-start(f32[76,8,128]{2,1,0:T(8,128)S(1)} %get-tuple-element.42.refs_1_.refs_10_), channel_id=1, source_target_pairs={{0,31},{1,2},{2,1},{3,4},{4,3},{5,6},{6,5},{7,8},{8,7},{9,10},{10,... | collective-permute-start | bytes 933896 | tf_op jit(solution)/shard_map/ppermute | solution.py:561
  10.7 7.9 %collective-permute-start = (f32[76,8,128]{2,1,0:T(8,128)S(1)}, f32[76,8,128]{2,1,0:T(8,128)S(1)}, u32[]{:S(2)}, u32[]{:S(2)}) collective-permute-start(f32[76,8,128]{2,1,0:T(8,128)S(1)} %get-tuple-element.42.refs_1_.refs_10_), channel_id=1, source_target_pairs={{0,1},{1,0},{2,3},{3,2},{4,5},{5,4},{6,7},{7,6},{8,9},{9,8},{10,11... | collective-permute-start | bytes 933896 | tf_op jit(solution)/shard_map/ppermute | solution.py:561
  18.6 11.1 %copy-start = (s32[3]{0:T(128)S(1)}, s32[3]{0:T(128)}, u32[]{:S(2)}) copy-start(s32[3]{0:T(128)} %sweeps.11) | copy-start | bytes 40
  18.9 10.9 %collective-permute-start.3 = (f32[144,8,128]{2,1,0:T(8,128)S(1)}, f32[144,8,128]{2,1,0:T(8,128)S(1)}, u32[]{:S(2)}, u32[]{:S(2)}) collective-permute-start(f32[144,8,128]{2,1,0:T(8,128)S(1)} %get-tuple-element.79), channel_id=1, source_target_pairs={{32,0},{64,32},{96,64},{128,96},{160,128},{192,160},{224,192},{0,2... | collective-permute-start | bytes 1769480 | tf_op jit(solution)/shard_map/ppermute | solution.py:554
  20.7 9.0 %collective-permute-start.2 = (f32[144,8,128]{2,1,0:T(8,128)S(1)}, f32[144,8,128]{2,1,0:T(8,128)S(1)}, u32[]{:S(2)}, u32[]{:S(2)}) collective-permute-start(f32[144,8,128]{2,1,0:T(8,128)S(1)} %get-tuple-element.80), channel_id=1, source_target_pairs={{0,32},{32,64},{64,96},{96,128},{128,160},{160,192},{192,224},{224... | collective-permute-start | bytes 1769480 | tf_op jit(solution)/shard_map/ppermute | solution.py:554
  31.9 3.5 %collective-permute-start.4 = (f32[2,4,16,128]{3,2,1,0:T(8,128)S(1)}, f32[2,4,16,128]{3,2,1,0:T(8,128)S(1)}, u32[]{:S(2)}, u32[]{:S(2)}) collective-permute-start(f32[2,4,16,128]{3,2,1,0:T(8,128)S(1)} %get-tuple-element.46), channel_id=1, source_target_pairs={{0,1},{1,0},{2,3},{3,2},{4,5},{5,4},{6,7},{7,6},{8,9},{9,8},{10,11... | collective-permute-start | bytes 196616 | tf_op jit(solution)/shard_map/ppermute | solution.py:561
  32.0 6.5 %collective-permute-start.5 = (f32[2,4,16,128]{3,2,1,0:T(8,128)S(1)}, f32[2,4,16,128]{3,2,1,0:T(8,128)S(1)}, u32[]{:S(2)}, u32[]{:S(2)}) collective-permute-start(f32[2,4,16,128]{3,2,1,0:T(8,128)S(1)} %get-tuple-element.47), channel_id=1, source_target_pairs={{0,31},{1,2},{2,1},{3,4},{4,3},{5,6},{6,5},{7,8},{8,7},{9,10},{10,... | collective-permute-start | bytes 196616 | tf_op jit(solution)/shard_map/ppermute | solution.py:561
  49.9 6.0 %collective-permute-start.6 = (f32[4,2,4,40,128]{4,3,2,1,0:T(8,128)S(1)}, f32[4,2,4,40,128]{4,3,2,1,0:T(8,128)S(1)}, u32[]{:S(2)}, u32[]{:S(2)}) collective-permute-start(f32[4,2,4,40,128]{4,3,2,1,0:T(8,128)S(1)} %all_to_all.32.refs_0_), channel_id=1, source_target_pairs={{0,32},{32,0},{64,96},{96,64},{128,160},{160,128},{192,224},{224,1... | collective-permute-start | bytes 1966088 | tf_op jit(solution)/shard_map/ppermute | solution.py:629
  75.9 7.8 %collective-permute-start.8 = (f32[44,8,128]{2,1,0:T(8,128)S(1)}, f32[44,8,128]{2,1,0:T(8,128)S(1)}, u32[]{:S(2)}, u32[]{:S(2)}) collective-permute-start(f32[44,8,128]{2,1,0:T(8,128)S(1)} %get-tuple-element.59.refs_1_), channel_id=1, source_target_pairs={{0,31},{1,2},{2,1},{3,4},{4,3},{5,6},{6,5},{7,8},{8,7},{9,10},{10,... | collective-permute-start | bytes 540680 | tf_op jit(solution)/shard_map/ppermute | solution.py:561
  77.0 6.7 %collective-permute-start.7 = (f32[44,8,128]{2,1,0:T(8,128)S(1)}, f32[44,8,128]{2,1,0:T(8,128)S(1)}, u32[]{:S(2)}, u32[]{:S(2)}) collective-permute-start(f32[44,8,128]{2,1,0:T(8,128)S(1)} %get-tuple-element.59.refs_1_), channel_id=1, source_target_pairs={{0,1},{1,0},{2,3},{3,2},{4,5},{5,4},{6,7},{7,6},{8,9},{9,8},{10,11... | collective-permute-start | bytes 540680 | tf_op jit(solution)/shard_map/ppermute | solution.py:561
  83.9 8.3 %collective-permute-start.10 = (f32[82,8,128]{2,1,0:T(8,128)S(1)}, f32[82,8,128]{2,1,0:T(8,128)S(1)}, u32[]{:S(2)}, u32[]{:S(2)}) collective-permute-start(f32[82,8,128]{2,1,0:T(8,128)S(1)} %get-tuple-element.91), channel_id=1, source_target_pairs={{32,0},{64,32},{96,64},{128,96},{160,128},{192,160},{224,192},{0,2... | collective-permute-start | bytes 1007624 | tf_op jit(solution)/shard_map/ppermute | solution.py:554
  86.9 5.3 %collective-permute-start.9 = (f32[82,8,128]{2,1,0:T(8,128)S(1)}, f32[82,8,128]{2,1,0:T(8,128)S(1)}, u32[]{:S(2)}, u32[]{:S(2)}) collective-permute-start(f32[82,8,128]{2,1,0:T(8,128)S(1)} %get-tuple-element.92), channel_id=1, source_target_pairs={{0,32},{32,64},{64,96},{96,128},{128,160},{160,192},{192,224},{224... | collective-permute-start | bytes 1007624 | tf_op jit(solution)/shard_map/ppermute | solution.py:554
  94.2 2.9 %collective-permute-start.11 = (f32[1,4,16,128]{3,2,1,0:T(8,128)S(1)}, f32[1,4,16,128]{3,2,1,0:T(8,128)S(1)}, u32[]{:S(2)}, u32[]{:S(2)}) collective-permute-start(f32[1,4,16,128]{3,2,1,0:T(8,128)S(1)} %get-tuple-element.61), channel_id=1, source_target_pairs={{0,1},{1,0},{2,3},{3,2},{4,5},{5,4},{6,7},{7,6},{8,9},{9,8},{10,11... | collective-permute-start | bytes 98312 | tf_op jit(solution)/shard_map/ppermute | solution.py:561
  94.3 6.2 %collective-permute-start.12 = (f32[1,4,16,128]{3,2,1,0:T(8,128)S(1)}, f32[1,4,16,128]{3,2,1,0:T(8,128)S(1)}, u32[]{:S(2)}, u32[]{:S(2)}) collective-permute-start(f32[1,4,16,128]{3,2,1,0:T(8,128)S(1)} %get-tuple-element.62), channel_id=1, source_target_pairs={{0,31},{1,2},{2,1},{3,4},{4,3},{5,6},{6,5},{7,8},{8,7},{9,10},{10,... | collective-permute-start | bytes 98312 | tf_op jit(solution)/shard_map/ppermute | solution.py:561
  109.6 5.3 %collective-permute-start.13 = (f32[4,1,4,40,128]{4,3,2,1,0:T(8,128)S(1)}, f32[4,1,4,40,128]{4,3,2,1,0:T(8,128)S(1)}, u32[]{:S(2)}, u32[]{:S(2)}) collective-permute-start(f32[4,1,4,40,128]{4,3,2,1,0:T(8,128)S(1)} %all_to_all.34.refs_0_), channel_id=1, source_target_pairs={{0,32},{32,0},{64,96},{96,64},{128,160},{160,128},{192,224},{224,1... | collective-permute-start | bytes 983048 | tf_op jit(solution)/shard_map/ppermute | solution.py:629

commit v10 on v9

--- a/solution.py
+++ b/solution.py
@@ -279,8 +279,6 @@
                 gain = k[(*p, row)]
             start = gain * rhs
             q[(*p, row)] = start
-            a[(*p, row)] = start
-            b[(*p, row)] = start
 
     for yb in range(3):
         over(1, YB - 1, YB, functools.partial(right_side, yb))
@@ -291,13 +289,21 @@
 
     @pl.when(sweeps[0] >= 4)
     def _():
-        fine_sweep(a, b, q, k, 2, 22, FINE, lanes)
+        fine_sweep(q, b, q, k, 2, 22, FINE, lanes)
+        fine_sweep(b, a, q, k, 3, 21, FINE, lanes)
+
+    @pl.when(sweeps[0] == 3)
+    def _():
+        fine_sweep(q, a, q, k, 3, 21, FINE, lanes)
 
     @pl.when(sweeps[0] >= 3)
     def _():
-        fine_sweep(b, a, q, k, 3, 21, FINE, lanes)
-
-    fine_sweep(a, epre, q, k, 4, 20, FINE, lanes, shift=4)
+        fine_sweep(a, epre, q, k, 4, 20, FINE, lanes, shift=4)
+
+    @pl.when(sweeps[0] < 3)
+    def _():
+        fine_sweep(q, epre, q, k, 4, 20, FINE, lanes, shift=4)
+
     zero = jnp.zeros((ZW, LANES), F32)
     odd = (lax.axis_index("fast") & 1) == 1
 
@@ -362,21 +368,29 @@
                 else:
                     start = (4.0 * k1[PADM + y]) * rhs
                 q1[PADM + y] = start
-                va[PADM + y] = start
-                e1[PADM + y] = start
 
     over(0, YM // 8, 4, opening)
     of_q1, of_k1 = (lambda y: q1[y]), (lambda y: k1[y])
 
+    def middle_sweep(source, target):
+        flat_sweep(source, target, of_q1, of_k1, PADM, PADM + YM, FLAT, lanes, 1)
+
     @pl.when(sweeps[1] >= 4)
     def _():
-        flat_sweep(va, e1, of_q1, of_k1, PADM, PADM + YM, FLAT, lanes, 1)
+        middle_sweep(q1, e1)
+        middle_sweep(e1, va)
+
+    @pl.when(sweeps[1] == 3)
+    def _():
+        middle_sweep(q1, va)
 
     @pl.when(sweeps[1] >= 3)
     def _():
-        flat_sweep(e1, va, of_q1, of_k1, PADM, PADM + YM, FLAT, lanes, 1)
-
-    flat_sweep(va, e1, of_q1, of_k1, PADM, PADM + YM, FLAT, lanes, 1)
+        middle_sweep(va, e1)
+
+    @pl.when(sweeps[1] < 3)
+    def _():
+        middle_sweep(q1, e1)
 
     def pair_sum(value):
         return value + jnp.where(even, pltpu.roll(value, LANES - 1, 1), pltpu.roll(value, 1, 1))
@@ -460,9 +474,11 @@
 
 def after_kernel(last, faces, sweeps, *refs):
     if last:
-        parts, e1, q1, k1, e2, epre, q, k, field, out, va, vb, a, b, halves = refs
+        parts, e1, q1, k1, e2, epre, q, k, field, out, va, vb, ab, halves = refs
     else:
-        parts, e1, q1, k1, e2, epre, q, k, field, later, pack, out, field_out, va, vb, a, b, s = refs
+        parts, e1, q1, k1, e2, epre, q, k, field, later, pack, out, field_out, va, vb, ab, s = refs
+    a, b = ab.at[0], ab.at[1]
+    begin = 1 - (sweeps[0] & 1)
     lanes = lane_iota(ZW)
     lanes_p = lane_iota(parts.shape[0])
     every = parts[...]
@@ -500,8 +516,7 @@
             y = 2 * ym + half
             for p in PARITIES:
                 raised = jnp.where(k[(*p, y + 4)] > 0.0, epre[(*p, y)] + value, 0.0)
-                a[(*p, y)] = raised
-                b[(*p, y)] = raised
+                ab[(begin, *p, y)] = raised
 
     over(0, YPOST // 2, 8, raise_fine)
 
@@ -643,7 +658,7 @@
             kept_low = got[4:]
         parts = lax.all_to_all(part, "fast", 0, 0, tiled=True)
         given = (parts, e1, q1, kept_low[0], e2, epre, q, kept_fine[0], field)
-        scratch = [(YPOST, ZW, LANES)] * 2 + [post] * 2
+        scratch = [(YPOST, ZW, LANES)] * 2 + [(2, *post)]
         kernel = functools.partial(after_kernel, not opening, faces)
         if opening:
             outs = [(pack_tiles(4), ZB, LANES), block]

time: 134 us -> 133 us (level)
  no operation moved by 1% of the time
where the time goes in v10:
time: 133 us; the launch traced here: 134 us
  blocking collectives  45.6 us (34%)
  waiting for transfers between devices  36.7 us (28%)
  starting transfers between devices  29.6 us (22%)
  Pallas kernels  21.1 us (16%)
    all_to_all x2, blocking collectives, body(): parts = lax.all_to_all(part, 'fast', 0, 0, tiled=True)  25.2 us
    pallas_call x8, Pallas kernels, call(): pl.pallas_call(kernel, out_shape=[pltpu.VMEM(s, F32) if kept else jax.Sha...  21.1 us
    all_to_all x2, blocking collectives, body(): lax.all_to_all(strip, 'slow', 0, 0, axis_index_groups=chips, tiled=True)  20.4 us
    ppermute x4, waiting for transfers between devices, swap_fast(): lax.ppermute(second, 'fast', outer)  20.3 us
    ppermute x4, starting transfers between devices, swap_fast(): lax.ppermute(second, 'fast', outer)  14.9 us
    ppermute x4, waiting for transfers between devices, both_ways(): return (lax.ppermute(to_right, axis, up), lax.ppermute(to_left, axis, down))  11.7 us
    ppermute x2, starting transfers between devices, body(): other = lax.ppermute(mine, 'slow', [(n, n ^ 1) for n in range(slow_count)])  8.22 us
    ppermute x4, starting transfers between devices, both_ways(): return (lax.ppermute(to_right, axis, up), lax.ppermute(to_left, axis, down))  6.24 us
  transfers between devices with their start and end apart: 14, of which 10 were waited for; matrix products, arithmetic and copies ran while one was open for 0% of the time, Pallas kernels for 1%

profile of v10, /device:TPU:1, one launch (start us, length us, event | category | flops | bytes accessed | tf_op | source)
XLA Modules:
  0.0 133.7 jit_solution(14660803283271944649)
XLA Ops:
  0.0 2.0 %shard_map.55 = (f32[76,8,128]{2,1,0:T(8,128)S(1)}, f32[2,2,8,8,128]{4,3,2,1,0:T(8,128)S(1)}) custom-call(f32[8,16,256]{2,1,0:T(8,128)} %observed.3, f32[8,16,256]{2,1,0:T(8,128)} %start.1, f32[8,16,256]{2,1,0:T(8,128)} %diagonal.1, f32[2,8,16,256]{3,2,1,0:T(8,128)} %noise.3), custom_call_target="tpu_custom_call" | custom-call | tf_op jit(solution)/shard_map/pallas_call | solution.py:555
  2.0 8.7 %collective-permute-start.1 = (f32[76,8,128]{2,1,0:T(8,128)S(1)}, f32[76,8,128]{2,1,0:T(8,128)S(1)}, u32[]{:S(2)}, u32[]{:S(2)}) collective-permute-start(f32[76,8,128]{2,1,0:T(8,128)S(1)} %get-tuple-element.42.refs_1_.refs_10_), channel_id=1, source_target_pairs={{0,31},{1,2},{2,1},{3,4},{4,3},{5,6},{6,5},{7,8},{8,7},{9,10},{10,... | collective-permute-start | bytes 933896 | tf_op jit(solution)/shard_map/ppermute | solution.py:576
  10.7 0.0 collective-permute-start
  10.7 7.1 %collective-permute-done.1 = f32[76,8,128]{2,1,0:T(8,128)S(1)} collective-permute-done((f32[76,8,128]{2,1,0:T(8,128)S(1)}, f32[76,8,128]{2,1,0:T(8,128)S(1)}, u32[]{:S(2)}, u32[]{:S(2)}) %collective-permute-start.1) | collective-permute-done | bytes 311328 | tf_op jit(solution)/shard_map/ppermute | solution.py:576
  17.7 0.8 collective-permute-done
  18.6 0.0 copy-start
  18.9 1.9 %collective-permute-start.3 = (f32[144,8,128]{2,1,0:T(8,128)S(1)}, f32[144,8,128]{2,1,0:T(8,128)S(1)}, u32[]{:S(2)}, u32[]{:S(2)}) collective-permute-start(f32[144,8,128]{2,1,0:T(8,128)S(1)} %get-tuple-element.79), channel_id=1, source_target_pairs={{32,0},{64,32},{96,64},{128,96},{160,128},{192,160},{224,192},{0,2... | collective-permute-start | bytes 1769480 | tf_op jit(solution)/shard_map/ppermute | solution.py:569
  20.7 1.2 collective-permute-start.2
  21.9 1.3 shard_map.56.refs_9_
  23.2 6.5 %collective-permute-done.3.refs_4_ = f32[144,8,128]{2,1,0:T(8,128)S(1)} collective-permute-done((f32[144,8,128]{2,1,0:T(8,128)S(1)}, f32[144,8,128]{2,1,0:T(8,128)S(1)}, u32[]{:S(2)}, u32[]{:S(2)}) %collective-permute-start.3) | collective-permute-done | bytes 589856 | tf_op jit(solution)/shard_map/ppermute | solution.py:569
  29.8 0.0 collective-permute-done.2.refs_3_
  29.8 0.0 copy-done
  29.8 2.5 %shard_map.57 = (f32[2,4,16,128]{3,2,1,0:T(8,128)S(1)}, f32[2,4,8,128]{3,2,1,0:T(8,128)S(1)}, f32[2,4,16,128]{3,2,1,0:T(8,128)S(1)}, f32[2,2,16,24,128]{4,3,2,1,...) custom-call(s32[3]{0:T(128)S(1)} %copy-done, ...), custom_call_target="tpu_custom_call" | custom-call | tf_op jit(solution)/shard_map/pallas_call | solution.py:555
  32.3 0.1 collective-permute-start.4
  32.4 3.4 %collective-permute-start.5 = (f32[2,4,16,128]{3,2,1,0:T(8,128)S(1)}, f32[2,4,16,128]{3,2,1,0:T(8,128)S(1)}, u32[]{:S(2)}, u32[]{:S(2)}) collective-permute-start(f32[2,4,16,128]{3,2,1,0:T(8,128)S(1)} %get-tuple-element.47), channel_id=1, source_target_pairs={{0,31},{1,2},{2,1},{3,4},{4,3},{5,6},{6,5},{7,8},{8,7},{9,10},{10,... | collective-permute-start | bytes 196616 | tf_op jit(solution)/shard_map/ppermute | solution.py:576
  35.8 0.0 collective-permute-done.4
  35.8 3.1 %collective-permute-done.5 = f32[2,4,16,128]{3,2,1,0:T(8,128)S(1)} collective-permute-done((f32[2,4,16,128]{3,2,1,0:T(8,128)S(1)}, f32[2,4,16,128]{3,2,1,0:T(8,128)S(1)}, u32[]{:S(2)}, u32[]{:S(2)}) %collective-permute-start.5) | collective-permute-done | bytes 65568 | tf_op jit(solution)/shard_map/ppermute | solution.py:576
  39.0 11.3 %all_to_all.32.refs_0_ = f32[4,2,4,40,128]{4,3,2,1,0:T(8,128)S(1)} all-to-all(f32[4,2,4,40,128]{4,3,2,1,0:T(8,128)S(1)} %broadcast_in_dim.6), channel_id=1, replica_groups={{0,64,128,192},{32,96,160,224},{1,65,129,193},{33,97,161,225},{2,66,130..., dimensions={0} | all-to-all | bytes 1310720 | tf_op jit(solution)/shard_map/all_to_all | solution.py:643
  50.3 4.2 %collective-permute-start.6 = (f32[4,2,4,40,128]{4,3,2,1,0:T(8,128)S(1)}, f32[4,2,4,40,128]{4,3,2,1,0:T(8,128)S(1)}, u32[]{:S(2)}, u32[]{:S(2)}) collective-permute-start(f32[4,2,4,40,128]{4,3,2,1,0:T(8,128)S(1)} %all_to_all.32.refs_0_), channel_id=1, source_target_pairs={{0,32},{32,0},{64,96},{96,64},{128,160},{160,128},{192,224},{224,1... | collective-permute-start | bytes 1966088 | tf_op jit(solution)/shard_map/ppermute | solution.py:644
  54.6 1.7 %collective-permute-done.6.refs_1_ = f32[4,2,4,40,128]{4,3,2,1,0:T(8,128)S(1)} collective-permute-done((f32[4,2,4,40,128]{4,3,2,1,0:T(8,128)S(1)}, f32[4,2,4,40,128]{4,3,2,1,0:T(8,128)S(1)}, u32[]{:S(2)}, u32[]{:S(2)}) %collective-permute-start.6) | collective-permute-done | bytes 655392 | tf_op jit(solution)/shard_map/ppermute | solution.py:644
  56.3 3.9 %shard_map.58 = (f32[32,128]{1,0:T(8,128)S(1)}, f32[48,40,128]{2,1,0:T(8,128)S(1)}, f32[48,40,128]{2,1,0:T(8,128)S(1)}, f32[8,24,128]{2,1,0:T(8,128)S(1)}, f32[4...) custom-call(s32[3]{0:T(128)S(1)} %copy-done, ...), custom_call_target="tpu_custom_call" | custom-call | tf_op jit(solution)/shard_map/pallas_call | solution.py:555
  60.2 13.4 %all_to_all.33 = f32[32,1,128]{2,1,0:T(1,128)S(1)} all-to-all(f32[32,1,128]{2,1,0:T(1,128)S(1)} %bitcast.36), channel_id=1, replica_groups=mesh['slow'=8,'fast'=32] {'fast'}, dimensions={0} | all-to-all | bytes 32768 | tf_op jit(solution)/shard_map/all_to_all | solution.py:659
  73.6 2.6 %shard_map.59 = (f32[44,8,128]{2,1,0:T(8,128)S(1)}, f32[2,2,8,8,128]{4,3,2,1,0:T(8,128)S(1)}) custom-call(s32[3]{0:T(128)S(1)} %copy-done, f32[32,128]{1,0:T(8,128)S(1)} %bitcast.34, f32[48,40,128]{2,1,0:T(8,128)S(1)} %get-tuple-element.50.refs_1_, f32[48,40,128]{2,1,0:T(8,128)S(1)} %get-tuple-element.51.refs_2_, ...), custom_call_target="tpu_custom_call" | custom-call | tf_op jit(solution)/shard_map/pallas_call | solution.py:555
  76.2 1.0 collective-permute-start.8
  77.2 0.0 collective-permute-start.7
  77.2 6.7 %collective-permute-done.8 = f32[44,8,128]{2,1,0:T(8,128)S(1)} collective-permute-done((f32[44,8,128]{2,1,0:T(8,128)S(1)}, f32[44,8,128]{2,1,0:T(8,128)S(1)}, u32[]{:S(2)}, u32[]{:S(2)}) %collective-permute-start.8) | collective-permute-done | bytes 180256 | tf_op jit(solution)/shard_map/ppermute | solution.py:576
  83.9 0.0 collective-permute-done.7
  84.1 3.0 %collective-permute-start.10 = (f32[82,8,128]{2,1,0:T(8,128)S(1)}, f32[82,8,128]{2,1,0:T(8,128)S(1)}, u32[]{:S(2)}, u32[]{:S(2)}) collective-permute-start(f32[82,8,128]{2,1,0:T(8,128)S(1)} %get-tuple-element.91), channel_id=1, source_target_pairs={{32,0},{64,32},{96,64},{128,96},{160,128},{192,160},{224,192},{0,2... | collective-permute-start | bytes 1007624 | tf_op jit(solution)/shard_map/ppermute | solution.py:569
  87.1 0.2 collective-permute-start.9
  87.3 5.1 %collective-permute-done.10.refs_4_ = f32[82,8,128]{2,1,0:T(8,128)S(1)} collective-permute-done((f32[82,8,128]{2,1,0:T(8,128)S(1)}, f32[82,8,128]{2,1,0:T(8,128)S(1)}, u32[]{:S(2)}, u32[]{:S(2)}) %collective-permute-start.10) | collective-permute-done | bytes 335904 | tf_op jit(solution)/shard_map/ppermute | solution.py:569
  92.4 0.0 collective-permute-done.9.refs_3_
  92.4 2.3 %shard_map.60 = (f32[1,4,16,128]{3,2,1,0:T(8,128)S(1)}, f32[1,4,8,128]{3,2,1,0:T(8,128)S(1)}, f32[1,4,16,128]{3,2,1,0:T(8,128)S(1)}, f32[2,2,16,24,128]{4,3,2,1,0:T(8,128)S(1)}, f32[2,2,24,24,128]{4,3,2,1,0:T(8,128)S(1)}) custom-call(s32[3]{0:T(128)S(1)} %copy-done, f32[44,8,128]{2,1,0:T(8,128)S(1)} %get-tuple-element.78.refs_0_, ...), custom_call_target="tpu_custom_call" | custom-call | tf_op jit(solution)/shard_map/pallas_call | solution.py:555
  94.8 0.1 collective-permute-start.11
  94.9 1.8 %collective-permute-start.12 = (f32[1,4,16,128]{3,2,1,0:T(8,128)S(1)}, f32[1,4,16,128]{3,2,1,0:T(8,128)S(1)}, u32[]{:S(2)}, u32[]{:S(2)}) collective-permute-start(f32[1,4,16,128]{3,2,1,0:T(8,128)S(1)} %get-tuple-element.62), channel_id=1, source_target_pairs={{0,31},{1,2},{2,1},{3,4},{4,3},{5,6},{6,5},{7,8},{8,7},{9,10},{10,... | collective-permute-start | bytes 98312 | tf_op jit(solution)/shard_map/ppermute | solution.py:576
  96.7 0.9 collective-permute-done.11
  97.6 3.4 %collective-permute-done.12 = f32[1,4,16,128]{3,2,1,0:T(8,128)S(1)} collective-permute-done((f32[1,4,16,128]{3,2,1,0:T(8,128)S(1)}, f32[1,4,16,128]{3,2,1,0:T(8,128)S(1)}, u32[]{:S(2)}, u32[]{:S(2)}) %collective-permute-start.12) | collective-permute-done | bytes 32800 | tf_op jit(solution)/shard_map/ppermute | solution.py:576
  101.1 9.1 %all_to_all.34.refs_0_ = f32[4,1,4,40,128]{4,3,2,1,0:T(8,128)S(1)} all-to-all(f32[4,1,4,40,128]{4,3,2,1,0:T(8,128)S(1)} %broadcast_in_dim.16), channel_id=1, replica_groups={{0,64,128,192},{32,96,160,224},{1,65,129,193},{33,97,161,225},{2,66,130..., dimensions={0} | all-to-all | bytes 655360 | tf_op jit(solution)/shard_map/all_to_all | solution.py:643
  110.2 4.0 %collective-permute-start.13 = (f32[4,1,4,40,128]{4,3,2,1,0:T(8,128)S(1)}, f32[4,1,4,40,128]{4,3,2,1,0:T(8,128)S(1)}, u32[]{:S(2)}, u32[]{:S(2)}) collective-permute-start(f32[4,1,4,40,128]{4,3,2,1,0:T(8,128)S(1)} %all_to_all.34.refs_0_), channel_id=1, source_target_pairs={{0,32},{32,0},{64,96},{96,64},{128,160},{160,128},{192,224},{224,1... | collective-permute-start | bytes 983048 | tf_op jit(solution)/shard_map/ppermute | solution.py:644
  114.2 1.3 collective-permute-done.13.refs_1_
  115.4 3.3 %shard_map.61 = (f32[32,128]{1,0:T(8,128)S(1)}, f32[48,40,128]{2,1,0:T(8,128)S(1)}, f32[48,40,128]{2,1,0:T(8,128)S(1)}, f32[8,24,128]{2,1,0:T(8,128)S(1)}) custom-call(s32[3]{0:T(128)S(1)} %copy-done, f32[4,1,4,40,128]{4,3,2,1,0:T(8,128)S(1)} %all_to_all.34.refs_0_, f32[4,1,4,40,128]{4,3,2,1,0:T(8,128)S(1)} %collective-permute-done.13.refs_1_, ...), custom_call_target="tpu_custom_call" | custom-call | tf_op jit(solution)/shard_map/pallas_call | solution.py:555
  118.7 11.8 %all_to_all.35 = f32[32,1,128]{2,1,0:T(1,128)S(1)} all-to-all(f32[32,1,128]{2,1,0:T(1,128)S(1)} %bitcast.37), channel_id=1, replica_groups=mesh['slow'=8,'fast'=32] {'fast'}, dimensions={0} | all-to-all | bytes 32768 | tf_op jit(solution)/shard_map/all_to_all | solution.py:659
  130.5 3.2 %shard_map.62 = f32[8,16,256]{2,1,0:T(8,128)} custom-call(s32[3]{0:T(128)S(1)} %copy-done, f32[32,128]{1,0:T(8,128)S(1)} %bitcast.35, f32[48,40,128]{2,1,0:T(8,128)S(1)} %get-tuple-element.69.refs_1_, f32[48,40,128]{2,1,0:T(8,128)S(1)} %get-tuple-element.70.refs_2_, f32[48,40,128]{2,1,0:T(8,128)S(1)} %get-tuple-element.52.refs_3_.refs_2_, ...), custom_call_target="tpu_custom_call" | custom-call | tf_op jit(solution)/shard_map/pallas_call | solution.py:555
  (33 shorter events, 0.4 us)
Async XLA Ops:
  2.0 15.8 %collective-permute-start.1 = (f32[76,8,128]{2,1,0:T(8,128)S(1)}, f32[76,8,128]{2,1,0:T(8,128)S(1)}, u32[]{:S(2)}, u32[]{:S(2)}) collective-permute-start(f32[76,8,128]{2,1,0:T(8,128)S(1)} %get-tuple-element.42.refs_1_.refs_10_), channel_id=1, source_target_pairs={{0,31},{1,2},{2,1},{3,4},{4,3},{5,6},{6,5},{7,8},{8,7},{9,10},{10,... | collective-permute-start | bytes 933896 | tf_op jit(solution)/shard_map/ppermute | solution.py:576
  10.7 7.9 %collective-permute-start = (f32[76,8,128]{2,1,0:T(8,128)S(1)}, f32[76,8,128]{2,1,0:T(8,128)S(1)}, u32[]{:S(2)}, u32[]{:S(2)}) collective-permute-start(f32[76,8,128]{2,1,0:T(8,128)S(1)} %get-tuple-element.42.refs_1_.refs_10_), channel_id=1, source_target_pairs={{0,1},{1,0},{2,3},{3,2},{4,5},{5,4},{6,7},{7,6},{8,9},{9,8},{10,11... | collective-permute-start | bytes 933896 | tf_op jit(solution)/shard_map/ppermute | solution.py:576
  18.6 11.1 %copy-start = (s32[3]{0:T(128)S(1)}, s32[3]{0:T(128)}, u32[]{:S(2)}) copy-start(s32[3]{0:T(128)} %sweeps.11) | copy-start | bytes 40
  18.9 10.9 %collective-permute-start.3 = (f32[144,8,128]{2,1,0:T(8,128)S(1)}, f32[144,8,128]{2,1,0:T(8,128)S(1)}, u32[]{:S(2)}, u32[]{:S(2)}) collective-permute-start(f32[144,8,128]{2,1,0:T(8,128)S(1)} %get-tuple-element.79), channel_id=1, source_target_pairs={{32,0},{64,32},{96,64},{128,96},{160,128},{192,160},{224,192},{0,2... | collective-permute-start | bytes 1769480 | tf_op jit(solution)/shard_map/ppermute | solution.py:569
  20.7 9.0 %collective-permute-start.2 = (f32[144,8,128]{2,1,0:T(8,128)S(1)}, f32[144,8,128]{2,1,0:T(8,128)S(1)}, u32[]{:S(2)}, u32[]{:S(2)}) collective-permute-start(f32[144,8,128]{2,1,0:T(8,128)S(1)} %get-tuple-element.80), channel_id=1, source_target_pairs={{0,32},{32,64},{64,96},{96,128},{128,160},{160,192},{192,224},{224... | collective-permute-start | bytes 1769480 | tf_op jit(solution)/shard_map/ppermute | solution.py:569
  32.3 3.5 %collective-permute-start.4 = (f32[2,4,16,128]{3,2,1,0:T(8,128)S(1)}, f32[2,4,16,128]{3,2,1,0:T(8,128)S(1)}, u32[]{:S(2)}, u32[]{:S(2)}) collective-permute-start(f32[2,4,16,128]{3,2,1,0:T(8,128)S(1)} %get-tuple-element.46), channel_id=1, source_target_pairs={{0,1},{1,0},{2,3},{3,2},{4,5},{5,4},{6,7},{7,6},{8,9},{9,8},{10,11... | collective-permute-start | bytes 196616 | tf_op jit(solution)/shard_map/ppermute | solution.py:576
  32.4 6.5 %collective-permute-start.5 = (f32[2,4,16,128]{3,2,1,0:T(8,128)S(1)}, f32[2,4,16,128]{3,2,1,0:T(8,128)S(1)}, u32[]{:S(2)}, u32[]{:S(2)}) collective-permute-start(f32[2,4,16,128]{3,2,1,0:T(8,128)S(1)} %get-tuple-element.47), channel_id=1, source_target_pairs={{0,31},{1,2},{2,1},{3,4},{4,3},{5,6},{6,5},{7,8},{8,7},{9,10},{10,... | collective-permute-start | bytes 196616 | tf_op jit(solution)/shard_map/ppermute | solution.py:576
  50.3 6.0 %collective-permute-start.6 = (f32[4,2,4,40,128]{4,3,2,1,0:T(8,128)S(1)}, f32[4,2,4,40,128]{4,3,2,1,0:T(8,128)S(1)}, u32[]{:S(2)}, u32[]{:S(2)}) collective-permute-start(f32[4,2,4,40,128]{4,3,2,1,0:T(8,128)S(1)} %all_to_all.32.refs_0_), channel_id=1, source_target_pairs={{0,32},{32,0},{64,96},{96,64},{128,160},{160,128},{192,224},{224,1... | collective-permute-start | bytes 1966088 | tf_op jit(solution)/shard_map/ppermute | solution.py:644
  76.2 7.8 %collective-permute-start.8 = (f32[44,8,128]{2,1,0:T(8,128)S(1)}, f32[44,8,128]{2,1,0:T(8,128)S(1)}, u32[]{:S(2)}, u32[]{:S(2)}) collective-permute-start(f32[44,8,128]{2,1,0:T(8,128)S(1)} %get-tuple-element.59.refs_1_), channel_id=1, source_target_pairs={{0,31},{1,2},{2,1},{3,4},{4,3},{5,6},{6,5},{7,8},{8,7},{9,10},{10,... | collective-permute-start | bytes 540680 | tf_op jit(solution)/shard_map/ppermute | solution.py:576
  77.2 6.7 %collective-permute-start.7 = (f32[44,8,128]{2,1,0:T(8,128)S(1)}, f32[44,8,128]{2,1,0:T(8,128)S(1)}, u32[]{:S(2)}, u32[]{:S(2)}) collective-permute-start(f32[44,8,128]{2,1,0:T(8,128)S(1)} %get-tuple-element.59.refs_1_), channel_id=1, source_target_pairs={{0,1},{1,0},{2,3},{3,2},{4,5},{5,4},{6,7},{7,6},{8,9},{9,8},{10,11... | collective-permute-start | bytes 540680 | tf_op jit(solution)/shard_map/ppermute | solution.py:576
  84.1 8.3 %collective-permute-start.10 = (f32[82,8,128]{2,1,0:T(8,128)S(1)}, f32[82,8,128]{2,1,0:T(8,128)S(1)}, u32[]{:S(2)}, u32[]{:S(2)}) collective-permute-start(f32[82,8,128]{2,1,0:T(8,128)S(1)} %get-tuple-element.91), channel_id=1, source_target_pairs={{32,0},{64,32},{96,64},{128,96},{160,128},{192,160},{224,192},{0,2... | collective-permute-start | bytes 1007624 | tf_op jit(solution)/shard_map/ppermute | solution.py:569
  87.1 5.3 %collective-permute-start.9 = (f32[82,8,128]{2,1,0:T(8,128)S(1)}, f32[82,8,128]{2,1,0:T(8,128)S(1)}, u32[]{:S(2)}, u32[]{:S(2)}) collective-permute-start(f32[82,8,128]{2,1,0:T(8,128)S(1)} %get-tuple-element.92), channel_id=1, source_target_pairs={{0,32},{32,64},{64,96},{96,128},{128,160},{160,192},{192,224},{224... | collective-permute-start | bytes 1007624 | tf_op jit(solution)/shard_map/ppermute | solution.py:569
  94.8 2.9 %collective-permute-start.11 = (f32[1,4,16,128]{3,2,1,0:T(8,128)S(1)}, f32[1,4,16,128]{3,2,1,0:T(8,128)S(1)}, u32[]{:S(2)}, u32[]{:S(2)}) collective-permute-start(f32[1,4,16,128]{3,2,1,0:T(8,128)S(1)} %get-tuple-element.61), channel_id=1, source_target_pairs={{0,1},{1,0},{2,3},{3,2},{4,5},{5,4},{6,7},{7,6},{8,9},{9,8},{10,11... | collective-permute-start | bytes 98312 | tf_op jit(solution)/shard_map/ppermute | solution.py:576
  94.9 6.2 %collective-permute-start.12 = (f32[1,4,16,128]{3,2,1,0:T(8,128)S(1)}, f32[1,4,16,128]{3,2,1,0:T(8,128)S(1)}, u32[]{:S(2)}, u32[]{:S(2)}) collective-permute-start(f32[1,4,16,128]{3,2,1,0:T(8,128)S(1)} %get-tuple-element.62), channel_id=1, source_target_pairs={{0,31},{1,2},{2,1},{3,4},{4,3},{5,6},{6,5},{7,8},{8,7},{9,10},{10,... | collective-permute-start | bytes 98312 | tf_op jit(solution)/shard_map/ppermute | solution.py:576
  110.2 5.3 %collective-permute-start.13 = (f32[4,1,4,40,128]{4,3,2,1,0:T(8,128)S(1)}, f32[4,1,4,40,128]{4,3,2,1,0:T(8,128)S(1)}, u32[]{:S(2)}, u32[]{:S(2)}) collective-permute-start(f32[4,1,4,40,128]{4,3,2,1,0:T(8,128)S(1)} %all_to_all.34.refs_0_), channel_id=1, source_target_pairs={{0,32},{32,0},{64,96},{96,64},{128,160},{160,128},{192,224},{224,1... | collective-permute-start | bytes 983048 | tf_op jit(solution)/shard_map/ppermute | solution.py:644
